TPU v7x, 32 devices: a whole 2x2x4 slice. The times are simulated.
32 devices in a mesh: ctx: 4 (over y, x), exp: 8 (over z, core).
Axes of the slice: x: 2, y: 2, z: 4, core: 2. Of those that a mesh axis runs over, the one named last changes fastest.
Arguments:
- queries: bfloat16 [4, 256, 6144], P(None, 'ctx', 'exp'), may hold values from -6 to 6
- keys: bfloat16 [4, 256, 6144], P(None, 'ctx', 'exp'), may hold values from -6 to 6
- values: bfloat16 [4, 256, 6144], P(None, 'ctx', 'exp'), may hold values from -6 to 6
- log_decay: float32 [4, 256, 48], P(None, 'ctx', 'exp'), may hold values from -1 to 0
- norm_gain: float32 [6144], P('exp'), may hold values from 0.1 to 1.9
- router: bfloat16 [6144, 16], replicated, may hold values from -0.078125 to 0.078125
- expert_up: bfloat16 [16, 6144, 6144], P('exp', None, 'ctx'), may hold values from -0.078125 to 0.078125
- expert_down: bfloat16 [16, 6144, 6144], P('exp', 'ctx'), may hold values from -0.078125 to 0.078125
- expert_ids: int32 [256, 4, 2], P('ctx'), may hold values from 0 to 15, all different within a row; in each aligned block of 256 rows (0 to 255, 256 to 511, ..., all dimensions but the last counted through in order) at most 40 rows name the same one
Outputs:
- layer_out: bfloat16 [4, 256, 6144], P(None, 'ctx', 'exp')
Inputs may be any that keep to these rules, and one draw needn't show every extreme that they name: `expert_ids`: within each block of 256 rows (the positions of one group for all requests), no expert is named more than 40 times; the two ids of a row differ.
All inputs are finite; a program needn't handle non-finite values.
Results may differ from a plain program's by a relative error of at most 0.012.
Values may be sent and summed in bfloat16 or wider, within the bound.
No kernel may reach another device: no remote copies, remote signals or barrier semaphores. Data moves between devices by JAX's collectives and lax.ppermute only.
A program may use at most 128 MiB of HBM per device.

v0:
```python
import jax
import jax.numpy as jnp
from jax import lax
from jax.sharding import PartitionSpec as P

CAP = 40


def prefix_2(part, axis, combine, identity):
    place = lax.axis_index(axis)
    gathered = jax.tree.map(lambda a: lax.all_gather(a, axis), part)
    state = jax.tree.map(lambda a, e: jnp.zeros_like(a) + jnp.asarray(e, a.dtype), part, identity)

    def one(lap, state):
        return combine(
            state, jax.tree.map(lambda a: lax.dynamic_index_in_dim(a, lap, 0, False), gathered)
        )

    return lax.fori_loop(0, place, one, state)


def link_states(earlier, later):
    return (earlier[0] * later[0], later[0][..., None, None] * earlier[1] + later[1])


def body(queries, keys, values, log_decay, norm_gain, router, expert_up, expert_down, expert_ids):
    requests, length, features = queries.shape
    head_count = log_decay.shape[2]
    head_dim = features // head_count
    experts = router.shape[1]
    own_experts = expert_up.shape[0]
    shape4 = (requests, length, head_count, head_dim)
    query4 = queries.reshape(shape4)
    key4 = keys.reshape(shape4)
    value4 = values.reshape(shape4)
    cumulative = jnp.cumsum(log_decay, axis=1)
    last_cum = cumulative[:, -1, :]
    key_decay = key4.astype(jnp.float32) * jnp.exp(last_cum[:, None, :] - cumulative)[..., None]
    local_state = jnp.einsum(
        "bshd,bshe->bhde", key_decay, value4.astype(jnp.float32), precision=lax.Precision.HIGHEST
    )
    block_decay = jnp.exp(last_cum)
    prefix = prefix_2(
        (block_decay, local_state),
        "ctx",
        link_states,
        (jnp.ones_like(block_decay), jnp.zeros_like(local_state)),
    )
    incoming = prefix[1]
    cum_first = jnp.transpose(cumulative, (0, 2, 1))
    spread = cum_first[..., :, None] - cum_first[..., None, :]
    causal = jnp.tril(jnp.ones((length, length), dtype=bool))
    decay_mask = jnp.where(causal, jnp.exp(jnp.minimum(spread, 0.0)), 0.0)
    scores = jnp.einsum("bthd,bshd->bhts", query4, key4, preferred_element_type=jnp.float32)
    weights = (scores * decay_mask).astype(jnp.bfloat16)
    inside = jnp.einsum("bhts,bshd->bthd", weights, value4, preferred_element_type=jnp.float32)
    carried = jnp.einsum(
        "bthd,bhde->bthe", query4.astype(jnp.float32), incoming, precision=lax.Precision.HIGHEST
    )
    output = inside + jnp.exp(cumulative)[..., None] * carried
    mean_square = jnp.mean(output * output, axis=-1, keepdims=True) + 1e-05
    normed = (
        (output * lax.rsqrt(mean_square)).reshape(requests, length, features) * norm_gain
    ).astype(jnp.bfloat16)
    token_rows = jnp.transpose(normed, (1, 0, 2)).reshape(length * requests, features)
    id_rows = expert_ids.reshape(length * requests, 2)
    choice_hot = (id_rows[..., None] == jnp.arange(experts)).astype(jnp.int32)
    flat_hot = choice_hot.reshape(-1, experts)
    before = jnp.cumsum(flat_hot, axis=0) - flat_hot
    slot_index = jnp.sum(before * flat_hot, axis=1).reshape(-1, 2)
    slot_hot = (slot_index[..., None] == jnp.arange(CAP)).astype(jnp.float32)
    choice_float = choice_hot.astype(jnp.float32)
    placement = jnp.einsum("tje,tjc->cet", choice_float, slot_hot).astype(jnp.bfloat16)
    outgoing = jnp.einsum(
        "cet,td->ced", placement, token_rows, preferred_element_type=jnp.float32
    ).astype(jnp.bfloat16)
    arrived = lax.all_to_all(outgoing, "exp", split_axis=1, concat_axis=2, tiled=True)
    hidden = jax.nn.silu(
        jnp.einsum(
            "ned,edf->nef",
            lax.all_gather(arrived, "ctx", axis=0, tiled=True),
            expert_up,
            preferred_element_type=jnp.float32,
        )
    ).astype(jnp.bfloat16)
    expert_out = lax.psum_scatter(
        jnp.einsum("nef,efd->ned", hidden, expert_down, preferred_element_type=jnp.float32).astype(
            jnp.bfloat16
        ),
        "ctx",
        scatter_dimension=0,
        tiled=True,
    ).astype(jnp.float32)
    logits = jnp.einsum("ced,dx->cex", arrived, router, preferred_element_type=jnp.float32)
    first_owned = lax.axis_index("exp") * own_experts
    partner = jnp.einsum("tje,tjc,tjx->cex", choice_float, slot_hot, choice_float[:, ::-1, :])
    partner_own = lax.dynamic_slice_in_dim(partner, first_owned, own_experts, 1)
    own_hot = ((first_owned + jnp.arange(own_experts))[:, None] == jnp.arange(experts)).astype(
        jnp.float32
    )
    self_logit = jnp.sum(logits * own_hot[None], axis=-1)
    other_logit = jnp.sum(logits * partner_own, axis=-1)
    gate_weight = jax.nn.sigmoid(self_logit - other_logit)
    replies = (gate_weight[..., None] * expert_out).astype(jnp.bfloat16)
    returned = lax.all_to_all(replies, "exp", split_axis=2, concat_axis=1, tiled=True)
    combined = jnp.einsum("cet,ced->td", placement, returned, preferred_element_type=jnp.float32)
    mixed = (token_rows.astype(jnp.float32) + combined).astype(jnp.bfloat16)
    return jnp.transpose(mixed.reshape(length, requests, features), (1, 0, 2))


def solution(mesh):
    in_specs = (
        P(None, "ctx", "exp"),
        P(None, "ctx", "exp"),
        P(None, "ctx", "exp"),
        P(None, "ctx", "exp"),
        P("exp"),
        P(),
        P("exp", None, "ctx"),
        P("exp", "ctx", None),
        P("ctx", None, None),
    )
    out_specs = P(None, "ctx", "exp")
    return jax.shard_map(body, mesh=mesh, in_specs=in_specs, out_specs=out_specs, check_vma=False)
```

profile of v0, /device:TPU:0, one launch (start us, length us, event | category | flops | bytes accessed | tf_op | source)
XLA Modules:
  0.0 374.5 jit_solution(15324092064908175059)
XLA Ops:
  6.5 0.9 copy.55
  7.4 0.1 reduce_window_sum.26
  7.6 1.5 reshape.102
  9.1 0.3 convert_multiply_fusion
  9.4 2.6 fusion.9
  12.1 0.1 copy.65
  12.2 0.2 eq.70
  12.4 0.2 eq.66
  12.6 0.1 copy.56
  12.8 1.2 reduce-window.6
  13.9 0.2 slice_reduce_fusion
  14.3 0.1 eq.74
  14.5 0.3 copy.71
  14.8 1.4 fusion.1
  16.2 1.1 copy.72
  17.4 9.5 %all-gather = f32[16,1,6]{2,1,0:T(1,128)S(1)} all-gather(f32[4,1,6]{2,1,0:T(1,128)S(1)} %get-tuple-element.65), channel_id=2, replica_groups=mesh['ctx'=4,'exp'=8] {'ctx'}, dimensions={0}, use_global_device_ids=true | all-gather | bytes 480 | tf_op jit(solution)/shard_map/all_gather | solution.py:11
  26.9 58.1 %all-gather.7.cloned.1.call-done = f32[16,6,128,128]{3,2,1,0:T(8,128)} async-done(((f32[4,6,128,128]{3,2,1,0:T(8,128)}), f32[16,6,128,128]{3,2,1,0:T(8,128)}) %all-gather.7.cloned.1.call-update) | async-done | bytes 6291472 | tf_op jit(solution)/shard_map/all_gather | solution.py:11
  85.0 0.2 broadcast_in_dim.13
  85.2 1.9 fusion.3
  87.1 1.8 multiply_reduce_fusion
  88.9 0.3 fusion.16
  89.2 0.3 copy.64
  89.6 0.4 convolution_convert_fusion.2
  90.0 0.3 copy.73
  90.3 29.6 %all_to_all.36 = bf16[40,16,768]{2,0,1:T(8,128)(2,1)S(1)} all-to-all(bf16[40,16,768]{2,0,1:T(8,128)(2,1)S(1)} %copy.73), channel_id=1, replica_groups=mesh['ctx'=4,'exp'=8] {'exp'}, dimensions={1} | all-to-all | bytes 1966080 | tf_op jit(solution)/shard_map/all_to_all | solution.py:77
  119.9 0.3 copy.136
  120.2 1.5 all_to_all.29
  121.7 0.2 all-reduce.3.cloned.1.call-start
  121.9 53.6 %all-gather.5.cloned.1.call-done = bf16[160,2,6144]{2,0,1:T(8,128)(2,1)} async-done(((bf16[40,2,6144]{2,0,1:T(8,128)(2,1)}), bf16[160,2,6144]{2,0,1:T(8,128)(2,1)}) %all-gather.5.cloned.1.call-update) | async-done | bytes 3932176 | tf_op jit(solution)/shard_map/all_gather | solution.py:81
  175.6 16.2 %multiply_convert_fusion.1 = bf16[160,2,1536]{2,0,1:T(8,128)(2,1)S(1)} fusion(bf16[160,2,6144]{2,0,1:T(8,128)(2,1)} %all-gather.5.cloned.1.call-done, bf16[2,6144,1536]{2,1,0:T(8,128)(2,1)} %param.17), kind=kOutput, calls=%fused_computation.6 | convolution fusion | flops 6042255360 | bytes 42663936 | tf_op jit(solution)/shard_map/ned,edf->nef/dot_general | solution.py:79
  191.8 17.0 %fusion = bf16[160,2,6144]{2,0,1:T(8,128)(2,1)} fusion(bf16[160,2,1536]{2,0,1:T(8,128)(2,1)S(1)} %multiply_convert_fusion.1, bf16[2,1536,6144]{2,1,0:T(8,128)(2,1)} %param.18), kind=kOutput, calls=%fused_computation.3 | convolution fusion | flops 6041763840 | bytes 42663936 | tf_op jit(solution)/shard_map/nef,efd->ned/dot_general | solution.py:87
  208.8 0.3 fusion.35
  209.2 0.6 rev.3
  209.9 0.1 copy.75
  210.1 0.6 dynamic-slice.4
  211.3 0.2 convolution_bitcast_fusion.4
  211.6 0.7 fusion.46
  212.3 97.0 %all-reduce.3.cloned.1.call-done = bf16[160,2,6144]{2,0,1:T(8,128)(2,1)} async-done(((bf16[160,2,6144]{2,0,1:T(8,128)(2,1)}), bf16[160,2,6144]{2,0,1:T(8,128)(2,1)}) %all-reduce.3.cloned.1.call-update) | async-done | bytes 3932176
  309.3 2.4 multiply_convert_fusion
  311.7 6.7 %copy.78 = bf16[40,2,6144]{0,1,2:T(2,128)(2,1)S(1)} copy(bf16[40,2,6144]{2,0,1:T(8,128)(2,1)} %multiply_convert_fusion) | data formatting | bytes 1966080 | tf_op jit(solution)/shard_map/convert_element_type | solution.py:104
  318.4 5.8 %reshape.120 = bf16[8,2,30720]{2,1,0:T(2,128)(2,1)} reshape(bf16[6144,2,40]{2,1,0:T(2,128)(2,1)S(1)} %bitcast.153) | data formatting | bytes 1966080
  324.2 4.6 %all-to-all-start.1 = ((bf16[8,2,30720]{2,1,0:T(2,128)(2,1)}), bf16[8,2,30720]{2,1,0:T(2,128)(2,1)}, u32[]{:S(2)}, u32[]{:S(2)}) async-start(bf16[8,2,30720]{2,1,0:T(2,128)(2,1)} %reshape.120), calls=%async_computation.1 | async-start | bytes 1966080 | tf_op jit(solution)/shard_map/all_to_all | solution.py:105
  328.8 0.8 reshape.105
  329.7 24.5 %all-to-all-done.1 = bf16[8,2,30720]{2,1,0:T(2,128)(2,1)} async-done(((bf16[8,2,30720]{2,1,0:T(2,128)(2,1)}), bf16[8,2,30720]{2,1,0:T(2,128)(2,1)}, u32[]{:S(2)}, u32[]{:S(2)}) %all-to-all-start.1) | async-done | bytes 983072 | tf_op jit(solution)/shard_map/all_to_all | solution.py:105
  354.1 5.7 %reshape.121 = bf16[6144,2,40]{2,1,0:T(2,128)(2,1)S(1)} reshape(bf16[8,2,30720]{2,1,0:T(2,128)(2,1)} %all-to-all-done.1) | data formatting | bytes 1966080
  359.8 4.9 %copy.79 = bf16[40,2,8,768]{3,0,1,2:T(8,128)(2,1)} copy(bf16[40,2,8,768]{0,1,3,2:T(2,128)(2,1)S(1)} %bitcast.154) | data formatting | bytes 1966080 | tf_op jit(solution)/shard_map/all_to_all | solution.py:105
  364.7 2.4 fusion.5
  367.2 0.8 copy.137
  (40 shorter events, 0.9 us)
Async XLA Ops:
  6.5 2.9 copy-start
  6.5 78.5 %all-gather.7.cloned.1.call-start = ((), (), s32[]{:S(2)}) async-start(), calls=%async_computation.3 | async-start | bytes 7864320 | tf_op jit(solution)/shard_map/all_gather | solution.py:11
  9.4 2.6 copy-start.6
  12.0 163.6 %all-gather.5.cloned.1.call-start = ((), (), s32[]{:S(2)}) async-start(), calls=%async_computation.2 | async-start | bytes 4915200 | tf_op jit(solution)/shard_map/all_gather | solution.py:81
  16.2 68.8 %copy-start.3 = (bf16[40,16,256]{0,1,2:T(8,128)(2,1)}, bf16[40,16,256]{0,1,2:T(8,128)(2,1)S(1)}, u32[]{:S(2)}) copy-start(bf16[40,16,256]{0,1,2:T(8,128)(2,1)S(1)} %fusion.1) | copy-start | bytes 983044
  87.1 1.8 copy-start.5
  121.7 187.6 %all-reduce.3.cloned.1.call-start = ((), (), s32[]{:S(2)}) async-start(), calls=%async_computation.4 | async-start | bytes 7864320
  208.8 1.3 copy-start.7
  208.8 2.8 copy-start.2
  208.8 2.8 copy-start.4
  324.2 29.9 %all-to-all-start.1 = ((bf16[8,2,30720]{2,1,0:T(2,128)(2,1)}), bf16[8,2,30720]{2,1,0:T(2,128)(2,1)}, u32[]{:S(2)}, u32[]{:S(2)}) async-start(bf16[8,2,30720]{2,1,0:T(2,128)(2,1)} %reshape.120), calls=%async_computation.1 | async-start | bytes 1966080 | tf_op jit(solution)/shard_map/all_to_all | solution.py:105
  364.7 3.3 copy-start.1
Sparse Core Ops, SparseCore 0:
  12.1 72.8 all-gather.6
  121.8 53.7 all-gather.4
  208.9 100.3 all-reduce.2
where the time goes:
time: 375 us
  waiting for transfers between devices  233 us (62%)
  matrix products  44.5 us (12%)
  blocking collectives  39.1 us (10%)
  local copies, waits for them, and re-layouts  33.7 us (9%)
  between operations  14.1 us (4%)
  other arithmetic  4.94 us (1%)
  starting transfers between devices  4.87 us (1%)
    unnamed x4, waiting for transfers between devices  97.1 us
    all_gather x1, waiting for transfers between devices, prefix_2(): gathered = jax.tree.map(lambda a: lax.all_gather(a, axis), part)  58.1 us
    all_gather x1, waiting for transfers between devices, body(): lax.all_gather(arrived, 'ctx', axis=0, tiled=True)  53.6 us
    all_to_all x1, blocking collectives, body(): lax.all_to_all(outgoing, 'exp', split_axis=1, concat_axis=2, tiled=True)  29.6 us
    all_to_all x1, waiting for transfers between devices, body(): lax.all_to_all(replies, 'exp', split_axis=2, concat_axis=1, tiled=True)  24.5 us
    dot_general x1, matrix products, body(): jnp.einsum('nef,efd->ned', hidden, expert_down, preferred_element_type=jn...  17 us
    dot_general x1, matrix products, body(): jnp.einsum('ned,edf->nef', lax.all_gather(arrived, 'ctx', axis=0, tiled=T...  16.2 us
    unnamed x21, local copies, waits for them, and re-layouts  13.1 us
  transfers between devices with their start and end apart: 4, of which 4 were waited for; matrix products, arithmetic and copies ran while one was open for 2% of the time, Pallas kernels for 0%

commit v1 on v0

v1 whole, which is shorter than its diff:
```python
import functools

import jax
import jax.numpy as jnp
from jax import lax
from jax.experimental import pallas as pl
from jax.experimental.pallas import tpu as pltpu
from jax.sharding import PartitionSpec as P

CAP = 40
F32 = jnp.float32
BF16 = jnp.bfloat16
VMEM = pl.BlockSpec(memory_space=pltpu.VMEM)
SMEM = pl.BlockSpec(memory_space=pltpu.SMEM)


def params(mib, n=0):
    return pltpu.CompilerParams(
        vmem_limit_bytes=mib << 20, dimension_semantics=("arbitrary",) * n if n else None
    )


def bits_of(n):
    return [1 << b for b in range(n.bit_length() - 1)]


def swap(x, axis, n, k, keep=lambda i: True):
    return lax.ppermute(x, axis, [(i, i ^ k) for i in range(n) if keep(i)])


def dot(a, b, ca=1, cb=0, **kw):
    return lax.dot_general(a, b, (((ca,), (cb,)), ((), ())), preferred_element_type=F32, **kw)


def iota(shape, dim):
    return lax.broadcasted_iota(jnp.int32, shape, dim)


def running_sum(log_decay):
    length = log_decay.shape[0]
    tril = (iota((length, length), 0) >= iota((length, length), 1)).astype(F32)
    return dot(tril, log_decay, precision=lax.Precision.HIGHEST)


def running_sum_rows(log_decay):
    length = log_decay.shape[0]
    triu = (iota((length, length), 0) <= iota((length, length), 1)).astype(F32)
    return dot(log_decay, triu, 0, 0, precision=lax.Precision.HIGHEST)


def state_kernel(keys, values, log_decay, *states):
    requests, length, features = keys.shape
    heads = log_decay.shape[2]
    dim = features // heads
    per = requests // len(states)
    for r in range(requests):
        cum = running_sum(log_decay[r])
        fade = jnp.exp(cum[length - 1 : length, :] - cum)
        for h in range(heads):
            lanes = slice(h * dim, (h + 1) * dim)
            faded = (keys[r, :, lanes].astype(F32) * fade[:, h : h + 1]).astype(BF16)
            states[r // per][(r % per) * heads + h] = dot(faded, values[r, :, lanes], 0, 0).astype(BF16)


def inside_kernel(place, queries, keys, values, log_decay, ids, inside, placement, other):
    requests, length, features = keys.shape
    heads = log_decay.shape[2]
    dim = features // heads
    causal = iota((length, length), 0) >= iota((length, length), 1)
    for r in range(requests):
        cum = running_sum(log_decay[r])
        rows = running_sum_rows(log_decay[r])
        for h in range(heads):
            lanes = slice(h * dim, (h + 1) * dim)
            spread = cum[:, h : h + 1] - rows[h : h + 1, :]
            mask = jnp.where(causal, jnp.exp(jnp.minimum(spread, 0.0)), 0.0)
            scores = dot(queries[r, :, lanes], keys[r, :, lanes], 1, 1)
            inside[r, :, lanes] = dot((scores * mask).astype(BF16), values[r, :, lanes])
    slots, tokens = placement.shape
    experts = slots // CAP
    own = other.shape[0] // CAP
    owner = place[1]
    expert_row = iota((experts, tokens), 0)
    relative = sum((expert_row >= own * k).astype(jnp.int32) for k in range(1, experts // own))
    expert = (relative ^ owner) * own + (expert_row - relative * own)
    first, second = ids[0:1, :], ids[1:2, :]
    named = (first == expert) | (second == expert)
    row = iota((tokens, tokens), 0)
    col = iota((tokens, tokens), 1)

    def order(i):
        request = sum((i >= length * k).astype(jnp.int32) for k in range(1, requests))
        return (i - request * length) * requests + request

    earlier = (order(row) < order(col)).astype(BF16)
    before = dot(named.astype(BF16), earlier)
    code = jnp.where(named, before, -1.0).astype(BF16)
    slot_row = iota((slots, experts), 0)
    slot_expert = iota((slots, experts), 1)
    spread_rows = (slot_row >= slot_expert * CAP) & (slot_row < slot_expert * CAP + CAP)
    codes = dot(spread_rows.astype(BF16), code)
    row_of = iota((slots, tokens), 0)
    expert_of = ((row_of.astype(F32) + 0.5) * (1.0 / CAP)).astype(jnp.int32)
    taken = codes == (row_of - expert_of * CAP).astype(F32)
    placement[...] = taken.astype(BF16)
    both = (first + second).astype(F32)
    mine = jnp.sum(jnp.where(taken[: own * CAP], both, 0.0), axis=1, keepdims=True)
    me = owner * own + expert_of[: own * CAP, :1]
    other[...] = jnp.broadcast_to(mine.astype(jnp.int32) - me, other.shape)


def output_kernel(queries, inside, log_decay, gain, placement, *refs, halves):
    incoming, normed, blocks = refs[:halves], refs[halves], refs[halves + 1 : -1]
    rows = refs[-1]
    requests, length, features = queries.shape
    heads = log_decay.shape[2]
    dim = features // heads
    per = requests // halves
    for r in range(requests):
        grow = jnp.exp(running_sum(log_decay[r]))
        for h in range(heads):
            lanes = slice(h * dim, (h + 1) * dim)
            carried = dot(queries[r, :, lanes], incoming[r // per][(r % per) * heads + h])
            out = inside[r, :, lanes] + grow[:, h : h + 1] * carried
            square = jnp.mean(out * out, axis=1, keepdims=True) + 1e-05
            value = (out * lax.rsqrt(square) * gain[0:1, lanes]).astype(BF16)
            normed[r, :, lanes] = value
            rows[r * length : (r + 1) * length, lanes] = value
    routed = dot(placement[...], rows[...])
    own = blocks[0].shape[0]
    for k, block in enumerate(blocks):
        for j in range(own):
            at = (k * own + j) * CAP
            block[j] = routed[at : at + CAP].astype(BF16)


def stack_rows(refs, j):
    return jnp.concatenate([ref[j].astype(F32) for ref in refs], axis=0).astype(BF16)


def gate_kernel(place, other, router, *refs):
    blocks, weight = refs[:-1], refs[-1]
    own, cap, width = blocks[0].shape
    owner = place[1]
    experts = router.shape[1]
    for j in range(own):
        logits = jnp.zeros((cap, experts), F32)
        for k, block in enumerate(blocks):
            at = pl.multiple_of((owner ^ k) * width, width)
            logits = logits + dot(block[j], router[pl.ds(at, width), :])
        col = iota((cap, experts), 1)
        mine = jnp.sum(jnp.where(col == owner * own + j, logits, 0.0), axis=1, keepdims=True)
        theirs_at = other[j * cap : (j + 1) * cap, :1]
        theirs = jnp.sum(jnp.where(col == theirs_at, logits, 0.0), axis=1, keepdims=True)
        weight[j] = jnp.broadcast_to(1.0 / (1.0 + jnp.exp(theirs - mine)), (cap, 128))


def up_kernel(place, *refs, parts, first, last):
    blocks = refs[: 2 * parts]
    left, right = refs[2 * parts], refs[2 * parts + 1]
    out = refs[-1]
    j = pl.program_id(0)
    total = dot(stack_rows(blocks[:parts], j), left[0]) + dot(stack_rows(blocks[parts:], j), right[0])
    if not first:
        total = total + refs[-2][0]
    out[0] = (total / (1.0 + jnp.exp(-total))).astype(BF16) if last else total


def up_chunk(place, chunk, left, right, weights, total, last):
    own, depth, hidden = weights.shape
    cap, width = left[0].shape[1:]
    parts = len(left)
    rows = parts * cap
    tile = hidden // 2 if hidden % 256 == 0 else hidden
    first = total is None

    def weight_spec(k):
        return pl.BlockSpec((1, width, tile), lambda j, n, at: (j, at[1] ^ k, n))

    total_spec = pl.BlockSpec((1, rows, tile), lambda j, n, at: (j, 0, n))
    return pl.pallas_call(
        functools.partial(up_kernel, parts=parts, first=first, last=last),
        grid_spec=pltpu.PrefetchScalarGridSpec(
            num_scalar_prefetch=1,
            grid=(own, hidden // tile),
            in_specs=[VMEM] * (2 * parts)
            + [weight_spec(2 * chunk), weight_spec(2 * chunk + 1)]
            + ([] if first else [total_spec]),
            out_specs=total_spec,
        ),
        out_shape=jax.ShapeDtypeStruct((own, rows, hidden), BF16 if last else F32),
        compiler_params=params(32, 2),
        cost_estimate=pl.CostEstimate(
            flops=4 * own * rows * width * hidden,
            bytes_accessed=4 * own * width * hidden,
            transcendentals=0,
        ),
        name=f"up_{chunk}",
    )(place, *left, *right, weights, weights, *([] if first else [total]))


def down_kernel(place, hidden, left, right, *outs, routes):
    for weights, sides, route in zip((left, right), (outs[:2], outs[2:]), routes):
        result = dot(hidden[0], weights[0])
        for out, members in zip(sides, route):
            for i, member in enumerate(members):
                out[i, 0] = result[member * CAP : (member + 1) * CAP].astype(BF16)


def down_chunk(place, chunk, hidden, weights, width, routes):
    own, rows, depth = hidden.shape
    parts = rows // CAP
    tile = width // 2 if width % 256 == 0 else width
    steps = width // tile

    def weight_spec(k):
        return pl.BlockSpec((1, depth, tile), lambda j, n, at: (j, 0, (at[1] ^ k) * steps + n))

    out_spec = pl.BlockSpec((parts // 2, 1, CAP, tile), lambda j, n, at: (0, j, 0, n))
    return pl.pallas_call(
        functools.partial(down_kernel, routes=routes),
        grid_spec=pltpu.PrefetchScalarGridSpec(
            num_scalar_prefetch=1,
            grid=(own, steps),
            in_specs=[
                pl.BlockSpec((1, rows, depth), lambda j, n, at: (j, 0, 0)),
                weight_spec(2 * chunk),
                weight_spec(2 * chunk + 1),
            ],
            out_specs=[out_spec] * 4,
        ),
        out_shape=[jax.ShapeDtypeStruct((parts // 2, own, CAP, width), BF16)] * 4,
        compiler_params=params(32, 2),
        cost_estimate=pl.CostEstimate(
            flops=4 * own * rows * width * depth,
            bytes_accessed=4 * own * width * depth,
            transcendentals=0,
        ),
        name=f"down_{chunk}",
    )(place, hidden, weights, weights)


def combine_kernel(normed, placement, *refs):
    blocks, out = refs[:-1], refs[-1]
    requests, length, _ = normed.shape
    own = blocks[0].shape[0]
    replies = jnp.concatenate(
        [block[j].astype(F32) for block in blocks for j in range(own)], axis=0
    ).astype(BF16)
    combined = dot(placement[...], replies, 0, 0)
    for r in range(requests):
        rows = slice(r * length, (r + 1) * length)
        out[r] = (normed[r].astype(F32) + combined[rows]).astype(BF16)


def gather_ctx(block, bits, n):
    have = {0: block}
    for bit in bits:
        have.update({rel | bit: swap(a, "ctx", n, bit) for rel, a in list(have.items())})
    return [have[rel] for rel in range(n)]


def route_of(bits, n):
    keep = [0]
    for bit in reversed(bits[1:]):
        keep = keep + [m | bit for m in keep]
    return [m | bits[0] for m in keep], keep


def reduce_ctx(sent, kept, bits, n):
    kept = kept.astype(F32)
    for step, bit in enumerate(bits):
        total = kept + swap(sent, "ctx", n, bit).astype(F32)
        if step + 1 < len(bits):
            half = total.shape[0] // 2
            kept, sent = total[:half], total[half:].astype(BF16)
    return total[0]


def body(n_ctx, n_exp, queries, keys, values, log_decay, norm_gain, router, expert_up, expert_down, expert_ids):
    requests, length, features = queries.shape
    heads = log_decay.shape[2]
    dim = features // heads
    experts = router.shape[1]
    own = expert_up.shape[0]
    tokens = requests * length
    halves = 2 if requests % 2 == 0 else 1
    pairs = requests * heads // halves
    me = lax.axis_index("ctx")
    place = jnp.stack([me, lax.axis_index("exp")]).astype(jnp.int32)
    struct = jax.ShapeDtypeStruct

    states = pl.pallas_call(
        state_kernel,
        in_specs=[VMEM] * 3,
        out_specs=[VMEM] * halves,
        out_shape=[struct((pairs, dim, dim), BF16)] * halves,
        compiler_params=params(32),
        name="local_state",
    )(keys, values, log_decay)

    block_decay = jnp.exp(jnp.sum(log_decay, axis=1)).reshape(halves, pairs, 1, 1)
    bits = bits_of(n_ctx)
    decay_total = block_decay
    decay_before = jnp.ones_like(block_decay)
    steps = []
    for bit in bits:
        upper = (me & bit) != 0
        partner_decay = swap(decay_total, "ctx", n_ctx, bit)
        steps.append((upper, decay_before, decay_total, partner_decay))
        decay_before = jnp.where(upper, decay_before * partner_decay, decay_before)
        decay_total = decay_total * partner_decay
    incoming = []
    for half in range(halves):
        total, before = states[half], jnp.zeros((), F32)
        for bit, (upper, d_before, d_total, d_partner) in zip(bits, steps):
            last = bit == bits[-1]
            partner = swap(total, "ctx", n_ctx, bit, lambda i: not last or not i & bit).astype(F32)
            before = before + jnp.where(upper, d_before[half], 0.0) * partner
            if not last:
                mine = total.astype(F32)
                total = (
                    jnp.where(upper, 1.0, d_partner[half]) * mine
                    + jnp.where(upper, d_total[half], 1.0) * partner
                ).astype(BF16)
        incoming.append(before.astype(BF16))

    ids = jnp.transpose(expert_ids, (2, 1, 0)).reshape(2, tokens)
    inside, placement, other = pl.pallas_call(
        inside_kernel,
        in_specs=[SMEM] + [VMEM] * 5,
        out_specs=[VMEM] * 3,
        out_shape=[
            struct((requests, length, features), F32),
            struct((experts * CAP, tokens), BF16),
            struct((own * CAP, 128), jnp.int32),
        ],
        compiler_params=params(32),
        name="inside_and_placement",
    )(place, queries, keys, values, log_decay, ids)

    normed, *outgoing = pl.pallas_call(
        functools.partial(output_kernel, halves=halves),
        in_specs=[VMEM] * (5 + halves),
        out_specs=[VMEM] * (1 + n_exp),
        out_shape=[struct((requests, length, features), BF16)]
        + [struct((own, CAP, features), BF16)] * n_exp,
        scratch_shapes=[pltpu.VMEM((tokens, features), BF16)],
        compiler_params=params(32),
        name="output_and_dispatch",
    )(queries, inside, log_decay, norm_gain.reshape(1, features), placement, *incoming)

    arrived = [outgoing[0]] + [swap(outgoing[k], "exp", n_exp, k) for k in range(1, n_exp)]
    weight = pl.pallas_call(
        gate_kernel,
        in_specs=[SMEM] + [VMEM] * (2 + n_exp),
        out_specs=VMEM,
        out_shape=struct((own, CAP, 128), F32),
        compiler_params=params(32),
        name="gate",
    )(place, other, router, *arrived)

    there, back = bits, bits[::-1]
    chunks = n_exp // 2
    total = None
    for chunk in range(chunks):
        left = gather_ctx(arrived[2 * chunk], there, n_ctx)
        right = gather_ctx(arrived[2 * chunk + 1], back, n_ctx)
        total = up_chunk(place, chunk, left, right, expert_up, total, chunk == chunks - 1)

    routes = (route_of(there, n_ctx), route_of(back, n_ctx))
    returned = [None] * n_exp
    for chunk in reversed(range(chunks)):
        outs = down_chunk(place, chunk, total, expert_down, features, routes)
        for side, order in enumerate((there, back)):
            k = 2 * chunk + side
            summed = reduce_ctx(outs[2 * side], outs[2 * side + 1], order, n_ctx)
            reply = (summed * weight[:, :, :1]).astype(BF16)
            returned[k] = swap(reply, "exp", n_exp, k) if k else reply

    return pl.pallas_call(
        combine_kernel,
        in_specs=[VMEM] * (2 + n_exp),
        out_specs=VMEM,
        out_shape=struct((requests, length, features), BF16),
        compiler_params=params(32),
        name="combine",
    )(normed, placement, *returned)


def solution(mesh):
    in_specs = (
        P(None, "ctx", "exp"),
        P(None, "ctx", "exp"),
        P(None, "ctx", "exp"),
        P(None, "ctx", "exp"),
        P("exp"),
        P(),
        P("exp", None, "ctx"),
        P("exp", "ctx", None),
        P("ctx", None, None),
    )
    out_specs = P(None, "ctx", "exp")
    run = functools.partial(body, mesh.shape["ctx"], mesh.shape["exp"])
    return jax.shard_map(run, mesh=mesh, in_specs=in_specs, out_specs=out_specs, check_vma=False)
```

time: 375 us -> 207 us (0.55)
  the two profiles are of different devices: /device:TPU:0 before, /device:TPU:19 now
where the time goes in v1:
time: 207 us; the launch traced here: 206 us
  starting transfers between devices  81.4 us (39%)
  Pallas kernels  59.9 us (29%)
  waiting for transfers between devices  46.2 us (22%)
  local copies, waits for them, and re-layouts  13.8 us (7%)
  other arithmetic  3.97 us (2%)
    ppermute x59, starting transfers between devices, swap(): return lax.ppermute(x, axis, [(i, i ^ k) for i in range(n) if keep(i)])  81.4 us
    ppermute x59, waiting for transfers between devices, swap(): return lax.ppermute(x, axis, [(i, i ^ k) for i in range(n) if keep(i)])  46.2 us
    pallas_call x4, Pallas kernels, down_chunk(): pl.pallas_call(functools.partial(down_kernel, routes=routes), grid_spec=p...  25.1 us
    pallas_call x4, Pallas kernels, up_chunk(): pl.pallas_call(functools.partial(up_kernel, parts=parts, first=first, las...  24.1 us
    unnamed x56, local copies, waits for them, and re-layouts  8.19 us
    pallas_call x1, Pallas kernels, body(): pl.pallas_call(inside_kernel, in_specs=[SMEM] + [VMEM] * 5, out_specs=[VM...  4.64 us
  transfers between devices with their start and end apart: 59, of which 17 were waited for; matrix products, arithmetic and copies ran while one was open for 5% of the time, Pallas kernels for 18%

profile of v1, /device:TPU:19, one launch (start us, length us, event | category | flops | bytes accessed | tf_op | source)
XLA Modules:
  0.0 206.0 jit_solution(13970395347284201433)
XLA Ops:
  2.8 1.7 local_state.1
  12.3 4.6 %inside_and_placement.1 = (f32[4,64,768]{2,1,0:T(8,128)S(1)}, bf16[640,256]{1,0:T(8,128)(2,1)S(1)}, s32[80,128]{1,0:T(8,128)S(1)}) custom-call(s32[2]{0:T(128)S(1)} %pad_add_fusion.place, bf16[4,64,768]{2,1,0:T(8,128)(2,1)S(1)} %copy-done.4, bf16[4,64,768]{2,1,0:T(8,128)(2,1)S(1)} %copy-done.1, bf16[4,64,768]{2,1,0:T(8,128)(2,1)S(1)} %copy-done.3, ...), custom_call_target="tpu_custom_call" | custom-call | tf_op jit(solution)/shard_map/inside_and_placement/pallas_call | solution.py:329
  17.2 3.2 %collective-permute-start.2 = (bf16[12,128,128]{2,1,0:T(8,128)(2,1)S(1)}, bf16[12,128,128]{2,1,0:T(8,128)(2,1)S(1)}, u32[]{:S(2)}, u32[]{:S(2)}) collective-permute-start(bf16[12,128,128]{2,1,0:T(8,128)(2,1)S(1)} %fusion.3), channel_id=1, source_target_pairs={{0,16},{8,24},{1,17},{9,25},{2,18},{10,26},{3,19},{11,27},{4,20},{... | collective-permute-start | bytes 1179656 | tf_op jit(solution)/shard_map/ppermute | solution.py:28
  20.4 2.7 %collective-permute-done.3 = bf16[12,128,128]{2,1,0:T(8,128)(2,1)S(1)} collective-permute-done((bf16[12,128,128]{2,1,0:T(8,128)(2,1)S(1)}, bf16[12,128,128]{2,1,0:T(8,128)(2,1)S(1)}, u32[]{:S(2)}, u32[]{:S(2)}) %collective-permute-start.3) | collective-permute-done | bytes 393248 | tf_op jit(solution)/shard_map/ppermute | solution.py:28
  23.3 3.2 %collective-permute-start.4 = (bf16[12,128,128]{2,1,0:T(8,128)(2,1)S(1)}, bf16[12,128,128]{2,1,0:T(8,128)(2,1)S(1)}, u32[]{:S(2)}, u32[]{:S(2)}) collective-permute-start(bf16[12,128,128]{2,1,0:T(8,128)(2,1)S(1)} %fusion.7), channel_id=1, source_target_pairs={{0,16},{8,24},{1,17},{9,25},{2,18},{10,26},{3,19},{11,27},{4,20},{... | collective-permute-start | bytes 1179656 | tf_op jit(solution)/shard_map/ppermute | solution.py:28
  27.4 8.2 %collective-permute-done.4 = bf16[12,128,128]{2,1,0:T(8,128)(2,1)S(1)} collective-permute-done((bf16[12,128,128]{2,1,0:T(8,128)(2,1)S(1)}, bf16[12,128,128]{2,1,0:T(8,128)(2,1)S(1)}, u32[]{:S(2)}, u32[]{:S(2)}) %collective-permute-start.4) | collective-permute-done | bytes 393248 | tf_op jit(solution)/shard_map/ppermute | solution.py:28
  35.9 1.8 output_and_dispatch.1
  37.9 3.9 %collective-permute-start.9 = (bf16[2,40,768]{2,1,0:T(8,128)(2,1)S(1)}, bf16[2,40,768]{2,1,0:T(8,128)(2,1)S(1)}, u32[]{:S(2)}, u32[]{:S(2)}) collective-permute-start(bf16[2,40,768]{2,1,0:T(8,128)(2,1)S(1)} %get-tuple-element.41), channel_id=1, source_target_pairs={{0,7},{1,6},{2,5},{3,4},{4,3},{5,2},{6,1},{7,0},{8,15},{9,14},{10,... | collective-permute-start | bytes 368648 | tf_op jit(solution)/shard_map/ppermute | solution.py:28
  41.8 1.9 collective-permute-start.13
  43.7 1.5 collective-permute-start.21
  45.2 4.1 %collective-permute-start.25 = (bf16[2,40,768]{2,1,0:T(8,128)(2,1)S(1)}, bf16[2,40,768]{2,1,0:T(8,128)(2,1)S(1)}, u32[]{:S(2)}, u32[]{:S(2)}) collective-permute-start(bf16[2,40,768]{2,1,0:T(8,128)(2,1)S(1)} %get-tuple-element.45), channel_id=1, source_target_pairs={{0,3},{1,2},{2,1},{3,0},{4,7},{5,6},{6,5},{7,4},{8,11},{9,10},{10,... | collective-permute-start | bytes 368648 | tf_op jit(solution)/shard_map/ppermute | solution.py:28
  49.4 8.5 %collective-permute-done.9.refs_4_.refs_7_ = bf16[2,40,768]{2,1,0:T(8,128)(2,1)S(1)} collective-permute-done((bf16[2,40,768]{2,1,0:T(8,128)(2,1)S(1)}, bf16[2,40,768]{2,1,0:T(8,128)(2,1)S(1)}, u32[]{:S(2)}, u32[]{:S(2)}) %collective-permute-start.9) | collective-permute-done | bytes 122912 | tf_op jit(solution)/shard_map/ppermute | solution.py:28
  59.3 2.2 %collective-permute-start.30 = (bf16[2,40,768]{2,1,0:T(8,128)(2,1)S(1)}, bf16[2,40,768]{2,1,0:T(8,128)(2,1)S(1)}, u32[]{:S(2)}, u32[]{:S(2)}) collective-permute-start(bf16[2,40,768]{2,1,0:T(8,128)(2,1)S(1)} %get-tuple-element.46.refs_0_), channel_id=1, source_target_pairs={{0,16},{8,24},{16,0},{24,8},{1,17},{9,25},{17,1},{25,9},{2,18},{10... | collective-permute-start | bytes 368648 | tf_op jit(solution)/shard_map/ppermute | solution.py:28
  63.0 1.3 collective-permute-start.22
  64.4 1.3 collective-permute-start.27
  65.7 1.4 collective-permute-start.31
  70.5 1.8 collective-permute-start.23
  73.6 1.5 collective-permute-start.24
  76.1 6.1 %up_0.1.refs_10_ = f32[2,160,1536]{2,1,0:T(8,128)S(1)} custom-call(s32[2]{0:T(128)S(1)} %pad_add_fusion.place, bf16[2,40,768]{2,1,0:T(8,128)(2,1)S(1)} %get-tuple-element.46.refs_0_, bf16[2,40,768]{2,1,0:T(8,128)(2,1)S(1)} %collective-permute-done.29.refs_1_, bf16[2,40,768]{2,1,0:T(8,128)(2,1)S(1)} %collective-permute-done.30.refs_2_, ...), custom_call_target="tpu_custom_call" | custom-call | flops 1509949440 | bytes 9437184 | tf_op jit(solution)/shard_map/up_0/pallas_call | solution.py:181
  82.3 1.8 collective-permute-start.15
  84.4 1.4 collective-permute-start.16
  87.0 6.0 %up_1.1.refs_10_ = f32[2,160,1536]{2,1,0:T(8,128)S(1)} custom-call(s32[2]{0:T(128)S(1)} %pad_add_fusion.place, bf16[2,40,768]{2,1,0:T(8,128)(2,1)S(1)} %collective-permute-done.21.refs_0_.refs_2_, bf16[2,40,768]{2,1,0:T(8,128)(2,1)S(1)} %collective-permute-done.22.refs_1_, bf16[2,40,768]{2,1,0:T(8,128)(2,1)S(1)} %collective-permute-done.23.refs_2_, ...), custom_call_target="tpu_custom_call" | custom-call | flops 1509949440 | bytes 9437184 | tf_op jit(solution)/shard_map/up_1/pallas_call | solution.py:181
  93.4 1.4 collective-permute-start.8
  96.0 6.0 %up_2.1.refs_10_ = f32[2,160,1536]{2,1,0:T(8,128)S(1)} custom-call(s32[2]{0:T(128)S(1)} %pad_add_fusion.place, bf16[2,40,768]{2,1,0:T(8,128)(2,1)S(1)} %collective-permute-done.13.refs_0_.refs_4_, bf16[2,40,768]{2,1,0:T(8,128)(2,1)S(1)} %collective-permute-done.14.refs_1_, bf16[2,40,768]{2,1,0:T(8,128)(2,1)S(1)} %collective-permute-done.15.refs_2_, ...), custom_call_target="tpu_custom_call" | custom-call | flops 1509949440 | bytes 9437184 | tf_op jit(solution)/shard_map/up_2/pallas_call | solution.py:181
  102.0 6.0 %up_3.1.hidden = bf16[2,160,1536]{2,1,0:T(8,128)(2,1)S(1)} custom-call(s32[2]{0:T(128)S(1)} %pad_add_fusion.place, bf16[2,40,768]{2,1,0:T(8,128)(2,1)S(1)} %collective-permute-done.5.refs_0_.refs_6_, bf16[2,40,768]{2,1,0:T(8,128)(2,1)S(1)} %collective-permute-done.6.refs_1_, bf16[2,40,768]{2,1,0:T(8,128)(2,1)S(1)} %collective-permute-done.7.refs_2_, ...), custom_call_target="tpu_custom_call" | custom-call | flops 1509949440 | bytes 9437184 | tf_op jit(solution)/shard_map/up_3/pallas_call | solution.py:181
  108.0 6.3 %down_3.1 = (bf16[2,2,40,768]{3,2,1,0:T(8,128)(2,1)S(1)}, bf16[2,2,40,768]{3,2,1,0:T(8,128)(2,1)S(1)}, bf16[2,2,40,768]{3,2,1,0:T(8,128)(2,1)S(1)}, bf16[2,2,40,768]{3,2,1,0:T(8,128)(2,1)S(1)}) custom-call(s32[2]{0:T(128)S(1)} %pad_add_fusion.place, bf16[2,160,1536]{2,1,0:T(8,128)(2,1)S(1)} %up_3.1.hidden, bf16[2,1536,6144]{2,1,0:T(8,128)(2,1)} %right.7, ...), custom_call_target="tpu_custom_call" | custom-call | flops 1509949440 | bytes 9437184 | tf_op jit(solution)/shard_map/down_3/pallas_call | solution.py:220
  114.3 6.3 %down_0.1 = (bf16[2,2,40,768]{3,2,1,0:T(8,128)(2,1)S(1)}, bf16[2,2,40,768]{3,2,1,0:T(8,128)(2,1)S(1)}, bf16[2,2,40,768]{3,2,1,0:T(8,128)(2,1)S(1)}, bf16[2,2,40,768]{3,2,1,0:T(8,128)(2,1)S(1)}) custom-call(s32[2]{0:T(128)S(1)} %pad_add_fusion.place, bf16[2,160,1536]{2,1,0:T(8,128)(2,1)S(1)} %up_3.1.hidden, bf16[2,1536,6144]{2,1,0:T(8,128)(2,1)} %right.7, ...), custom_call_target="tpu_custom_call" | custom-call | flops 1509949440 | bytes 9437184 | tf_op jit(solution)/shard_map/down_0/pallas_call | solution.py:220
  120.8 1.4 collective-permute-start.38
  122.2 6.3 %down_1.1 = (bf16[2,2,40,768]{3,2,1,0:T(8,128)(2,1)S(1)}, bf16[2,2,40,768]{3,2,1,0:T(8,128)(2,1)S(1)}, bf16[2,2,40,768]{3,2,1,0:T(8,128)(2,1)S(1)}, bf16[2,2,40,768]{3,2,1,0:T(8,128)(2,1)S(1)}) custom-call(s32[2]{0:T(128)S(1)} %pad_add_fusion.place, bf16[2,160,1536]{2,1,0:T(8,128)(2,1)S(1)} %up_3.1.hidden, bf16[2,1536,6144]{2,1,0:T(8,128)(2,1)} %right.7, ...), custom_call_target="tpu_custom_call" | custom-call | flops 1509949440 | bytes 9437184 | tf_op jit(solution)/shard_map/down_1/pallas_call | solution.py:220
  128.9 6.3 %down_2.1 = (bf16[2,2,40,768]{3,2,1,0:T(8,128)(2,1)S(1)}, bf16[2,2,40,768]{3,2,1,0:T(8,128)(2,1)S(1)}, bf16[2,2,40,768]{3,2,1,0:T(8,128)(2,1)S(1)}, bf16[2,2,40,768]{3,2,1,0:T(8,128)(2,1)S(1)}) custom-call(s32[2]{0:T(128)S(1)} %pad_add_fusion.place, bf16[2,160,1536]{2,1,0:T(8,128)(2,1)S(1)} %up_3.1.hidden, bf16[2,1536,6144]{2,1,0:T(8,128)(2,1)} %right.7, ...), custom_call_target="tpu_custom_call" | custom-call | flops 1509949440 | bytes 9437184 | tf_op jit(solution)/shard_map/down_2/pallas_call | solution.py:220
  135.2 1.3 collective-permute-start.47
  136.4 1.4 collective-permute-start.50
  138.3 1.3 collective-permute-start.36
  141.9 2.2 %collective-permute-start.39 = (bf16[1,2,40,768]{3,2,1,0:T(8,128)(2,1)S(1)}, bf16[1,2,40,768]{3,2,1,0:T(8,128)(2,1)S(1)}, u32[]{:S(2)}, u32[]{:S(2)}) collective-permute-start(bf16[1,2,40,768]{3,2,1,0:T(8,128)(2,1)S(1)} %slice.203), channel_id=1, source_target_pairs={{0,8},{8,0},{16,24},{24,16},{1,9},{9,1},{17,25},{25,17},{2,10},{10... | collective-permute-start | bytes 368648 | tf_op jit(solution)/shard_map/ppermute | solution.py:28
  144.9 1.4 collective-permute-start.42
  146.8 2.8 %collective-permute-done.36 = bf16[2,2,40,768]{3,2,1,0:T(8,128)(2,1)S(1)} collective-permute-done((bf16[2,2,40,768]{3,2,1,0:T(8,128)(2,1)S(1)}, bf16[2,2,40,768]{3,2,1,0:T(8,128)(2,1)S(1)}, u32[]{:S(2)}, u32[]{:S(2)}) %collective-permute-start.36) | collective-permute-done | bytes 245792 | tf_op jit(solution)/shard_map/ppermute | solution.py:28
  149.7 2.1 collective-permute-start.48
  155.0 2.1 collective-permute-start.54
  158.3 1.7 copy.27.router
  162.4 1.8 fusion.10
  164.2 11.3 %collective-permute-start.40 = (bf16[2,40,768]{2,1,0:T(8,128)(2,1)S(1)}, bf16[2,40,768]{2,1,0:T(8,128)(2,1)S(1)}, u32[]{:S(2)}, u32[]{:S(2)}) collective-permute-start(bf16[2,40,768]{2,1,0:T(8,128)(2,1)S(1)} %get-tuple-element.68), channel_id=1, source_target_pairs={{0,1},{1,0},{2,3},{3,2},{4,5},{5,4},{6,7},{7,6},{8,9},{9,8},{10,11... | collective-permute-start | bytes 368648 | tf_op jit(solution)/shard_map/ppermute | solution.py:28
  175.5 4.3 %collective-permute-start.43 = (bf16[2,40,768]{2,1,0:T(8,128)(2,1)S(1)}, bf16[2,40,768]{2,1,0:T(8,128)(2,1)S(1)}, u32[]{:S(2)}, u32[]{:S(2)}) collective-permute-start(bf16[2,40,768]{2,1,0:T(8,128)(2,1)S(1)} %get-tuple-element.69), channel_id=1, source_target_pairs={{0,2},{1,3},{2,0},{3,1},{4,6},{5,7},{6,4},{7,5},{8,10},{9,11},{10,... | collective-permute-start | bytes 368648 | tf_op jit(solution)/shard_map/ppermute | solution.py:28
  180.1 2.7 %collective-permute-start.52 = (bf16[2,40,768]{2,1,0:T(8,128)(2,1)S(1)}, bf16[2,40,768]{2,1,0:T(8,128)(2,1)S(1)}, u32[]{:S(2)}, u32[]{:S(2)}) collective-permute-start(bf16[2,40,768]{2,1,0:T(8,128)(2,1)S(1)} %get-tuple-element.72), channel_id=1, source_target_pairs={{0,5},{1,4},{2,7},{3,6},{4,1},{5,0},{6,3},{7,2},{8,13},{9,12},{10,... | collective-permute-start | bytes 368648 | tf_op jit(solution)/shard_map/ppermute | solution.py:28
  183.4 3.5 %collective-permute-start.58 = (bf16[2,40,768]{2,1,0:T(8,128)(2,1)S(1)}, bf16[2,40,768]{2,1,0:T(8,128)(2,1)S(1)}, u32[]{:S(2)}, u32[]{:S(2)}) collective-permute-start(bf16[2,40,768]{2,1,0:T(8,128)(2,1)S(1)} %get-tuple-element.67), channel_id=1, source_target_pairs={{0,7},{1,6},{2,5},{3,4},{4,3},{5,2},{6,1},{7,0},{8,15},{9,14},{10,... | collective-permute-start | bytes 368648 | tf_op jit(solution)/shard_map/ppermute | solution.py:28
  187.3 9.0 %collective-permute-done.52.refs_5_ = bf16[2,40,768]{2,1,0:T(8,128)(2,1)S(1)} collective-permute-done((bf16[2,40,768]{2,1,0:T(8,128)(2,1)S(1)}, bf16[2,40,768]{2,1,0:T(8,128)(2,1)S(1)}, u32[]{:S(2)}, u32[]{:S(2)}) %collective-permute-start.52) | collective-permute-done | bytes 122912 | tf_op jit(solution)/shard_map/ppermute | solution.py:28
  196.3 5.5 %collective-permute-done.55.refs_6_ = bf16[2,40,768]{2,1,0:T(8,128)(2,1)S(1)} collective-permute-done((bf16[2,40,768]{2,1,0:T(8,128)(2,1)S(1)}, bf16[2,40,768]{2,1,0:T(8,128)(2,1)S(1)}, u32[]{:S(2)}, u32[]{:S(2)}) %collective-permute-start.55) | collective-permute-done | bytes 122912 | tf_op jit(solution)/shard_map/ppermute | solution.py:28
  201.8 2.9 %collective-permute-done.58.refs_7_ = bf16[2,40,768]{2,1,0:T(8,128)(2,1)S(1)} collective-permute-done((bf16[2,40,768]{2,1,0:T(8,128)(2,1)S(1)}, bf16[2,40,768]{2,1,0:T(8,128)(2,1)S(1)}, u32[]{:S(2)}, u32[]{:S(2)}) %collective-permute-start.58) | collective-permute-done | bytes 122912 | tf_op jit(solution)/shard_map/ppermute | solution.py:28
  204.7 1.3 combine.1
  (177 shorter events, 37.1 us)
Async XLA Ops:
  4.6 12.4 %collective-permute-start = (bf16[12,128,128]{2,1,0:T(8,128)(2,1)S(1)}, bf16[12,128,128]{2,1,0:T(8,128)(2,1)S(1)}, u32[]{:S(2)}, u32[]{:S(2)}) collective-permute-start(bf16[12,128,128]{2,1,0:T(8,128)(2,1)S(1)} %get-tuple-element.37), channel_id=1, source_target_pairs={{0,8},{8,0},{16,24},{24,16},{1,9},{9,1},{17,25},{25,17},{2,10},{10... | collective-permute-start | bytes 1179656 | tf_op jit(solution)/shard_map/ppermute | solution.py:28
  5.9 11.1 %collective-permute-start.1 = (f32[2,12,1,1]{1,0,3,2:T(2,128)S(1)}, f32[2,12,1,1]{1,0,3,2:T(2,128)S(1)}, u32[]{:S(2)}, u32[]{:S(2)}) collective-permute-start(f32[2,12,1,1]{1,0,3,2:T(2,128)S(1)} %exp.14), channel_id=1, source_target_pairs={{0,8},{8,0},{16,24},{24,16},{1,9},{9,1},{17,25},{25,17},{2,10},{10... | collective-permute-start | bytes 296 | tf_op jit(solution)/shard_map/ppermute | solution.py:28
  7.1 16.0 %collective-permute-start.3 = (bf16[12,128,128]{2,1,0:T(8,128)(2,1)S(1)}, bf16[12,128,128]{2,1,0:T(8,128)(2,1)S(1)}, u32[]{:S(2)}, u32[]{:S(2)}) collective-permute-start(bf16[12,128,128]{2,1,0:T(8,128)(2,1)S(1)} %get-tuple-element.38), channel_id=1, source_target_pairs={{0,8},{8,0},{16,24},{24,16},{1,9},{9,1},{17,25},{25,17},{2,10},{10... | collective-permute-start | bytes 1179656 | tf_op jit(solution)/shard_map/ppermute | solution.py:28
  17.2 10.0 %collective-permute-start.2 = (bf16[12,128,128]{2,1,0:T(8,128)(2,1)S(1)}, bf16[12,128,128]{2,1,0:T(8,128)(2,1)S(1)}, u32[]{:S(2)}, u32[]{:S(2)}) collective-permute-start(bf16[12,128,128]{2,1,0:T(8,128)(2,1)S(1)} %fusion.3), channel_id=1, source_target_pairs={{0,16},{8,24},{1,17},{9,25},{2,18},{10,26},{3,19},{11,27},{4,20},{... | collective-permute-start | bytes 1179656 | tf_op jit(solution)/shard_map/ppermute | solution.py:28
  23.3 12.4 %collective-permute-start.4 = (bf16[12,128,128]{2,1,0:T(8,128)(2,1)S(1)}, bf16[12,128,128]{2,1,0:T(8,128)(2,1)S(1)}, u32[]{:S(2)}, u32[]{:S(2)}) collective-permute-start(bf16[12,128,128]{2,1,0:T(8,128)(2,1)S(1)} %fusion.7), channel_id=1, source_target_pairs={{0,16},{8,24},{1,17},{9,25},{2,18},{10,26},{3,19},{11,27},{4,20},{... | collective-permute-start | bytes 1179656 | tf_op jit(solution)/shard_map/ppermute | solution.py:28
  37.7 7.6 %collective-permute-start.5 = (bf16[2,40,768]{2,1,0:T(8,128)(2,1)S(1)}, bf16[2,40,768]{2,1,0:T(8,128)(2,1)S(1)}, u32[]{:S(2)}, u32[]{:S(2)}) collective-permute-start(bf16[2,40,768]{2,1,0:T(8,128)(2,1)S(1)} %get-tuple-element.40), channel_id=1, source_target_pairs={{0,6},{1,7},{2,4},{3,5},{4,2},{5,3},{6,0},{7,1},{8,14},{9,15},{10,... | collective-permute-start | bytes 368648 | tf_op jit(solution)/shard_map/ppermute | solution.py:28
  37.9 20.0 %collective-permute-start.9 = (bf16[2,40,768]{2,1,0:T(8,128)(2,1)S(1)}, bf16[2,40,768]{2,1,0:T(8,128)(2,1)S(1)}, u32[]{:S(2)}, u32[]{:S(2)}) collective-permute-start(bf16[2,40,768]{2,1,0:T(8,128)(2,1)S(1)} %get-tuple-element.41), channel_id=1, source_target_pairs={{0,7},{1,6},{2,5},{3,4},{4,3},{5,2},{6,1},{7,0},{8,15},{9,14},{10,... | collective-permute-start | bytes 368648 | tf_op jit(solution)/shard_map/ppermute | solution.py:28
  41.8 16.1 %collective-permute-start.13 = (bf16[2,40,768]{2,1,0:T(8,128)(2,1)S(1)}, bf16[2,40,768]{2,1,0:T(8,128)(2,1)S(1)}, u32[]{:S(2)}, u32[]{:S(2)}) collective-permute-start(bf16[2,40,768]{2,1,0:T(8,128)(2,1)S(1)} %get-tuple-element.42), channel_id=1, source_target_pairs={{0,4},{1,5},{2,6},{3,7},{4,0},{5,1},{6,2},{7,3},{8,12},{9,13},{10,... | collective-permute-start | bytes 368648 | tf_op jit(solution)/shard_map/ppermute | solution.py:28
  43.7 15.7 %collective-permute-start.17 = (bf16[2,40,768]{2,1,0:T(8,128)(2,1)S(1)}, bf16[2,40,768]{2,1,0:T(8,128)(2,1)S(1)}, u32[]{:S(2)}, u32[]{:S(2)}) collective-permute-start(bf16[2,40,768]{2,1,0:T(8,128)(2,1)S(1)} %get-tuple-element.43), channel_id=1, source_target_pairs={{0,5},{1,4},{2,7},{3,6},{4,1},{5,0},{6,3},{7,2},{8,13},{9,12},{10,... | collective-permute-start | bytes 368648 | tf_op jit(solution)/shard_map/ppermute | solution.py:28
  43.7 17.8 %collective-permute-start.21 = (bf16[2,40,768]{2,1,0:T(8,128)(2,1)S(1)}, bf16[2,40,768]{2,1,0:T(8,128)(2,1)S(1)}, u32[]{:S(2)}, u32[]{:S(2)}) collective-permute-start(bf16[2,40,768]{2,1,0:T(8,128)(2,1)S(1)} %get-tuple-element.44), channel_id=1, source_target_pairs={{0,2},{1,3},{2,0},{3,1},{4,6},{5,7},{6,4},{7,5},{8,10},{9,11},{10,... | collective-permute-start | bytes 368648 | tf_op jit(solution)/shard_map/ppermute | solution.py:28
  45.2 17.5 %collective-permute-start.25 = (bf16[2,40,768]{2,1,0:T(8,128)(2,1)S(1)}, bf16[2,40,768]{2,1,0:T(8,128)(2,1)S(1)}, u32[]{:S(2)}, u32[]{:S(2)}) collective-permute-start(bf16[2,40,768]{2,1,0:T(8,128)(2,1)S(1)} %get-tuple-element.45), channel_id=1, source_target_pairs={{0,3},{1,2},{2,1},{3,0},{4,7},{5,6},{6,5},{7,4},{8,11},{9,10},{10,... | collective-permute-start | bytes 368648 | tf_op jit(solution)/shard_map/ppermute | solution.py:28
  63.0 7.5 %collective-permute-start.22 = (bf16[2,40,768]{2,1,0:T(8,128)(2,1)S(1)}, bf16[2,40,768]{2,1,0:T(8,128)(2,1)S(1)}, u32[]{:S(2)}, u32[]{:S(2)}) collective-permute-start(bf16[2,40,768]{2,1,0:T(8,128)(2,1)S(1)} %collective-permute-done.21.refs_0_.refs_2_), channel_id=1, source_target_pairs={{0,8},{8,0},{16,24},{24,16},{1,9},{9,1},{17,25},{25,17},{2,10},{10... | collective-permute-start | bytes 368648 | tf_op jit(solution)/shard_map/ppermute | solution.py:28
  64.4 7.9 %collective-permute-start.27 = (bf16[2,40,768]{2,1,0:T(8,128)(2,1)S(1)}, bf16[2,40,768]{2,1,0:T(8,128)(2,1)S(1)}, u32[]{:S(2)}, u32[]{:S(2)}) collective-permute-start(bf16[2,40,768]{2,1,0:T(8,128)(2,1)S(1)} %collective-permute-done.25.refs_4_.refs_3_), channel_id=1, source_target_pairs={{0,16},{8,24},{16,0},{24,8},{1,17},{9,25},{17,1},{25,9},{2,18},{10... | collective-permute-start | bytes 368648 | tf_op jit(solution)/shard_map/ppermute | solution.py:28
  65.7 7.8 %collective-permute-start.31 = (bf16[2,40,768]{2,1,0:T(8,128)(2,1)S(1)}, bf16[2,40,768]{2,1,0:T(8,128)(2,1)S(1)}, u32[]{:S(2)}, u32[]{:S(2)}) collective-permute-start(bf16[2,40,768]{2,1,0:T(8,128)(2,1)S(1)} %collective-permute-done.29.refs_1_), channel_id=1, source_target_pairs={{0,16},{8,24},{16,0},{24,8},{1,17},{9,25},{17,1},{25,9},{2,18},{10... | collective-permute-start | bytes 368648 | tf_op jit(solution)/shard_map/ppermute | solution.py:28
  70.5 13.5 %collective-permute-start.23 = (bf16[2,40,768]{2,1,0:T(8,128)(2,1)S(1)}, bf16[2,40,768]{2,1,0:T(8,128)(2,1)S(1)}, u32[]{:S(2)}, u32[]{:S(2)}) collective-permute-start(bf16[2,40,768]{2,1,0:T(8,128)(2,1)S(1)} %collective-permute-done.21.refs_0_.refs_2_), channel_id=1, source_target_pairs={{0,16},{8,24},{16,0},{24,8},{1,17},{9,25},{17,1},{25,9},{2,18},{10... | collective-permute-start | bytes 368648 | tf_op jit(solution)/shard_map/ppermute | solution.py:28
  72.3 12.0 %collective-permute-start.26 = (bf16[2,40,768]{2,1,0:T(8,128)(2,1)S(1)}, bf16[2,40,768]{2,1,0:T(8,128)(2,1)S(1)}, u32[]{:S(2)}, u32[]{:S(2)}) collective-permute-start(bf16[2,40,768]{2,1,0:T(8,128)(2,1)S(1)} %collective-permute-done.25.refs_4_.refs_3_), channel_id=1, source_target_pairs={{0,8},{8,0},{16,24},{24,16},{1,9},{9,1},{17,25},{25,17},{2,10},{10... | collective-permute-start | bytes 368648 | tf_op jit(solution)/shard_map/ppermute | solution.py:28
  73.6 8.7 %collective-permute-start.19 = (bf16[2,40,768]{2,1,0:T(8,128)(2,1)S(1)}, bf16[2,40,768]{2,1,0:T(8,128)(2,1)S(1)}, u32[]{:S(2)}, u32[]{:S(2)}) collective-permute-start(bf16[2,40,768]{2,1,0:T(8,128)(2,1)S(1)} %collective-permute-done.17.refs_4_.refs_5_), channel_id=1, source_target_pairs={{0,16},{8,24},{16,0},{24,8},{1,17},{9,25},{17,1},{25,9},{2,18},{10... | collective-permute-start | bytes 368648 | tf_op jit(solution)/shard_map/ppermute | solution.py:28
  73.6 10.8 %collective-permute-start.24 = (bf16[2,40,768]{2,1,0:T(8,128)(2,1)S(1)}, bf16[2,40,768]{2,1,0:T(8,128)(2,1)S(1)}, u32[]{:S(2)}, u32[]{:S(2)}) collective-permute-start(bf16[2,40,768]{2,1,0:T(8,128)(2,1)S(1)} %collective-permute-done.22.refs_1_), channel_id=1, source_target_pairs={{0,16},{8,24},{16,0},{24,8},{1,17},{9,25},{17,1},{25,9},{2,18},{10... | collective-permute-start | bytes 368648 | tf_op jit(solution)/shard_map/ppermute | solution.py:28
  75.0 10.7 %collective-permute-start.28 = (bf16[2,40,768]{2,1,0:T(8,128)(2,1)S(1)}, bf16[2,40,768]{2,1,0:T(8,128)(2,1)S(1)}, u32[]{:S(2)}, u32[]{:S(2)}) collective-permute-start(bf16[2,40,768]{2,1,0:T(8,128)(2,1)S(1)} %collective-permute-done.27.refs_6_), channel_id=1, source_target_pairs={{0,8},{8,0},{16,24},{24,16},{1,9},{9,1},{17,25},{25,17},{2,10},{10... | collective-permute-start | bytes 368648 | tf_op jit(solution)/shard_map/ppermute | solution.py:28
  82.3 10.8 %collective-permute-start.15 = (bf16[2,40,768]{2,1,0:T(8,128)(2,1)S(1)}, bf16[2,40,768]{2,1,0:T(8,128)(2,1)S(1)}, u32[]{:S(2)}, u32[]{:S(2)}) collective-permute-start(bf16[2,40,768]{2,1,0:T(8,128)(2,1)S(1)} %collective-permute-done.13.refs_0_.refs_4_), channel_id=1, source_target_pairs={{0,16},{8,24},{16,0},{24,8},{1,17},{9,25},{17,1},{25,9},{2,18},{10... | collective-permute-start | bytes 368648 | tf_op jit(solution)/shard_map/ppermute | solution.py:28
  84.1 9.3 %collective-permute-start.18 = (bf16[2,40,768]{2,1,0:T(8,128)(2,1)S(1)}, bf16[2,40,768]{2,1,0:T(8,128)(2,1)S(1)}, u32[]{:S(2)}, u32[]{:S(2)}) collective-permute-start(bf16[2,40,768]{2,1,0:T(8,128)(2,1)S(1)} %collective-permute-done.17.refs_4_.refs_5_), channel_id=1, source_target_pairs={{0,8},{8,0},{16,24},{24,16},{1,9},{9,1},{17,25},{25,17},{2,10},{10... | collective-permute-start | bytes 368648 | tf_op jit(solution)/shard_map/ppermute | solution.py:28
  84.3 8.7 %collective-permute-start.11 = (bf16[2,40,768]{2,1,0:T(8,128)(2,1)S(1)}, bf16[2,40,768]{2,1,0:T(8,128)(2,1)S(1)}, u32[]{:S(2)}, u32[]{:S(2)}) collective-permute-start(bf16[2,40,768]{2,1,0:T(8,128)(2,1)S(1)} %collective-permute-done.9.refs_4_.refs_7_), channel_id=1, source_target_pairs={{0,16},{8,24},{16,0},{24,8},{1,17},{9,25},{17,1},{25,9},{2,18},{10... | collective-permute-start | bytes 368648 | tf_op jit(solution)/shard_map/ppermute | solution.py:28
  84.4 10.4 %collective-permute-start.16 = (bf16[2,40,768]{2,1,0:T(8,128)(2,1)S(1)}, bf16[2,40,768]{2,1,0:T(8,128)(2,1)S(1)}, u32[]{:S(2)}, u32[]{:S(2)}) collective-permute-start(bf16[2,40,768]{2,1,0:T(8,128)(2,1)S(1)} %collective-permute-done.14.refs_1_), channel_id=1, source_target_pairs={{0,16},{8,24},{16,0},{24,8},{1,17},{9,25},{17,1},{25,9},{2,18},{10... | collective-permute-start | bytes 368648 | tf_op jit(solution)/shard_map/ppermute | solution.py:28
  85.8 10.2 %collective-permute-start.20 = (bf16[2,40,768]{2,1,0:T(8,128)(2,1)S(1)}, bf16[2,40,768]{2,1,0:T(8,128)(2,1)S(1)}, u32[]{:S(2)}, u32[]{:S(2)}) collective-permute-start(bf16[2,40,768]{2,1,0:T(8,128)(2,1)S(1)} %collective-permute-done.19.refs_6_), channel_id=1, source_target_pairs={{0,8},{8,0},{16,24},{24,16},{1,9},{9,1},{17,25},{25,17},{2,10},{10... | collective-permute-start | bytes 368648 | tf_op jit(solution)/shard_map/ppermute | solution.py:28
  93.0 9.0 %collective-permute-start.7 = (bf16[2,40,768]{2,1,0:T(8,128)(2,1)S(1)}, bf16[2,40,768]{2,1,0:T(8,128)(2,1)S(1)}, u32[]{:S(2)}, u32[]{:S(2)}) collective-permute-start(bf16[2,40,768]{2,1,0:T(8,128)(2,1)S(1)} %collective-permute-done.5.refs_0_.refs_6_), channel_id=1, source_target_pairs={{0,16},{8,24},{16,0},{24,8},{1,17},{9,25},{17,1},{25,9},{2,18},{10... | collective-permute-start | bytes 368648 | tf_op jit(solution)/shard_map/ppermute | solution.py:28
  93.1 8.8 %collective-permute-start.10 = (bf16[2,40,768]{2,1,0:T(8,128)(2,1)S(1)}, bf16[2,40,768]{2,1,0:T(8,128)(2,1)S(1)}, u32[]{:S(2)}, u32[]{:S(2)}) collective-permute-start(bf16[2,40,768]{2,1,0:T(8,128)(2,1)S(1)} %collective-permute-done.9.refs_4_.refs_7_), channel_id=1, source_target_pairs={{0,8},{8,0},{16,24},{24,16},{1,9},{9,1},{17,25},{25,17},{2,10},{10... | collective-permute-start | bytes 368648 | tf_op jit(solution)/shard_map/ppermute | solution.py:28
  93.4 8.6 %collective-permute-start.8 = (bf16[2,40,768]{2,1,0:T(8,128)(2,1)S(1)}, bf16[2,40,768]{2,1,0:T(8,128)(2,1)S(1)}, u32[]{:S(2)}, u32[]{:S(2)}) collective-permute-start(bf16[2,40,768]{2,1,0:T(8,128)(2,1)S(1)} %collective-permute-done.6.refs_1_), channel_id=1, source_target_pairs={{0,16},{8,24},{16,0},{24,8},{1,17},{9,25},{17,1},{25,9},{2,18},{10... | collective-permute-start | bytes 368648 | tf_op jit(solution)/shard_map/ppermute | solution.py:28
  94.8 7.2 %collective-permute-start.12 = (bf16[2,40,768]{2,1,0:T(8,128)(2,1)S(1)}, bf16[2,40,768]{2,1,0:T(8,128)(2,1)S(1)}, u32[]{:S(2)}, u32[]{:S(2)}) collective-permute-start(bf16[2,40,768]{2,1,0:T(8,128)(2,1)S(1)} %collective-permute-done.11.refs_6_), channel_id=1, source_target_pairs={{0,8},{8,0},{16,24},{24,16},{1,9},{9,1},{17,25},{25,17},{2,10},{10... | collective-permute-start | bytes 368648 | tf_op jit(solution)/shard_map/ppermute | solution.py:28
  120.6 15.8 %collective-permute-start.56 = (bf16[2,2,40,768]{3,2,1,0:T(8,128)(2,1)S(1)}, bf16[2,2,40,768]{3,2,1,0:T(8,128)(2,1)S(1)}, u32[]{:S(2)}, u32[]{:S(2)}) collective-permute-start(bf16[2,2,40,768]{3,2,1,0:T(8,128)(2,1)S(1)} %get-tuple-element.64), channel_id=1, source_target_pairs={{0,16},{8,24},{16,0},{24,8},{1,17},{9,25},{17,1},{25,9},{2,18},{10... | collective-permute-start | bytes 737288 | tf_op jit(solution)/shard_map/ppermute | solution.py:28
  120.8 17.1 %collective-permute-start.38 = (bf16[2,2,40,768]{3,2,1,0:T(8,128)(2,1)S(1)}, bf16[2,2,40,768]{3,2,1,0:T(8,128)(2,1)S(1)}, u32[]{:S(2)}, u32[]{:S(2)}) collective-permute-start(bf16[2,2,40,768]{3,2,1,0:T(8,128)(2,1)S(1)} %get-tuple-element.52), channel_id=1, source_target_pairs={{0,16},{8,24},{16,0},{24,8},{1,17},{9,25},{17,1},{25,9},{2,18},{10... | collective-permute-start | bytes 737288 | tf_op jit(solution)/shard_map/ppermute | solution.py:28
  128.5 9.9 %collective-permute-start.41 = (bf16[2,2,40,768]{3,2,1,0:T(8,128)(2,1)S(1)}, bf16[2,2,40,768]{3,2,1,0:T(8,128)(2,1)S(1)}, u32[]{:S(2)}, u32[]{:S(2)}) collective-permute-start(bf16[2,2,40,768]{3,2,1,0:T(8,128)(2,1)S(1)} %get-tuple-element.54), channel_id=1, source_target_pairs={{0,8},{8,0},{16,24},{24,16},{1,9},{9,1},{17,25},{25,17},{2,10},{10... | collective-permute-start | bytes 737288 | tf_op jit(solution)/shard_map/ppermute | solution.py:28
  128.8 10.9 %collective-permute-start.44 = (bf16[2,2,40,768]{3,2,1,0:T(8,128)(2,1)S(1)}, bf16[2,2,40,768]{3,2,1,0:T(8,128)(2,1)S(1)}, u32[]{:S(2)}, u32[]{:S(2)}) collective-permute-start(bf16[2,2,40,768]{3,2,1,0:T(8,128)(2,1)S(1)} %get-tuple-element.56), channel_id=1, source_target_pairs={{0,16},{8,24},{16,0},{24,8},{1,17},{9,25},{17,1},{25,9},{2,18},{10... | collective-permute-start | bytes 737288 | tf_op jit(solution)/shard_map/ppermute | solution.py:28
  136.4 8.4 %collective-permute-start.50 = (bf16[2,2,40,768]{3,2,1,0:T(8,128)(2,1)S(1)}, bf16[2,2,40,768]{3,2,1,0:T(8,128)(2,1)S(1)}, u32[]{:S(2)}, u32[]{:S(2)}) collective-permute-start(bf16[2,2,40,768]{3,2,1,0:T(8,128)(2,1)S(1)} %get-tuple-element.60), channel_id=1, source_target_pairs={{0,16},{8,24},{16,0},{24,8},{1,17},{9,25},{17,1},{25,9},{2,18},{10... | collective-permute-start | bytes 737288 | tf_op jit(solution)/shard_map/ppermute | solution.py:28
  137.9 8.5 %collective-permute-start.53 = (bf16[2,2,40,768]{3,2,1,0:T(8,128)(2,1)S(1)}, bf16[2,2,40,768]{3,2,1,0:T(8,128)(2,1)S(1)}, u32[]{:S(2)}, u32[]{:S(2)}) collective-permute-start(bf16[2,2,40,768]{3,2,1,0:T(8,128)(2,1)S(1)} %get-tuple-element.62), channel_id=1, source_target_pairs={{0,8},{8,0},{16,24},{24,16},{1,9},{9,1},{17,25},{25,17},{2,10},{10... | collective-permute-start | bytes 737288 | tf_op jit(solution)/shard_map/ppermute | solution.py:28
  138.3 11.4 %collective-permute-start.36 = (bf16[2,2,40,768]{3,2,1,0:T(8,128)(2,1)S(1)}, bf16[2,2,40,768]{3,2,1,0:T(8,128)(2,1)S(1)}, u32[]{:S(2)}, u32[]{:S(2)}) collective-permute-start(bf16[2,2,40,768]{3,2,1,0:T(8,128)(2,1)S(1)} %get-tuple-element.49), channel_id=1, source_target_pairs={{0,8},{8,0},{16,24},{24,16},{1,9},{9,1},{17,25},{25,17},{2,10},{10... | collective-permute-start | bytes 737288 | tf_op jit(solution)/shard_map/ppermute | solution.py:28
  139.7 14.2 %collective-permute-start.57 = (bf16[1,2,40,768]{3,2,1,0:T(8,128)(2,1)S(1)}, bf16[1,2,40,768]{3,2,1,0:T(8,128)(2,1)S(1)}, u32[]{:S(2)}, u32[]{:S(2)}) collective-permute-start(bf16[1,2,40,768]{3,2,1,0:T(8,128)(2,1)S(1)} %slice.197), channel_id=1, source_target_pairs={{0,8},{8,0},{16,24},{24,16},{1,9},{9,1},{17,25},{25,17},{2,10},{10... | collective-permute-start | bytes 368648 | tf_op jit(solution)/shard_map/ppermute | solution.py:28
  141.9 13.1 %collective-permute-start.39 = (bf16[1,2,40,768]{3,2,1,0:T(8,128)(2,1)S(1)}, bf16[1,2,40,768]{3,2,1,0:T(8,128)(2,1)S(1)}, u32[]{:S(2)}, u32[]{:S(2)}) collective-permute-start(bf16[1,2,40,768]{3,2,1,0:T(8,128)(2,1)S(1)} %slice.203), channel_id=1, source_target_pairs={{0,8},{8,0},{16,24},{24,16},{1,9},{9,1},{17,25},{25,17},{2,10},{10... | collective-permute-start | bytes 368648 | tf_op jit(solution)/shard_map/ppermute | solution.py:28
  144.9 12.2 %collective-permute-start.42 = (bf16[1,2,40,768]{3,2,1,0:T(8,128)(2,1)S(1)}, bf16[1,2,40,768]{3,2,1,0:T(8,128)(2,1)S(1)}, u32[]{:S(2)}, u32[]{:S(2)}) collective-permute-start(bf16[1,2,40,768]{3,2,1,0:T(8,128)(2,1)S(1)} %slice.202), channel_id=1, source_target_pairs={{0,16},{8,24},{16,0},{24,8},{1,17},{9,25},{17,1},{25,9},{2,18},{10... | collective-permute-start | bytes 368648 | tf_op jit(solution)/shard_map/ppermute | solution.py:28
  146.4 15.1 %collective-permute-start.45 = (bf16[1,2,40,768]{3,2,1,0:T(8,128)(2,1)}, bf16[1,2,40,768]{3,2,1,0:T(8,128)(2,1)}, u32[]{:S(2)}, u32[]{:S(2)}) collective-permute-start(bf16[1,2,40,768]{3,2,1,0:T(8,128)(2,1)} %slice.201), channel_id=1, source_target_pairs={{0,8},{8,0},{16,24},{24,16},{1,9},{9,1},{17,25},{25,17},{2,10},{10... | collective-permute-start | bytes 368648 | tf_op jit(solution)/shard_map/ppermute | solution.py:28
  149.7 11.8 %collective-permute-start.48 = (bf16[1,2,40,768]{3,2,1,0:T(8,128)(2,1)}, bf16[1,2,40,768]{3,2,1,0:T(8,128)(2,1)}, u32[]{:S(2)}, u32[]{:S(2)}) collective-permute-start(bf16[1,2,40,768]{3,2,1,0:T(8,128)(2,1)} %slice.200), channel_id=1, source_target_pairs={{0,16},{8,24},{16,0},{24,8},{1,17},{9,25},{17,1},{25,9},{2,18},{10... | collective-permute-start | bytes 368648 | tf_op jit(solution)/shard_map/ppermute | solution.py:28
  153.9 7.6 %collective-permute-start.51 = (bf16[1,2,40,768]{3,2,1,0:T(8,128)(2,1)}, bf16[1,2,40,768]{3,2,1,0:T(8,128)(2,1)}, u32[]{:S(2)}, u32[]{:S(2)}) collective-permute-start(bf16[1,2,40,768]{3,2,1,0:T(8,128)(2,1)} %slice.199), channel_id=1, source_target_pairs={{0,8},{8,0},{16,24},{24,16},{1,9},{9,1},{17,25},{25,17},{2,10},{10... | collective-permute-start | bytes 368648 | tf_op jit(solution)/shard_map/ppermute | solution.py:28
  164.2 18.5 %collective-permute-start.40 = (bf16[2,40,768]{2,1,0:T(8,128)(2,1)S(1)}, bf16[2,40,768]{2,1,0:T(8,128)(2,1)S(1)}, u32[]{:S(2)}, u32[]{:S(2)}) collective-permute-start(bf16[2,40,768]{2,1,0:T(8,128)(2,1)S(1)} %get-tuple-element.68), channel_id=1, source_target_pairs={{0,1},{1,0},{2,3},{3,2},{4,5},{5,4},{6,7},{7,6},{8,9},{9,8},{10,11... | collective-permute-start | bytes 368648 | tf_op jit(solution)/shard_map/ppermute | solution.py:28
  175.5 7.9 %collective-permute-start.43 = (bf16[2,40,768]{2,1,0:T(8,128)(2,1)S(1)}, bf16[2,40,768]{2,1,0:T(8,128)(2,1)S(1)}, u32[]{:S(2)}, u32[]{:S(2)}) collective-permute-start(bf16[2,40,768]{2,1,0:T(8,128)(2,1)S(1)} %get-tuple-element.69), channel_id=1, source_target_pairs={{0,2},{1,3},{2,0},{3,1},{4,6},{5,7},{6,4},{7,5},{8,10},{9,11},{10,... | collective-permute-start | bytes 368648 | tf_op jit(solution)/shard_map/ppermute | solution.py:28
  179.8 7.1 %collective-permute-start.46 = (bf16[2,40,768]{2,1,0:T(8,128)(2,1)S(1)}, bf16[2,40,768]{2,1,0:T(8,128)(2,1)S(1)}, u32[]{:S(2)}, u32[]{:S(2)}) collective-permute-start(bf16[2,40,768]{2,1,0:T(8,128)(2,1)S(1)} %get-tuple-element.70), channel_id=1, source_target_pairs={{0,3},{1,2},{2,1},{3,0},{4,7},{5,6},{6,5},{7,4},{8,11},{9,10},{10,... | collective-permute-start | bytes 368648 | tf_op jit(solution)/shard_map/ppermute | solution.py:28
  179.8 7.5 %collective-permute-start.49 = (bf16[2,40,768]{2,1,0:T(8,128)(2,1)S(1)}, bf16[2,40,768]{2,1,0:T(8,128)(2,1)S(1)}, u32[]{:S(2)}, u32[]{:S(2)}) collective-permute-start(bf16[2,40,768]{2,1,0:T(8,128)(2,1)S(1)} %get-tuple-element.71), channel_id=1, source_target_pairs={{0,4},{1,5},{2,6},{3,7},{4,0},{5,1},{6,2},{7,3},{8,12},{9,13},{10,... | collective-permute-start | bytes 368648 | tf_op jit(solution)/shard_map/ppermute | solution.py:28
  180.1 16.2 %collective-permute-start.52 = (bf16[2,40,768]{2,1,0:T(8,128)(2,1)S(1)}, bf16[2,40,768]{2,1,0:T(8,128)(2,1)S(1)}, u32[]{:S(2)}, u32[]{:S(2)}) collective-permute-start(bf16[2,40,768]{2,1,0:T(8,128)(2,1)S(1)} %get-tuple-element.72), channel_id=1, source_target_pairs={{0,5},{1,4},{2,7},{3,6},{4,1},{5,0},{6,3},{7,2},{8,13},{9,12},{10,... | collective-permute-start | bytes 368648 | tf_op jit(solution)/shard_map/ppermute | solution.py:28
  182.8 19.0 %collective-permute-start.55 = (bf16[2,40,768]{2,1,0:T(8,128)(2,1)S(1)}, bf16[2,40,768]{2,1,0:T(8,128)(2,1)S(1)}, u32[]{:S(2)}, u32[]{:S(2)}) collective-permute-start(bf16[2,40,768]{2,1,0:T(8,128)(2,1)S(1)} %get-tuple-element.73), channel_id=1, source_target_pairs={{0,6},{1,7},{2,4},{3,5},{4,2},{5,3},{6,0},{7,1},{8,14},{9,15},{10,... | collective-permute-start | bytes 368648 | tf_op jit(solution)/shard_map/ppermute | solution.py:28
  183.4 21.3 %collective-permute-start.58 = (bf16[2,40,768]{2,1,0:T(8,128)(2,1)S(1)}, bf16[2,40,768]{2,1,0:T(8,128)(2,1)S(1)}, u32[]{:S(2)}, u32[]{:S(2)}) collective-permute-start(bf16[2,40,768]{2,1,0:T(8,128)(2,1)S(1)} %get-tuple-element.67), channel_id=1, source_target_pairs={{0,7},{1,6},{2,5},{3,4},{4,3},{5,2},{6,1},{7,0},{8,15},{9,14},{10,... | collective-permute-start | bytes 368648 | tf_op jit(solution)/shard_map/ppermute | solution.py:28
  (38 other events, 299.3 us)

commit v2 on v1

v2 whole, which is shorter than its diff:
```python
import functools

import jax
import jax.numpy as jnp
from jax import lax
from jax.experimental import pallas as pl
from jax.experimental.pallas import tpu as pltpu
from jax.sharding import PartitionSpec as P

CAP = 40
F32 = jnp.float32
BF16 = jnp.bfloat16
VMEM = pl.BlockSpec(memory_space=pltpu.VMEM)
SMEM = pl.BlockSpec(memory_space=pltpu.SMEM)


def params(mib, n=0):
    return pltpu.CompilerParams(
        vmem_limit_bytes=mib << 20, dimension_semantics=("arbitrary",) * n if n else None
    )


def bits_of(n):
    return [1 << b for b in range(n.bit_length() - 1)]


def swap(x, axis, n, k, keep=lambda i: True):
    return lax.ppermute(x, axis, [(i, i ^ k) for i in range(n) if keep(i)])


def dot(a, b, ca=1, cb=0, **kw):
    return lax.dot_general(a, b, (((ca,), (cb,)), ((), ())), preferred_element_type=F32, **kw)


def iota(shape, dim):
    return lax.broadcasted_iota(jnp.int32, shape, dim)


def running_sum(log_decay):
    length = log_decay.shape[1]
    tril = (iota((length, length), 0) >= iota((length, length), 1)).astype(F32)
    return dot(tril, log_decay, 1, 1, precision=lax.Precision.HIGHEST)


def running_sum_rows(log_decay):
    length = log_decay.shape[1]
    triu = (iota((length, length), 0) <= iota((length, length), 1)).astype(F32)
    return dot(log_decay, triu, precision=lax.Precision.HIGHEST)


def state_kernel(keys, values, log_decay, *refs):
    states, (key_buf, value_buf, sems) = refs[:-3], refs[-3:]
    requests, length, features = keys.shape
    heads = log_decay.shape[0] // requests
    dim = features // heads
    per = requests // len(states)
    copies = []
    for r in range(requests):
        pair = (
            pltpu.make_async_copy(keys.at[r], key_buf.at[r], sems.at[0, r]),
            pltpu.make_async_copy(values.at[r], value_buf.at[r], sems.at[1, r]),
        )
        for copy in pair:
            copy.start()
        copies.append(pair)
    cum = running_sum(log_decay[...])
    fade = jnp.exp(cum[length - 1 : length, :] - cum)
    for r in range(requests):
        for copy in copies[r]:
            copy.wait()
        for h in range(heads):
            lanes = slice(h * dim, (h + 1) * dim)
            at = h * requests + r
            faded = (key_buf[r, :, lanes].astype(F32) * fade[:, at : at + 1]).astype(BF16)
            states[r // per][(r % per) * heads + h] = dot(
                faded, value_buf[r, :, lanes], 0, 0
            ).astype(BF16)


def inside_kernel(place, queries, keys, values, log_decay, ids, inside, placement, other):
    requests, length, features = keys.shape
    heads = log_decay.shape[0] // requests
    dim = features // heads
    causal = iota((length, length), 0) >= iota((length, length), 1)
    cum = running_sum(log_decay[...])
    rows = running_sum_rows(log_decay[...])
    for r in range(requests):
        for h in range(heads):
            lanes = slice(h * dim, (h + 1) * dim)
            at = h * requests + r
            spread = cum[:, at : at + 1] - rows[at : at + 1, :]
            mask = jnp.where(causal, jnp.exp(jnp.minimum(spread, 0.0)), 0.0)
            scores = dot(queries[r, :, lanes], keys[r, :, lanes], 1, 1)
            inside[r, :, lanes] = dot((scores * mask).astype(BF16), values[r, :, lanes])
    slots, tokens = placement.shape
    experts = slots // CAP
    own = other.shape[0] // CAP
    owner = place[1]
    expert_row = iota((experts, tokens), 0)
    relative = sum((expert_row >= own * k).astype(jnp.int32) for k in range(1, experts // own))
    expert = ((2 * relative) ^ owner) * own + (expert_row - relative * own)
    first = jnp.concatenate([ids[r, 0:1, :] for r in range(requests)], axis=1)
    second = jnp.concatenate([ids[r, 1:2, :] for r in range(requests)], axis=1)
    named = (first == expert) | (second == expert)
    row = iota((tokens, tokens), 0)
    col = iota((tokens, tokens), 1)

    def order(i):
        request = sum((i >= length * k).astype(jnp.int32) for k in range(1, requests))
        return (i - request * length) * requests + request

    earlier = (order(row) < order(col)).astype(BF16)
    before = dot(named.astype(BF16), earlier)
    code = jnp.where(named, before, -1.0).astype(BF16)
    slot_row = iota((slots, experts), 0)
    slot_expert = iota((slots, experts), 1)
    spread_rows = (slot_row >= slot_expert * CAP) & (slot_row < slot_expert * CAP + CAP)
    codes = dot(spread_rows.astype(BF16), code)
    row_of = iota((slots, tokens), 0)
    expert_of = ((row_of.astype(F32) + 0.5) * (1.0 / CAP)).astype(jnp.int32)
    taken = codes == (row_of - expert_of * CAP).astype(F32)
    placement[...] = taken.astype(BF16)
    both = (first + second).astype(F32)
    mine = jnp.sum(jnp.where(taken[: own * CAP], both, 0.0), axis=1, keepdims=True)
    me = owner * own + expert_of[: own * CAP, :1]
    other[...] = jnp.broadcast_to(mine.astype(jnp.int32) - me, other.shape)


def output_kernel(queries, inside, log_decay, gain, *refs):
    incoming, normed = refs[:-1], refs[-1]
    requests, length, features = queries.shape
    heads = log_decay.shape[0] // requests
    dim = features // heads
    per = requests // len(incoming)
    grow = jnp.exp(running_sum(log_decay[...]))
    for r in range(requests):
        for h in range(heads):
            lanes = slice(h * dim, (h + 1) * dim)
            at = h * requests + r
            carried = dot(queries[r, :, lanes], incoming[r // per][(r % per) * heads + h])
            out = inside[r, :, lanes] + grow[:, at : at + 1] * carried
            square = jnp.mean(out * out, axis=1, keepdims=True) + 1e-05
            normed[r * length : (r + 1) * length, lanes] = (
                out * lax.rsqrt(square) * gain[0:1, lanes]
            ).astype(BF16)


def dispatch_kernel(placement, *refs):
    sides, blocks = refs[:2], refs[2:]
    own, cap, width = blocks[0].shape
    for i, side in enumerate(sides):
        routed = dot(placement[...], side[...])
        lanes = slice(i * width // 2, (i + 1) * width // 2)
        for k, block in enumerate(blocks):
            for j in range(own):
                at = (k * own + j) * cap
                block[j, :, lanes] = routed[at : at + cap].astype(BF16)


def gate_kernel(place, other, router, *refs):
    blocks, weight = refs[:-1], refs[-1]
    own, cap, width = blocks[0].shape
    half = width // 2
    owner = place[1]
    experts = router.shape[0]
    for j in range(own):
        logits = jnp.zeros((cap, experts), F32)
        for k, block in enumerate(blocks):
            for side in range(2):
                at = pl.multiple_of((owner ^ (2 * k + side)) * half, half)
                logits = logits + dot(
                    block[j, :, side * half : (side + 1) * half], router[:, pl.ds(at, half)], 1, 1
                )
        col = iota((cap, experts), 1)
        mine = jnp.sum(jnp.where(col == owner * own + j, logits, 0.0), axis=1, keepdims=True)
        theirs_at = other[j * cap : (j + 1) * cap, :1]
        theirs = jnp.sum(jnp.where(col == theirs_at, logits, 0.0), axis=1, keepdims=True)
        weight[j] = jnp.broadcast_to(1.0 / (1.0 + jnp.exp(theirs - mine)), (cap, 128))


def tiles_of(width):
    return 2 if width % 512 == 0 else 1


def up_kernel(place, *refs, parts, first, last):
    blocks, weights = refs[:parts], refs[parts]
    out, acc = refs[-2:]
    j, k = pl.program_id(0), pl.program_id(1)
    depth = weights.shape[1]
    steps = blocks[0].shape[2] // depth
    for step in range(steps):

        @pl.when(k == step)
        def _():
            lanes = slice(step * depth, (step + 1) * depth)
            x = jnp.concatenate([b[j, :, lanes].astype(F32) for b in blocks], axis=0).astype(BF16)
            total = dot(x, weights[0])
            if step:
                total = total + acc[...]
            elif not first:
                total = total + refs[parts + 1][0]
            if step < steps - 1:
                acc[...] = total
            elif last:
                out[0] = (total / (1.0 + jnp.exp(-total))).astype(BF16)
            else:
                out[0] = total


def up_chunk(place, chunk, blocks, weights, total, last):
    own, depth, hidden = weights.shape
    cap, width = blocks[0].shape[1:]
    parts = len(blocks)
    rows = parts * cap
    tiles = tiles_of(width)
    tile = width // 2 // tiles
    first = total is None
    total_spec = pl.BlockSpec((1, rows, hidden), lambda j, k, at: (j, 0, 0))
    return pl.pallas_call(
        functools.partial(up_kernel, parts=parts, first=first, last=last),
        grid_spec=pltpu.PrefetchScalarGridSpec(
            num_scalar_prefetch=1,
            grid=(own, 2 * tiles),
            in_specs=[VMEM] * parts
            + [
                pl.BlockSpec(
                    (1, tile, hidden),
                    lambda j, k, at: (j, (at[1] ^ (2 * chunk + k // tiles)) * tiles + k % tiles, 0),
                )
            ]
            + ([] if first else [total_spec]),
            out_specs=total_spec,
            scratch_shapes=[pltpu.VMEM((rows, hidden), F32)],
        ),
        out_shape=jax.ShapeDtypeStruct((own, rows, hidden), BF16 if last else F32),
        compiler_params=params(32, 2),
        cost_estimate=pl.CostEstimate(
            flops=2 * own * rows * width * hidden,
            bytes_accessed=2 * own * width * hidden,
            transcendentals=0,
        ),
        name=f"up_{chunk}",
    )(place, *blocks, weights, *([] if first else [total]))


def down_kernel(place, hidden, weights, *outs, route):
    result = dot(hidden[0], weights[0])
    for out, members in zip(outs, route):
        for i, member in enumerate(members):
            out[i, 0] = result[member * CAP : (member + 1) * CAP].astype(BF16)


def down_chunk(place, chunk, hidden, weights, width, route):
    own, rows, depth = hidden.shape
    parts = rows // CAP
    tiles = tiles_of(width)
    tile = width // 2 // tiles
    out_spec = pl.BlockSpec((parts // 2, 1, CAP, tile), lambda j, n, at: (0, j, 0, n))
    return pl.pallas_call(
        functools.partial(down_kernel, route=route),
        grid_spec=pltpu.PrefetchScalarGridSpec(
            num_scalar_prefetch=1,
            grid=(own, 2 * tiles),
            in_specs=[
                pl.BlockSpec((1, rows, depth), lambda j, n, at: (j, 0, 0)),
                pl.BlockSpec(
                    (1, depth, tile),
                    lambda j, n, at: (j, 0, (at[1] ^ (2 * chunk + n // tiles)) * tiles + n % tiles),
                ),
            ],
            out_specs=[out_spec] * 2,
        ),
        out_shape=[jax.ShapeDtypeStruct((parts // 2, own, CAP, width), BF16)] * 2,
        compiler_params=params(32, 2),
        cost_estimate=pl.CostEstimate(
            flops=2 * own * rows * width * depth,
            bytes_accessed=2 * own * width * depth,
            transcendentals=0,
        ),
        name=f"down_{chunk}",
    )(place, hidden, weights)


def combine_kernel(normed, placement, *refs):
    blocks, (mine, theirs) = refs[:-2], refs[-2:]
    own = blocks[0].shape[0]
    features = normed.shape[1]
    replies = jnp.concatenate(
        [block[j].astype(F32) for block in blocks for j in range(own)], axis=0
    ).astype(BF16)
    combined = dot(placement[...], replies, 0, 0)
    mine[...] = normed[...].astype(F32) + combined[:, :features]
    theirs[...] = combined[:, features:].astype(BF16)


def after(x, *others):
    return lax.optimization_barrier((x, *others))[0]


def route_of(bits, n):
    keep = [0]
    for bit in reversed(bits[1:]):
        keep = keep + [m | bit for m in keep]
    return [m | bits[0] for m in keep], keep


def halve_kernel(kept, got, keep, send):
    half = keep.shape[0]
    total = kept[...].astype(F32) + got[...].astype(F32)
    keep[...] = total[:half]
    send[...] = total[half:].astype(BF16)


def halve(kept, got):
    shape = (kept.shape[0] // 2,) + kept.shape[1:]
    return pl.pallas_call(
        halve_kernel,
        in_specs=[VMEM] * 2,
        out_specs=[VMEM] * 2,
        out_shape=[jax.ShapeDtypeStruct(shape, F32), jax.ShapeDtypeStruct(shape, BF16)],
        compiler_params=params(32),
        name="partial_sums",
    )(kept, got)


def reply_kernel(kept, got, weight, out):
    total = kept[0].astype(F32) + got[0].astype(F32)
    out[...] = (total * weight[:, :, :1]).astype(BF16)


def reply_of(kept, got, weight):
    return pl.pallas_call(
        reply_kernel,
        in_specs=[VMEM] * 3,
        out_specs=VMEM,
        out_shape=jax.ShapeDtypeStruct(kept.shape[1:], BF16),
        compiler_params=params(32),
        name="reply",
    )(kept, got, weight)


def prefix_by_doubling(states, decay, me, n):
    decay_before, steps = jnp.ones_like(decay), []
    bits = bits_of(n)
    for bit in bits:
        upper = (me & bit) != 0
        partner_decay = swap(decay, "ctx", n, bit)
        steps.append((upper, decay_before, decay, partner_decay))
        decay_before = jnp.where(upper, decay_before * partner_decay, decay_before)
        decay = decay * partner_decay
    incoming = []
    for half, total in enumerate(states):
        before = jnp.zeros((), F32)
        for bit, (upper, d_before, d_total, d_partner) in zip(bits, steps):
            last = bit == bits[-1]
            partner = swap(total, "ctx", n, bit, lambda i: not last or not i & bit).astype(F32)
            before = before + jnp.where(upper, d_before[half], 0.0) * partner
            if not last:
                total = (
                    jnp.where(upper, 1.0, d_partner[half]) * total.astype(F32)
                    + jnp.where(upper, d_total[half], 1.0) * partner
                ).astype(BF16)
        incoming.append(before.astype(BF16))
    return incoming


def prefix_of_four(states, decay, me):
    high, low = (me & 2) != 0, (me & 1) != 0
    near = swap(decay, "ctx", 4, 1)
    far = swap(decay, "ctx", 4, 3)
    one, two = states
    got_one = swap(one, "ctx", 4, 1, lambda i: i != 3).astype(F32)
    got_two = swap(two, "ctx", 4, 2, lambda i: i < 2).astype(F32)
    sent_one = jnp.where(low, 1.0, near[0]) * one.astype(F32) + jnp.where(low, decay[0], 1.0) * got_one
    sent_two = (
        jnp.where(high & low, 0.0, 1.0) * two.astype(F32)
        + jnp.where(high, jnp.where(low, 1.0, far[1] * decay[1]), 0.0) * got_two
    )
    last_one = swap(sent_one.astype(BF16), "ctx", 4, 2, lambda i: i < 2).astype(F32)
    last_two = swap(sent_two.astype(BF16), "ctx", 4, 1, lambda i: i != 1).astype(F32)
    return [
        (jnp.where(low, 1.0, 0.0) * got_one + jnp.where(low, near[0], 1.0) * last_one).astype(BF16),
        (jnp.where(low, near[1], far[1]) * got_two + last_two).astype(BF16),
    ]


def body(n_ctx, n_exp, queries, keys, values, log_decay, norm_gain, router, expert_up, expert_down, expert_ids):
    requests, length, features = queries.shape
    heads = log_decay.shape[2]
    dim = features // heads
    experts = router.shape[1]
    own = expert_up.shape[0]
    tokens = requests * length
    halves = 2 if requests % 2 == 0 else 1
    pairs = requests * heads // halves
    chunks = n_exp // 2
    width = 2 * features
    me = lax.axis_index("ctx")
    place = jnp.stack([me, lax.axis_index("exp")]).astype(jnp.int32)
    struct = jax.ShapeDtypeStruct
    decay_rows = jnp.transpose(log_decay, (2, 0, 1)).reshape(heads * requests, length)

    states = pl.pallas_call(
        state_kernel,
        in_specs=[pl.BlockSpec(memory_space=pl.ANY)] * 2 + [VMEM],
        out_specs=[VMEM] * halves,
        out_shape=[struct((pairs, dim, dim), BF16)] * halves,
        scratch_shapes=[
            pltpu.VMEM(keys.shape, BF16),
            pltpu.VMEM(values.shape, BF16),
            pltpu.SemaphoreType.DMA((2, requests)),
        ],
        compiler_params=params(32),
        name="local_state",
    )(keys, values, decay_rows)
    decay = jnp.exp(jnp.sum(log_decay, axis=1)).reshape(halves, pairs, 1, 1)
    if n_ctx == 4 and halves == 2:
        incoming = prefix_of_four(states, decay, me)
    else:
        incoming = prefix_by_doubling(states, decay, me, n_ctx)

    inside, placement, other = pl.pallas_call(
        inside_kernel,
        in_specs=[SMEM] + [VMEM] * 5,
        out_specs=[VMEM] * 3,
        out_shape=[
            struct((requests, length, features), F32),
            struct((chunks * own * CAP, tokens), BF16),
            struct((own * CAP, 128), jnp.int32),
        ],
        compiler_params=params(32),
        name="inside_and_placement",
    )(place, queries, keys, values, decay_rows, jnp.transpose(expert_ids, (1, 2, 0)))

    normed = pl.pallas_call(
        output_kernel,
        in_specs=[VMEM] * (4 + halves),
        out_specs=VMEM,
        out_shape=struct((tokens, features), BF16),
        compiler_params=params(32),
        name="normed",
    )(queries, inside, decay_rows, norm_gain.reshape(1, features), *incoming)

    outgoing = pl.pallas_call(
        dispatch_kernel,
        in_specs=[VMEM] * 3,
        out_specs=[VMEM] * chunks,
        out_shape=[struct((own, CAP, width), BF16)] * chunks,
        compiler_params=params(32),
        name="dispatch",
    )(placement, normed, swap(normed, "exp", n_exp, 1))
    arrived = [outgoing[0]] + [swap(outgoing[k], "exp", n_exp, 2 * k) for k in range(1, chunks)]
    weight = pl.pallas_call(
        gate_kernel,
        in_specs=[SMEM] + [VMEM] * (2 + chunks),
        out_specs=VMEM,
        out_shape=struct((own, CAP, 128), F32),
        compiler_params=params(32),
        name="gate",
    )(place, other, router.T, *arrived)

    bits = bits_of(n_ctx)
    orders = [bits if k % 2 == 0 else bits[::-1] for k in range(chunks)]

    def gather_round(have, bit, token):
        found = {}
        for rel, block in have.items():
            found[rel | bit] = swap(block if token is None else after(block, token), "ctx", n_ctx, bit)
        return {**have, **found}

    total = None
    gathered = [None] * chunks
    for k in range(chunks):
        have = {0: arrived[k]}
        for bit in orders[k]:
            have = gather_round(have, bit, total if k >= 2 else None)
        gathered[k] = [have[rel] for rel in range(n_ctx)]
        if k >= 1:
            total = up_chunk(place, k - 1, gathered[k - 1], expert_up, total, False)
    hidden = up_chunk(place, chunks - 1, gathered[-1], expert_up, after(total, weight), True)

    pending, returned = [], [None] * chunks

    def advance(token):
        k, step, kept, got = pending.pop(0)
        got = after(got, token)
        if step + 1 < len(bits):
            kept, sent = halve(kept, got)
            pending.append((k, step + 1, kept, swap(sent, "ctx", n_ctx, orders[k][step + 1])))
            return sent
        reply = reply_of(kept, got, weight)
        returned[k] = swap(reply, "exp", n_exp, 2 * k) if k else reply
        return reply

    token = hidden
    for k in reversed(range(chunks)):
        sent, kept = down_chunk(
            place, k, after(hidden, token), expert_down, width, route_of(orders[k], n_ctx)
        )
        pending.append((k, 0, kept, swap(sent, "ctx", n_ctx, orders[k][0])))
        token = advance(sent) if k < chunks - 2 else sent
    while pending:
        token = advance(token)

    mine, theirs = pl.pallas_call(
        combine_kernel,
        in_specs=[VMEM] * (2 + chunks),
        out_specs=[VMEM] * 2,
        out_shape=[struct((tokens, features), F32), struct((tokens, features), BF16)],
        compiler_params=params(32),
        name="combine",
    )(normed, placement, *returned)
    out = mine + swap(theirs, "exp", n_exp, 1).astype(F32)
    return out.astype(BF16).reshape(requests, length, features)


def solution(mesh):
    in_specs = (
        P(None, "ctx", "exp"),
        P(None, "ctx", "exp"),
        P(None, "ctx", "exp"),
        P(None, "ctx", "exp"),
        P("exp"),
        P(),
        P("exp", None, "ctx"),
        P("exp", "ctx", None),
        P("ctx", None, None),
    )
    out_specs = P(None, "ctx", "exp")
    run = functools.partial(body, mesh.shape["ctx"], mesh.shape["exp"])
    return jax.shard_map(run, mesh=mesh, in_specs=in_specs, out_specs=out_specs, check_vma=False)
```

time: 207 us -> 198 us (0.957)
  the two profiles are of different devices: /device:TPU:19 before, /device:TPU:0 now
where the time goes in v2:
time: 198 us; the launch traced here: 196 us
  Pallas kernels  78.2 us (39%)
  waiting for transfers between devices  56.8 us (29%)
  starting transfers between devices  54.1 us (27%)
  other arithmetic  3.36 us (2%)
  local copies, waits for them, and re-layouts  3.28 us (2%)
    ppermute x34, waiting for transfers between devices, swap(): return lax.ppermute(x, axis, [(i, i ^ k) for i in range(n) if keep(i)])  56.8 us
    ppermute x34, starting transfers between devices, swap(): return lax.ppermute(x, axis, [(i, i ^ k) for i in range(n) if keep(i)])  54.1 us
    pallas_call x4, Pallas kernels, down_chunk(): pl.pallas_call(functools.partial(down_kernel, route=route), grid_spec=plt...  33.2 us
    pallas_call x4, Pallas kernels, up_chunk(): pl.pallas_call(functools.partial(up_kernel, parts=parts, first=first, las...  33.1 us
    pallas_call x1, Pallas kernels, body(): pl.pallas_call(inside_kernel, in_specs=[SMEM] + [VMEM] * 5, out_specs=[VM...  4.27 us
  transfers between devices with their start and end apart: 34, of which 14 were waited for; matrix products, arithmetic and copies ran while one was open for 1% of the time, Pallas kernels for 30%

profile of v2, /device:TPU:0, one launch (start us, length us, event | category | flops | bytes accessed | tf_op | source)
XLA Modules:
  0.0 196.2 jit_solution(17815494453380372076)
XLA Ops:
  1.0 3.9 %collective-permute-start.3 = (f32[2,12,1,1]{1,0,3,2:T(2,128)S(1)}, f32[2,12,1,1]{1,0,3,2:T(2,128)S(1)}, u32[]{:S(2)}, u32[]{:S(2)}) collective-permute-start(f32[2,12,1,1]{1,0,3,2:T(2,128)S(1)} %exp.14), channel_id=1, source_target_pairs={{0,24},{8,16},{16,8},{24,0},{1,25},{9,17},{17,9},{25,1},{2,26},{10... | collective-permute-start | bytes 296 | tf_op jit(solution)/shard_map/ppermute | solution.py:28
  5.5 1.0 copy-done.1
  6.5 1.0 copy-done.3
  8.2 2.6 %local_state.1 = (bf16[12,128,128]{2,1,0:T(8,128)(2,1)S(1)}, bf16[12,128,128]{2,1,0:T(8,128)(2,1)S(1)}) custom-call(bf16[4,64,768]{2,1,0:T(8,128)(2,1)S(1)} %copy-done.1, bf16[4,64,768]{2,1,0:T(8,128)(2,1)S(1)} %copy-done.3, f32[24,64]{1,0:T(8,128)S(1)} %bitcast.19), custom_call_target="tpu_custom_call" | custom-call | tf_op jit(solution)/shard_map/local_state/pallas_call | solution.py:403
  10.8 3.4 %collective-permute-start = (bf16[12,128,128]{2,1,0:T(8,128)(2,1)S(1)}, bf16[12,128,128]{2,1,0:T(8,128)(2,1)S(1)}, u32[]{:S(2)}, u32[]{:S(2)}) collective-permute-start(bf16[12,128,128]{2,1,0:T(8,128)(2,1)S(1)} %get-tuple-element.50), channel_id=1, source_target_pairs={{0,8},{8,0},{16,24},{1,9},{9,1},{17,25},{2,10},{10,2},{18,26},{3,1... | collective-permute-start | bytes 1179656 | tf_op jit(solution)/shard_map/ppermute | solution.py:28
  14.3 2.5 %collective-permute-start.4 = (bf16[12,128,128]{2,1,0:T(8,128)(2,1)S(1)}, bf16[12,128,128]{2,1,0:T(8,128)(2,1)S(1)}, u32[]{:S(2)}, u32[]{:S(2)}) collective-permute-start(bf16[12,128,128]{2,1,0:T(8,128)(2,1)S(1)} %get-tuple-element.51), channel_id=1, source_target_pairs={{0,16},{8,24},{1,17},{9,25},{2,18},{10,26},{3,19},{11,27},{4,20},{... | collective-permute-start | bytes 1179656 | tf_op jit(solution)/shard_map/ppermute | solution.py:28
  17.2 7.0 %collective-permute-done.4 = bf16[12,128,128]{2,1,0:T(8,128)(2,1)S(1)} collective-permute-done((bf16[12,128,128]{2,1,0:T(8,128)(2,1)S(1)}, bf16[12,128,128]{2,1,0:T(8,128)(2,1)S(1)}, u32[]{:S(2)}, u32[]{:S(2)}) %collective-permute-start.4) | collective-permute-done | bytes 393248 | tf_op jit(solution)/shard_map/ppermute | solution.py:28
  24.4 1.6 collective-permute-start.5
  27.0 4.7 %collective-permute-start.2 = (bf16[12,128,128]{2,1,0:T(8,128)(2,1)}, bf16[12,128,128]{2,1,0:T(8,128)(2,1)S(1)}, u32[]{:S(2)}, u32[]{:S(2)}) collective-permute-start(bf16[12,128,128]{2,1,0:T(8,128)(2,1)} %fusion.3), channel_id=1, source_target_pairs={{0,16},{8,24},{1,17},{9,25},{2,18},{10,26},{3,19},{11,27},{4,20},{... | collective-permute-start | bytes 1179656 | tf_op jit(solution)/shard_map/ppermute | solution.py:28
  31.8 4.3 %inside_and_placement.1 = (f32[4,64,768]{2,1,0:T(8,128)S(1)}, bf16[320,256]{1,0:T(8,128)(2,1)S(1)}, s32[80,128]{1,0:T(8,128)S(1)}) custom-call(s32[2]{0:T(128)S(1)} %pad_add_fusion.place, bf16[4,64,768]{2,1,0:T(8,128)(2,1)S(1)} %copy-done, bf16[4,64,768]{2,1,0:T(8,128)(2,1)S(1)} %copy-done.2, bf16[4,64,768]{2,1,0:T(8,128)(2,1)S(1)} %copy-done.4, ...), custom_call_target="tpu_custom_call" | custom-call | tf_op jit(solution)/shard_map/inside_and_placement/pallas_call | solution.py:422
  36.3 2.3 %collective-permute-done.2 = bf16[12,128,128]{2,1,0:T(8,128)(2,1)S(1)} collective-permute-done((bf16[12,128,128]{2,1,0:T(8,128)(2,1)}, bf16[12,128,128]{2,1,0:T(8,128)(2,1)S(1)}, u32[]{:S(2)}, u32[]{:S(2)}) %collective-permute-start.2) | collective-permute-done | bytes 393248 | tf_op jit(solution)/shard_map/ppermute | solution.py:28
  38.8 2.0 %normed.1.refs_0_ = bf16[256,768]{1,0:T(8,128)(2,1)S(1)} custom-call(bf16[4,64,768]{2,1,0:T(8,128)(2,1)S(1)} %copy-done, f32[4,64,768]{2,1,0:T(8,128)S(1)} %get-tuple-element.49.inside, f32[24,64]{1,0:T(8,128)S(1)} %bitcast.21, f32[1,768]{1,0:T(1,128)S(1)} %reshape.84.gain, bf16[12,128,128]{2,1,0:T(8,128)(2,1)S(1)} %fusion.1.refs_0_, ...), custom_call_target="tpu_custom_call" | custom-call | tf_op jit(solution)/shard_map/normed/pallas_call | solution.py:435
  40.9 1.7 collective-permute-done.6.refs_1_
  43.0 1.6 collective-permute-start.8
  44.7 1.7 collective-permute-start.12
  46.4 4.7 %collective-permute-done.8.refs_0_.refs_1_ = bf16[2,40,1536]{2,1,0:T(8,128)(2,1)S(1)} collective-permute-done((bf16[2,40,1536]{2,1,0:T(8,128)(2,1)S(1)}, bf16[2,40,1536]{2,1,0:T(8,128)(2,1)S(1)}, u32[]{:S(2)}, u32[]{:S(2)}) %collective-permute-start.8) | collective-permute-done | bytes 245792 | tf_op jit(solution)/shard_map/ppermute | solution.py:28
  51.1 2.4 %collective-permute-start.10 = (bf16[2,40,1536]{2,1,0:T(8,128)(2,1)S(1)}, bf16[2,40,1536]{2,1,0:T(8,128)(2,1)S(1)}, u32[]{:S(2)}, u32[]{:S(2)}) collective-permute-start(bf16[2,40,1536]{2,1,0:T(8,128)(2,1)S(1)} %collective-permute-done.8.refs_0_.refs_1_), channel_id=1, source_target_pairs={{0,16},{8,24},{16,0},{24,8},{1,17},{9,25},{17,1},{25,9},{2,18},{10... | collective-permute-start | bytes 737288 | tf_op jit(solution)/shard_map/ppermute | solution.py:28
  53.5 2.0 %collective-permute-start.14 = (bf16[2,40,1536]{2,1,0:T(8,128)(2,1)S(1)}, bf16[2,40,1536]{2,1,0:T(8,128)(2,1)S(1)}, u32[]{:S(2)}, u32[]{:S(2)}) collective-permute-start(bf16[2,40,1536]{2,1,0:T(8,128)(2,1)S(1)} %collective-permute-done.12.refs_1_), channel_id=1, source_target_pairs={{0,16},{8,24},{16,0},{24,8},{1,17},{9,25},{17,1},{25,9},{2,18},{10... | collective-permute-start | bytes 737288 | tf_op jit(solution)/shard_map/ppermute | solution.py:28
  55.5 2.6 %collective-permute-start.18 = (bf16[2,40,1536]{2,1,0:T(8,128)(2,1)S(1)}, bf16[2,40,1536]{2,1,0:T(8,128)(2,1)S(1)}, u32[]{:S(2)}, u32[]{:S(2)}) collective-permute-start(bf16[2,40,1536]{2,1,0:T(8,128)(2,1)S(1)} %get-tuple-element.58), channel_id=1, source_target_pairs={{0,4},{1,5},{2,6},{3,7},{4,0},{5,1},{6,2},{7,3},{8,12},{9,13},{10,... | collective-permute-start | bytes 737288 | tf_op jit(solution)/shard_map/ppermute | solution.py:28
  58.1 1.7 collective-permute-start.9
  60.3 1.7 collective-permute-start.11
  62.1 3.5 %collective-permute-done.13.refs_2_ = bf16[2,40,1536]{2,1,0:T(8,128)(2,1)S(1)} collective-permute-done((bf16[2,40,1536]{2,1,0:T(8,128)(2,1)S(1)}, bf16[2,40,1536]{2,1,0:T(8,128)(2,1)S(1)}, u32[]{:S(2)}, u32[]{:S(2)}) %collective-permute-start.13) | collective-permute-done | bytes 245792 | tf_op jit(solution)/shard_map/ppermute | solution.py:28
  65.6 3.6 %collective-permute-start.7 = (bf16[2,40,1536]{2,1,0:T(8,128)(2,1)S(1)}, bf16[2,40,1536]{2,1,0:T(8,128)(2,1)S(1)}, u32[]{:S(2)}, u32[]{:S(2)}) collective-permute-start(bf16[2,40,1536]{2,1,0:T(8,128)(2,1)S(1)} %get-tuple-element.53), channel_id=1, source_target_pairs={{0,6},{1,7},{2,4},{3,5},{4,2},{5,3},{6,0},{7,1},{8,14},{9,15},{10,... | collective-permute-start | bytes 737288 | tf_op jit(solution)/shard_map/ppermute | solution.py:28
  69.4 8.4 %up_0.1.refs_5_ = f32[2,160,1536]{2,1,0:T(8,128)S(1)} custom-call(s32[2]{0:T(128)S(1)} %pad_add_fusion.place, bf16[2,40,1536]{2,1,0:T(8,128)(2,1)S(1)} %get-tuple-element.55.refs_0_, bf16[2,40,1536]{2,1,0:T(8,128)(2,1)S(1)} %collective-permute-done.12.refs_1_, bf16[2,40,1536]{2,1,0:T(8,128)(2,1)S(1)} %collective-permute-done.13.refs_2_, ...), custom_call_target="tpu_custom_call" | custom-call | flops 1509949440 | bytes 9437184 | tf_op jit(solution)/shard_map/up_0/pallas_call | solution.py:219
  77.8 1.8 collective-permute-start.19
  79.6 8.2 %up_1.1.refs_5_ = f32[2,160,1536]{2,1,0:T(8,128)S(1)} custom-call(s32[2]{0:T(128)S(1)} %pad_add_fusion.place, bf16[2,40,1536]{2,1,0:T(8,128)(2,1)S(1)} %collective-permute-done.8.refs_0_.refs_1_, bf16[2,40,1536]{2,1,0:T(8,128)(2,1)S(1)} %collective-permute-done.9.refs_1_, bf16[2,40,1536]{2,1,0:T(8,128)(2,1)S(1)} %collective-permute-done.10.refs_2_, ...), custom_call_target="tpu_custom_call" | custom-call | flops 1509949440 | bytes 9437184 | tf_op jit(solution)/shard_map/up_1/pallas_call | solution.py:219
  87.8 1.9 collective-permute-start.16
  89.9 1.8 collective-permute-start.21
  92.0 4.8 %collective-permute-done.16.refs_2_ = bf16[2,40,1536]{2,1,0:T(8,128)(2,1)S(1)} collective-permute-done((bf16[2,40,1536]{2,1,0:T(8,128)(2,1)S(1)}, bf16[2,40,1536]{2,1,0:T(8,128)(2,1)S(1)}, u32[]{:S(2)}, u32[]{:S(2)}) %collective-permute-start.16) | collective-permute-done | bytes 245792 | tf_op jit(solution)/shard_map/ppermute | solution.py:28
  97.1 1.1 gate.1.weight
  98.2 3.9 %collective-permute-done.20.refs_2_ = bf16[2,40,1536]{2,1,0:T(8,128)(2,1)S(1)} collective-permute-done((bf16[2,40,1536]{2,1,0:T(8,128)(2,1)S(1)}, bf16[2,40,1536]{2,1,0:T(8,128)(2,1)S(1)}, u32[]{:S(2)}, u32[]{:S(2)}) %collective-permute-start.20) | collective-permute-done | bytes 245792 | tf_op jit(solution)/shard_map/ppermute | solution.py:28
  102.1 2.6 %collective-permute-done.21.refs_3_ = bf16[2,40,1536]{2,1,0:T(8,128)(2,1)S(1)} collective-permute-done((bf16[2,40,1536]{2,1,0:T(8,128)(2,1)S(1)}, bf16[2,40,1536]{2,1,0:T(8,128)(2,1)S(1)}, u32[]{:S(2)}, u32[]{:S(2)}) %collective-permute-start.21) | collective-permute-done | bytes 245792 | tf_op jit(solution)/shard_map/ppermute | solution.py:28
  104.7 8.2 %up_2.1.refs_5_ = f32[2,160,1536]{2,1,0:T(8,128)S(1)} custom-call(s32[2]{0:T(128)S(1)} %pad_add_fusion.place, bf16[2,40,1536]{2,1,0:T(8,128)(2,1)S(1)} %collective-permute-done.18.refs_0_.refs_2_, bf16[2,40,1536]{2,1,0:T(8,128)(2,1)S(1)} %collective-permute-done.19.refs_1_, bf16[2,40,1536]{2,1,0:T(8,128)(2,1)S(1)} %collective-permute-done.20.refs_2_, ...), custom_call_target="tpu_custom_call" | custom-call | flops 1509949440 | bytes 9437184 | tf_op jit(solution)/shard_map/up_2/pallas_call | solution.py:219
  112.9 8.3 %up_3.1.hidden = bf16[2,160,1536]{2,1,0:T(8,128)(2,1)S(1)} custom-call(s32[2]{0:T(128)S(1)} %pad_add_fusion.place, bf16[2,40,1536]{2,1,0:T(8,128)(2,1)S(1)} %collective-permute-done.7.refs_3_.refs_0_, bf16[2,40,1536]{2,1,0:T(8,128)(2,1)S(1)} %collective-permute-done.15.refs_1_, bf16[2,40,1536]{2,1,0:T(8,128)(2,1)S(1)} %collective-permute-done.16.refs_2_, ...), custom_call_target="tpu_custom_call" | custom-call | flops 1509949440 | bytes 9437184 | tf_op jit(solution)/shard_map/up_3/pallas_call | solution.py:219
  121.3 8.3 %down_3.1 = (bf16[2,2,40,1536]{3,2,1,0:T(8,128)(2,1)S(1)}, bf16[2,2,40,1536]{3,2,1,0:T(8,128)(2,1)S(1)}) custom-call(s32[2]{0:T(128)S(1)} %pad_add_fusion.place, bf16[2,160,1536]{2,1,0:T(8,128)(2,1)S(1)} %up_3.1.hidden, bf16[2,1536,6144]{2,1,0:T(8,128)(2,1)} %weights.7), custom_call_target="tpu_custom_call" | custom-call | flops 1509949440 | bytes 9437184 | tf_op jit(solution)/shard_map/down_3/pallas_call | solution.py:259
  129.6 1.5 collective-permute-start.22
  131.1 8.3 %down_2.1 = (bf16[2,2,40,1536]{3,2,1,0:T(8,128)(2,1)S(1)}, bf16[2,2,40,1536]{3,2,1,0:T(8,128)(2,1)S(1)}) custom-call(s32[2]{0:T(128)S(1)} %pad_add_fusion.place, bf16[2,160,1536]{2,1,0:T(8,128)(2,1)S(1)} %up_3.1.hidden, bf16[2,1536,6144]{2,1,0:T(8,128)(2,1)} %weights.7), custom_call_target="tpu_custom_call" | custom-call | flops 1509949440 | bytes 9437184 | tf_op jit(solution)/shard_map/down_2/pallas_call | solution.py:259
  139.8 8.3 %down_1.1 = (bf16[2,2,40,1536]{3,2,1,0:T(8,128)(2,1)S(1)}, bf16[2,2,40,1536]{3,2,1,0:T(8,128)(2,1)S(1)}) custom-call(s32[2]{0:T(128)S(1)} %pad_add_fusion.place, bf16[2,160,1536]{2,1,0:T(8,128)(2,1)S(1)} %up_3.1.hidden, bf16[2,1536,6144]{2,1,0:T(8,128)(2,1)} %weights.7), custom_call_target="tpu_custom_call" | custom-call | flops 1509949440 | bytes 9437184 | tf_op jit(solution)/shard_map/down_1/pallas_call | solution.py:259
  148.9 8.3 %down_0.1 = (bf16[2,2,40,1536]{3,2,1,0:T(8,128)(2,1)S(1)}, bf16[2,2,40,1536]{3,2,1,0:T(8,128)(2,1)S(1)}) custom-call(s32[2]{0:T(128)S(1)} %pad_add_fusion.place, bf16[2,160,1536]{2,1,0:T(8,128)(2,1)S(1)} %up_3.1.hidden, bf16[2,1536,6144]{2,1,0:T(8,128)(2,1)} %weights.7), custom_call_target="tpu_custom_call" | custom-call | flops 1509949440 | bytes 9437184 | tf_op jit(solution)/shard_map/down_0/pallas_call | solution.py:259
  157.2 1.8 collective-permute-start.23
  159.4 1.5 collective-permute-start.29
  161.0 1.8 collective-permute-start.28
  162.8 12.1 %collective-permute-done.24.got = bf16[1,2,40,1536]{3,2,1,0:T(8,128)(2,1)S(1)} collective-permute-done((bf16[1,2,40,1536]{3,2,1,0:T(8,128)(2,1)S(1)}, bf16[1,2,40,1536]{3,2,1,0:T(8,128)(2,1)S(1)}, u32[]{:S(2)}, u32[]{:S(2)}) %collective-permute-start.24) | collective-permute-done | bytes 245792 | tf_op jit(solution)/shard_map/ppermute | solution.py:28
  175.0 3.7 %collective-permute-start.32 = (bf16[2,40,1536]{2,1,0:T(8,128)(2,1)S(1)}, bf16[2,40,1536]{2,1,0:T(8,128)(2,1)S(1)}, u32[]{:S(2)}, u32[]{:S(2)}) collective-permute-start(bf16[2,40,1536]{2,1,0:T(8,128)(2,1)S(1)} %reply.4), channel_id=1, source_target_pairs={{0,6},{1,7},{2,4},{3,5},{4,2},{5,3},{6,0},{7,1},{8,14},{9,15},{10,... | collective-permute-start | bytes 737288 | tf_op jit(solution)/shard_map/ppermute | solution.py:28
  178.8 1.2 collective-permute-start.27
  181.1 4.0 %collective-permute-done.27.got = bf16[1,2,40,1536]{3,2,1,0:T(8,128)(2,1)S(1)} collective-permute-done((bf16[1,2,40,1536]{3,2,1,0:T(8,128)(2,1)S(1)}, bf16[1,2,40,1536]{3,2,1,0:T(8,128)(2,1)S(1)}, u32[]{:S(2)}, u32[]{:S(2)}) %collective-permute-start.27) | collective-permute-done | bytes 245792 | tf_op jit(solution)/shard_map/ppermute | solution.py:28
  185.2 7.7 %collective-permute-done.31.refs_2_ = bf16[2,40,1536]{2,1,0:T(8,128)(2,1)S(1)} collective-permute-done((bf16[2,40,1536]{2,1,0:T(8,128)(2,1)S(1)}, bf16[2,40,1536]{2,1,0:T(8,128)(2,1)S(1)}, u32[]{:S(2)}, u32[]{:S(2)}) %collective-permute-start.31) | collective-permute-done | bytes 245792 | tf_op jit(solution)/shard_map/ppermute | solution.py:28
  193.6 1.7 collective-permute-done.33
  (80 shorter events, 10.9 us)
Async XLA Ops:
  0.0 31.8 %copy-start = (bf16[4,64,768]{2,1,0:T(8,128)(2,1)S(1)}, bf16[4,64,768]{2,1,0:T(8,128)(2,1)}, u32[]{:S(2)}) copy-start(bf16[4,64,768]{2,1,0:T(8,128)(2,1)} %queries.3) | copy-start | bytes 1179652
  1.0 16.1 %collective-permute-start.3 = (f32[2,12,1,1]{1,0,3,2:T(2,128)S(1)}, f32[2,12,1,1]{1,0,3,2:T(2,128)S(1)}, u32[]{:S(2)}, u32[]{:S(2)}) collective-permute-start(f32[2,12,1,1]{1,0,3,2:T(2,128)S(1)} %exp.14), channel_id=1, source_target_pairs={{0,24},{8,16},{16,8},{24,0},{1,25},{9,17},{17,9},{25,1},{2,26},{10... | collective-permute-start | bytes 296 | tf_op jit(solution)/shard_map/ppermute | solution.py:28
  4.9 12.2 %collective-permute-start.1 = (f32[2,12,1,1]{1,0,3,2:T(2,128)S(1)}, f32[2,12,1,1]{1,0,3,2:T(2,128)S(1)}, u32[]{:S(2)}, u32[]{:S(2)}) collective-permute-start(f32[2,12,1,1]{1,0,3,2:T(2,128)S(1)} %exp.14), channel_id=1, source_target_pairs={{0,8},{8,0},{16,24},{24,16},{1,9},{9,1},{17,25},{25,17},{2,10},{10... | collective-permute-start | bytes 296 | tf_op jit(solution)/shard_map/ppermute | solution.py:28
  5.5 1.0 copy-start.1
  6.5 1.0 copy-start.3
  7.5 0.7 copy-start.5
  8.2 23.5 %copy-start.9 = (f32[768]{0:T(1024)S(1)}, f32[768]{0:T(1024)}, u32[]{:S(2)}) copy-start(f32[768]{0:T(1024)} %param.13) | copy-start | bytes 9220
  8.2 23.6 %copy-start.2 = (bf16[4,64,768]{2,1,0:T(8,128)(2,1)S(1)}, bf16[4,64,768]{2,1,0:T(8,128)(2,1)}, u32[]{:S(2)}) copy-start(bf16[4,64,768]{2,1,0:T(8,128)(2,1)} %keys.3) | copy-start | bytes 1179652
  8.2 23.6 %copy-start.4 = (bf16[4,64,768]{2,1,0:T(8,128)(2,1)S(1)}, bf16[4,64,768]{2,1,0:T(8,128)(2,1)}, u32[]{:S(2)}) copy-start(bf16[4,64,768]{2,1,0:T(8,128)(2,1)} %values.3) | copy-start | bytes 1179652
  8.2 23.6 %copy-start.6 = (f32[4,64,6]{1,0,2:T(4,128)S(1)}, f32[4,64,6]{1,0,2:T(4,128)}, u32[]{:S(2)}) copy-start(f32[4,64,6]{1,0,2:T(4,128)} %param.12) | copy-start | bytes 18436
  8.2 23.6 %copy-start.8 = (s32[64,4,2]{0,2,1:T(2,128)S(1)}, s32[64,4,2]{0,2,1:T(2,128)}, u32[]{:S(2)}) copy-start(s32[64,4,2]{0,2,1:T(2,128)} %param.17) | copy-start | bytes 6148
  10.8 15.2 %collective-permute-start = (bf16[12,128,128]{2,1,0:T(8,128)(2,1)S(1)}, bf16[12,128,128]{2,1,0:T(8,128)(2,1)S(1)}, u32[]{:S(2)}, u32[]{:S(2)}) collective-permute-start(bf16[12,128,128]{2,1,0:T(8,128)(2,1)S(1)} %get-tuple-element.50), channel_id=1, source_target_pairs={{0,8},{8,0},{16,24},{1,9},{9,1},{17,25},{2,10},{10,2},{18,26},{3,1... | collective-permute-start | bytes 1179656 | tf_op jit(solution)/shard_map/ppermute | solution.py:28
  14.3 10.0 %collective-permute-start.4 = (bf16[12,128,128]{2,1,0:T(8,128)(2,1)S(1)}, bf16[12,128,128]{2,1,0:T(8,128)(2,1)S(1)}, u32[]{:S(2)}, u32[]{:S(2)}) collective-permute-start(bf16[12,128,128]{2,1,0:T(8,128)(2,1)S(1)} %get-tuple-element.51), channel_id=1, source_target_pairs={{0,16},{8,24},{1,17},{9,25},{2,18},{10,26},{3,19},{11,27},{4,20},{... | collective-permute-start | bytes 1179656 | tf_op jit(solution)/shard_map/ppermute | solution.py:28
  24.4 11.7 %collective-permute-start.5 = (bf16[12,128,128]{2,1,0:T(8,128)(2,1)S(1)}, bf16[12,128,128]{2,1,0:T(8,128)(2,1)S(1)}, u32[]{:S(2)}, u32[]{:S(2)}) collective-permute-start(bf16[12,128,128]{2,1,0:T(8,128)(2,1)S(1)} %fusion.7), channel_id=1, source_target_pairs={{0,8},{16,24},{24,16},{1,9},{17,25},{25,17},{2,10},{18,26},{26,18}... | collective-permute-start | bytes 1179656 | tf_op jit(solution)/shard_map/ppermute | solution.py:28
  27.0 11.6 %collective-permute-start.2 = (bf16[12,128,128]{2,1,0:T(8,128)(2,1)}, bf16[12,128,128]{2,1,0:T(8,128)(2,1)S(1)}, u32[]{:S(2)}, u32[]{:S(2)}) collective-permute-start(bf16[12,128,128]{2,1,0:T(8,128)(2,1)} %fusion.3), channel_id=1, source_target_pairs={{0,16},{8,24},{1,17},{9,25},{2,18},{10,26},{3,19},{11,27},{4,20},{... | collective-permute-start | bytes 1179656 | tf_op jit(solution)/shard_map/ppermute | solution.py:28
  40.8 1.8 collective-permute-start.6
  43.0 8.1 %collective-permute-start.8 = (bf16[2,40,1536]{2,1,0:T(8,128)(2,1)S(1)}, bf16[2,40,1536]{2,1,0:T(8,128)(2,1)S(1)}, u32[]{:S(2)}, u32[]{:S(2)}) collective-permute-start(bf16[2,40,1536]{2,1,0:T(8,128)(2,1)S(1)} %get-tuple-element.54), channel_id=1, source_target_pairs={{0,2},{1,3},{2,0},{3,1},{4,6},{5,7},{6,4},{7,5},{8,10},{9,11},{10,... | collective-permute-start | bytes 737288 | tf_op jit(solution)/shard_map/ppermute | solution.py:28
  44.7 8.8 %collective-permute-start.12 = (bf16[2,40,1536]{2,1,0:T(8,128)(2,1)S(1)}, bf16[2,40,1536]{2,1,0:T(8,128)(2,1)S(1)}, u32[]{:S(2)}, u32[]{:S(2)}) collective-permute-start(bf16[2,40,1536]{2,1,0:T(8,128)(2,1)S(1)} %get-tuple-element.55.refs_0_), channel_id=1, source_target_pairs={{0,8},{8,0},{16,24},{24,16},{1,9},{9,1},{17,25},{25,17},{2,10},{10... | collective-permute-start | bytes 737288 | tf_op jit(solution)/shard_map/ppermute | solution.py:28
  51.1 9.2 %collective-permute-start.10 = (bf16[2,40,1536]{2,1,0:T(8,128)(2,1)S(1)}, bf16[2,40,1536]{2,1,0:T(8,128)(2,1)S(1)}, u32[]{:S(2)}, u32[]{:S(2)}) collective-permute-start(bf16[2,40,1536]{2,1,0:T(8,128)(2,1)S(1)} %collective-permute-done.8.refs_0_.refs_1_), channel_id=1, source_target_pairs={{0,16},{8,24},{16,0},{24,8},{1,17},{9,25},{17,1},{25,9},{2,18},{10... | collective-permute-start | bytes 737288 | tf_op jit(solution)/shard_map/ppermute | solution.py:28
  53.5 12.1 %collective-permute-start.13 = (bf16[2,40,1536]{2,1,0:T(8,128)(2,1)S(1)}, bf16[2,40,1536]{2,1,0:T(8,128)(2,1)S(1)}, u32[]{:S(2)}, u32[]{:S(2)}) collective-permute-start(bf16[2,40,1536]{2,1,0:T(8,128)(2,1)S(1)} %get-tuple-element.55.refs_0_), channel_id=1, source_target_pairs={{0,16},{8,24},{16,0},{24,8},{1,17},{9,25},{17,1},{25,9},{2,18},{10... | collective-permute-start | bytes 737288 | tf_op jit(solution)/shard_map/ppermute | solution.py:28
  53.5 15.9 %collective-permute-start.14 = (bf16[2,40,1536]{2,1,0:T(8,128)(2,1)S(1)}, bf16[2,40,1536]{2,1,0:T(8,128)(2,1)S(1)}, u32[]{:S(2)}, u32[]{:S(2)}) collective-permute-start(bf16[2,40,1536]{2,1,0:T(8,128)(2,1)S(1)} %collective-permute-done.12.refs_1_), channel_id=1, source_target_pairs={{0,16},{8,24},{16,0},{24,8},{1,17},{9,25},{17,1},{25,9},{2,18},{10... | collective-permute-start | bytes 737288 | tf_op jit(solution)/shard_map/ppermute | solution.py:28
  55.5 22.3 %collective-permute-start.18 = (bf16[2,40,1536]{2,1,0:T(8,128)(2,1)S(1)}, bf16[2,40,1536]{2,1,0:T(8,128)(2,1)S(1)}, u32[]{:S(2)}, u32[]{:S(2)}) collective-permute-start(bf16[2,40,1536]{2,1,0:T(8,128)(2,1)S(1)} %get-tuple-element.58), channel_id=1, source_target_pairs={{0,4},{1,5},{2,6},{3,7},{4,0},{5,1},{6,2},{7,3},{8,12},{9,13},{10,... | collective-permute-start | bytes 737288 | tf_op jit(solution)/shard_map/ppermute | solution.py:28
  58.1 21.5 %collective-permute-start.9 = (bf16[2,40,1536]{2,1,0:T(8,128)(2,1)S(1)}, bf16[2,40,1536]{2,1,0:T(8,128)(2,1)S(1)}, u32[]{:S(2)}, u32[]{:S(2)}) collective-permute-start(bf16[2,40,1536]{2,1,0:T(8,128)(2,1)S(1)} %collective-permute-done.8.refs_0_.refs_1_), channel_id=1, source_target_pairs={{0,8},{8,0},{16,24},{24,16},{1,9},{9,1},{17,25},{25,17},{2,10},{10... | collective-permute-start | bytes 737288 | tf_op jit(solution)/shard_map/ppermute | solution.py:28
  60.3 19.3 %collective-permute-start.11 = (bf16[2,40,1536]{2,1,0:T(8,128)(2,1)S(1)}, bf16[2,40,1536]{2,1,0:T(8,128)(2,1)S(1)}, u32[]{:S(2)}, u32[]{:S(2)}) collective-permute-start(bf16[2,40,1536]{2,1,0:T(8,128)(2,1)S(1)} %collective-permute-done.10.refs_2_), channel_id=1, source_target_pairs={{0,8},{8,0},{16,24},{24,16},{1,9},{9,1},{17,25},{25,17},{2,10},{10... | collective-permute-start | bytes 737288 | tf_op jit(solution)/shard_map/ppermute | solution.py:28
  65.6 22.2 %collective-permute-start.7 = (bf16[2,40,1536]{2,1,0:T(8,128)(2,1)S(1)}, bf16[2,40,1536]{2,1,0:T(8,128)(2,1)S(1)}, u32[]{:S(2)}, u32[]{:S(2)}) collective-permute-start(bf16[2,40,1536]{2,1,0:T(8,128)(2,1)S(1)} %get-tuple-element.53), channel_id=1, source_target_pairs={{0,6},{1,7},{2,4},{3,5},{4,2},{5,3},{6,0},{7,1},{8,14},{9,15},{10,... | collective-permute-start | bytes 737288 | tf_op jit(solution)/shard_map/ppermute | solution.py:28
  77.8 19.3 %copy-start.7 = (bf16[6144,16]{0,1:T(8,128)(2,1)S(1)}, bf16[6144,16]{0,1:T(8,128)(2,1)}, u32[]{:S(2)}) copy-start(bf16[6144,16]{0,1:T(8,128)(2,1)} %param.14) | copy-start | bytes 589828
  77.8 12.1 %collective-permute-start.19 = (bf16[2,40,1536]{2,1,0:T(8,128)(2,1)S(1)}, bf16[2,40,1536]{2,1,0:T(8,128)(2,1)S(1)}, u32[]{:S(2)}, u32[]{:S(2)}) collective-permute-start(bf16[2,40,1536]{2,1,0:T(8,128)(2,1)S(1)} %collective-permute-done.18.refs_0_.refs_2_), channel_id=1, source_target_pairs={{0,8},{8,0},{16,24},{24,16},{1,9},{9,1},{17,25},{25,17},{2,10},{10... | collective-permute-start | bytes 737288 | tf_op jit(solution)/shard_map/ppermute | solution.py:28
  87.8 9.0 %collective-permute-start.16 = (bf16[2,40,1536]{2,1,0:T(8,128)(2,1)S(1)}, bf16[2,40,1536]{2,1,0:T(8,128)(2,1)S(1)}, u32[]{:S(2)}, u32[]{:S(2)}) collective-permute-start(bf16[2,40,1536]{2,1,0:T(8,128)(2,1)S(1)} %collective-permute-done.7.refs_3_.refs_0_), channel_id=1, source_target_pairs={{0,16},{8,24},{16,0},{24,8},{1,17},{9,25},{17,1},{25,9},{2,18},{10... | collective-permute-start | bytes 737288 | tf_op jit(solution)/shard_map/ppermute | solution.py:28
  89.7 12.3 %collective-permute-start.20 = (bf16[2,40,1536]{2,1,0:T(8,128)(2,1)S(1)}, bf16[2,40,1536]{2,1,0:T(8,128)(2,1)S(1)}, u32[]{:S(2)}, u32[]{:S(2)}) collective-permute-start(bf16[2,40,1536]{2,1,0:T(8,128)(2,1)S(1)} %collective-permute-done.18.refs_0_.refs_2_), channel_id=1, source_target_pairs={{0,16},{8,24},{16,0},{24,8},{1,17},{9,25},{17,1},{25,9},{2,18},{10... | collective-permute-start | bytes 737288 | tf_op jit(solution)/shard_map/ppermute | solution.py:28
  89.9 14.8 %collective-permute-start.21 = (bf16[2,40,1536]{2,1,0:T(8,128)(2,1)S(1)}, bf16[2,40,1536]{2,1,0:T(8,128)(2,1)S(1)}, u32[]{:S(2)}, u32[]{:S(2)}) collective-permute-start(bf16[2,40,1536]{2,1,0:T(8,128)(2,1)S(1)} %collective-permute-done.19.refs_1_), channel_id=1, source_target_pairs={{0,16},{8,24},{16,0},{24,8},{1,17},{9,25},{17,1},{25,9},{2,18},{10... | collective-permute-start | bytes 737288 | tf_op jit(solution)/shard_map/ppermute | solution.py:28
  91.8 21.2 %collective-permute-start.15 = (bf16[2,40,1536]{2,1,0:T(8,128)(2,1)S(1)}, bf16[2,40,1536]{2,1,0:T(8,128)(2,1)S(1)}, u32[]{:S(2)}, u32[]{:S(2)}) collective-permute-start(bf16[2,40,1536]{2,1,0:T(8,128)(2,1)S(1)} %collective-permute-done.7.refs_3_.refs_0_), channel_id=1, source_target_pairs={{0,8},{8,0},{16,24},{24,16},{1,9},{9,1},{17,25},{25,17},{2,10},{10... | collective-permute-start | bytes 737288 | tf_op jit(solution)/shard_map/ppermute | solution.py:28
  96.8 16.1 %collective-permute-start.17 = (bf16[2,40,1536]{2,1,0:T(8,128)(2,1)S(1)}, bf16[2,40,1536]{2,1,0:T(8,128)(2,1)S(1)}, u32[]{:S(2)}, u32[]{:S(2)}) collective-permute-start(bf16[2,40,1536]{2,1,0:T(8,128)(2,1)S(1)} %collective-permute-done.16.refs_2_), channel_id=1, source_target_pairs={{0,8},{8,0},{16,24},{24,16},{1,9},{9,1},{17,25},{25,17},{2,10},{10... | collective-permute-start | bytes 737288 | tf_op jit(solution)/shard_map/ppermute | solution.py:28
  129.6 19.2 %collective-permute-start.22 = (bf16[2,2,40,1536]{3,2,1,0:T(8,128)(2,1)S(1)}, bf16[2,2,40,1536]{3,2,1,0:T(8,128)(2,1)S(1)}, u32[]{:S(2)}, u32[]{:S(2)}) collective-permute-start(bf16[2,2,40,1536]{3,2,1,0:T(8,128)(2,1)S(1)} %get-tuple-element.65), channel_id=1, source_target_pairs={{0,16},{8,24},{16,0},{24,8},{1,17},{9,25},{17,1},{25,9},{2,18},{10... | collective-permute-start | bytes 1474568 | tf_op jit(solution)/shard_map/ppermute | solution.py:28
  139.4 19.8 %collective-permute-start.26 = (bf16[2,2,40,1536]{3,2,1,0:T(8,128)(2,1)S(1)}, bf16[2,2,40,1536]{3,2,1,0:T(8,128)(2,1)S(1)}, u32[]{:S(2)}, u32[]{:S(2)}) collective-permute-start(bf16[2,2,40,1536]{3,2,1,0:T(8,128)(2,1)S(1)} %get-tuple-element.67), channel_id=1, source_target_pairs={{0,8},{8,0},{16,24},{24,16},{1,9},{9,1},{17,25},{25,17},{2,10},{10... | collective-permute-start | bytes 1474568 | tf_op jit(solution)/shard_map/ppermute | solution.py:28
  148.1 12.8 %collective-permute-start.25 = (bf16[2,2,40,1536]{3,2,1,0:T(8,128)(2,1)S(1)}, bf16[2,2,40,1536]{3,2,1,0:T(8,128)(2,1)S(1)}, u32[]{:S(2)}, u32[]{:S(2)}) collective-permute-start(bf16[2,2,40,1536]{3,2,1,0:T(8,128)(2,1)S(1)} %get-tuple-element.69), channel_id=1, source_target_pairs={{0,16},{8,24},{16,0},{24,8},{1,17},{9,25},{17,1},{25,9},{2,18},{10... | collective-permute-start | bytes 1474568 | tf_op jit(solution)/shard_map/ppermute | solution.py:28
  157.2 21.5 %collective-permute-start.23 = (bf16[2,2,40,1536]{3,2,1,0:T(8,128)(2,1)S(1)}, bf16[2,2,40,1536]{3,2,1,0:T(8,128)(2,1)S(1)}, u32[]{:S(2)}, u32[]{:S(2)}) collective-permute-start(bf16[2,2,40,1536]{3,2,1,0:T(8,128)(2,1)S(1)} %get-tuple-element.74), channel_id=1, source_target_pairs={{0,8},{8,0},{16,24},{24,16},{1,9},{9,1},{17,25},{25,17},{2,10},{10... | collective-permute-start | bytes 1474568 | tf_op jit(solution)/shard_map/ppermute | solution.py:28
  159.0 15.9 %collective-permute-start.24 = (bf16[1,2,40,1536]{3,2,1,0:T(8,128)(2,1)S(1)}, bf16[1,2,40,1536]{3,2,1,0:T(8,128)(2,1)S(1)}, u32[]{:S(2)}, u32[]{:S(2)}) collective-permute-start(bf16[1,2,40,1536]{3,2,1,0:T(8,128)(2,1)S(1)} %get-tuple-element.71), channel_id=1, source_target_pairs={{0,8},{8,0},{16,24},{24,16},{1,9},{9,1},{17,25},{25,17},{2,10},{10... | collective-permute-start | bytes 737288 | tf_op jit(solution)/shard_map/ppermute | solution.py:28
  159.4 20.6 %collective-permute-start.29 = (bf16[1,2,40,1536]{3,2,1,0:T(8,128)(2,1)S(1)}, bf16[1,2,40,1536]{3,2,1,0:T(8,128)(2,1)S(1)}, u32[]{:S(2)}, u32[]{:S(2)}) collective-permute-start(bf16[1,2,40,1536]{3,2,1,0:T(8,128)(2,1)S(1)} %get-tuple-element.79), channel_id=1, source_target_pairs={{0,16},{8,24},{16,0},{24,8},{1,17},{9,25},{17,1},{25,9},{2,18},{10... | collective-permute-start | bytes 737288 | tf_op jit(solution)/shard_map/ppermute | solution.py:28
  161.0 19.2 %collective-permute-start.28 = (bf16[1,2,40,1536]{3,2,1,0:T(8,128)(2,1)S(1)}, bf16[1,2,40,1536]{3,2,1,0:T(8,128)(2,1)S(1)}, u32[]{:S(2)}, u32[]{:S(2)}) collective-permute-start(bf16[1,2,40,1536]{3,2,1,0:T(8,128)(2,1)S(1)} %get-tuple-element.81), channel_id=1, source_target_pairs={{0,8},{8,0},{16,24},{24,16},{1,9},{9,1},{17,25},{25,17},{2,10},{10... | collective-permute-start | bytes 737288 | tf_op jit(solution)/shard_map/ppermute | solution.py:28
  175.0 10.2 %collective-permute-start.32 = (bf16[2,40,1536]{2,1,0:T(8,128)(2,1)S(1)}, bf16[2,40,1536]{2,1,0:T(8,128)(2,1)S(1)}, u32[]{:S(2)}, u32[]{:S(2)}) collective-permute-start(bf16[2,40,1536]{2,1,0:T(8,128)(2,1)S(1)} %reply.4), channel_id=1, source_target_pairs={{0,6},{1,7},{2,4},{3,5},{4,2},{5,3},{6,0},{7,1},{8,14},{9,15},{10,... | collective-permute-start | bytes 737288 | tf_op jit(solution)/shard_map/ppermute | solution.py:28
  178.8 6.3 %collective-permute-start.27 = (bf16[1,2,40,1536]{3,2,1,0:T(8,128)(2,1)S(1)}, bf16[1,2,40,1536]{3,2,1,0:T(8,128)(2,1)S(1)}, u32[]{:S(2)}, u32[]{:S(2)}) collective-permute-start(bf16[1,2,40,1536]{3,2,1,0:T(8,128)(2,1)S(1)} %get-tuple-element.85), channel_id=1, source_target_pairs={{0,16},{8,24},{16,0},{24,8},{1,17},{9,25},{17,1},{25,9},{2,18},{10... | collective-permute-start | bytes 737288 | tf_op jit(solution)/shard_map/ppermute | solution.py:28
  180.1 12.8 %collective-permute-start.31 = (bf16[2,40,1536]{2,1,0:T(8,128)(2,1)S(1)}, bf16[2,40,1536]{2,1,0:T(8,128)(2,1)S(1)}, u32[]{:S(2)}, u32[]{:S(2)}) collective-permute-start(bf16[2,40,1536]{2,1,0:T(8,128)(2,1)S(1)} %reply.5), channel_id=1, source_target_pairs={{0,4},{1,5},{2,6},{3,7},{4,0},{5,1},{6,2},{7,3},{8,12},{9,13},{10,... | collective-permute-start | bytes 737288 | tf_op jit(solution)/shard_map/ppermute | solution.py:28
  180.3 12.6 %collective-permute-start.30 = (bf16[2,40,1536]{2,1,0:T(8,128)(2,1)S(1)}, bf16[2,40,1536]{2,1,0:T(8,128)(2,1)S(1)}, u32[]{:S(2)}, u32[]{:S(2)}) collective-permute-start(bf16[2,40,1536]{2,1,0:T(8,128)(2,1)S(1)} %reply.6), channel_id=1, source_target_pairs={{0,2},{1,3},{2,0},{3,1},{4,6},{5,7},{6,4},{7,5},{8,10},{9,11},{10,... | collective-permute-start | bytes 737288 | tf_op jit(solution)/shard_map/ppermute | solution.py:28
  193.5 1.8 collective-permute-start.33

commit v3 on v2

--- a/solution.py
+++ b/solution.py
@@ -12,12 +12,11 @@
 BF16 = jnp.bfloat16
 VMEM = pl.BlockSpec(memory_space=pltpu.VMEM)
 SMEM = pl.BlockSpec(memory_space=pltpu.SMEM)
-
-
-def params(mib, n=0):
-    return pltpu.CompilerParams(
-        vmem_limit_bytes=mib << 20, dimension_semantics=("arbitrary",) * n if n else None
-    )
+ANY = pl.BlockSpec(memory_space=pl.ANY)
+
+
+def params(mib):
+    return pltpu.CompilerParams(vmem_limit_bytes=mib << 20)
 
 
 def bits_of(n):
@@ -178,107 +177,114 @@
         weight[j] = jnp.broadcast_to(1.0 / (1.0 + jnp.exp(theirs - mine)), (cap, 128))
 
 
-def tiles_of(width):
-    return 2 if width % 512 == 0 else 1
-
-
-def up_kernel(place, *refs, parts, first, last):
-    blocks, weights = refs[:parts], refs[parts]
-    out, acc = refs[-2:]
-    j, k = pl.program_id(0), pl.program_id(1)
-    depth = weights.shape[1]
-    steps = blocks[0].shape[2] // depth
-    for step in range(steps):
-
-        @pl.when(k == step)
-        def _():
-            lanes = slice(step * depth, (step + 1) * depth)
+def tiles_of(rows):
+    return 2 if rows % 512 == 0 else 1
+
+
+def up_kernel(place, weights, *refs, chunk, parts, first, last):
+    blocks, (out, buffer, sems) = refs[:parts], refs[-3:]
+    own, steps, depth, _ = buffer.shape
+    tiles = steps // 2
+    owner = place[1]
+
+    def at(t):
+        return pl.multiple_of(((owner ^ (2 * chunk + t // tiles)) * tiles + t % tiles) * depth, depth)
+
+    copies = []
+    for j in range(own):
+        for t in range(steps):
+            copy = pltpu.make_async_copy(
+                weights.at[j, pl.ds(at(t), depth), :], buffer.at[j, t], sems.at[j, t]
+            )
+            copy.start()
+            copies.append(copy)
+    for j in range(own):
+        total = None if first else refs[parts][j]
+        for t in range(steps):
+            lanes = slice(t * depth, (t + 1) * depth)
             x = jnp.concatenate([b[j, :, lanes].astype(F32) for b in blocks], axis=0).astype(BF16)
-            total = dot(x, weights[0])
-            if step:
-                total = total + acc[...]
-            elif not first:
-                total = total + refs[parts + 1][0]
-            if step < steps - 1:
-                acc[...] = total
-            elif last:
-                out[0] = (total / (1.0 + jnp.exp(-total))).astype(BF16)
-            else:
-                out[0] = total
+            copies[j * steps + t].wait()
+            part = dot(x, buffer[j, t])
+            total = part if total is None else total + part
+        out[j] = (total / (1.0 + jnp.exp(-total))).astype(BF16) if last else total
 
 
 def up_chunk(place, chunk, blocks, weights, total, last):
-    own, depth, hidden = weights.shape
+    own, _, hidden = weights.shape
     cap, width = blocks[0].shape[1:]
     parts = len(blocks)
     rows = parts * cap
-    tiles = tiles_of(width)
-    tile = width // 2 // tiles
+    steps = 2 * tiles_of(width // 2)
     first = total is None
-    total_spec = pl.BlockSpec((1, rows, hidden), lambda j, k, at: (j, 0, 0))
     return pl.pallas_call(
-        functools.partial(up_kernel, parts=parts, first=first, last=last),
-        grid_spec=pltpu.PrefetchScalarGridSpec(
-            num_scalar_prefetch=1,
-            grid=(own, 2 * tiles),
-            in_specs=[VMEM] * parts
-            + [
-                pl.BlockSpec(
-                    (1, tile, hidden),
-                    lambda j, k, at: (j, (at[1] ^ (2 * chunk + k // tiles)) * tiles + k % tiles, 0),
-                )
-            ]
-            + ([] if first else [total_spec]),
-            out_specs=total_spec,
-            scratch_shapes=[pltpu.VMEM((rows, hidden), F32)],
-        ),
+        functools.partial(up_kernel, chunk=chunk, parts=parts, first=first, last=last),
+        in_specs=[SMEM, ANY] + [VMEM] * (parts + (not first)),
+        out_specs=VMEM,
         out_shape=jax.ShapeDtypeStruct((own, rows, hidden), BF16 if last else F32),
-        compiler_params=params(32, 2),
+        scratch_shapes=[
+            pltpu.VMEM((own, steps, width // steps, hidden), BF16),
+            pltpu.SemaphoreType.DMA((own, steps)),
+        ],
+        compiler_params=params(32),
         cost_estimate=pl.CostEstimate(
             flops=2 * own * rows * width * hidden,
             bytes_accessed=2 * own * width * hidden,
             transcendentals=0,
         ),
         name=f"up_{chunk}",
-    )(place, *blocks, weights, *([] if first else [total]))
-
-
-def down_kernel(place, hidden, weights, *outs, route):
-    result = dot(hidden[0], weights[0])
-    for out, members in zip(outs, route):
-        for i, member in enumerate(members):
-            out[i, 0] = result[member * CAP : (member + 1) * CAP].astype(BF16)
+    )(place, weights, *blocks, *([] if first else [total]))
+
+
+def down_kernel(place, weights, hidden, *refs, chunk, route):
+    outs, (buffer, sems) = refs[:-2], refs[-2:]
+    own, steps, depth, half = buffer.shape
+    owner = place[1]
+    copies = []
+    for j in range(own):
+        for t in range(steps):
+            col = pl.multiple_of((owner ^ (2 * chunk + t // (steps // 2))) * half, half)
+            row = (t % (steps // 2)) * depth
+            copy = pltpu.make_async_copy(
+                weights.at[j, row : row + depth, pl.ds(col, half)], buffer.at[j, t], sems.at[j, t]
+            )
+            copy.start()
+            copies.append(copy)
+    for j in range(own):
+        for side in range(2):
+            total = None
+            for t in range(steps // 2):
+                copies[j * steps + side * (steps // 2) + t].wait()
+                part = dot(
+                    hidden[j, :, t * depth : (t + 1) * depth], buffer[j, side * (steps // 2) + t]
+                )
+                total = part if total is None else total + part
+            lanes = slice(side * half, (side + 1) * half)
+            for out, members in zip(outs, route):
+                for i, member in enumerate(members):
+                    out[i, j, :, lanes] = total[member * CAP : (member + 1) * CAP].astype(BF16)
 
 
 def down_chunk(place, chunk, hidden, weights, width, route):
     own, rows, depth = hidden.shape
     parts = rows // CAP
-    tiles = tiles_of(width)
-    tile = width // 2 // tiles
-    out_spec = pl.BlockSpec((parts // 2, 1, CAP, tile), lambda j, n, at: (0, j, 0, n))
+    tiles = tiles_of(depth)
     return pl.pallas_call(
-        functools.partial(down_kernel, route=route),
-        grid_spec=pltpu.PrefetchScalarGridSpec(
-            num_scalar_prefetch=1,
-            grid=(own, 2 * tiles),
-            in_specs=[
-                pl.BlockSpec((1, rows, depth), lambda j, n, at: (j, 0, 0)),
-                pl.BlockSpec(
-                    (1, depth, tile),
-                    lambda j, n, at: (j, 0, (at[1] ^ (2 * chunk + n // tiles)) * tiles + n % tiles),
-                ),
-            ],
-            out_specs=[out_spec] * 2,
-        ),
+        functools.partial(down_kernel, chunk=chunk, route=route),
+        in_specs=[SMEM, ANY, VMEM],
+        out_specs=[VMEM] * 2,
         out_shape=[jax.ShapeDtypeStruct((parts // 2, own, CAP, width), BF16)] * 2,
-        compiler_params=params(32, 2),
+        scratch_shapes=[
+            pltpu.VMEM((own, 2 * tiles, depth // tiles, width // 2), BF16),
+            pltpu.SemaphoreType.DMA((own, 2 * tiles)),
+        ],
+        compiler_params=params(32),
         cost_estimate=pl.CostEstimate(
             flops=2 * own * rows * width * depth,
             bytes_accessed=2 * own * width * depth,
             transcendentals=0,
         ),
         name=f"down_{chunk}",
-    )(place, hidden, weights)
+    )(place, weights, hidden)
 
 
 def combine_kernel(normed, placement, *refs):
@@ -402,7 +408,7 @@
 
     states = pl.pallas_call(
         state_kernel,
-        in_specs=[pl.BlockSpec(memory_space=pl.ANY)] * 2 + [VMEM],
+        in_specs=[ANY] * 2 + [VMEM],
         out_specs=[VMEM] * halves,
         out_shape=[struct((pairs, dim, dim), BF16)] * halves,
         scratch_shapes=[
@@ -410,10 +416,10 @@
             pltpu.VMEM(values.shape, BF16),
             pltpu.SemaphoreType.DMA((2, requests)),
         ],
-        compiler_params=params(32),
+        compiler_params=params(60),
         name="local_state",
     )(keys, values, decay_rows)
-    decay = jnp.exp(jnp.sum(log_decay, axis=1)).reshape(halves, pairs, 1, 1)
+    decay = jnp.exp(jnp.sum(after(log_decay, *states), axis=1)).reshape(halves, pairs, 1, 1)
     if n_ctx == 4 and halves == 2:
         incoming = prefix_of_four(states, decay, me)
     else:
@@ -473,11 +479,12 @@
     for k in range(chunks):
         have = {0: arrived[k]}
         for bit in orders[k]:
-            have = gather_round(have, bit, total if k >= 2 else None)
+            have = gather_round(have, bit, None)
         gathered[k] = [have[rel] for rel in range(n_ctx)]
-        if k >= 1:
-            total = up_chunk(place, k - 1, gathered[k - 1], expert_up, total, False)
-    hidden = up_chunk(place, chunks - 1, gathered[-1], expert_up, after(total, weight), True)
+    gathered[0][0] = after(gathered[0][0], weight)
+    for k in range(chunks):
+        total = up_chunk(place, k, gathered[k], expert_up, total, k == chunks - 1)
+    hidden = total
 
     pending, returned = [], [None] * chunks
 

time: 198 us -> 160 us (0.81)
  Pallas kernels: 78.2 us -> 54.4 us
  waiting for transfers between devices: 56.8 us -> 42.2 us
  other arithmetic: 3.36 us -> 6.31 us
  local copies, waits for them, and re-layouts: 3.28 us -> 1.26 us
    pallas_call x9, Pallas kernels: 68.9 us -> 45.2 us  [the longest x4 21.2 us: down_chunk(): pl.pallas_call(functools.partial(down_kernel, chunk=chunk, route=route),...]
    ppermute x34, waiting for transfers between devices: 56.8 us -> 42.2 us  [swap(): return lax.ppermute(x, axis, [(i, i ^ k) for i in range(n) if keep(i)])]
    unnamed x20 -> x14, local copies, waits for them, and re-layouts: 2.73 us -> 0.03 us
  transfers between devices with their start and end apart: 34 -> 34, of which waited for: 14 -> 13; matrix products, arithmetic and copies ran while one was open for 1% -> 3% of each run, Pallas kernels for 30% -> 23%
where the time goes in v3:
time: 160 us
  starting transfers between devices  55.5 us (35%)
  Pallas kernels  54.4 us (34%)
  waiting for transfers between devices  42.2 us (26%)
  other arithmetic  6.31 us (4%)
    ppermute x34, starting transfers between devices, swap(): return lax.ppermute(x, axis, [(i, i ^ k) for i in range(n) if keep(i)])  55.5 us
    ppermute x34, waiting for transfers between devices, swap(): return lax.ppermute(x, axis, [(i, i ^ k) for i in range(n) if keep(i)])  42.2 us
    pallas_call x4, Pallas kernels, down_chunk(): pl.pallas_call(functools.partial(down_kernel, chunk=chunk, route=route),...  21.2 us
    pallas_call x4, Pallas kernels, up_chunk(): pl.pallas_call(functools.partial(up_kernel, chunk=chunk, parts=parts, fir...  20.1 us
    pallas_call x1, Pallas kernels, body(): pl.pallas_call(inside_kernel, in_specs=[SMEM] + [VMEM] * 5, out_specs=[VM...  4.26 us
    pallas_call x1, Pallas kernels, body(): pl.pallas_call(state_kernel, in_specs=[ANY] * 2 + [VMEM], out_specs=[VMEM...  3.93 us
  transfers between devices with their start and end apart: 34, of which 13 were waited for; matrix products, arithmetic and copies ran while one was open for 3% of the time, Pallas kernels for 23%

profile of v3, /device:TPU:0, one launch (start us, length us, event | category | flops | bytes accessed | tf_op | source)
XLA Modules:
  0.0 160.1 jit_solution(11213196152423358673)
XLA Ops:
  0.0 3.9 %local_state.1 = (bf16[12,128,128]{2,1,0:T(8,128)(2,1)}, bf16[12,128,128]{2,1,0:T(8,128)(2,1)}) custom-call(bf16[4,64,768]{2,1,0:T(8,128)(2,1)} %keys.3, bf16[4,64,768]{2,1,0:T(8,128)(2,1)} %values.3, f32[24,64]{1,0:T(8,128)} %bitcast.19), custom_call_target="tpu_custom_call" | custom-call | tf_op jit(solution)/shard_map/local_state/pallas_call | solution.py:409
  4.9 3.0 %collective-permute-start.1 = (f32[2,12,1,1]{1,0,3,2:T(2,128)S(1)}, f32[2,12,1,1]{1,0,3,2:T(2,128)S(1)}, u32[]{:S(2)}, u32[]{:S(2)}) collective-permute-start(f32[2,12,1,1]{1,0,3,2:T(2,128)S(1)} %exp.14), channel_id=1, source_target_pairs={{0,8},{8,0},{16,24},{24,16},{1,9},{9,1},{17,25},{25,17},{2,10},{10... | collective-permute-start | bytes 296 | tf_op jit(solution)/shard_map/ppermute | solution.py:27
  7.9 1.5 collective-permute-start.3
  9.4 1.9 %collective-permute-start.4 = (bf16[12,128,128]{2,1,0:T(8,128)(2,1)}, bf16[12,128,128]{2,1,0:T(8,128)(2,1)S(1)}, u32[]{:S(2)}, u32[]{:S(2)}) collective-permute-start(bf16[12,128,128]{2,1,0:T(8,128)(2,1)} %get-tuple-element.48), channel_id=1, source_target_pairs={{0,16},{8,24},{1,17},{9,25},{2,18},{10,26},{3,19},{11,27},{4,20},{... | collective-permute-start | bytes 1179656 | tf_op jit(solution)/shard_map/ppermute | solution.py:27
  11.3 3.9 %collective-permute-start = (bf16[12,128,128]{2,1,0:T(8,128)(2,1)}, bf16[12,128,128]{2,1,0:T(8,128)(2,1)S(1)}, u32[]{:S(2)}, u32[]{:S(2)}) collective-permute-start(bf16[12,128,128]{2,1,0:T(8,128)(2,1)} %get-tuple-element.47), channel_id=1, source_target_pairs={{0,8},{8,0},{16,24},{1,9},{9,1},{17,25},{2,10},{10,2},{18,26},{3,1... | collective-permute-start | bytes 1179656 | tf_op jit(solution)/shard_map/ppermute | solution.py:27
  16.8 2.9 %collective-permute-done.4 = bf16[12,128,128]{2,1,0:T(8,128)(2,1)S(1)} collective-permute-done((bf16[12,128,128]{2,1,0:T(8,128)(2,1)}, bf16[12,128,128]{2,1,0:T(8,128)(2,1)S(1)}, u32[]{:S(2)}, u32[]{:S(2)}) %collective-permute-start.4) | collective-permute-done | bytes 393248 | tf_op jit(solution)/shard_map/ppermute | solution.py:27
  19.7 1.2 fusion.7
  20.9 3.6 %collective-permute-start.5 = (bf16[12,128,128]{2,1,0:T(8,128)(2,1)S(1)}, bf16[12,128,128]{2,1,0:T(8,128)(2,1)S(1)}, u32[]{:S(2)}, u32[]{:S(2)}) collective-permute-start(bf16[12,128,128]{2,1,0:T(8,128)(2,1)S(1)} %fusion.7), channel_id=1, source_target_pairs={{0,8},{16,24},{24,16},{1,9},{17,25},{25,17},{2,10},{18,26},{26,18}... | collective-permute-start | bytes 1179656 | tf_op jit(solution)/shard_map/ppermute | solution.py:27
  24.5 1.2 fusion.3
  25.7 4.3 %collective-permute-start.2 = (bf16[12,128,128]{2,1,0:T(8,128)(2,1)S(1)}, bf16[12,128,128]{2,1,0:T(8,128)(2,1)S(1)}, u32[]{:S(2)}, u32[]{:S(2)}) collective-permute-start(bf16[12,128,128]{2,1,0:T(8,128)(2,1)S(1)} %fusion.3), channel_id=1, source_target_pairs={{0,16},{8,24},{1,17},{9,25},{2,18},{10,26},{3,19},{11,27},{4,20},{... | collective-permute-start | bytes 1179656 | tf_op jit(solution)/shard_map/ppermute | solution.py:27
  30.8 4.3 %inside_and_placement.1 = (f32[4,64,768]{2,1,0:T(8,128)S(1)}, bf16[320,256]{1,0:T(8,128)(2,1)S(1)}, s32[80,128]{1,0:T(8,128)S(1)}) custom-call(s32[2]{0:T(128)S(1)} %pad_add_fusion.place, bf16[4,64,768]{2,1,0:T(8,128)(2,1)S(1)} %copy-done, bf16[4,64,768]{2,1,0:T(8,128)(2,1)S(1)} %copy-done.1, bf16[4,64,768]{2,1,0:T(8,128)(2,1)S(1)} %copy-done.2, ...), custom_call_target="tpu_custom_call" | custom-call | tf_op jit(solution)/shard_map/inside_and_placement/pallas_call | solution.py:428
  36.8 2.0 %normed.1.refs_0_ = bf16[256,768]{1,0:T(8,128)(2,1)S(1)} custom-call(bf16[4,64,768]{2,1,0:T(8,128)(2,1)S(1)} %copy-done, f32[4,64,768]{2,1,0:T(8,128)S(1)} %get-tuple-element.46.inside, f32[24,64]{1,0:T(8,128)S(1)} %bitcast.21, f32[1,768]{1,0:T(1,128)S(1)} %reshape.84.gain, bf16[12,128,128]{2,1,0:T(8,128)(2,1)S(1)} %fusion.1.refs_0_, ...), custom_call_target="tpu_custom_call" | custom-call | tf_op jit(solution)/shard_map/normed/pallas_call | solution.py:441
  38.9 1.7 %collective-permute-done.6.refs_1_ = bf16[256,768]{1,0:T(8,128)(2,1)S(1)} collective-permute-done((bf16[256,768]{1,0:T(8,128)(2,1)S(1)}, bf16[256,768]{1,0:T(8,128)(2,1)S(1)}, u32[]{:S(2)}, u32[]{:S(2)}) %collective-permute-start.6) | collective-permute-done | bytes 393248 | tf_op jit(solution)/shard_map/ppermute | solution.py:27
  41.1 1.6 %collective-permute-start.15 = (bf16[2,40,1536]{2,1,0:T(8,128)(2,1)S(1)}, bf16[2,40,1536]{2,1,0:T(8,128)(2,1)S(1)}, u32[]{:S(2)}, u32[]{:S(2)}) collective-permute-start(bf16[2,40,1536]{2,1,0:T(8,128)(2,1)S(1)} %get-tuple-element.53), channel_id=1, source_target_pairs={{0,2},{1,3},{2,0},{3,1},{4,6},{5,7},{6,4},{7,5},{8,10},{9,11},{10,... | collective-permute-start | bytes 737288 | tf_op jit(solution)/shard_map/ppermute | solution.py:27
  43.3 2.6 %collective-permute-start.11 = (bf16[2,40,1536]{2,1,0:T(8,128)(2,1)S(1)}, bf16[2,40,1536]{2,1,0:T(8,128)(2,1)S(1)}, u32[]{:S(2)}, u32[]{:S(2)}) collective-permute-start(bf16[2,40,1536]{2,1,0:T(8,128)(2,1)S(1)} %get-tuple-element.52), channel_id=1, source_target_pairs={{0,4},{1,5},{2,6},{3,7},{4,0},{5,1},{6,2},{7,3},{8,12},{9,13},{10,... | collective-permute-start | bytes 737288 | tf_op jit(solution)/shard_map/ppermute | solution.py:27
  46.2 2.5 %collective-permute-start.20 = (bf16[2,40,1536]{2,1,0:T(8,128)(2,1)S(1)}, bf16[2,40,1536]{2,1,0:T(8,128)(2,1)S(1)}, u32[]{:S(2)}, u32[]{:S(2)}) collective-permute-start(bf16[2,40,1536]{2,1,0:T(8,128)(2,1)S(1)} %get-tuple-element.56.refs_0_), channel_id=1, source_target_pairs={{0,16},{8,24},{16,0},{24,8},{1,17},{9,25},{17,1},{25,9},{2,18},{10... | collective-permute-start | bytes 737288 | tf_op jit(solution)/shard_map/ppermute | solution.py:27
  48.7 4.8 %collective-permute-done.15.refs_1_.refs_0_ = bf16[2,40,1536]{2,1,0:T(8,128)(2,1)S(1)} collective-permute-done((bf16[2,40,1536]{2,1,0:T(8,128)(2,1)S(1)}, bf16[2,40,1536]{2,1,0:T(8,128)(2,1)S(1)}, u32[]{:S(2)}, u32[]{:S(2)}) %collective-permute-start.15) | collective-permute-done | bytes 245792 | tf_op jit(solution)/shard_map/ppermute | solution.py:27
  53.5 2.5 %collective-permute-start.17 = (bf16[2,40,1536]{2,1,0:T(8,128)(2,1)S(1)}, bf16[2,40,1536]{2,1,0:T(8,128)(2,1)S(1)}, u32[]{:S(2)}, u32[]{:S(2)}) collective-permute-start(bf16[2,40,1536]{2,1,0:T(8,128)(2,1)S(1)} %collective-permute-done.15.refs_1_.refs_0_), channel_id=1, source_target_pairs={{0,16},{8,24},{16,0},{24,8},{1,17},{9,25},{17,1},{25,9},{2,18},{10... | collective-permute-start | bytes 737288 | tf_op jit(solution)/shard_map/ppermute | solution.py:27
  56.0 7.6 %collective-permute-done.11.refs_2_.refs_0_ = bf16[2,40,1536]{2,1,0:T(8,128)(2,1)S(1)} collective-permute-done((bf16[2,40,1536]{2,1,0:T(8,128)(2,1)S(1)}, bf16[2,40,1536]{2,1,0:T(8,128)(2,1)S(1)}, u32[]{:S(2)}, u32[]{:S(2)}) %collective-permute-start.11) | collective-permute-done | bytes 245792 | tf_op jit(solution)/shard_map/ppermute | solution.py:27
  63.6 1.5 collective-permute-start.12
  65.6 2.5 %collective-permute-start.9 = (bf16[2,40,1536]{2,1,0:T(8,128)(2,1)S(1)}, bf16[2,40,1536]{2,1,0:T(8,128)(2,1)S(1)}, u32[]{:S(2)}, u32[]{:S(2)}) collective-permute-start(bf16[2,40,1536]{2,1,0:T(8,128)(2,1)S(1)} %collective-permute-done.7.refs_3_.refs_0_), channel_id=1, source_target_pairs={{0,16},{8,24},{16,0},{24,8},{1,17},{9,25},{17,1},{25,9},{2,18},{10... | collective-permute-start | bytes 737288 | tf_op jit(solution)/shard_map/ppermute | solution.py:27
  68.1 1.5 collective-permute-start.18
  69.6 1.1 gate.1.weight
  71.5 2.5 %collective-permute-start.14 = (bf16[2,40,1536]{2,1,0:T(8,128)(2,1)S(1)}, bf16[2,40,1536]{2,1,0:T(8,128)(2,1)S(1)}, u32[]{:S(2)}, u32[]{:S(2)}) collective-permute-start(bf16[2,40,1536]{2,1,0:T(8,128)(2,1)S(1)} %collective-permute-done.12.refs_1_), channel_id=1, source_target_pairs={{0,16},{8,24},{16,0},{24,8},{1,17},{9,25},{17,1},{25,9},{2,18},{10... | collective-permute-start | bytes 737288 | tf_op jit(solution)/shard_map/ppermute | solution.py:27
  74.0 5.3 %up_0.1.refs_4_ = f32[2,160,1536]{2,1,0:T(8,128)S(1)} custom-call(s32[2]{0:T(128)S(1)} %pad_add_fusion.place, bf16[2,6144,1536]{2,1,0:T(8,128)(2,1)} %weights.11, bf16[2,40,1536]{2,1,0:T(8,128)(2,1)S(1)} %get-tuple-element.56.refs_0_, bf16[2,40,1536]{2,1,0:T(8,128)(2,1)S(1)} %collective-permute-done.19.refs_1_, ...), custom_call_target="tpu_custom_call" | custom-call | flops 1509949440 | bytes 9437184 | tf_op jit(solution)/shard_map/up_0/pallas_call | solution.py:219
  79.9 1.5 collective-permute-start.10
  81.4 4.9 %up_1.1.refs_4_ = f32[2,160,1536]{2,1,0:T(8,128)S(1)} custom-call(s32[2]{0:T(128)S(1)} %pad_add_fusion.place, bf16[2,6144,1536]{2,1,0:T(8,128)(2,1)} %weights.11, bf16[2,40,1536]{2,1,0:T(8,128)(2,1)S(1)} %collective-permute-done.15.refs_1_.refs_0_, bf16[2,40,1536]{2,1,0:T(8,128)(2,1)S(1)} %collective-permute-done.16.refs_1_, ...), custom_call_target="tpu_custom_call" | custom-call | flops 1509949440 | bytes 9437184 | tf_op jit(solution)/shard_map/up_1/pallas_call | solution.py:219
  86.3 4.9 %up_2.1.refs_4_ = f32[2,160,1536]{2,1,0:T(8,128)S(1)} custom-call(s32[2]{0:T(128)S(1)} %pad_add_fusion.place, bf16[2,6144,1536]{2,1,0:T(8,128)(2,1)} %weights.11, bf16[2,40,1536]{2,1,0:T(8,128)(2,1)S(1)} %collective-permute-done.11.refs_2_.refs_0_, bf16[2,40,1536]{2,1,0:T(8,128)(2,1)S(1)} %collective-permute-done.12.refs_1_, ...), custom_call_target="tpu_custom_call" | custom-call | flops 1509949440 | bytes 9437184 | tf_op jit(solution)/shard_map/up_2/pallas_call | solution.py:219
  91.3 5.0 %up_3.1.hidden = bf16[2,160,1536]{2,1,0:T(8,128)(2,1)S(1)} custom-call(s32[2]{0:T(128)S(1)} %pad_add_fusion.place, bf16[2,6144,1536]{2,1,0:T(8,128)(2,1)} %weights.11, bf16[2,40,1536]{2,1,0:T(8,128)(2,1)S(1)} %collective-permute-done.7.refs_3_.refs_0_, bf16[2,40,1536]{2,1,0:T(8,128)(2,1)S(1)} %collective-permute-done.8.refs_1_, ...), custom_call_target="tpu_custom_call" | custom-call | flops 1509949440 | bytes 9437184 | tf_op jit(solution)/shard_map/up_3/pallas_call | solution.py:219
  96.3 5.5 %down_3.1 = (bf16[2,2,40,1536]{3,2,1,0:T(8,128)(2,1)S(1)}, bf16[2,2,40,1536]{3,2,1,0:T(8,128)(2,1)S(1)}) custom-call(s32[2]{0:T(128)S(1)} %pad_add_fusion.place, bf16[2,1536,6144]{2,1,0:T(8,128)(2,1)} %weights.15, bf16[2,160,1536]{2,1,0:T(8,128)(2,1)S(1)} %up_3.1.hidden), custom_call_target="tpu_custom_call" | custom-call | flops 1509949440 | bytes 9437184 | tf_op jit(solution)/shard_map/down_3/pallas_call | solution.py:271
  101.7 0.9 collective-permute-start.22
  102.6 5.2 %down_2.1 = (bf16[2,2,40,1536]{3,2,1,0:T(8,128)(2,1)S(1)}, bf16[2,2,40,1536]{3,2,1,0:T(8,128)(2,1)S(1)}) custom-call(s32[2]{0:T(128)S(1)} %pad_add_fusion.place, bf16[2,1536,6144]{2,1,0:T(8,128)(2,1)} %weights.15, bf16[2,160,1536]{2,1,0:T(8,128)(2,1)S(1)} %up_3.1.hidden), custom_call_target="tpu_custom_call" | custom-call | flops 1509949440 | bytes 9437184 | tf_op jit(solution)/shard_map/down_2/pallas_call | solution.py:271
  107.9 0.9 collective-permute-start.26
  108.8 5.2 %down_1.1 = (bf16[2,2,40,1536]{3,2,1,0:T(8,128)(2,1)S(1)}, bf16[2,2,40,1536]{3,2,1,0:T(8,128)(2,1)S(1)}) custom-call(s32[2]{0:T(128)S(1)} %pad_add_fusion.place, bf16[2,1536,6144]{2,1,0:T(8,128)(2,1)} %weights.15, bf16[2,160,1536]{2,1,0:T(8,128)(2,1)S(1)} %up_3.1.hidden), custom_call_target="tpu_custom_call" | custom-call | flops 1509949440 | bytes 9437184 | tf_op jit(solution)/shard_map/down_1/pallas_call | solution.py:271
  114.0 1.0 collective-permute-start.25
  115.1 5.2 %down_0.1 = (bf16[2,2,40,1536]{3,2,1,0:T(8,128)(2,1)S(1)}, bf16[2,2,40,1536]{3,2,1,0:T(8,128)(2,1)S(1)}) custom-call(s32[2]{0:T(128)S(1)} %pad_add_fusion.place, bf16[2,1536,6144]{2,1,0:T(8,128)(2,1)} %weights.15, bf16[2,160,1536]{2,1,0:T(8,128)(2,1)S(1)} %up_3.1.hidden), custom_call_target="tpu_custom_call" | custom-call | flops 1509949440 | bytes 9437184 | tf_op jit(solution)/shard_map/down_0/pallas_call | solution.py:271
  120.4 1.5 collective-permute-start.23
  122.6 1.2 collective-permute-start.29
  123.8 1.0 collective-permute-done.25.got
  124.8 1.7 %collective-permute-start.28 = (bf16[1,2,40,1536]{3,2,1,0:T(8,128)(2,1)S(1)}, bf16[1,2,40,1536]{3,2,1,0:T(8,128)(2,1)S(1)}, u32[]{:S(2)}, u32[]{:S(2)}) collective-permute-start(bf16[1,2,40,1536]{3,2,1,0:T(8,128)(2,1)S(1)} %get-tuple-element.75), channel_id=1, source_target_pairs={{0,8},{8,0},{16,24},{24,16},{1,9},{9,1},{17,25},{25,17},{2,10},{10... | collective-permute-start | bytes 737288 | tf_op jit(solution)/shard_map/ppermute | solution.py:27
  126.6 8.6 %collective-permute-done.24.got = bf16[1,2,40,1536]{3,2,1,0:T(8,128)(2,1)S(1)} collective-permute-done((bf16[1,2,40,1536]{3,2,1,0:T(8,128)(2,1)S(1)}, bf16[1,2,40,1536]{3,2,1,0:T(8,128)(2,1)S(1)}, u32[]{:S(2)}, u32[]{:S(2)}) %collective-permute-start.24) | collective-permute-done | bytes 245792 | tf_op jit(solution)/shard_map/ppermute | solution.py:27
  135.3 5.8 %collective-permute-start.32 = (bf16[2,40,1536]{2,1,0:T(8,128)(2,1)S(1)}, bf16[2,40,1536]{2,1,0:T(8,128)(2,1)S(1)}, u32[]{:S(2)}, u32[]{:S(2)}) collective-permute-start(bf16[2,40,1536]{2,1,0:T(8,128)(2,1)S(1)} %reply.4), channel_id=1, source_target_pairs={{0,6},{1,7},{2,4},{3,5},{4,2},{5,3},{6,0},{7,1},{8,14},{9,15},{10,... | collective-permute-start | bytes 737288 | tf_op jit(solution)/shard_map/ppermute | solution.py:27
  142.0 1.0 collective-permute-start.30
  143.0 1.3 collective-permute-start.31
  144.3 3.2 %collective-permute-done.27.got = bf16[1,2,40,1536]{3,2,1,0:T(8,128)(2,1)S(1)} collective-permute-done((bf16[1,2,40,1536]{3,2,1,0:T(8,128)(2,1)S(1)}, bf16[1,2,40,1536]{3,2,1,0:T(8,128)(2,1)S(1)}, u32[]{:S(2)}, u32[]{:S(2)}) %collective-permute-start.27) | collective-permute-done | bytes 245792 | tf_op jit(solution)/shard_map/ppermute | solution.py:27
  148.1 1.8 %collective-permute-done.30.refs_1_ = bf16[2,40,1536]{2,1,0:T(8,128)(2,1)S(1)} collective-permute-done((bf16[2,40,1536]{2,1,0:T(8,128)(2,1)S(1)}, bf16[2,40,1536]{2,1,0:T(8,128)(2,1)S(1)}, u32[]{:S(2)}, u32[]{:S(2)}) %collective-permute-start.30) | collective-permute-done | bytes 245792 | tf_op jit(solution)/shard_map/ppermute | solution.py:27
  149.9 7.0 %collective-permute-done.31.refs_2_ = bf16[2,40,1536]{2,1,0:T(8,128)(2,1)S(1)} collective-permute-done((bf16[2,40,1536]{2,1,0:T(8,128)(2,1)S(1)}, bf16[2,40,1536]{2,1,0:T(8,128)(2,1)S(1)}, u32[]{:S(2)}, u32[]{:S(2)}) %collective-permute-start.31) | collective-permute-done | bytes 245792 | tf_op jit(solution)/shard_map/ppermute | solution.py:27
  157.5 1.7 %collective-permute-done.33 = bf16[256,768]{1,0:T(8,128)(2,1)S(1)} collective-permute-done((bf16[256,768]{1,0:T(8,128)(2,1)S(1)}, bf16[256,768]{1,0:T(8,128)(2,1)S(1)}, u32[]{:S(2)}, u32[]{:S(2)}) %collective-permute-start.33) | collective-permute-done | bytes 393248 | tf_op jit(solution)/shard_map/ppermute | solution.py:27
  (74 shorter events, 12.4 us)
Async XLA Ops:
  0.0 30.8 %copy-start.3 = (f32[4,64,6]{1,0,2:T(4,128)S(1)}, f32[4,64,6]{1,0,2:T(4,128)}, u32[]{:S(2)}) copy-start(f32[4,64,6]{1,0,2:T(4,128)} %param.12) | copy-start | bytes 18436
  0.0 30.8 %copy-start.1 = (bf16[4,64,768]{2,1,0:T(8,128)(2,1)S(1)}, bf16[4,64,768]{2,1,0:T(8,128)(2,1)}, u32[]{:S(2)}) copy-start(bf16[4,64,768]{2,1,0:T(8,128)(2,1)} %keys.3) | copy-start | bytes 1179652
  0.0 30.8 %copy-start.2 = (bf16[4,64,768]{2,1,0:T(8,128)(2,1)S(1)}, bf16[4,64,768]{2,1,0:T(8,128)(2,1)}, u32[]{:S(2)}) copy-start(bf16[4,64,768]{2,1,0:T(8,128)(2,1)} %values.3) | copy-start | bytes 1179652
  0.0 30.8 %copy-start.5 = (s32[64,4,2]{0,2,1:T(2,128)S(1)}, s32[64,4,2]{0,2,1:T(2,128)}, u32[]{:S(2)}) copy-start(s32[64,4,2]{0,2,1:T(2,128)} %param.17) | copy-start | bytes 6148
  0.0 30.8 %copy-start = (bf16[4,64,768]{2,1,0:T(8,128)(2,1)S(1)}, bf16[4,64,768]{2,1,0:T(8,128)(2,1)}, u32[]{:S(2)}) copy-start(bf16[4,64,768]{2,1,0:T(8,128)(2,1)} %queries.3) | copy-start | bytes 1179652
  4.9 10.7 %collective-permute-start.1 = (f32[2,12,1,1]{1,0,3,2:T(2,128)S(1)}, f32[2,12,1,1]{1,0,3,2:T(2,128)S(1)}, u32[]{:S(2)}, u32[]{:S(2)}) collective-permute-start(f32[2,12,1,1]{1,0,3,2:T(2,128)S(1)} %exp.14), channel_id=1, source_target_pairs={{0,8},{8,0},{16,24},{24,16},{1,9},{9,1},{17,25},{25,17},{2,10},{10... | collective-permute-start | bytes 296 | tf_op jit(solution)/shard_map/ppermute | solution.py:27
  7.9 7.8 %collective-permute-start.3 = (f32[2,12,1,1]{1,0,3,2:T(2,128)S(1)}, f32[2,12,1,1]{1,0,3,2:T(2,128)S(1)}, u32[]{:S(2)}, u32[]{:S(2)}) collective-permute-start(f32[2,12,1,1]{1,0,3,2:T(2,128)S(1)} %exp.14), channel_id=1, source_target_pairs={{0,24},{8,16},{16,8},{24,0},{1,25},{9,17},{17,9},{25,1},{2,26},{10... | collective-permute-start | bytes 296 | tf_op jit(solution)/shard_map/ppermute | solution.py:27
  9.4 10.3 %collective-permute-start.4 = (bf16[12,128,128]{2,1,0:T(8,128)(2,1)}, bf16[12,128,128]{2,1,0:T(8,128)(2,1)S(1)}, u32[]{:S(2)}, u32[]{:S(2)}) collective-permute-start(bf16[12,128,128]{2,1,0:T(8,128)(2,1)} %get-tuple-element.48), channel_id=1, source_target_pairs={{0,16},{8,24},{1,17},{9,25},{2,18},{10,26},{3,19},{11,27},{4,20},{... | collective-permute-start | bytes 1179656 | tf_op jit(solution)/shard_map/ppermute | solution.py:27
  11.3 13.2 %collective-permute-start = (bf16[12,128,128]{2,1,0:T(8,128)(2,1)}, bf16[12,128,128]{2,1,0:T(8,128)(2,1)S(1)}, u32[]{:S(2)}, u32[]{:S(2)}) collective-permute-start(bf16[12,128,128]{2,1,0:T(8,128)(2,1)} %get-tuple-element.47), channel_id=1, source_target_pairs={{0,8},{8,0},{16,24},{1,9},{9,1},{17,25},{2,10},{10,2},{18,26},{3,1... | collective-permute-start | bytes 1179656 | tf_op jit(solution)/shard_map/ppermute | solution.py:27
  20.9 14.2 %collective-permute-start.5 = (bf16[12,128,128]{2,1,0:T(8,128)(2,1)S(1)}, bf16[12,128,128]{2,1,0:T(8,128)(2,1)S(1)}, u32[]{:S(2)}, u32[]{:S(2)}) collective-permute-start(bf16[12,128,128]{2,1,0:T(8,128)(2,1)S(1)} %fusion.7), channel_id=1, source_target_pairs={{0,8},{16,24},{24,16},{1,9},{17,25},{25,17},{2,10},{18,26},{26,18}... | collective-permute-start | bytes 1179656 | tf_op jit(solution)/shard_map/ppermute | solution.py:27
  25.7 10.9 %collective-permute-start.2 = (bf16[12,128,128]{2,1,0:T(8,128)(2,1)S(1)}, bf16[12,128,128]{2,1,0:T(8,128)(2,1)S(1)}, u32[]{:S(2)}, u32[]{:S(2)}) collective-permute-start(bf16[12,128,128]{2,1,0:T(8,128)(2,1)S(1)} %fusion.3), channel_id=1, source_target_pairs={{0,16},{8,24},{1,17},{9,25},{2,18},{10,26},{3,19},{11,27},{4,20},{... | collective-permute-start | bytes 1179656 | tf_op jit(solution)/shard_map/ppermute | solution.py:27
  30.0 6.6 %copy-start.6 = (f32[12]{0:T(128)S(1)}, f32[12]{0:T(128)}, u32[]{:S(2)}) copy-start(f32[12]{0:T(128)} %get-tuple-element.91) | copy-start | bytes 148
  36.6 33.0 %copy-start.4 = (bf16[6144,16]{0,1:T(8,128)(2,1)S(1)}, bf16[6144,16]{0,1:T(8,128)(2,1)}, u32[]{:S(2)}) copy-start(bf16[6144,16]{0,1:T(8,128)(2,1)} %param.14) | copy-start | bytes 589828
  38.8 1.8 %collective-permute-start.6 = (bf16[256,768]{1,0:T(8,128)(2,1)S(1)}, bf16[256,768]{1,0:T(8,128)(2,1)S(1)}, u32[]{:S(2)}, u32[]{:S(2)}) collective-permute-start(bf16[256,768]{1,0:T(8,128)(2,1)S(1)} %normed.1.refs_0_), channel_id=1, source_target_pairs={{0,1},{1,0},{2,3},{3,2},{4,5},{5,4},{6,7},{7,6},{8,9},{9,8},{10,11... | collective-permute-start | bytes 1179656 | tf_op jit(solution)/shard_map/ppermute | solution.py:27
  41.1 12.4 %collective-permute-start.15 = (bf16[2,40,1536]{2,1,0:T(8,128)(2,1)S(1)}, bf16[2,40,1536]{2,1,0:T(8,128)(2,1)S(1)}, u32[]{:S(2)}, u32[]{:S(2)}) collective-permute-start(bf16[2,40,1536]{2,1,0:T(8,128)(2,1)S(1)} %get-tuple-element.53), channel_id=1, source_target_pairs={{0,2},{1,3},{2,0},{3,1},{4,6},{5,7},{6,4},{7,5},{8,10},{9,11},{10,... | collective-permute-start | bytes 737288 | tf_op jit(solution)/shard_map/ppermute | solution.py:27
  42.7 13.3 %collective-permute-start.19 = (bf16[2,40,1536]{2,1,0:T(8,128)(2,1)S(1)}, bf16[2,40,1536]{2,1,0:T(8,128)(2,1)S(1)}, u32[]{:S(2)}, u32[]{:S(2)}) collective-permute-start(bf16[2,40,1536]{2,1,0:T(8,128)(2,1)S(1)} %get-tuple-element.56.refs_0_), channel_id=1, source_target_pairs={{0,8},{8,0},{16,24},{24,16},{1,9},{9,1},{17,25},{25,17},{2,10},{10... | collective-permute-start | bytes 737288 | tf_op jit(solution)/shard_map/ppermute | solution.py:27
  43.3 20.3 %collective-permute-start.11 = (bf16[2,40,1536]{2,1,0:T(8,128)(2,1)S(1)}, bf16[2,40,1536]{2,1,0:T(8,128)(2,1)S(1)}, u32[]{:S(2)}, u32[]{:S(2)}) collective-permute-start(bf16[2,40,1536]{2,1,0:T(8,128)(2,1)S(1)} %get-tuple-element.52), channel_id=1, source_target_pairs={{0,4},{1,5},{2,6},{3,7},{4,0},{5,1},{6,2},{7,3},{8,12},{9,13},{10,... | collective-permute-start | bytes 737288 | tf_op jit(solution)/shard_map/ppermute | solution.py:27
  45.8 19.2 %collective-permute-start.7 = (bf16[2,40,1536]{2,1,0:T(8,128)(2,1)S(1)}, bf16[2,40,1536]{2,1,0:T(8,128)(2,1)S(1)}, u32[]{:S(2)}, u32[]{:S(2)}) collective-permute-start(bf16[2,40,1536]{2,1,0:T(8,128)(2,1)S(1)} %get-tuple-element.51), channel_id=1, source_target_pairs={{0,6},{1,7},{2,4},{3,5},{4,2},{5,3},{6,0},{7,1},{8,14},{9,15},{10,... | collective-permute-start | bytes 737288 | tf_op jit(solution)/shard_map/ppermute | solution.py:27
  46.2 19.4 %collective-permute-start.20 = (bf16[2,40,1536]{2,1,0:T(8,128)(2,1)S(1)}, bf16[2,40,1536]{2,1,0:T(8,128)(2,1)S(1)}, u32[]{:S(2)}, u32[]{:S(2)}) collective-permute-start(bf16[2,40,1536]{2,1,0:T(8,128)(2,1)S(1)} %get-tuple-element.56.refs_0_), channel_id=1, source_target_pairs={{0,16},{8,24},{16,0},{24,8},{1,17},{9,25},{17,1},{25,9},{2,18},{10... | collective-permute-start | bytes 737288 | tf_op jit(solution)/shard_map/ppermute | solution.py:27
  53.5 14.6 %collective-permute-start.17 = (bf16[2,40,1536]{2,1,0:T(8,128)(2,1)S(1)}, bf16[2,40,1536]{2,1,0:T(8,128)(2,1)S(1)}, u32[]{:S(2)}, u32[]{:S(2)}) collective-permute-start(bf16[2,40,1536]{2,1,0:T(8,128)(2,1)S(1)} %collective-permute-done.15.refs_1_.refs_0_), channel_id=1, source_target_pairs={{0,16},{8,24},{16,0},{24,8},{1,17},{9,25},{17,1},{25,9},{2,18},{10... | collective-permute-start | bytes 737288 | tf_op jit(solution)/shard_map/ppermute | solution.py:27
  56.0 14.7 %collective-permute-start.21 = (bf16[2,40,1536]{2,1,0:T(8,128)(2,1)S(1)}, bf16[2,40,1536]{2,1,0:T(8,128)(2,1)S(1)}, u32[]{:S(2)}, u32[]{:S(2)}) collective-permute-start(bf16[2,40,1536]{2,1,0:T(8,128)(2,1)S(1)} %collective-permute-done.19.refs_1_), channel_id=1, source_target_pairs={{0,16},{8,24},{16,0},{24,8},{1,17},{9,25},{17,1},{25,9},{2,18},{10... | collective-permute-start | bytes 737288 | tf_op jit(solution)/shard_map/ppermute | solution.py:27
  63.6 8.0 %collective-permute-start.12 = (bf16[2,40,1536]{2,1,0:T(8,128)(2,1)S(1)}, bf16[2,40,1536]{2,1,0:T(8,128)(2,1)S(1)}, u32[]{:S(2)}, u32[]{:S(2)}) collective-permute-start(bf16[2,40,1536]{2,1,0:T(8,128)(2,1)S(1)} %collective-permute-done.11.refs_2_.refs_0_), channel_id=1, source_target_pairs={{0,8},{8,0},{16,24},{24,16},{1,9},{9,1},{17,25},{25,17},{2,10},{10... | collective-permute-start | bytes 737288 | tf_op jit(solution)/shard_map/ppermute | solution.py:27
  65.1 14.2 %collective-permute-start.16 = (bf16[2,40,1536]{2,1,0:T(8,128)(2,1)S(1)}, bf16[2,40,1536]{2,1,0:T(8,128)(2,1)S(1)}, u32[]{:S(2)}, u32[]{:S(2)}) collective-permute-start(bf16[2,40,1536]{2,1,0:T(8,128)(2,1)S(1)} %collective-permute-done.15.refs_1_.refs_0_), channel_id=1, source_target_pairs={{0,8},{8,0},{16,24},{24,16},{1,9},{9,1},{17,25},{25,17},{2,10},{10... | collective-permute-start | bytes 737288 | tf_op jit(solution)/shard_map/ppermute | solution.py:27
  65.6 14.3 %collective-permute-start.9 = (bf16[2,40,1536]{2,1,0:T(8,128)(2,1)S(1)}, bf16[2,40,1536]{2,1,0:T(8,128)(2,1)S(1)}, u32[]{:S(2)}, u32[]{:S(2)}) collective-permute-start(bf16[2,40,1536]{2,1,0:T(8,128)(2,1)S(1)} %collective-permute-done.7.refs_3_.refs_0_), channel_id=1, source_target_pairs={{0,16},{8,24},{16,0},{24,8},{1,17},{9,25},{17,1},{25,9},{2,18},{10... | collective-permute-start | bytes 737288 | tf_op jit(solution)/shard_map/ppermute | solution.py:27
  68.1 13.3 %collective-permute-start.18 = (bf16[2,40,1536]{2,1,0:T(8,128)(2,1)S(1)}, bf16[2,40,1536]{2,1,0:T(8,128)(2,1)S(1)}, u32[]{:S(2)}, u32[]{:S(2)}) collective-permute-start(bf16[2,40,1536]{2,1,0:T(8,128)(2,1)S(1)} %collective-permute-done.17.refs_2_), channel_id=1, source_target_pairs={{0,8},{8,0},{16,24},{24,16},{1,9},{9,1},{17,25},{25,17},{2,10},{10... | collective-permute-start | bytes 737288 | tf_op jit(solution)/shard_map/ppermute | solution.py:27
  70.7 15.6 %collective-permute-start.13 = (bf16[2,40,1536]{2,1,0:T(8,128)(2,1)S(1)}, bf16[2,40,1536]{2,1,0:T(8,128)(2,1)S(1)}, u32[]{:S(2)}, u32[]{:S(2)}) collective-permute-start(bf16[2,40,1536]{2,1,0:T(8,128)(2,1)S(1)} %collective-permute-done.11.refs_2_.refs_0_), channel_id=1, source_target_pairs={{0,16},{8,24},{16,0},{24,8},{1,17},{9,25},{17,1},{25,9},{2,18},{10... | collective-permute-start | bytes 737288 | tf_op jit(solution)/shard_map/ppermute | solution.py:27
  71.5 14.8 %collective-permute-start.14 = (bf16[2,40,1536]{2,1,0:T(8,128)(2,1)S(1)}, bf16[2,40,1536]{2,1,0:T(8,128)(2,1)S(1)}, u32[]{:S(2)}, u32[]{:S(2)}) collective-permute-start(bf16[2,40,1536]{2,1,0:T(8,128)(2,1)S(1)} %collective-permute-done.12.refs_1_), channel_id=1, source_target_pairs={{0,16},{8,24},{16,0},{24,8},{1,17},{9,25},{17,1},{25,9},{2,18},{10... | collective-permute-start | bytes 737288 | tf_op jit(solution)/shard_map/ppermute | solution.py:27
  79.3 12.0 %collective-permute-start.8 = (bf16[2,40,1536]{2,1,0:T(8,128)(2,1)S(1)}, bf16[2,40,1536]{2,1,0:T(8,128)(2,1)S(1)}, u32[]{:S(2)}, u32[]{:S(2)}) collective-permute-start(bf16[2,40,1536]{2,1,0:T(8,128)(2,1)S(1)} %collective-permute-done.7.refs_3_.refs_0_), channel_id=1, source_target_pairs={{0,8},{8,0},{16,24},{24,16},{1,9},{9,1},{17,25},{25,17},{2,10},{10... | collective-permute-start | bytes 737288 | tf_op jit(solution)/shard_map/ppermute | solution.py:27
  79.9 11.3 %collective-permute-start.10 = (bf16[2,40,1536]{2,1,0:T(8,128)(2,1)S(1)}, bf16[2,40,1536]{2,1,0:T(8,128)(2,1)S(1)}, u32[]{:S(2)}, u32[]{:S(2)}) collective-permute-start(bf16[2,40,1536]{2,1,0:T(8,128)(2,1)S(1)} %collective-permute-done.9.refs_2_), channel_id=1, source_target_pairs={{0,8},{8,0},{16,24},{24,16},{1,9},{9,1},{17,25},{25,17},{2,10},{10... | collective-permute-start | bytes 737288 | tf_op jit(solution)/shard_map/ppermute | solution.py:27
  101.7 13.3 %collective-permute-start.22 = (bf16[2,2,40,1536]{3,2,1,0:T(8,128)(2,1)S(1)}, bf16[2,2,40,1536]{3,2,1,0:T(8,128)(2,1)S(1)}, u32[]{:S(2)}, u32[]{:S(2)}) collective-permute-start(bf16[2,2,40,1536]{3,2,1,0:T(8,128)(2,1)S(1)} %get-tuple-element.59), channel_id=1, source_target_pairs={{0,16},{8,24},{16,0},{24,8},{1,17},{9,25},{17,1},{25,9},{2,18},{10... | collective-permute-start | bytes 1474568 | tf_op jit(solution)/shard_map/ppermute | solution.py:27
  107.9 14.6 %collective-permute-start.26 = (bf16[2,2,40,1536]{3,2,1,0:T(8,128)(2,1)S(1)}, bf16[2,2,40,1536]{3,2,1,0:T(8,128)(2,1)S(1)}, u32[]{:S(2)}, u32[]{:S(2)}) collective-permute-start(bf16[2,2,40,1536]{3,2,1,0:T(8,128)(2,1)S(1)} %get-tuple-element.61), channel_id=1, source_target_pairs={{0,8},{8,0},{16,24},{24,16},{1,9},{9,1},{17,25},{25,17},{2,10},{10... | collective-permute-start | bytes 1474568 | tf_op jit(solution)/shard_map/ppermute | solution.py:27
  114.0 10.7 %collective-permute-start.25 = (bf16[2,2,40,1536]{3,2,1,0:T(8,128)(2,1)S(1)}, bf16[2,2,40,1536]{3,2,1,0:T(8,128)(2,1)S(1)}, u32[]{:S(2)}, u32[]{:S(2)}) collective-permute-start(bf16[2,2,40,1536]{3,2,1,0:T(8,128)(2,1)S(1)} %get-tuple-element.63), channel_id=1, source_target_pairs={{0,16},{8,24},{16,0},{24,8},{1,17},{9,25},{17,1},{25,9},{2,18},{10... | collective-permute-start | bytes 1474568 | tf_op jit(solution)/shard_map/ppermute | solution.py:27
  120.4 20.7 %collective-permute-start.23 = (bf16[2,2,40,1536]{3,2,1,0:T(8,128)(2,1)S(1)}, bf16[2,2,40,1536]{3,2,1,0:T(8,128)(2,1)S(1)}, u32[]{:S(2)}, u32[]{:S(2)}) collective-permute-start(bf16[2,2,40,1536]{3,2,1,0:T(8,128)(2,1)S(1)} %get-tuple-element.68), channel_id=1, source_target_pairs={{0,8},{8,0},{16,24},{24,16},{1,9},{9,1},{17,25},{25,17},{2,10},{10... | collective-permute-start | bytes 1474568 | tf_op jit(solution)/shard_map/ppermute | solution.py:27
  121.9 13.3 %collective-permute-start.24 = (bf16[1,2,40,1536]{3,2,1,0:T(8,128)(2,1)S(1)}, bf16[1,2,40,1536]{3,2,1,0:T(8,128)(2,1)S(1)}, u32[]{:S(2)}, u32[]{:S(2)}) collective-permute-start(bf16[1,2,40,1536]{3,2,1,0:T(8,128)(2,1)S(1)} %get-tuple-element.65), channel_id=1, source_target_pairs={{0,8},{8,0},{16,24},{24,16},{1,9},{9,1},{17,25},{25,17},{2,10},{10... | collective-permute-start | bytes 737288 | tf_op jit(solution)/shard_map/ppermute | solution.py:27
  122.6 19.2 %collective-permute-start.29 = (bf16[1,2,40,1536]{3,2,1,0:T(8,128)(2,1)S(1)}, bf16[1,2,40,1536]{3,2,1,0:T(8,128)(2,1)S(1)}, u32[]{:S(2)}, u32[]{:S(2)}) collective-permute-start(bf16[1,2,40,1536]{3,2,1,0:T(8,128)(2,1)S(1)} %get-tuple-element.73), channel_id=1, source_target_pairs={{0,16},{8,24},{16,0},{24,8},{1,17},{9,25},{17,1},{25,9},{2,18},{10... | collective-permute-start | bytes 737288 | tf_op jit(solution)/shard_map/ppermute | solution.py:27
  124.8 17.0 %collective-permute-start.28 = (bf16[1,2,40,1536]{3,2,1,0:T(8,128)(2,1)S(1)}, bf16[1,2,40,1536]{3,2,1,0:T(8,128)(2,1)S(1)}, u32[]{:S(2)}, u32[]{:S(2)}) collective-permute-start(bf16[1,2,40,1536]{3,2,1,0:T(8,128)(2,1)S(1)} %get-tuple-element.75), channel_id=1, source_target_pairs={{0,8},{8,0},{16,24},{24,16},{1,9},{9,1},{17,25},{25,17},{2,10},{10... | collective-permute-start | bytes 737288 | tf_op jit(solution)/shard_map/ppermute | solution.py:27
  135.3 12.7 %collective-permute-start.32 = (bf16[2,40,1536]{2,1,0:T(8,128)(2,1)S(1)}, bf16[2,40,1536]{2,1,0:T(8,128)(2,1)S(1)}, u32[]{:S(2)}, u32[]{:S(2)}) collective-permute-start(bf16[2,40,1536]{2,1,0:T(8,128)(2,1)S(1)} %reply.4), channel_id=1, source_target_pairs={{0,6},{1,7},{2,4},{3,5},{4,2},{5,3},{6,0},{7,1},{8,14},{9,15},{10,... | collective-permute-start | bytes 737288 | tf_op jit(solution)/shard_map/ppermute | solution.py:27
  141.2 6.3 %collective-permute-start.27 = (bf16[1,2,40,1536]{3,2,1,0:T(8,128)(2,1)S(1)}, bf16[1,2,40,1536]{3,2,1,0:T(8,128)(2,1)S(1)}, u32[]{:S(2)}, u32[]{:S(2)}) collective-permute-start(bf16[1,2,40,1536]{3,2,1,0:T(8,128)(2,1)S(1)} %get-tuple-element.79), channel_id=1, source_target_pairs={{0,16},{8,24},{16,0},{24,8},{1,17},{9,25},{17,1},{25,9},{2,18},{10... | collective-permute-start | bytes 737288 | tf_op jit(solution)/shard_map/ppermute | solution.py:27
  142.0 7.9 %collective-permute-start.30 = (bf16[2,40,1536]{2,1,0:T(8,128)(2,1)S(1)}, bf16[2,40,1536]{2,1,0:T(8,128)(2,1)S(1)}, u32[]{:S(2)}, u32[]{:S(2)}) collective-permute-start(bf16[2,40,1536]{2,1,0:T(8,128)(2,1)S(1)} %reply.6), channel_id=1, source_target_pairs={{0,2},{1,3},{2,0},{3,1},{4,6},{5,7},{6,4},{7,5},{8,10},{9,11},{10,... | collective-permute-start | bytes 737288 | tf_op jit(solution)/shard_map/ppermute | solution.py:27
  143.0 13.9 %collective-permute-start.31 = (bf16[2,40,1536]{2,1,0:T(8,128)(2,1)S(1)}, bf16[2,40,1536]{2,1,0:T(8,128)(2,1)S(1)}, u32[]{:S(2)}, u32[]{:S(2)}) collective-permute-start(bf16[2,40,1536]{2,1,0:T(8,128)(2,1)S(1)} %reply.5), channel_id=1, source_target_pairs={{0,4},{1,5},{2,6},{3,7},{4,0},{5,1},{6,2},{7,3},{8,12},{9,13},{10,... | collective-permute-start | bytes 737288 | tf_op jit(solution)/shard_map/ppermute | solution.py:27
  157.4 1.8 %collective-permute-start.33 = (bf16[256,768]{1,0:T(8,128)(2,1)S(1)}, bf16[256,768]{1,0:T(8,128)(2,1)S(1)}, u32[]{:S(2)}, u32[]{:S(2)}) collective-permute-start(bf16[256,768]{1,0:T(8,128)(2,1)S(1)} %get-tuple-element.86), channel_id=1, source_target_pairs={{0,1},{1,0},{2,3},{3,2},{4,5},{5,4},{6,7},{7,6},{8,9},{9,8},{10,11... | collective-permute-start | bytes 1179656 | tf_op jit(solution)/shard_map/ppermute | solution.py:27

commit v4 on v3

--- a/solution.py
+++ b/solution.py
@@ -183,28 +183,32 @@
 
 def up_kernel(place, weights, *refs, chunk, parts, first, last):
     blocks, (out, buffer, sems) = refs[:parts], refs[-3:]
-    own, steps, depth, _ = buffer.shape
-    tiles = steps // 2
+    own, _, half, _ = buffer.shape
+    tiles = sems.shape[2]
+    depth = half // tiles
     owner = place[1]
-
-    def at(t):
-        return pl.multiple_of(((owner ^ (2 * chunk + t // tiles)) * tiles + t % tiles) * depth, depth)
-
     copies = []
     for j in range(own):
-        for t in range(steps):
-            copy = pltpu.make_async_copy(
-                weights.at[j, pl.ds(at(t), depth), :], buffer.at[j, t], sems.at[j, t]
-            )
-            copy.start()
-            copies.append(copy)
+        for side in range(2):
+            row = pl.multiple_of((owner ^ (2 * chunk + side)) * half, half)
+            tile_copies = []
+            for t in range(tiles):
+                copy = pltpu.make_async_copy(
+                    weights.at[j, pl.ds(row + t * depth, depth), :],
+                    buffer.at[j, side, t * depth : (t + 1) * depth],
+                    sems.at[j, side, t],
+                )
+                copy.start()
+                tile_copies.append(copy)
+            copies.append(tile_copies)
     for j in range(own):
         total = None if first else refs[parts][j]
-        for t in range(steps):
-            lanes = slice(t * depth, (t + 1) * depth)
+        for side in range(2):
+            lanes = slice(side * half, (side + 1) * half)
             x = jnp.concatenate([b[j, :, lanes].astype(F32) for b in blocks], axis=0).astype(BF16)
-            copies[j * steps + t].wait()
-            part = dot(x, buffer[j, t])
+            for copy in copies[2 * j + side]:
+                copy.wait()
+            part = dot(x, buffer[j, side])
             total = part if total is None else total + part
         out[j] = (total / (1.0 + jnp.exp(-total))).astype(BF16) if last else total
 
@@ -214,7 +218,7 @@
     cap, width = blocks[0].shape[1:]
     parts = len(blocks)
     rows = parts * cap
-    steps = 2 * tiles_of(width // 2)
+    tiles = tiles_of(width // 2)
     first = total is None
     return pl.pallas_call(
         functools.partial(up_kernel, chunk=chunk, parts=parts, first=first, last=last),
@@ -222,8 +226,8 @@
         out_specs=VMEM,
         out_shape=jax.ShapeDtypeStruct((own, rows, hidden), BF16 if last else F32),
         scratch_shapes=[
-            pltpu.VMEM((own, steps, width // steps, hidden), BF16),
-            pltpu.SemaphoreType.DMA((own, steps)),
+            pltpu.VMEM((own, 2, width // 2, hidden), BF16),
+            pltpu.SemaphoreType.DMA((own, 2, tiles)),
         ],
         compiler_params=params(32),
         cost_estimate=pl.CostEstimate(
@@ -468,46 +472,57 @@
     bits = bits_of(n_ctx)
     orders = [bits if k % 2 == 0 else bits[::-1] for k in range(chunks)]
 
-    def gather_round(have, bit, token):
-        found = {}
-        for rel, block in have.items():
-            found[rel | bit] = swap(block if token is None else after(block, token), "ctx", n_ctx, bit)
-        return {**have, **found}
-
-    total = None
+    totals = [None] * chunks
     gathered = [None] * chunks
+
+    def project(k):
+        total = totals[k - 1] if k else None
+        if k == chunks - 2:
+            total = after(total, weight)
+        totals[k] = up_chunk(place, k, gathered[k], expert_up, total, k == chunks - 1)
+        return totals[k]
+
     for k in range(chunks):
         have = {0: arrived[k]}
         for bit in orders[k]:
-            have = gather_round(have, bit, None)
+            token = project(k - 3) if k >= 3 and bit == orders[k][0] else None
+            if k == chunks - 1 and k >= 2 and bit == orders[k][-1] and len(bits) > 1:
+                token = project(k - 2)
+            found = {}
+            for rel, block in have.items():
+                if token is not None:
+                    block = after(block, token)
+                found[rel | bit] = swap(block, "ctx", n_ctx, bit)
+            have.update(found)
         gathered[k] = [have[rel] for rel in range(n_ctx)]
-    gathered[0][0] = after(gathered[0][0], weight)
     for k in range(chunks):
-        total = up_chunk(place, k, gathered[k], expert_up, total, k == chunks - 1)
-    hidden = total
-
-    pending, returned = [], [None] * chunks
-
-    def advance(token):
-        k, step, kept, got = pending.pop(0)
-        got = after(got, token)
-        if step + 1 < len(bits):
-            kept, sent = halve(kept, got)
-            pending.append((k, step + 1, kept, swap(sent, "ctx", n_ctx, orders[k][step + 1])))
-            return sent
-        reply = reply_of(kept, got, weight)
-        returned[k] = swap(reply, "exp", n_exp, 2 * k) if k else reply
-        return reply
-
-    token = hidden
-    for k in reversed(range(chunks)):
-        sent, kept = down_chunk(
-            place, k, after(hidden, token), expert_down, width, route_of(orders[k], n_ctx)
-        )
-        pending.append((k, 0, kept, swap(sent, "ctx", n_ctx, orders[k][0])))
-        token = advance(sent) if k < chunks - 2 else sent
-    while pending:
-        token = advance(token)
+        if totals[k] is None:
+            project(k)
+    hidden = totals[-1]
+
+    order = list(reversed(range(chunks)))
+    open_sums, returned, token = {}, [None] * chunks, hidden
+    for i in range(chunks + 3):
+        if i < chunks:
+            k = order[i]
+            sent, kept = down_chunk(
+                place, k, after(hidden, token), expert_down, width, route_of(orders[k], n_ctx)
+            )
+            open_sums[k] = kept, swap(sent, "ctx", n_ctx, orders[k][0])
+            token = sent
+        if 2 <= i < chunks + 2:
+            k = order[i - 2]
+            for bit in orders[k][1:]:
+                kept, got = open_sums[k]
+                kept, sent = halve(kept, after(got, token))
+                open_sums[k] = kept, swap(sent, "ctx", n_ctx, bit)
+                token = sent
+        if i >= 3:
+            k = order[i - 3]
+            kept, got = open_sums[k]
+            early = [returned[order[i - 5]]] if i >= 5 else []
+            token = reply_of(kept, after(got, token, *early), weight)
+            returned[k] = swap(token, "exp", n_exp, 2 * k) if k else token
 
     mine, theirs = pl.pallas_call(
         combine_kernel,

time: 160 us -> 157 us (0.981)
  waiting for transfers between devices: 42.2 us -> 35.7 us
  starting transfers between devices: 55.5 us -> 59 us
    ppermute x34, waiting for transfers between devices: 42.2 us -> 35.7 us  [swap(): return lax.ppermute(x, axis, [(i, i ^ k) for i in range(n) if keep(i)])]
    ppermute x34, starting transfers between devices: 55.5 us -> 59 us  [swap(): return lax.ppermute(x, axis, [(i, i ^ k) for i in range(n) if keep(i)])]
  transfers between devices with their start and end apart: 34 -> 34, of which waited for: 13 -> 15; matrix products, arithmetic and copies ran while one was open for 3% -> 4% of each run, Pallas kernels for 23% -> 24%
where the time goes in v4:
time: 157 us
  starting transfers between devices  59 us (38%)
  Pallas kernels  54.4 us (35%)
  waiting for transfers between devices  35.7 us (23%)
  other arithmetic  6.3 us (4%)
    ppermute x34, starting transfers between devices, swap(): return lax.ppermute(x, axis, [(i, i ^ k) for i in range(n) if keep(i)])  59 us
    ppermute x34, waiting for transfers between devices, swap(): return lax.ppermute(x, axis, [(i, i ^ k) for i in range(n) if keep(i)])  35.7 us
    pallas_call x4, Pallas kernels, down_chunk(): pl.pallas_call(functools.partial(down_kernel, chunk=chunk, route=route),...  21.2 us
    pallas_call x4, Pallas kernels, up_chunk(): pl.pallas_call(functools.partial(up_kernel, chunk=chunk, parts=parts, fir...  20.1 us
    pallas_call x1, Pallas kernels, body(): pl.pallas_call(inside_kernel, in_specs=[SMEM] + [VMEM] * 5, out_specs=[VM...  4.27 us
    pallas_call x1, Pallas kernels, body(): pl.pallas_call(state_kernel, in_specs=[ANY] * 2 + [VMEM], out_specs=[VMEM...  3.93 us
  transfers between devices with their start and end apart: 34, of which 15 were waited for; matrix products, arithmetic and copies ran while one was open for 4% of the time, Pallas kernels for 24%

profile of v4, /device:TPU:0, one launch (start us, length us, event | category | flops | bytes accessed | tf_op | source)
XLA Modules:
  0.0 157.0 jit_solution(4061054071691309578)
XLA Ops:
  0.0 3.9 %local_state.1 = (bf16[12,128,128]{2,1,0:T(8,128)(2,1)}, bf16[12,128,128]{2,1,0:T(8,128)(2,1)}) custom-call(bf16[4,64,768]{2,1,0:T(8,128)(2,1)} %keys.3, bf16[4,64,768]{2,1,0:T(8,128)(2,1)} %values.3, f32[24,64]{1,0:T(8,128)} %bitcast.19), custom_call_target="tpu_custom_call" | custom-call | tf_op jit(solution)/shard_map/local_state/pallas_call | solution.py:413
  3.9 4.9 %collective-permute-start = (bf16[12,128,128]{2,1,0:T(8,128)(2,1)}, bf16[12,128,128]{2,1,0:T(8,128)(2,1)S(1)}, u32[]{:S(2)}, u32[]{:S(2)}) collective-permute-start(bf16[12,128,128]{2,1,0:T(8,128)(2,1)} %get-tuple-element.50), channel_id=1, source_target_pairs={{0,8},{8,0},{16,24},{1,9},{9,1},{17,25},{2,10},{10,2},{18,26},{3,1... | collective-permute-start | bytes 1179656 | tf_op jit(solution)/shard_map/ppermute | solution.py:27
  8.8 3.5 %collective-permute-start.4 = (bf16[12,128,128]{2,1,0:T(8,128)(2,1)}, bf16[12,128,128]{2,1,0:T(8,128)(2,1)S(1)}, u32[]{:S(2)}, u32[]{:S(2)}) collective-permute-start(bf16[12,128,128]{2,1,0:T(8,128)(2,1)} %get-tuple-element.51), channel_id=1, source_target_pairs={{0,16},{8,24},{1,17},{9,25},{2,18},{10,26},{3,19},{11,27},{4,20},{... | collective-permute-start | bytes 1179656 | tf_op jit(solution)/shard_map/ppermute | solution.py:27
  14.5 3.7 %collective-permute-done.1 = f32[2,12,1,1]{1,0,3,2:T(2,128)S(1)} collective-permute-done((f32[2,12,1,1]{1,0,3,2:T(2,128)S(1)}, f32[2,12,1,1]{1,0,3,2:T(2,128)S(1)}, u32[]{:S(2)}, u32[]{:S(2)}) %collective-permute-start.1) | collective-permute-done | bytes 128 | tf_op jit(solution)/shard_map/ppermute | solution.py:27
  19.3 1.3 collective-permute-done.4
  20.7 1.2 fusion.7
  21.9 3.2 %collective-permute-start.5 = (bf16[12,128,128]{2,1,0:T(8,128)(2,1)S(1)}, bf16[12,128,128]{2,1,0:T(8,128)(2,1)S(1)}, u32[]{:S(2)}, u32[]{:S(2)}) collective-permute-start(bf16[12,128,128]{2,1,0:T(8,128)(2,1)S(1)} %fusion.7), channel_id=1, source_target_pairs={{0,8},{16,24},{24,16},{1,9},{17,25},{25,17},{2,10},{18,26},{26,18}... | collective-permute-start | bytes 1179656 | tf_op jit(solution)/shard_map/ppermute | solution.py:27
  25.1 1.2 fusion.3
  26.4 3.0 %collective-permute-start.2 = (bf16[12,128,128]{2,1,0:T(8,128)(2,1)S(1)}, bf16[12,128,128]{2,1,0:T(8,128)(2,1)S(1)}, u32[]{:S(2)}, u32[]{:S(2)}) collective-permute-start(bf16[12,128,128]{2,1,0:T(8,128)(2,1)S(1)} %fusion.3), channel_id=1, source_target_pairs={{0,16},{8,24},{1,17},{9,25},{2,18},{10,26},{3,19},{11,27},{4,20},{... | collective-permute-start | bytes 1179656 | tf_op jit(solution)/shard_map/ppermute | solution.py:27
  30.1 4.3 %inside_and_placement.1 = (f32[4,64,768]{2,1,0:T(8,128)S(1)}, bf16[320,256]{1,0:T(8,128)(2,1)S(1)}, s32[80,128]{1,0:T(8,128)S(1)}) custom-call(s32[2]{0:T(128)S(1)} %pad_add_fusion.place, bf16[4,64,768]{2,1,0:T(8,128)(2,1)S(1)} %copy-done, bf16[4,64,768]{2,1,0:T(8,128)(2,1)S(1)} %copy-done.1, bf16[4,64,768]{2,1,0:T(8,128)(2,1)S(1)} %copy-done.2, ...), custom_call_target="tpu_custom_call" | custom-call | tf_op jit(solution)/shard_map/inside_and_placement/pallas_call | solution.py:432
  35.3 1.2 collective-permute-done.2
  36.7 2.0 %normed.1.refs_0_ = bf16[256,768]{1,0:T(8,128)(2,1)S(1)} custom-call(bf16[4,64,768]{2,1,0:T(8,128)(2,1)S(1)} %copy-done, f32[4,64,768]{2,1,0:T(8,128)S(1)} %get-tuple-element.49.inside, f32[24,64]{1,0:T(8,128)S(1)} %bitcast.21, f32[1,768]{1,0:T(1,128)S(1)} %reshape.84.gain, bf16[12,128,128]{2,1,0:T(8,128)(2,1)S(1)} %fusion.1.refs_0_, ...), custom_call_target="tpu_custom_call" | custom-call | tf_op jit(solution)/shard_map/normed/pallas_call | solution.py:445
  38.8 1.7 %collective-permute-done.6.refs_1_ = bf16[256,768]{1,0:T(8,128)(2,1)S(1)} collective-permute-done((bf16[256,768]{1,0:T(8,128)(2,1)S(1)}, bf16[256,768]{1,0:T(8,128)(2,1)S(1)}, u32[]{:S(2)}, u32[]{:S(2)}) %collective-permute-start.6) | collective-permute-done | bytes 393248 | tf_op jit(solution)/shard_map/ppermute | solution.py:27
  40.9 1.6 %collective-permute-start.8 = (bf16[2,40,1536]{2,1,0:T(8,128)(2,1)S(1)}, bf16[2,40,1536]{2,1,0:T(8,128)(2,1)S(1)}, u32[]{:S(2)}, u32[]{:S(2)}) collective-permute-start(bf16[2,40,1536]{2,1,0:T(8,128)(2,1)S(1)} %get-tuple-element.55), channel_id=1, source_target_pairs={{0,2},{1,3},{2,0},{3,1},{4,6},{5,7},{6,4},{7,5},{8,10},{9,11},{10,... | collective-permute-start | bytes 737288 | tf_op jit(solution)/shard_map/ppermute | solution.py:27
  42.6 1.7 %collective-permute-start.12 = (bf16[2,40,1536]{2,1,0:T(8,128)(2,1)S(1)}, bf16[2,40,1536]{2,1,0:T(8,128)(2,1)S(1)}, u32[]{:S(2)}, u32[]{:S(2)}) collective-permute-start(bf16[2,40,1536]{2,1,0:T(8,128)(2,1)S(1)} %get-tuple-element.56.refs_0_), channel_id=1, source_target_pairs={{0,8},{8,0},{16,24},{24,16},{1,9},{9,1},{17,25},{25,17},{2,10},{10... | collective-permute-start | bytes 737288 | tf_op jit(solution)/shard_map/ppermute | solution.py:27
  44.3 2.5 %collective-permute-start.13 = (bf16[2,40,1536]{2,1,0:T(8,128)(2,1)S(1)}, bf16[2,40,1536]{2,1,0:T(8,128)(2,1)S(1)}, u32[]{:S(2)}, u32[]{:S(2)}) collective-permute-start(bf16[2,40,1536]{2,1,0:T(8,128)(2,1)S(1)} %get-tuple-element.56.refs_0_), channel_id=1, source_target_pairs={{0,16},{8,24},{16,0},{24,8},{1,17},{9,25},{17,1},{25,9},{2,18},{10... | collective-permute-start | bytes 737288 | tf_op jit(solution)/shard_map/ppermute | solution.py:27
  46.8 2.6 %collective-permute-start.18 = (bf16[2,40,1536]{2,1,0:T(8,128)(2,1)S(1)}, bf16[2,40,1536]{2,1,0:T(8,128)(2,1)S(1)}, u32[]{:S(2)}, u32[]{:S(2)}) collective-permute-start(bf16[2,40,1536]{2,1,0:T(8,128)(2,1)S(1)} %get-tuple-element.60), channel_id=1, source_target_pairs={{0,4},{1,5},{2,6},{3,7},{4,0},{5,1},{6,2},{7,3},{8,12},{9,13},{10,... | collective-permute-start | bytes 737288 | tf_op jit(solution)/shard_map/ppermute | solution.py:27
  49.4 5.8 %collective-permute-start.10 = (bf16[2,40,1536]{2,1,0:T(8,128)(2,1)S(1)}, bf16[2,40,1536]{2,1,0:T(8,128)(2,1)S(1)}, u32[]{:S(2)}, u32[]{:S(2)}) collective-permute-start(bf16[2,40,1536]{2,1,0:T(8,128)(2,1)S(1)} %collective-permute-done.8.refs_0_.refs_1_), channel_id=1, source_target_pairs={{0,16},{8,24},{16,0},{24,8},{1,17},{9,25},{17,1},{25,9},{2,18},{10... | collective-permute-start | bytes 737288 | tf_op jit(solution)/shard_map/ppermute | solution.py:27
  55.2 2.5 %collective-permute-start.7 = (bf16[2,40,1536]{2,1,0:T(8,128)(2,1)S(1)}, bf16[2,40,1536]{2,1,0:T(8,128)(2,1)S(1)}, u32[]{:S(2)}, u32[]{:S(2)}) collective-permute-start(bf16[2,40,1536]{2,1,0:T(8,128)(2,1)S(1)} %get-tuple-element.54), channel_id=1, source_target_pairs={{0,6},{1,7},{2,4},{3,5},{4,2},{5,3},{6,0},{7,1},{8,14},{9,15},{10,... | collective-permute-start | bytes 737288 | tf_op jit(solution)/shard_map/ppermute | solution.py:27
  57.7 3.1 %collective-permute-start.9 = (bf16[2,40,1536]{2,1,0:T(8,128)(2,1)S(1)}, bf16[2,40,1536]{2,1,0:T(8,128)(2,1)S(1)}, u32[]{:S(2)}, u32[]{:S(2)}) collective-permute-start(bf16[2,40,1536]{2,1,0:T(8,128)(2,1)S(1)} %collective-permute-done.8.refs_0_.refs_1_), channel_id=1, source_target_pairs={{0,8},{8,0},{16,24},{24,16},{1,9},{9,1},{17,25},{25,17},{2,10},{10... | collective-permute-start | bytes 737288 | tf_op jit(solution)/shard_map/ppermute | solution.py:27
  60.8 5.8 %collective-permute-done.18.refs_2_.refs_0_ = bf16[2,40,1536]{2,1,0:T(8,128)(2,1)S(1)} collective-permute-done((bf16[2,40,1536]{2,1,0:T(8,128)(2,1)S(1)}, bf16[2,40,1536]{2,1,0:T(8,128)(2,1)S(1)}, u32[]{:S(2)}, u32[]{:S(2)}) %collective-permute-start.18) | collective-permute-done | bytes 245792 | tf_op jit(solution)/shard_map/ppermute | solution.py:27
  66.6 2.0 %collective-permute-start.11 = (bf16[2,40,1536]{2,1,0:T(8,128)(2,1)S(1)}, bf16[2,40,1536]{2,1,0:T(8,128)(2,1)S(1)}, u32[]{:S(2)}, u32[]{:S(2)}) collective-permute-start(bf16[2,40,1536]{2,1,0:T(8,128)(2,1)S(1)} %collective-permute-done.10.refs_2_), channel_id=1, source_target_pairs={{0,8},{8,0},{16,24},{24,16},{1,9},{9,1},{17,25},{25,17},{2,10},{10... | collective-permute-start | bytes 737288 | tf_op jit(solution)/shard_map/ppermute | solution.py:27
  68.6 5.3 %up_0.1.refs_4_ = f32[2,160,1536]{2,1,0:T(8,128)S(1)} custom-call(s32[2]{0:T(128)S(1)} %pad_add_fusion.place, bf16[2,6144,1536]{2,1,0:T(8,128)(2,1)} %weights.11, bf16[2,40,1536]{2,1,0:T(8,128)(2,1)S(1)} %get-tuple-element.56.refs_0_, bf16[2,40,1536]{2,1,0:T(8,128)(2,1)S(1)} %collective-permute-done.12.refs_1_, ...), custom_call_target="tpu_custom_call" | custom-call | flops 1509949440 | bytes 9437184 | tf_op jit(solution)/shard_map/up_0/pallas_call | solution.py:223
  74.5 1.5 collective-permute-start.20
  77.4 4.9 %up_1.1.refs_4_ = f32[2,160,1536]{2,1,0:T(8,128)S(1)} custom-call(s32[2]{0:T(128)S(1)} %pad_add_fusion.place, bf16[2,6144,1536]{2,1,0:T(8,128)(2,1)} %weights.11, bf16[2,40,1536]{2,1,0:T(8,128)(2,1)S(1)} %collective-permute-done.8.refs_0_.refs_1_, bf16[2,40,1536]{2,1,0:T(8,128)(2,1)S(1)} %collective-permute-done.9.refs_1_, ...), custom_call_target="tpu_custom_call" | custom-call | flops 1509949440 | bytes 9437184 | tf_op jit(solution)/shard_map/up_1/pallas_call | solution.py:223
  83.2 1.2 collective-permute-start.17
  84.4 1.1 gate.1.weight
  85.5 1.4 collective-permute-done.20.refs_2_
  86.9 2.6 %collective-permute-done.21.refs_3_ = bf16[2,40,1536]{2,1,0:T(8,128)(2,1)S(1)} collective-permute-done((bf16[2,40,1536]{2,1,0:T(8,128)(2,1)S(1)}, bf16[2,40,1536]{2,1,0:T(8,128)(2,1)S(1)}, u32[]{:S(2)}, u32[]{:S(2)}) %collective-permute-start.21) | collective-permute-done | bytes 245792 | tf_op jit(solution)/shard_map/ppermute | solution.py:27
  89.5 4.9 %up_2.1.refs_4_ = f32[2,160,1536]{2,1,0:T(8,128)S(1)} custom-call(s32[2]{0:T(128)S(1)} %pad_add_fusion.place, bf16[2,6144,1536]{2,1,0:T(8,128)(2,1)} %weights.11, bf16[2,40,1536]{2,1,0:T(8,128)(2,1)S(1)} %collective-permute-done.18.refs_2_.refs_0_, bf16[2,40,1536]{2,1,0:T(8,128)(2,1)S(1)} %collective-permute-done.19.refs_1_, ...), custom_call_target="tpu_custom_call" | custom-call | flops 1509949440 | bytes 9437184 | tf_op jit(solution)/shard_map/up_2/pallas_call | solution.py:223
  94.5 5.0 %up_3.1.hidden = bf16[2,160,1536]{2,1,0:T(8,128)(2,1)S(1)} custom-call(s32[2]{0:T(128)S(1)} %pad_add_fusion.place, bf16[2,6144,1536]{2,1,0:T(8,128)(2,1)} %weights.11, bf16[2,40,1536]{2,1,0:T(8,128)(2,1)S(1)} %collective-permute-done.7.refs_3_.refs_0_, bf16[2,40,1536]{2,1,0:T(8,128)(2,1)S(1)} %collective-permute-done.15.refs_1_, ...), custom_call_target="tpu_custom_call" | custom-call | flops 1509949440 | bytes 9437184 | tf_op jit(solution)/shard_map/up_3/pallas_call | solution.py:223
  99.4 5.5 %down_3.1 = (bf16[2,2,40,1536]{3,2,1,0:T(8,128)(2,1)S(1)}, bf16[2,2,40,1536]{3,2,1,0:T(8,128)(2,1)S(1)}) custom-call(s32[2]{0:T(128)S(1)} %pad_add_fusion.place, bf16[2,1536,6144]{2,1,0:T(8,128)(2,1)} %weights.15, bf16[2,160,1536]{2,1,0:T(8,128)(2,1)S(1)} %up_3.1.hidden), custom_call_target="tpu_custom_call" | custom-call | flops 1509949440 | bytes 9437184 | tf_op jit(solution)/shard_map/down_3/pallas_call | solution.py:275
  105.3 5.2 %down_2.1 = (bf16[2,2,40,1536]{3,2,1,0:T(8,128)(2,1)S(1)}, bf16[2,2,40,1536]{3,2,1,0:T(8,128)(2,1)S(1)}) custom-call(s32[2]{0:T(128)S(1)} %pad_add_fusion.place, bf16[2,1536,6144]{2,1,0:T(8,128)(2,1)} %weights.15, bf16[2,160,1536]{2,1,0:T(8,128)(2,1)S(1)} %up_3.1.hidden), custom_call_target="tpu_custom_call" | custom-call | flops 1509949440 | bytes 9437184 | tf_op jit(solution)/shard_map/down_2/pallas_call | solution.py:275
  110.5 3.2 %collective-permute-start.24 = (bf16[2,2,40,1536]{3,2,1,0:T(8,128)(2,1)S(1)}, bf16[2,2,40,1536]{3,2,1,0:T(8,128)(2,1)S(1)}, u32[]{:S(2)}, u32[]{:S(2)}) collective-permute-start(bf16[2,2,40,1536]{3,2,1,0:T(8,128)(2,1)S(1)} %get-tuple-element.67), channel_id=1, source_target_pairs={{0,8},{8,0},{16,24},{24,16},{1,9},{9,1},{17,25},{25,17},{2,10},{10... | collective-permute-start | bytes 1474568 | tf_op jit(solution)/shard_map/ppermute | solution.py:27
  113.7 5.2 %down_1.1 = (bf16[2,2,40,1536]{3,2,1,0:T(8,128)(2,1)S(1)}, bf16[2,2,40,1536]{3,2,1,0:T(8,128)(2,1)S(1)}) custom-call(s32[2]{0:T(128)S(1)} %pad_add_fusion.place, bf16[2,1536,6144]{2,1,0:T(8,128)(2,1)} %weights.15, bf16[2,160,1536]{2,1,0:T(8,128)(2,1)S(1)} %up_3.1.hidden), custom_call_target="tpu_custom_call" | custom-call | flops 1509949440 | bytes 9437184 | tf_op jit(solution)/shard_map/down_1/pallas_call | solution.py:275
  119.9 5.2 %down_0.1 = (bf16[2,2,40,1536]{3,2,1,0:T(8,128)(2,1)S(1)}, bf16[2,2,40,1536]{3,2,1,0:T(8,128)(2,1)S(1)}) custom-call(s32[2]{0:T(128)S(1)} %pad_add_fusion.place, bf16[2,1536,6144]{2,1,0:T(8,128)(2,1)} %weights.15, bf16[2,160,1536]{2,1,0:T(8,128)(2,1)S(1)} %up_3.1.hidden), custom_call_target="tpu_custom_call" | custom-call | flops 1509949440 | bytes 9437184 | tf_op jit(solution)/shard_map/down_0/pallas_call | solution.py:275
  125.1 2.0 %collective-permute-start.23 = (bf16[2,2,40,1536]{3,2,1,0:T(8,128)(2,1)S(1)}, bf16[2,2,40,1536]{3,2,1,0:T(8,128)(2,1)S(1)}, u32[]{:S(2)}, u32[]{:S(2)}) collective-permute-start(bf16[2,2,40,1536]{3,2,1,0:T(8,128)(2,1)S(1)} %get-tuple-element.74), channel_id=1, source_target_pairs={{0,8},{8,0},{16,24},{24,16},{1,9},{9,1},{17,25},{25,17},{2,10},{10... | collective-permute-start | bytes 1474568 | tf_op jit(solution)/shard_map/ppermute | solution.py:27
  127.2 1.5 collective-permute-start.25
  128.8 1.6 %collective-permute-done.27.got = bf16[1,2,40,1536]{3,2,1,0:T(8,128)(2,1)S(1)} collective-permute-done((bf16[1,2,40,1536]{3,2,1,0:T(8,128)(2,1)S(1)}, bf16[1,2,40,1536]{3,2,1,0:T(8,128)(2,1)S(1)}, u32[]{:S(2)}, u32[]{:S(2)}) %collective-permute-start.27) | collective-permute-done | bytes 245792 | tf_op jit(solution)/shard_map/ppermute | solution.py:27
  130.5 1.2 collective-permute-done.26.got
  132.4 2.4 %collective-permute-start.30 = (bf16[2,40,1536]{2,1,0:T(8,128)(2,1)S(1)}, bf16[2,40,1536]{2,1,0:T(8,128)(2,1)S(1)}, u32[]{:S(2)}, u32[]{:S(2)}) collective-permute-start(bf16[2,40,1536]{2,1,0:T(8,128)(2,1)S(1)} %reply.4), channel_id=1, source_target_pairs={{0,6},{1,7},{2,4},{3,5},{4,2},{5,3},{6,0},{7,1},{8,14},{9,15},{10,... | collective-permute-start | bytes 737288 | tf_op jit(solution)/shard_map/ppermute | solution.py:27
  135.0 5.7 %collective-permute-done.23.got = bf16[2,2,40,1536]{3,2,1,0:T(8,128)(2,1)S(1)} collective-permute-done((bf16[2,2,40,1536]{3,2,1,0:T(8,128)(2,1)S(1)}, bf16[2,2,40,1536]{3,2,1,0:T(8,128)(2,1)S(1)}, u32[]{:S(2)}, u32[]{:S(2)}) %collective-permute-start.23) | collective-permute-done | bytes 491552 | tf_op jit(solution)/shard_map/ppermute | solution.py:27
  140.8 0.9 collective-permute-start.28
  141.7 1.7 %collective-permute-done.29.got = bf16[1,2,40,1536]{3,2,1,0:T(8,128)(2,1)S(1)} collective-permute-done((bf16[1,2,40,1536]{3,2,1,0:T(8,128)(2,1)S(1)}, bf16[1,2,40,1536]{3,2,1,0:T(8,128)(2,1)S(1)}, u32[]{:S(2)}, u32[]{:S(2)}) %collective-permute-start.29) | collective-permute-done | bytes 245792 | tf_op jit(solution)/shard_map/ppermute | solution.py:27
  143.4 5.1 %collective-permute-start.32 = (bf16[2,40,1536]{2,1,0:T(8,128)(2,1)S(1)}, bf16[2,40,1536]{2,1,0:T(8,128)(2,1)S(1)}, u32[]{:S(2)}, u32[]{:S(2)}) collective-permute-start(bf16[2,40,1536]{2,1,0:T(8,128)(2,1)S(1)} %reply.6), channel_id=1, source_target_pairs={{0,2},{1,3},{2,0},{3,1},{4,6},{5,7},{6,4},{7,5},{8,10},{9,11},{10,... | collective-permute-start | bytes 737288 | tf_op jit(solution)/shard_map/ppermute | solution.py:27
  148.5 2.3 %collective-permute-done.31.refs_2_ = bf16[2,40,1536]{2,1,0:T(8,128)(2,1)S(1)} collective-permute-done((bf16[2,40,1536]{2,1,0:T(8,128)(2,1)S(1)}, bf16[2,40,1536]{2,1,0:T(8,128)(2,1)S(1)}, u32[]{:S(2)}, u32[]{:S(2)}) %collective-permute-start.31) | collective-permute-done | bytes 245792 | tf_op jit(solution)/shard_map/ppermute | solution.py:27
  151.0 2.8 %collective-permute-done.32.refs_1_ = bf16[2,40,1536]{2,1,0:T(8,128)(2,1)S(1)} collective-permute-done((bf16[2,40,1536]{2,1,0:T(8,128)(2,1)S(1)}, bf16[2,40,1536]{2,1,0:T(8,128)(2,1)S(1)}, u32[]{:S(2)}, u32[]{:S(2)}) %collective-permute-start.32) | collective-permute-done | bytes 245792 | tf_op jit(solution)/shard_map/ppermute | solution.py:27
  154.5 1.7 %collective-permute-done.33 = bf16[256,768]{1,0:T(8,128)(2,1)S(1)} collective-permute-done((bf16[256,768]{1,0:T(8,128)(2,1)S(1)}, bf16[256,768]{1,0:T(8,128)(2,1)S(1)}, u32[]{:S(2)}, u32[]{:S(2)}) %collective-permute-start.33) | collective-permute-done | bytes 393248 | tf_op jit(solution)/shard_map/ppermute | solution.py:27
  (74 shorter events, 12.7 us)
Async XLA Ops:
  0.0 30.1 %copy-start.1 = (bf16[4,64,768]{2,1,0:T(8,128)(2,1)S(1)}, bf16[4,64,768]{2,1,0:T(8,128)(2,1)}, u32[]{:S(2)}) copy-start(bf16[4,64,768]{2,1,0:T(8,128)(2,1)} %keys.3) | copy-start | bytes 1179652
  0.0 30.1 %copy-start.2 = (bf16[4,64,768]{2,1,0:T(8,128)(2,1)S(1)}, bf16[4,64,768]{2,1,0:T(8,128)(2,1)}, u32[]{:S(2)}) copy-start(bf16[4,64,768]{2,1,0:T(8,128)(2,1)} %values.3) | copy-start | bytes 1179652
  0.0 30.1 %copy-start.3 = (f32[4,64,6]{1,0,2:T(4,128)S(1)}, f32[4,64,6]{1,0,2:T(4,128)}, u32[]{:S(2)}) copy-start(f32[4,64,6]{1,0,2:T(4,128)} %param.12) | copy-start | bytes 18436
  0.0 30.1 %copy-start = (bf16[4,64,768]{2,1,0:T(8,128)(2,1)S(1)}, bf16[4,64,768]{2,1,0:T(8,128)(2,1)}, u32[]{:S(2)}) copy-start(bf16[4,64,768]{2,1,0:T(8,128)(2,1)} %queries.3) | copy-start | bytes 1179652
  0.0 30.1 %copy-start.5 = (s32[64,4,2]{0,2,1:T(2,128)S(1)}, s32[64,4,2]{0,2,1:T(2,128)}, u32[]{:S(2)}) copy-start(s32[64,4,2]{0,2,1:T(2,128)} %param.17) | copy-start | bytes 6148
  3.9 21.2 %collective-permute-start = (bf16[12,128,128]{2,1,0:T(8,128)(2,1)}, bf16[12,128,128]{2,1,0:T(8,128)(2,1)S(1)}, u32[]{:S(2)}, u32[]{:S(2)}) collective-permute-start(bf16[12,128,128]{2,1,0:T(8,128)(2,1)} %get-tuple-element.50), channel_id=1, source_target_pairs={{0,8},{8,0},{16,24},{1,9},{9,1},{17,25},{2,10},{10,2},{18,26},{3,1... | collective-permute-start | bytes 1179656 | tf_op jit(solution)/shard_map/ppermute | solution.py:27
  8.8 11.9 %collective-permute-start.4 = (bf16[12,128,128]{2,1,0:T(8,128)(2,1)}, bf16[12,128,128]{2,1,0:T(8,128)(2,1)S(1)}, u32[]{:S(2)}, u32[]{:S(2)}) collective-permute-start(bf16[12,128,128]{2,1,0:T(8,128)(2,1)} %get-tuple-element.51), channel_id=1, source_target_pairs={{0,16},{8,24},{1,17},{9,25},{2,18},{10,26},{3,19},{11,27},{4,20},{... | collective-permute-start | bytes 1179656 | tf_op jit(solution)/shard_map/ppermute | solution.py:27
  13.3 4.9 %collective-permute-start.1 = (f32[2,12,1,1]{1,0,3,2:T(2,128)S(1)}, f32[2,12,1,1]{1,0,3,2:T(2,128)S(1)}, u32[]{:S(2)}, u32[]{:S(2)}) collective-permute-start(f32[2,12,1,1]{1,0,3,2:T(2,128)S(1)} %exp.14), channel_id=1, source_target_pairs={{0,8},{8,0},{16,24},{24,16},{1,9},{9,1},{17,25},{25,17},{2,10},{10... | collective-permute-start | bytes 296 | tf_op jit(solution)/shard_map/ppermute | solution.py:27
  13.3 4.9 %collective-permute-start.3 = (f32[2,12,1,1]{1,0,3,2:T(2,128)S(1)}, f32[2,12,1,1]{1,0,3,2:T(2,128)S(1)}, u32[]{:S(2)}, u32[]{:S(2)}) collective-permute-start(f32[2,12,1,1]{1,0,3,2:T(2,128)S(1)} %exp.14), channel_id=1, source_target_pairs={{0,24},{8,16},{16,8},{24,0},{1,25},{9,17},{17,9},{25,1},{2,26},{10... | collective-permute-start | bytes 296 | tf_op jit(solution)/shard_map/ppermute | solution.py:27
  21.9 12.6 %collective-permute-start.5 = (bf16[12,128,128]{2,1,0:T(8,128)(2,1)S(1)}, bf16[12,128,128]{2,1,0:T(8,128)(2,1)S(1)}, u32[]{:S(2)}, u32[]{:S(2)}) collective-permute-start(bf16[12,128,128]{2,1,0:T(8,128)(2,1)S(1)} %fusion.7), channel_id=1, source_target_pairs={{0,8},{16,24},{24,16},{1,9},{17,25},{25,17},{2,10},{18,26},{26,18}... | collective-permute-start | bytes 1179656 | tf_op jit(solution)/shard_map/ppermute | solution.py:27
  26.4 10.1 %collective-permute-start.2 = (bf16[12,128,128]{2,1,0:T(8,128)(2,1)S(1)}, bf16[12,128,128]{2,1,0:T(8,128)(2,1)S(1)}, u32[]{:S(2)}, u32[]{:S(2)}) collective-permute-start(bf16[12,128,128]{2,1,0:T(8,128)(2,1)S(1)} %fusion.3), channel_id=1, source_target_pairs={{0,16},{8,24},{1,17},{9,25},{2,18},{10,26},{3,19},{11,27},{4,20},{... | collective-permute-start | bytes 1179656 | tf_op jit(solution)/shard_map/ppermute | solution.py:27
  29.3 7.1 %copy-start.6 = (f32[12]{0:T(128)S(1)}, f32[12]{0:T(128)}, u32[]{:S(2)}) copy-start(f32[12]{0:T(128)} %get-tuple-element.97) | copy-start | bytes 148
  38.7 1.8 %collective-permute-start.6 = (bf16[256,768]{1,0:T(8,128)(2,1)S(1)}, bf16[256,768]{1,0:T(8,128)(2,1)S(1)}, u32[]{:S(2)}, u32[]{:S(2)}) collective-permute-start(bf16[256,768]{1,0:T(8,128)(2,1)S(1)} %normed.1.refs_0_), channel_id=1, source_target_pairs={{0,1},{1,0},{2,3},{3,2},{4,5},{5,4},{6,7},{7,6},{8,9},{9,8},{10,11... | collective-permute-start | bytes 1179656 | tf_op jit(solution)/shard_map/ppermute | solution.py:27
  40.9 8.4 %collective-permute-start.8 = (bf16[2,40,1536]{2,1,0:T(8,128)(2,1)S(1)}, bf16[2,40,1536]{2,1,0:T(8,128)(2,1)S(1)}, u32[]{:S(2)}, u32[]{:S(2)}) collective-permute-start(bf16[2,40,1536]{2,1,0:T(8,128)(2,1)S(1)} %get-tuple-element.55), channel_id=1, source_target_pairs={{0,2},{1,3},{2,0},{3,1},{4,6},{5,7},{6,4},{7,5},{8,10},{9,11},{10,... | collective-permute-start | bytes 737288 | tf_op jit(solution)/shard_map/ppermute | solution.py:27
  42.6 12.6 %collective-permute-start.12 = (bf16[2,40,1536]{2,1,0:T(8,128)(2,1)S(1)}, bf16[2,40,1536]{2,1,0:T(8,128)(2,1)S(1)}, u32[]{:S(2)}, u32[]{:S(2)}) collective-permute-start(bf16[2,40,1536]{2,1,0:T(8,128)(2,1)S(1)} %get-tuple-element.56.refs_0_), channel_id=1, source_target_pairs={{0,8},{8,0},{16,24},{24,16},{1,9},{9,1},{17,25},{25,17},{2,10},{10... | collective-permute-start | bytes 737288 | tf_op jit(solution)/shard_map/ppermute | solution.py:27
  44.3 13.4 %collective-permute-start.13 = (bf16[2,40,1536]{2,1,0:T(8,128)(2,1)S(1)}, bf16[2,40,1536]{2,1,0:T(8,128)(2,1)S(1)}, u32[]{:S(2)}, u32[]{:S(2)}) collective-permute-start(bf16[2,40,1536]{2,1,0:T(8,128)(2,1)S(1)} %get-tuple-element.56.refs_0_), channel_id=1, source_target_pairs={{0,16},{8,24},{16,0},{24,8},{1,17},{9,25},{17,1},{25,9},{2,18},{10... | collective-permute-start | bytes 737288 | tf_op jit(solution)/shard_map/ppermute | solution.py:27
  46.8 19.8 %collective-permute-start.18 = (bf16[2,40,1536]{2,1,0:T(8,128)(2,1)S(1)}, bf16[2,40,1536]{2,1,0:T(8,128)(2,1)S(1)}, u32[]{:S(2)}, u32[]{:S(2)}) collective-permute-start(bf16[2,40,1536]{2,1,0:T(8,128)(2,1)S(1)} %get-tuple-element.60), channel_id=1, source_target_pairs={{0,4},{1,5},{2,6},{3,7},{4,0},{5,1},{6,2},{7,3},{8,12},{9,13},{10,... | collective-permute-start | bytes 737288 | tf_op jit(solution)/shard_map/ppermute | solution.py:27
  49.4 17.2 %collective-permute-start.10 = (bf16[2,40,1536]{2,1,0:T(8,128)(2,1)S(1)}, bf16[2,40,1536]{2,1,0:T(8,128)(2,1)S(1)}, u32[]{:S(2)}, u32[]{:S(2)}) collective-permute-start(bf16[2,40,1536]{2,1,0:T(8,128)(2,1)S(1)} %collective-permute-done.8.refs_0_.refs_1_), channel_id=1, source_target_pairs={{0,16},{8,24},{16,0},{24,8},{1,17},{9,25},{17,1},{25,9},{2,18},{10... | collective-permute-start | bytes 737288 | tf_op jit(solution)/shard_map/ppermute | solution.py:27
  55.2 13.5 %collective-permute-start.14 = (bf16[2,40,1536]{2,1,0:T(8,128)(2,1)S(1)}, bf16[2,40,1536]{2,1,0:T(8,128)(2,1)S(1)}, u32[]{:S(2)}, u32[]{:S(2)}) collective-permute-start(bf16[2,40,1536]{2,1,0:T(8,128)(2,1)S(1)} %collective-permute-done.12.refs_1_), channel_id=1, source_target_pairs={{0,16},{8,24},{16,0},{24,8},{1,17},{9,25},{17,1},{25,9},{2,18},{10... | collective-permute-start | bytes 737288 | tf_op jit(solution)/shard_map/ppermute | solution.py:27
  55.2 18.7 %collective-permute-start.7 = (bf16[2,40,1536]{2,1,0:T(8,128)(2,1)S(1)}, bf16[2,40,1536]{2,1,0:T(8,128)(2,1)S(1)}, u32[]{:S(2)}, u32[]{:S(2)}) collective-permute-start(bf16[2,40,1536]{2,1,0:T(8,128)(2,1)S(1)} %get-tuple-element.54), channel_id=1, source_target_pairs={{0,6},{1,7},{2,4},{3,5},{4,2},{5,3},{6,0},{7,1},{8,14},{9,15},{10,... | collective-permute-start | bytes 737288 | tf_op jit(solution)/shard_map/ppermute | solution.py:27
  57.7 18.9 %collective-permute-start.9 = (bf16[2,40,1536]{2,1,0:T(8,128)(2,1)S(1)}, bf16[2,40,1536]{2,1,0:T(8,128)(2,1)S(1)}, u32[]{:S(2)}, u32[]{:S(2)}) collective-permute-start(bf16[2,40,1536]{2,1,0:T(8,128)(2,1)S(1)} %collective-permute-done.8.refs_0_.refs_1_), channel_id=1, source_target_pairs={{0,8},{8,0},{16,24},{24,16},{1,9},{9,1},{17,25},{25,17},{2,10},{10... | collective-permute-start | bytes 737288 | tf_op jit(solution)/shard_map/ppermute | solution.py:27
  66.6 9.4 %collective-permute-start.19 = (bf16[2,40,1536]{2,1,0:T(8,128)(2,1)S(1)}, bf16[2,40,1536]{2,1,0:T(8,128)(2,1)S(1)}, u32[]{:S(2)}, u32[]{:S(2)}) collective-permute-start(bf16[2,40,1536]{2,1,0:T(8,128)(2,1)S(1)} %collective-permute-done.18.refs_2_.refs_0_), channel_id=1, source_target_pairs={{0,8},{8,0},{16,24},{24,16},{1,9},{9,1},{17,25},{25,17},{2,10},{10... | collective-permute-start | bytes 737288 | tf_op jit(solution)/shard_map/ppermute | solution.py:27
  66.6 10.8 %collective-permute-start.11 = (bf16[2,40,1536]{2,1,0:T(8,128)(2,1)S(1)}, bf16[2,40,1536]{2,1,0:T(8,128)(2,1)S(1)}, u32[]{:S(2)}, u32[]{:S(2)}) collective-permute-start(bf16[2,40,1536]{2,1,0:T(8,128)(2,1)S(1)} %collective-permute-done.10.refs_2_), channel_id=1, source_target_pairs={{0,8},{8,0},{16,24},{24,16},{1,9},{9,1},{17,25},{25,17},{2,10},{10... | collective-permute-start | bytes 737288 | tf_op jit(solution)/shard_map/ppermute | solution.py:27
  73.9 10.5 %copy-start.4 = (bf16[6144,16]{0,1:T(8,128)(2,1)S(1)}, bf16[6144,16]{0,1:T(8,128)(2,1)}, u32[]{:S(2)}) copy-start(bf16[6144,16]{0,1:T(8,128)(2,1)} %param.14) | copy-start | bytes 589828
  73.9 9.2 %collective-permute-start.16 = (bf16[2,40,1536]{2,1,0:T(8,128)(2,1)S(1)}, bf16[2,40,1536]{2,1,0:T(8,128)(2,1)S(1)}, u32[]{:S(2)}, u32[]{:S(2)}) collective-permute-start(bf16[2,40,1536]{2,1,0:T(8,128)(2,1)S(1)} %collective-permute-done.7.refs_3_.refs_0_), channel_id=1, source_target_pairs={{0,16},{8,24},{16,0},{24,8},{1,17},{9,25},{17,1},{25,9},{2,18},{10... | collective-permute-start | bytes 737288 | tf_op jit(solution)/shard_map/ppermute | solution.py:27
  74.5 12.4 %collective-permute-start.20 = (bf16[2,40,1536]{2,1,0:T(8,128)(2,1)S(1)}, bf16[2,40,1536]{2,1,0:T(8,128)(2,1)S(1)}, u32[]{:S(2)}, u32[]{:S(2)}) collective-permute-start(bf16[2,40,1536]{2,1,0:T(8,128)(2,1)S(1)} %collective-permute-done.18.refs_2_.refs_0_), channel_id=1, source_target_pairs={{0,16},{8,24},{16,0},{24,8},{1,17},{9,25},{17,1},{25,9},{2,18},{10... | collective-permute-start | bytes 737288 | tf_op jit(solution)/shard_map/ppermute | solution.py:27
  76.0 13.5 %collective-permute-start.21 = (bf16[2,40,1536]{2,1,0:T(8,128)(2,1)S(1)}, bf16[2,40,1536]{2,1,0:T(8,128)(2,1)S(1)}, u32[]{:S(2)}, u32[]{:S(2)}) collective-permute-start(bf16[2,40,1536]{2,1,0:T(8,128)(2,1)S(1)} %collective-permute-done.19.refs_1_), channel_id=1, source_target_pairs={{0,16},{8,24},{16,0},{24,8},{1,17},{9,25},{17,1},{25,9},{2,18},{10... | collective-permute-start | bytes 737288 | tf_op jit(solution)/shard_map/ppermute | solution.py:27
  82.3 12.1 %collective-permute-start.15 = (bf16[2,40,1536]{2,1,0:T(8,128)(2,1)S(1)}, bf16[2,40,1536]{2,1,0:T(8,128)(2,1)S(1)}, u32[]{:S(2)}, u32[]{:S(2)}) collective-permute-start(bf16[2,40,1536]{2,1,0:T(8,128)(2,1)S(1)} %collective-permute-done.7.refs_3_.refs_0_), channel_id=1, source_target_pairs={{0,8},{8,0},{16,24},{24,16},{1,9},{9,1},{17,25},{25,17},{2,10},{10... | collective-permute-start | bytes 737288 | tf_op jit(solution)/shard_map/ppermute | solution.py:27
  83.2 11.3 %collective-permute-start.17 = (bf16[2,40,1536]{2,1,0:T(8,128)(2,1)S(1)}, bf16[2,40,1536]{2,1,0:T(8,128)(2,1)S(1)}, u32[]{:S(2)}, u32[]{:S(2)}) collective-permute-start(bf16[2,40,1536]{2,1,0:T(8,128)(2,1)S(1)} %collective-permute-done.16.refs_2_), channel_id=1, source_target_pairs={{0,8},{8,0},{16,24},{24,16},{1,9},{9,1},{17,25},{25,17},{2,10},{10... | collective-permute-start | bytes 737288 | tf_op jit(solution)/shard_map/ppermute | solution.py:27
  104.9 14.7 %collective-permute-start.22 = (bf16[2,2,40,1536]{3,2,1,0:T(8,128)(2,1)S(1)}, bf16[2,2,40,1536]{3,2,1,0:T(8,128)(2,1)S(1)}, u32[]{:S(2)}, u32[]{:S(2)}) collective-permute-start(bf16[2,2,40,1536]{3,2,1,0:T(8,128)(2,1)S(1)} %get-tuple-element.65), channel_id=1, source_target_pairs={{0,16},{8,24},{16,0},{24,8},{1,17},{9,25},{17,1},{25,9},{2,18},{10... | collective-permute-start | bytes 1474568 | tf_op jit(solution)/shard_map/ppermute | solution.py:27
  110.5 16.6 %collective-permute-start.24 = (bf16[2,2,40,1536]{3,2,1,0:T(8,128)(2,1)S(1)}, bf16[2,2,40,1536]{3,2,1,0:T(8,128)(2,1)S(1)}, u32[]{:S(2)}, u32[]{:S(2)}) collective-permute-start(bf16[2,2,40,1536]{3,2,1,0:T(8,128)(2,1)S(1)} %get-tuple-element.67), channel_id=1, source_target_pairs={{0,8},{8,0},{16,24},{24,16},{1,9},{9,1},{17,25},{25,17},{2,10},{10... | collective-permute-start | bytes 1474568 | tf_op jit(solution)/shard_map/ppermute | solution.py:27
  118.9 12.7 %collective-permute-start.26 = (bf16[2,2,40,1536]{3,2,1,0:T(8,128)(2,1)S(1)}, bf16[2,2,40,1536]{3,2,1,0:T(8,128)(2,1)S(1)}, u32[]{:S(2)}, u32[]{:S(2)}) collective-permute-start(bf16[2,2,40,1536]{3,2,1,0:T(8,128)(2,1)S(1)} %get-tuple-element.69), channel_id=1, source_target_pairs={{0,16},{8,24},{16,0},{24,8},{1,17},{9,25},{17,1},{25,9},{2,18},{10... | collective-permute-start | bytes 1474568 | tf_op jit(solution)/shard_map/ppermute | solution.py:27
  119.7 10.6 %collective-permute-start.27 = (bf16[1,2,40,1536]{3,2,1,0:T(8,128)(2,1)S(1)}, bf16[1,2,40,1536]{3,2,1,0:T(8,128)(2,1)S(1)}, u32[]{:S(2)}, u32[]{:S(2)}) collective-permute-start(bf16[1,2,40,1536]{3,2,1,0:T(8,128)(2,1)S(1)} %get-tuple-element.71), channel_id=1, source_target_pairs={{0,8},{8,0},{16,24},{24,16},{1,9},{9,1},{17,25},{25,17},{2,10},{10... | collective-permute-start | bytes 737288 | tf_op jit(solution)/shard_map/ppermute | solution.py:27
  125.1 15.6 %collective-permute-start.23 = (bf16[2,2,40,1536]{3,2,1,0:T(8,128)(2,1)S(1)}, bf16[2,2,40,1536]{3,2,1,0:T(8,128)(2,1)S(1)}, u32[]{:S(2)}, u32[]{:S(2)}) collective-permute-start(bf16[2,2,40,1536]{3,2,1,0:T(8,128)(2,1)S(1)} %get-tuple-element.74), channel_id=1, source_target_pairs={{0,8},{8,0},{16,24},{24,16},{1,9},{9,1},{17,25},{25,17},{2,10},{10... | collective-permute-start | bytes 1474568 | tf_op jit(solution)/shard_map/ppermute | solution.py:27
  127.2 7.6 %collective-permute-start.25 = (bf16[1,2,40,1536]{3,2,1,0:T(8,128)(2,1)S(1)}, bf16[1,2,40,1536]{3,2,1,0:T(8,128)(2,1)S(1)}, u32[]{:S(2)}, u32[]{:S(2)}) collective-permute-start(bf16[1,2,40,1536]{3,2,1,0:T(8,128)(2,1)S(1)} %get-tuple-element.78), channel_id=1, source_target_pairs={{0,16},{8,24},{16,0},{24,8},{1,17},{9,25},{17,1},{25,9},{2,18},{10... | collective-permute-start | bytes 737288 | tf_op jit(solution)/shard_map/ppermute | solution.py:27
  131.8 11.5 %collective-permute-start.29 = (bf16[1,2,40,1536]{3,2,1,0:T(8,128)(2,1)S(1)}, bf16[1,2,40,1536]{3,2,1,0:T(8,128)(2,1)S(1)}, u32[]{:S(2)}, u32[]{:S(2)}) collective-permute-start(bf16[1,2,40,1536]{3,2,1,0:T(8,128)(2,1)S(1)} %get-tuple-element.83), channel_id=1, source_target_pairs={{0,8},{8,0},{16,24},{24,16},{1,9},{9,1},{17,25},{25,17},{2,10},{10... | collective-permute-start | bytes 737288 | tf_op jit(solution)/shard_map/ppermute | solution.py:27
  132.4 10.9 %collective-permute-start.30 = (bf16[2,40,1536]{2,1,0:T(8,128)(2,1)S(1)}, bf16[2,40,1536]{2,1,0:T(8,128)(2,1)S(1)}, u32[]{:S(2)}, u32[]{:S(2)}) collective-permute-start(bf16[2,40,1536]{2,1,0:T(8,128)(2,1)S(1)} %reply.4), channel_id=1, source_target_pairs={{0,6},{1,7},{2,4},{3,5},{4,2},{5,3},{6,0},{7,1},{8,14},{9,15},{10,... | collective-permute-start | bytes 737288 | tf_op jit(solution)/shard_map/ppermute | solution.py:27
  134.9 15.9 %collective-permute-start.31 = (bf16[2,40,1536]{2,1,0:T(8,128)(2,1)S(1)}, bf16[2,40,1536]{2,1,0:T(8,128)(2,1)S(1)}, u32[]{:S(2)}, u32[]{:S(2)}) collective-permute-start(bf16[2,40,1536]{2,1,0:T(8,128)(2,1)S(1)} %reply.5), channel_id=1, source_target_pairs={{0,4},{1,5},{2,6},{3,7},{4,0},{5,1},{6,2},{7,3},{8,12},{9,13},{10,... | collective-permute-start | bytes 737288 | tf_op jit(solution)/shard_map/ppermute | solution.py:27
  140.8 10.0 %collective-permute-start.28 = (bf16[1,2,40,1536]{3,2,1,0:T(8,128)(2,1)S(1)}, bf16[1,2,40,1536]{3,2,1,0:T(8,128)(2,1)S(1)}, u32[]{:S(2)}, u32[]{:S(2)}) collective-permute-start(bf16[1,2,40,1536]{3,2,1,0:T(8,128)(2,1)S(1)} %get-tuple-element.87), channel_id=1, source_target_pairs={{0,16},{8,24},{16,0},{24,8},{1,17},{9,25},{17,1},{25,9},{2,18},{10... | collective-permute-start | bytes 737288 | tf_op jit(solution)/shard_map/ppermute | solution.py:27
  143.4 10.4 %collective-permute-start.32 = (bf16[2,40,1536]{2,1,0:T(8,128)(2,1)S(1)}, bf16[2,40,1536]{2,1,0:T(8,128)(2,1)S(1)}, u32[]{:S(2)}, u32[]{:S(2)}) collective-permute-start(bf16[2,40,1536]{2,1,0:T(8,128)(2,1)S(1)} %reply.6), channel_id=1, source_target_pairs={{0,2},{1,3},{2,0},{3,1},{4,6},{5,7},{6,4},{7,5},{8,10},{9,11},{10,... | collective-permute-start | bytes 737288 | tf_op jit(solution)/shard_map/ppermute | solution.py:27
  154.4 1.8 %collective-permute-start.33 = (bf16[256,768]{1,0:T(8,128)(2,1)S(1)}, bf16[256,768]{1,0:T(8,128)(2,1)S(1)}, u32[]{:S(2)}, u32[]{:S(2)}) collective-permute-start(bf16[256,768]{1,0:T(8,128)(2,1)S(1)} %get-tuple-element.92), channel_id=1, source_target_pairs={{0,1},{1,0},{2,3},{3,2},{4,5},{5,4},{6,7},{7,6},{8,9},{9,8},{10,11... | collective-permute-start | bytes 1179656 | tf_op jit(solution)/shard_map/ppermute | solution.py:27

commit v5 on v4

--- a/solution.py
+++ b/solution.py
@@ -45,6 +45,65 @@
     length = log_decay.shape[1]
     triu = (iota((length, length), 0) <= iota((length, length), 1)).astype(F32)
     return dot(log_decay, triu, precision=lax.Precision.HIGHEST)
+
+
+def piece_copies(weights, kind, expert, chunk, owner, buffer, sems):
+    copies = []
+    for side in range(2):
+        rows, cols = buffer.shape[1:]
+        tiles = sems.shape[1]
+        depth = rows // tiles
+        first = (owner ^ (2 * chunk + side)) * (rows if kind == "up" else cols)
+        for t in range(tiles):
+            if kind == "up":
+                source = weights.at[expert, pl.ds(pl.multiple_of(first + t * depth, depth), depth), :]
+            else:
+                source = weights.at[
+                    expert, t * depth : (t + 1) * depth, pl.ds(pl.multiple_of(first, cols), cols)
+                ]
+            copies.append(
+                pltpu.make_async_copy(
+                    source, buffer.at[side, t * depth : (t + 1) * depth], sems.at[side, t]
+                )
+            )
+    return copies
+
+
+def piece_shape(kind, weights, chunks):
+    rows, cols = weights.shape[1:]
+    return (2, rows // (2 * chunks), cols) if kind == "up" else (2, rows, cols // (2 * chunks))
+
+
+def with_held(kernel, pieces, place, up, down, *refs):
+    sems, refs = refs[-1], refs[:-1]
+    outs = refs[len(refs) - len(pieces) :] if pieces else ()
+    copies = []
+    for i, (kind, chunk) in enumerate(pieces):
+        source = up if kind == "up" else down
+        copies += piece_copies(source, kind, 0, chunk, place[1], outs[i], sems.at[i])
+    for copy in copies:
+        copy.start()
+    if kernel is not None:
+        kernel(place, *refs[: len(refs) - len(pieces)])
+    for copy in copies:
+        copy.wait()
+
+
+def call_with_held(kernel, pieces, chunks, place, up, down, args, out_shape, name):
+    shapes = [
+        jax.ShapeDtypeStruct(piece_shape(kind, up if kind == "up" else down, chunks), BF16)
+        for kind, _ in pieces
+    ]
+    outs = pl.pallas_call(
+        functools.partial(with_held, kernel, pieces),
+        in_specs=[SMEM, ANY, ANY] + [VMEM] * len(args),
+        out_specs=[VMEM] * (len(out_shape) + len(shapes)),
+        out_shape=list(out_shape) + shapes,
+        scratch_shapes=[pltpu.SemaphoreType.DMA((len(pieces), 2, 2))],
+        compiler_params=params(24),
+        name=name,
+    )(place, up, down, *args)
+    return outs[: len(out_shape)], dict(zip(pieces, outs[len(out_shape) :]))
 
 
 def state_kernel(keys, values, log_decay, *refs):
@@ -125,7 +184,7 @@
     other[...] = jnp.broadcast_to(mine.astype(jnp.int32) - me, other.shape)
 
 
-def output_kernel(queries, inside, log_decay, gain, *refs):
+def output_kernel(place, queries, inside, log_decay, gain, *refs):
     incoming, normed = refs[:-1], refs[-1]
     requests, length, features = queries.shape
     heads = log_decay.shape[0] // requests
@@ -177,111 +236,138 @@
         weight[j] = jnp.broadcast_to(1.0 / (1.0 + jnp.exp(theirs - mine)), (cap, 128))
 
 
-def tiles_of(rows):
-    return 2 if rows % 512 == 0 else 1
-
-
-def up_kernel(place, weights, *refs, chunk, parts, first, last):
-    blocks, (out, buffer, sems) = refs[:parts], refs[-3:]
-    own, _, half, _ = buffer.shape
-    tiles = sems.shape[2]
-    depth = half // tiles
-    owner = place[1]
+def project_kernel(place, up, down, *refs, chunks, parts, first, last, held, route):
+    refs = list(refs)
+    blocks = {k: [refs.pop(0) for _ in range(parts)] for k in chunks}
+    ready = {piece: refs.pop(0) for piece in held}
+    before = None if first else refs.pop(0)
+    sems, buffers = refs.pop(), {}
+    pieces = [("up", j, k) for j in range(up.shape[0]) for k in chunks]
+    if last:
+        pieces += [("down", j, chunks[-1]) for j in range(up.shape[0])]
+    pieces = [(kind, j, k) for kind, j, k in pieces if j or (kind, k) not in ready]
+    for piece in reversed(pieces):
+        buffers[piece] = refs.pop()
+    out, outs = refs[0], refs[1:]
+    copies = {}
+    for i, (kind, j, k) in enumerate(pieces):
+        copies[kind, j, k] = piece_copies(
+            up if kind == "up" else down, kind, j, k, place[1], buffers[kind, j, k], sems.at[i]
+        )
+        for copy in copies[kind, j, k]:
+            copy.start()
+
+    def weights_of(kind, j, k, side):
+        if (kind, j, k) not in buffers:
+            return ready[kind, k][side]
+        mine = copies[kind, j, k]
+        for copy in mine[side * len(mine) // 2 : (side + 1) * len(mine) // 2]:
+            copy.wait()
+        return buffers[kind, j, k][side]
+
+    for j in range(up.shape[0]):
+        total = None if first else before[j]
+        for k in chunks:
+            half = blocks[k][0].shape[2] // 2
+            for side in range(2):
+                lanes = slice(side * half, (side + 1) * half)
+                x = jnp.concatenate([b[j, :, lanes].astype(F32) for b in blocks[k]], axis=0)
+                part = dot(x.astype(BF16), weights_of("up", j, k, side))
+                total = part if total is None else total + part
+        out[j] = (total / (1.0 + jnp.exp(-total))).astype(BF16) if last else total
+    if last:
+        for j in range(up.shape[0]):
+            for side in range(2):
+                lanes = slice(side * half, (side + 1) * half)
+                result = dot(out[j], weights_of("down", j, chunks[-1], side))
+                for ref, members in zip(outs, route):
+                    for i, member in enumerate(members):
+                        ref[i, j, :, lanes] = result[member * CAP : (member + 1) * CAP].astype(BF16)
+
+
+def project(place, chunks, count, gathered, up, down, held, total, route):
+    own, _, hidden = up.shape
+    cap, width = gathered[chunks[0]][0].shape[1:]
+    parts = len(gathered[chunks[0]])
+    rows = parts * cap
+    first, last = total is None, route is not None
+    wanted = [("up", k) for k in chunks] + ([("down", chunks[-1])] if last else [])
+    ready = [piece for piece in wanted if piece in held]
+    loose = [(kind, k) for kind, k in wanted for j in range(own) if j or (kind, k) not in held]
+    scratch = [
+        pltpu.VMEM(piece_shape(kind, up if kind == "up" else down, count), BF16)
+        for kind in ("up", "down")
+        for other, _ in loose
+        if other == kind
+    ]
+    struct = jax.ShapeDtypeStruct
+    out_shape = [struct((own, rows, hidden), BF16 if last else F32)]
+    if last:
+        out_shape += [struct((parts // 2, own, cap, width), BF16)] * 2
+    work = (len(chunks) + last) * own * width * hidden
+    blocks = [block for k in chunks for block in gathered[k]]
+    return pl.pallas_call(
+        functools.partial(
+            project_kernel,
+            chunks=chunks,
+            parts=parts,
+            first=first,
+            last=last,
+            held=ready,
+            route=route,
+        ),
+        in_specs=[SMEM, ANY, ANY] + [VMEM] * (len(blocks) + len(ready) + (not first)),
+        out_specs=[VMEM] * len(out_shape),
+        out_shape=out_shape,
+        scratch_shapes=scratch + [pltpu.SemaphoreType.DMA((max(len(scratch), 1), 2, 2))],
+        compiler_params=params(24),
+        cost_estimate=pl.CostEstimate(
+            flops=2 * rows * work, bytes_accessed=2 * work, transcendentals=0
+        ),
+        name=f"project_{chunks[0]}",
+    )(
+        place,
+        up,
+        down,
+        *blocks,
+        *[held[piece] for piece in ready],
+        *([] if first else [total]),
+    )
+
+
+def down_kernel(place, weights, hidden, *refs, chunk, route):
+    outs, (buffer, sems) = refs[:-2], refs[-2:]
+    own = hidden.shape[0]
+    half = buffer.shape[3]
     copies = []
     for j in range(own):
-        for side in range(2):
-            row = pl.multiple_of((owner ^ (2 * chunk + side)) * half, half)
-            tile_copies = []
-            for t in range(tiles):
-                copy = pltpu.make_async_copy(
-                    weights.at[j, pl.ds(row + t * depth, depth), :],
-                    buffer.at[j, side, t * depth : (t + 1) * depth],
-                    sems.at[j, side, t],
-                )
-                copy.start()
-                tile_copies.append(copy)
-            copies.append(tile_copies)
-    for j in range(own):
-        total = None if first else refs[parts][j]
-        for side in range(2):
-            lanes = slice(side * half, (side + 1) * half)
-            x = jnp.concatenate([b[j, :, lanes].astype(F32) for b in blocks], axis=0).astype(BF16)
-            for copy in copies[2 * j + side]:
-                copy.wait()
-            part = dot(x, buffer[j, side])
-            total = part if total is None else total + part
-        out[j] = (total / (1.0 + jnp.exp(-total))).astype(BF16) if last else total
-
-
-def up_chunk(place, chunk, blocks, weights, total, last):
-    own, _, hidden = weights.shape
-    cap, width = blocks[0].shape[1:]
-    parts = len(blocks)
-    rows = parts * cap
-    tiles = tiles_of(width // 2)
-    first = total is None
-    return pl.pallas_call(
-        functools.partial(up_kernel, chunk=chunk, parts=parts, first=first, last=last),
-        in_specs=[SMEM, ANY] + [VMEM] * (parts + (not first)),
-        out_specs=VMEM,
-        out_shape=jax.ShapeDtypeStruct((own, rows, hidden), BF16 if last else F32),
-        scratch_shapes=[
-            pltpu.VMEM((own, 2, width // 2, hidden), BF16),
-            pltpu.SemaphoreType.DMA((own, 2, tiles)),
-        ],
-        compiler_params=params(32),
-        cost_estimate=pl.CostEstimate(
-            flops=2 * own * rows * width * hidden,
-            bytes_accessed=2 * own * width * hidden,
-            transcendentals=0,
-        ),
-        name=f"up_{chunk}",
-    )(place, weights, *blocks, *([] if first else [total]))
-
-
-def down_kernel(place, weights, hidden, *refs, chunk, route):
-    outs, (buffer, sems) = refs[:-2], refs[-2:]
-    own, steps, depth, half = buffer.shape
-    owner = place[1]
-    copies = []
-    for j in range(own):
-        for t in range(steps):
-            col = pl.multiple_of((owner ^ (2 * chunk + t // (steps // 2))) * half, half)
-            row = (t % (steps // 2)) * depth
-            copy = pltpu.make_async_copy(
-                weights.at[j, row : row + depth, pl.ds(col, half)], buffer.at[j, t], sems.at[j, t]
-            )
+        mine = piece_copies(weights, "down", j, chunk, place[1], buffer.at[j], sems.at[j])
+        for copy in mine:
             copy.start()
-            copies.append(copy)
+        copies.append(mine)
     for j in range(own):
         for side in range(2):
-            total = None
-            for t in range(steps // 2):
-                copies[j * steps + side * (steps // 2) + t].wait()
-                part = dot(
-                    hidden[j, :, t * depth : (t + 1) * depth], buffer[j, side * (steps // 2) + t]
-                )
-                total = part if total is None else total + part
+            for copy in copies[j][2 * side : 2 * side + 2]:
+                copy.wait()
+            result = dot(hidden[j], buffer[j, side])
             lanes = slice(side * half, (side + 1) * half)
             for out, members in zip(outs, route):
                 for i, member in enumerate(members):
-                    out[i, j, :, lanes] = total[member * CAP : (member + 1) * CAP].astype(BF16)
-
-
-def down_chunk(place, chunk, hidden, weights, width, route):
+                    out[i, j, :, lanes] = result[member * CAP : (member + 1) * CAP].astype(BF16)
+
+
+def down_chunk(place, chunk, count, hidden, weights, route):
     own, rows, depth = hidden.shape
     parts = rows // CAP
-    tiles = tiles_of(depth)
+    shape = piece_shape("down", weights, count)
+    width = 2 * shape[2]
     return pl.pallas_call(
         functools.partial(down_kernel, chunk=chunk, route=route),
         in_specs=[SMEM, ANY, VMEM],
         out_specs=[VMEM] * 2,
         out_shape=[jax.ShapeDtypeStruct((parts // 2, own, CAP, width), BF16)] * 2,
-        scratch_shapes=[
-            pltpu.VMEM((own, 2 * tiles, depth // tiles, width // 2), BF16),
-            pltpu.SemaphoreType.DMA((own, 2 * tiles)),
-        ],
-        compiler_params=params(32),
+        scratch_shapes=[pltpu.VMEM((own, *shape), BF16), pltpu.SemaphoreType.DMA((own, 2, 2))],
+        compiler_params=params(24),
         cost_estimate=pl.CostEstimate(
             flops=2 * own * rows * width * depth,
             bytes_accessed=2 * own * width * depth,
@@ -328,7 +414,7 @@
         in_specs=[VMEM] * 2,
         out_specs=[VMEM] * 2,
         out_shape=[jax.ShapeDtypeStruct(shape, F32), jax.ShapeDtypeStruct(shape, BF16)],
-        compiler_params=params(32),
+        compiler_params=params(24),
         name="partial_sums",
     )(kept, got)
 
@@ -344,7 +430,7 @@
         in_specs=[VMEM] * 3,
         out_specs=VMEM,
         out_shape=jax.ShapeDtypeStruct(kept.shape[1:], BF16),
-        compiler_params=params(32),
+        compiler_params=params(24),
         name="reply",
     )(kept, got, weight)
 
@@ -374,12 +460,12 @@
     return incoming
 
 
-def prefix_of_four(states, decay, me):
+def prefix_of_four(states, decay, me, token):
     high, low = (me & 2) != 0, (me & 1) != 0
     near = swap(decay, "ctx", 4, 1)
     far = swap(decay, "ctx", 4, 3)
     one, two = states
-    got_one = swap(one, "ctx", 4, 1, lambda i: i != 3).astype(F32)
+    got_one = after(swap(one, "ctx", 4, 1, lambda i: i != 3), *token).astype(F32)
     got_two = swap(two, "ctx", 4, 2, lambda i: i < 2).astype(F32)
     sent_one = jnp.where(low, 1.0, near[0]) * one.astype(F32) + jnp.where(low, decay[0], 1.0) * got_one
     sent_two = (
@@ -408,6 +494,9 @@
     me = lax.axis_index("ctx")
     place = jnp.stack([me, lax.axis_index("exp")]).astype(jnp.int32)
     struct = jax.ShapeDtypeStruct
+    early_pieces = [("up", k) for k in range(min(2, chunks - 2))]
+    later_pieces = [("up", k) for k in range(max(chunks - 2, 0), chunks)]
+    last_pieces = [("down", chunks - 1)]
     decay_rows = jnp.transpose(log_decay, (2, 0, 1)).reshape(heads * requests, length)
 
     states = pl.pallas_call(
@@ -424,39 +513,49 @@
         name="local_state",
     )(keys, values, decay_rows)
     decay = jnp.exp(jnp.sum(after(log_decay, *states), axis=1)).reshape(halves, pairs, 1, 1)
+    _, held = call_with_held(
+        None, early_pieces, chunks, after(place, *states), expert_up, expert_down, [], [], "early_weights"
+    )
     if n_ctx == 4 and halves == 2:
-        incoming = prefix_of_four(states, decay, me)
+        incoming = prefix_of_four(states, decay, me, list(held.values()))
     else:
         incoming = prefix_by_doubling(states, decay, me, n_ctx)
 
-    inside, placement, other = pl.pallas_call(
+    (inside, placement, other), more = call_with_held(
         inside_kernel,
-        in_specs=[SMEM] + [VMEM] * 5,
-        out_specs=[VMEM] * 3,
-        out_shape=[
+        later_pieces,
+        chunks,
+        place,
+        expert_up,
+        expert_down,
+        [queries, keys, values, decay_rows, jnp.transpose(expert_ids, (1, 2, 0))],
+        [
             struct((requests, length, features), F32),
             struct((chunks * own * CAP, tokens), BF16),
             struct((own * CAP, 128), jnp.int32),
         ],
-        compiler_params=params(32),
-        name="inside_and_placement",
-    )(place, queries, keys, values, decay_rows, jnp.transpose(expert_ids, (1, 2, 0)))
-
-    normed = pl.pallas_call(
+        "inside_and_placement",
+    )
+    held = {**held, **more}
+    (normed,), more = call_with_held(
         output_kernel,
-        in_specs=[VMEM] * (4 + halves),
-        out_specs=VMEM,
-        out_shape=struct((tokens, features), BF16),
-        compiler_params=params(32),
-        name="normed",
-    )(queries, inside, decay_rows, norm_gain.reshape(1, features), *incoming)
+        last_pieces,
+        chunks,
+        place,
+        expert_up,
+        expert_down,
+        [queries, inside, decay_rows, norm_gain.reshape(1, features), *incoming],
+        [struct((tokens, features), BF16)],
+        "normed",
+    )
+    held = {**held, **more}
 
     outgoing = pl.pallas_call(
         dispatch_kernel,
         in_specs=[VMEM] * 3,
         out_specs=[VMEM] * chunks,
         out_shape=[struct((own, CAP, width), BF16)] * chunks,
-        compiler_params=params(32),
+        compiler_params=params(24),
         name="dispatch",
     )(placement, normed, swap(normed, "exp", n_exp, 1))
     arrived = [outgoing[0]] + [swap(outgoing[k], "exp", n_exp, 2 * k) for k in range(1, chunks)]
@@ -465,49 +564,61 @@
         in_specs=[SMEM] + [VMEM] * (2 + chunks),
         out_specs=VMEM,
         out_shape=struct((own, CAP, 128), F32),
-        compiler_params=params(32),
+        compiler_params=params(24),
         name="gate",
     )(place, other, router.T, *arrived)
 
     bits = bits_of(n_ctx)
     orders = [bits if k % 2 == 0 else bits[::-1] for k in range(chunks)]
 
-    totals = [None] * chunks
+    routes = [route_of(order, n_ctx) for order in orders]
     gathered = [None] * chunks
-
-    def project(k):
-        total = totals[k - 1] if k else None
-        if k == chunks - 2:
-            total = after(total, weight)
-        totals[k] = up_chunk(place, k, gathered[k], expert_up, total, k == chunks - 1)
-        return totals[k]
+    total, done = None, 0
+
+    def advance(upto):
+        nonlocal total, done
+        for k in range(done, upto + 1):
+            (total,) = project(
+                place, [k], chunks, gathered, expert_up, expert_down, held, total, None
+            )
+        done = max(done, upto + 1)
+        return total
 
     for k in range(chunks):
         have = {0: arrived[k]}
         for bit in orders[k]:
-            token = project(k - 3) if k >= 3 and bit == orders[k][0] else None
+            token = advance(k - 3) if k >= 3 and bit == orders[k][0] else None
             if k == chunks - 1 and k >= 2 and bit == orders[k][-1] and len(bits) > 1:
-                token = project(k - 2)
+                token = advance(k - 2)
             found = {}
             for rel, block in have.items():
-                if token is not None:
+                if token is not None and (rel or bit == orders[k][0]):
                     block = after(block, token)
                 found[rel | bit] = swap(block, "ctx", n_ctx, bit)
             have.update(found)
         gathered[k] = [have[rel] for rel in range(n_ctx)]
-    for k in range(chunks):
-        if totals[k] is None:
-            project(k)
-    hidden = totals[-1]
+    hidden, *far = project(
+        after(place, weight),
+        list(range(done, chunks)),
+        chunks,
+        gathered,
+        expert_up,
+        expert_down,
+        held,
+        total,
+        routes[-1],
+    )
 
     order = list(reversed(range(chunks)))
     open_sums, returned, token = {}, [None] * chunks, hidden
     for i in range(chunks + 3):
         if i < chunks:
             k = order[i]
-            sent, kept = down_chunk(
-                place, k, after(hidden, token), expert_down, width, route_of(orders[k], n_ctx)
-            )
+            sent, kept = far
+            if i:
+                sent, kept = down_chunk(
+                    place, k, chunks, after(hidden, token), expert_down, routes[k]
+                )
             open_sums[k] = kept, swap(sent, "ctx", n_ctx, orders[k][0])
             token = sent
         if 2 <= i < chunks + 2:
@@ -529,7 +640,7 @@
         in_specs=[VMEM] * (2 + chunks),
         out_specs=[VMEM] * 2,
         out_shape=[struct((tokens, features), F32), struct((tokens, features), BF16)],
-        compiler_params=params(32),
+        compiler_params=params(24),
         name="combine",
     )(normed, placement, *returned)
     out = mine + swap(theirs, "exp", n_exp, 1).astype(F32)

time: 157 us -> 152 us (0.968)
  starting transfers between devices: 59 us -> 54.6 us
  waiting for transfers between devices: 35.7 us -> 31.6 us
  local copies, waits for them, and re-layouts: 1.26 us -> 4.95 us
  other arithmetic: 6.3 us -> 3.32 us
  Pallas kernels: 54.4 us -> 56.3 us
    pallas_call x6, Pallas kernels: 26.4 us -> 34.3 us  [the longest x3 17.5 us: project(): pl.pallas_call(functools.partial(project_kernel, chunks=chunks, parts=par...]
    pallas_call x4 -> x3, Pallas kernels: 21.2 us -> 15.3 us  [down_chunk(): pl.pallas_call(functools.partial(down_kernel, chunk=chunk, route=route),...]
    ppermute x34, starting transfers between devices: 59 us -> 54.6 us  [swap(): return lax.ppermute(x, axis, [(i, i ^ k) for i in range(n) if keep(i)])]
    unnamed x14 -> x30, local copies, waits for them, and re-layouts: 0.03 us -> 4.41 us
    ppermute x34, waiting for transfers between devices: 35.7 us -> 31.6 us  [swap(): return lax.ppermute(x, axis, [(i, i ^ k) for i in range(n) if keep(i)])]
  transfers between devices with their start and end apart: 34 -> 34, of which waited for: 15 -> 14; matrix products, arithmetic and copies ran while one was open for 4% -> 1% of each run, Pallas kernels for 24% -> 25%
where the time goes in v5:
time: 152 us; the launch traced here: 151 us
  Pallas kernels  56.3 us (37%)
  starting transfers between devices  54.6 us (36%)
  waiting for transfers between devices  31.6 us (21%)
  local copies, waits for them, and re-layouts  4.95 us (3%)
  other arithmetic  3.32 us (2%)
    ppermute x34, starting transfers between devices, swap(): return lax.ppermute(x, axis, [(i, i ^ k) for i in range(n) if keep(i)])  54.6 us
    ppermute x34, waiting for transfers between devices, swap(): return lax.ppermute(x, axis, [(i, i ^ k) for i in range(n) if keep(i)])  31.6 us
    pallas_call x3, Pallas kernels, project(): pl.pallas_call(functools.partial(project_kernel, chunks=chunks, parts=par...  17.5 us
    pallas_call x3, Pallas kernels, call_with_held(): pl.pallas_call(functools.partial(with_held, kernel, pieces), in_specs=[SM...  16.8 us
    pallas_call x3, Pallas kernels, down_chunk(): pl.pallas_call(functools.partial(down_kernel, chunk=chunk, route=route),...  15.3 us
    unnamed x30, local copies, waits for them, and re-layouts  4.41 us
    pallas_call x1, Pallas kernels, body(): pl.pallas_call(state_kernel, in_specs=[ANY] * 2 + [VMEM], out_specs=[VMEM...  3.84 us
  transfers between devices with their start and end apart: 34, of which 14 were waited for; matrix products, arithmetic and copies ran while one was open for 1% of the time, Pallas kernels for 25%

profile of v5, /device:TPU:0, one launch (start us, length us, event | category | flops | bytes accessed | tf_op | source)
XLA Modules:
  0.0 151.2 jit_solution(3135187122733543626)
XLA Ops:
  0.0 3.8 %local_state.1 = (bf16[12,128,128]{2,1,0:T(8,128)(2,1)}, bf16[12,128,128]{2,1,0:T(8,128)(2,1)}) custom-call(bf16[4,64,768]{2,1,0:T(8,128)(2,1)} %keys.1, bf16[4,64,768]{2,1,0:T(8,128)(2,1)} %values.1, f32[24,64]{1,0:T(8,128)} %bitcast.23), custom_call_target="tpu_custom_call" | custom-call | tf_op jit(solution)/shard_map/local_state/pallas_call | solution.py:502
  3.8 4.8 %collective-permute-start = (bf16[12,128,128]{2,1,0:T(8,128)(2,1)}, bf16[12,128,128]{2,1,0:T(8,128)(2,1)S(1)}, u32[]{:S(2)}, u32[]{:S(2)}) collective-permute-start(bf16[12,128,128]{2,1,0:T(8,128)(2,1)} %get-tuple-element.57), channel_id=1, source_target_pairs={{0,8},{8,0},{16,24},{1,9},{9,1},{17,25},{2,10},{10,2},{18,26},{3,1... | collective-permute-start | bytes 1179656 | tf_op jit(solution)/shard_map/ppermute | solution.py:27
  9.7 3.0 %collective-permute-start.3 = (f32[2,12,1,1]{1,0,3,2:T(2,128)S(1)}, f32[2,12,1,1]{1,0,3,2:T(2,128)S(1)}, u32[]{:S(2)}, u32[]{:S(2)}) collective-permute-start(f32[2,12,1,1]{1,0,3,2:T(2,128)S(1)} %exp.14), channel_id=1, source_target_pairs={{0,24},{8,16},{16,8},{24,0},{1,25},{9,17},{17,9},{25,1},{2,26},{10... | collective-permute-start | bytes 296 | tf_op jit(solution)/shard_map/ppermute | solution.py:27
  12.7 2.4 %collective-permute-start.4 = (bf16[12,128,128]{2,1,0:T(8,128)(2,1)}, bf16[12,128,128]{2,1,0:T(8,128)(2,1)S(1)}, u32[]{:S(2)}, u32[]{:S(2)}) collective-permute-start(bf16[12,128,128]{2,1,0:T(8,128)(2,1)} %get-tuple-element.58), channel_id=1, source_target_pairs={{0,16},{8,24},{1,17},{9,25},{2,18},{10,26},{3,19},{11,27},{4,20},{... | collective-permute-start | bytes 1179656 | tf_op jit(solution)/shard_map/ppermute | solution.py:27
  15.7 4.4 %early_weights.1 = (bf16[2,768,1536]{2,1,0:T(8,128)(2,1)S(1)}, bf16[2,768,1536]{2,1,0:T(8,128)(2,1)S(1)}) custom-call(s32[2]{0:T(128)S(1)} %pad_add_fusion.place, bf16[2,6144,1536]{2,1,0:T(8,128)(2,1)} %up.11, bf16[2,1536,6144]{2,1,0:T(8,128)(2,1)} %weights.5), custom_call_target="tpu_custom_call" | custom-call | tf_op jit(solution)/shard_map/early_weights/pallas_call | solution.py:97
  20.0 2.2 %copy-done = bf16[2,768,1536]{2,1,0:T(8,128)(2,1)} copy-done((bf16[2,768,1536]{2,1,0:T(8,128)(2,1)}, bf16[2,768,1536]{2,1,0:T(8,128)(2,1)S(1)}, u32[]{:S(2)}) %copy-start) | copy-done | bytes 4718616
  22.2 2.2 %copy-done.1 = bf16[2,768,1536]{2,1,0:T(8,128)(2,1)} copy-done((bf16[2,768,1536]{2,1,0:T(8,128)(2,1)}, bf16[2,768,1536]{2,1,0:T(8,128)(2,1)S(1)}, u32[]{:S(2)}) %copy-start.1) | copy-done | bytes 4718616
  24.4 0.9 fusion.7
  25.4 2.0 %collective-permute-start.5 = (bf16[12,128,128]{2,1,0:T(8,128)(2,1)}, bf16[12,128,128]{2,1,0:T(8,128)(2,1)S(1)}, u32[]{:S(2)}, u32[]{:S(2)}) collective-permute-start(bf16[12,128,128]{2,1,0:T(8,128)(2,1)} %fusion.7), channel_id=1, source_target_pairs={{0,8},{16,24},{24,16},{1,9},{17,25},{25,17},{2,10},{18,26},{26,18}... | collective-permute-start | bytes 1179656 | tf_op jit(solution)/shard_map/ppermute | solution.py:27
  27.6 3.0 %collective-permute-start.2 = (bf16[12,128,128]{2,1,0:T(8,128)(2,1)S(1)}, bf16[12,128,128]{2,1,0:T(8,128)(2,1)S(1)}, u32[]{:S(2)}, u32[]{:S(2)}) collective-permute-start(bf16[12,128,128]{2,1,0:T(8,128)(2,1)S(1)} %fusion.3), channel_id=1, source_target_pairs={{0,16},{8,24},{1,17},{9,25},{2,18},{10,26},{3,19},{11,27},{4,20},{... | collective-permute-start | bytes 1179656 | tf_op jit(solution)/shard_map/ppermute | solution.py:27
  30.8 7.5 %inside_and_placement.1 = (f32[4,64,768]{2,1,0:T(8,128)S(1)}, bf16[320,256]{1,0:T(8,128)(2,1)S(1)}, s32[80,128]{1,0:T(8,128)S(1)}, bf16[2,768,1536]{2,1,0:T(8,128)(2,1)S(1)}, bf16[2,768,1536]{2,1,0:T(8,128)(2,1)S(1)}) custom-call(s32[2]{0:T(128)S(1)} %pad_add_fusion.place, bf16[2,6144,1536]{2,1,0:T(8,128)(2,1)} %up.11, bf16[2,1536,6144]{2,1,0:T(8,128)(2,1)} %weights.5, ...), custom_call_target="tpu_custom_call" | custom-call | tf_op jit(solution)/shard_map/inside_and_placement/pallas_call | solution.py:97
  38.7 4.9 %normed.1 = (bf16[256,768]{1,0:T(8,128)(2,1)S(1)}, bf16[2,1536,768]{2,1,0:T(8,128)(2,1)S(1)}) custom-call(s32[2]{0:T(128)S(1)} %pad_add_fusion.place, bf16[2,6144,1536]{2,1,0:T(8,128)(2,1)} %up.11, bf16[2,1536,6144]{2,1,0:T(8,128)(2,1)} %weights.5, bf16[4,64,768]{2,1,0:T(8,128)(2,1)S(1)} %copy-done.2, f32[4,64,768]{2,1,0:T(8,128)S(1)} %get-tuple-element.56.refs_1_, ...), custom_call_target="tpu_custom_call" | custom-call | tf_op jit(solution)/shard_map/normed/pallas_call | solution.py:97
  43.7 1.7 %collective-permute-done.6.refs_1_ = bf16[256,768]{1,0:T(8,128)(2,1)S(1)} collective-permute-done((bf16[256,768]{1,0:T(8,128)(2,1)S(1)}, bf16[256,768]{1,0:T(8,128)(2,1)S(1)}, u32[]{:S(2)}, u32[]{:S(2)}) %collective-permute-start.6) | collective-permute-done | bytes 393248 | tf_op jit(solution)/shard_map/ppermute | solution.py:27
  45.9 1.8 %collective-permute-start.7 = (bf16[2,40,1536]{2,1,0:T(8,128)(2,1)S(1)}, bf16[2,40,1536]{2,1,0:T(8,128)(2,1)S(1)}, u32[]{:S(2)}, u32[]{:S(2)}) collective-permute-start(bf16[2,40,1536]{2,1,0:T(8,128)(2,1)S(1)} %get-tuple-element.68), channel_id=1, source_target_pairs={{0,2},{1,3},{2,0},{3,1},{4,6},{5,7},{6,4},{7,5},{8,10},{9,11},{10,... | collective-permute-start | bytes 737288 | tf_op jit(solution)/shard_map/ppermute | solution.py:27
  47.7 1.5 collective-permute-start.14
  50.1 2.6 %collective-permute-start.8 = (bf16[2,40,1536]{2,1,0:T(8,128)(2,1)S(1)}, bf16[2,40,1536]{2,1,0:T(8,128)(2,1)S(1)}, u32[]{:S(2)}, u32[]{:S(2)}) collective-permute-start(bf16[2,40,1536]{2,1,0:T(8,128)(2,1)S(1)} %get-tuple-element.69), channel_id=1, source_target_pairs={{0,4},{1,5},{2,6},{3,7},{4,0},{5,1},{6,2},{7,3},{8,12},{9,13},{10,... | collective-permute-start | bytes 737288 | tf_op jit(solution)/shard_map/ppermute | solution.py:27
  52.7 4.5 %collective-permute-done.7.refs_1_.refs_0_ = bf16[2,40,1536]{2,1,0:T(8,128)(2,1)S(1)} collective-permute-done((bf16[2,40,1536]{2,1,0:T(8,128)(2,1)S(1)}, bf16[2,40,1536]{2,1,0:T(8,128)(2,1)S(1)}, u32[]{:S(2)}, u32[]{:S(2)}) %collective-permute-start.7) | collective-permute-done | bytes 245792 | tf_op jit(solution)/shard_map/ppermute | solution.py:27
  57.2 1.0 collective-permute-start.19
  58.2 1.0 collective-permute-start.16
  59.3 2.6 %collective-permute-start.9 = (bf16[2,40,1536]{2,1,0:T(8,128)(2,1)S(1)}, bf16[2,40,1536]{2,1,0:T(8,128)(2,1)S(1)}, u32[]{:S(2)}, u32[]{:S(2)}) collective-permute-start(bf16[2,40,1536]{2,1,0:T(8,128)(2,1)S(1)} %get-tuple-element.70), channel_id=1, source_target_pairs={{0,6},{1,7},{2,4},{3,5},{4,2},{5,3},{6,0},{7,1},{8,14},{9,15},{10,... | collective-permute-start | bytes 737288 | tf_op jit(solution)/shard_map/ppermute | solution.py:27
  61.9 2.5 %collective-permute-start.18 = (bf16[2,40,1536]{2,1,0:T(8,128)(2,1)S(1)}, bf16[2,40,1536]{2,1,0:T(8,128)(2,1)S(1)}, u32[]{:S(2)}, u32[]{:S(2)}) collective-permute-start(bf16[2,40,1536]{2,1,0:T(8,128)(2,1)S(1)} %collective-permute-done.7.refs_1_.refs_0_), channel_id=1, source_target_pairs={{0,8},{8,0},{16,24},{24,16},{1,9},{9,1},{17,25},{25,17},{2,10},{10... | collective-permute-start | bytes 737288 | tf_op jit(solution)/shard_map/ppermute | solution.py:27
  64.4 6.1 %collective-permute-done.8.refs_2_.refs_0_ = bf16[2,40,1536]{2,1,0:T(8,128)(2,1)S(1)} collective-permute-done((bf16[2,40,1536]{2,1,0:T(8,128)(2,1)S(1)}, bf16[2,40,1536]{2,1,0:T(8,128)(2,1)S(1)}, u32[]{:S(2)}, u32[]{:S(2)}) %collective-permute-start.8) | collective-permute-done | bytes 245792 | tf_op jit(solution)/shard_map/ppermute | solution.py:27
  70.4 2.0 %collective-permute-start.20 = (bf16[2,40,1536]{2,1,0:T(8,128)(2,1)S(1)}, bf16[2,40,1536]{2,1,0:T(8,128)(2,1)S(1)}, u32[]{:S(2)}, u32[]{:S(2)}) collective-permute-start(bf16[2,40,1536]{2,1,0:T(8,128)(2,1)S(1)} %collective-permute-done.19.refs_2_), channel_id=1, source_target_pairs={{0,8},{8,0},{16,24},{24,16},{1,9},{9,1},{17,25},{25,17},{2,10},{10... | collective-permute-start | bytes 737288 | tf_op jit(solution)/shard_map/ppermute | solution.py:27
  72.5 4.6 %project_0.1.refs_5_ = f32[2,160,1536]{2,1,0:T(8,128)S(1)} custom-call(s32[2]{0:T(128)S(1)} %pad_add_fusion.place, bf16[2,6144,1536]{2,1,0:T(8,128)(2,1)} %up.11, bf16[2,1536,6144]{2,1,0:T(8,128)(2,1)} %weights.5, bf16[2,40,1536]{2,1,0:T(8,128)(2,1)S(1)} %get-tuple-element.67.refs_0_, bf16[2,40,1536]{2,1,0:T(8,128)(2,1)S(1)} %collective-permute-done.14.refs_1_, ...), custom_call_target="tpu_custom_call" | custom-call | flops 1509949440 | bytes 9437184 | tf_op jit(solution)/shard_map/project_0/pallas_call | solution.py:309
  77.1 1.2 collective-permute-start.17
  79.2 1.1 collective-permute-start.12
  81.2 4.2 %project_1.1.refs_11_ = f32[2,160,1536]{2,1,0:T(8,128)S(1)} custom-call(s32[2]{0:T(128)S(1)} %pad_add_fusion.place, bf16[2,6144,1536]{2,1,0:T(8,128)(2,1)} %up.11, bf16[2,1536,6144]{2,1,0:T(8,128)(2,1)} %weights.5, bf16[2,40,1536]{2,1,0:T(8,128)(2,1)S(1)} %collective-permute-done.7.refs_1_.refs_0_, bf16[2,40,1536]{2,1,0:T(8,128)(2,1)S(1)} %collective-permute-done.18.refs_1_, ...), custom_call_target="tpu_custom_call" | custom-call | flops 1509949440 | bytes 9437184 | tf_op jit(solution)/shard_map/project_1/pallas_call | solution.py:309
  85.4 1.8 %collective-permute-start.21 = (bf16[2,40,1536]{2,1,0:T(8,128)(2,1)S(1)}, bf16[2,40,1536]{2,1,0:T(8,128)(2,1)S(1)}, u32[]{:S(2)}, u32[]{:S(2)}) collective-permute-start(bf16[2,40,1536]{2,1,0:T(8,128)(2,1)S(1)} %collective-permute-done.17.refs_6_), channel_id=1, source_target_pairs={{0,8},{8,0},{16,24},{24,16},{1,9},{9,1},{17,25},{25,17},{2,10},{10... | collective-permute-start | bytes 737288 | tf_op jit(solution)/shard_map/ppermute | solution.py:27
  87.2 1.1 gate.1.weight
  88.3 1.4 collective-permute-done.12.refs_3_
  89.8 1.9 %collective-permute-done.21.refs_7_ = bf16[2,40,1536]{2,1,0:T(8,128)(2,1)S(1)} collective-permute-done((bf16[2,40,1536]{2,1,0:T(8,128)(2,1)S(1)}, bf16[2,40,1536]{2,1,0:T(8,128)(2,1)S(1)}, u32[]{:S(2)}, u32[]{:S(2)}) %collective-permute-start.21) | collective-permute-done | bytes 245792 | tf_op jit(solution)/shard_map/ppermute | solution.py:27
  91.7 8.7 %project_2.1 = (bf16[2,160,1536]{2,1,0:T(8,128)(2,1)S(1)}, bf16[2,2,40,1536]{3,2,1,0:T(8,128)(2,1)S(1)}, bf16[2,2,40,1536]{3,2,1,0:T(8,128)(2,1)S(1)}) custom-call(s32[2]{0:T(128)S(1)} %pad_add_fusion.place, bf16[2,6144,1536]{2,1,0:T(8,128)(2,1)} %up.11, bf16[2,1536,6144]{2,1,0:T(8,128)(2,1)} %weights.5, ...), custom_call_target="tpu_custom_call" | custom-call | flops 4529848320 | bytes 28311552 | tf_op jit(solution)/shard_map/project_2/pallas_call | solution.py:309
  100.3 1.1 collective-permute-start.22
  101.4 5.2 %down_2.1 = (bf16[2,2,40,1536]{3,2,1,0:T(8,128)(2,1)S(1)}, bf16[2,2,40,1536]{3,2,1,0:T(8,128)(2,1)S(1)}) custom-call(s32[2]{0:T(128)S(1)} %pad_add_fusion.place, bf16[2,1536,6144]{2,1,0:T(8,128)(2,1)} %weights.5, bf16[2,160,1536]{2,1,0:T(8,128)(2,1)S(1)} %get-tuple-element.86.hidden), custom_call_target="tpu_custom_call" | custom-call | flops 1509949440 | bytes 9437184 | tf_op jit(solution)/shard_map/down_2/pallas_call | solution.py:364
  106.6 1.9 %collective-permute-start.24 = (bf16[2,2,40,1536]{3,2,1,0:T(8,128)(2,1)S(1)}, bf16[2,2,40,1536]{3,2,1,0:T(8,128)(2,1)S(1)}, u32[]{:S(2)}, u32[]{:S(2)}) collective-permute-start(bf16[2,2,40,1536]{3,2,1,0:T(8,128)(2,1)S(1)} %get-tuple-element.81), channel_id=1, source_target_pairs={{0,8},{8,0},{16,24},{24,16},{1,9},{9,1},{17,25},{25,17},{2,10},{10... | collective-permute-start | bytes 1474568 | tf_op jit(solution)/shard_map/ppermute | solution.py:27
  108.5 5.0 %down_1.1 = (bf16[2,2,40,1536]{3,2,1,0:T(8,128)(2,1)S(1)}, bf16[2,2,40,1536]{3,2,1,0:T(8,128)(2,1)S(1)}) custom-call(s32[2]{0:T(128)S(1)} %pad_add_fusion.place, bf16[2,1536,6144]{2,1,0:T(8,128)(2,1)} %weights.5, bf16[2,160,1536]{2,1,0:T(8,128)(2,1)S(1)} %get-tuple-element.86.hidden), custom_call_target="tpu_custom_call" | custom-call | flops 1509949440 | bytes 9437184 | tf_op jit(solution)/shard_map/down_1/pallas_call | solution.py:364
  113.6 1.3 collective-permute-start.26
  115.1 5.0 %down_0.1 = (bf16[2,2,40,1536]{3,2,1,0:T(8,128)(2,1)S(1)}, bf16[2,2,40,1536]{3,2,1,0:T(8,128)(2,1)S(1)}) custom-call(s32[2]{0:T(128)S(1)} %pad_add_fusion.place, bf16[2,1536,6144]{2,1,0:T(8,128)(2,1)} %weights.5, bf16[2,160,1536]{2,1,0:T(8,128)(2,1)S(1)} %get-tuple-element.86.hidden), custom_call_target="tpu_custom_call" | custom-call | flops 1509949440 | bytes 9437184 | tf_op jit(solution)/shard_map/down_0/pallas_call | solution.py:364
  120.2 2.1 %collective-permute-start.23 = (bf16[2,2,40,1536]{3,2,1,0:T(8,128)(2,1)S(1)}, bf16[2,2,40,1536]{3,2,1,0:T(8,128)(2,1)S(1)}, u32[]{:S(2)}, u32[]{:S(2)}) collective-permute-start(bf16[2,2,40,1536]{3,2,1,0:T(8,128)(2,1)S(1)} %get-tuple-element.88), channel_id=1, source_target_pairs={{0,8},{8,0},{16,24},{24,16},{1,9},{9,1},{17,25},{25,17},{2,10},{10... | collective-permute-start | bytes 1474568 | tf_op jit(solution)/shard_map/ppermute | solution.py:27
  123.2 1.0 collective-permute-done.27.got
  124.3 1.0 collective-permute-done.26.got
  126.3 2.0 %collective-permute-start.30 = (bf16[2,40,1536]{2,1,0:T(8,128)(2,1)S(1)}, bf16[2,40,1536]{2,1,0:T(8,128)(2,1)S(1)}, u32[]{:S(2)}, u32[]{:S(2)}) collective-permute-start(bf16[2,40,1536]{2,1,0:T(8,128)(2,1)S(1)} %reply.4), channel_id=1, source_target_pairs={{0,6},{1,7},{2,4},{3,5},{4,2},{5,3},{6,0},{7,1},{8,14},{9,15},{10,... | collective-permute-start | bytes 737288 | tf_op jit(solution)/shard_map/ppermute | solution.py:27
  129.6 5.1 %collective-permute-done.23.got = bf16[2,2,40,1536]{3,2,1,0:T(8,128)(2,1)S(1)} collective-permute-done((bf16[2,2,40,1536]{3,2,1,0:T(8,128)(2,1)S(1)}, bf16[2,2,40,1536]{3,2,1,0:T(8,128)(2,1)S(1)}, u32[]{:S(2)}, u32[]{:S(2)}) %collective-permute-start.23) | collective-permute-done | bytes 491552 | tf_op jit(solution)/shard_map/ppermute | solution.py:27
  134.8 1.9 %collective-permute-start.28 = (bf16[1,2,40,1536]{3,2,1,0:T(8,128)(2,1)S(1)}, bf16[1,2,40,1536]{3,2,1,0:T(8,128)(2,1)S(1)}, u32[]{:S(2)}, u32[]{:S(2)}) collective-permute-start(bf16[1,2,40,1536]{3,2,1,0:T(8,128)(2,1)S(1)} %get-tuple-element.101), channel_id=1, source_target_pairs={{0,16},{8,24},{16,0},{24,8},{1,17},{9,25},{17,1},{25,9},{2,18},{10... | collective-permute-start | bytes 737288 | tf_op jit(solution)/shard_map/ppermute | solution.py:27
  137.7 5.0 %collective-permute-start.32 = (bf16[2,40,1536]{2,1,0:T(8,128)(2,1)S(1)}, bf16[2,40,1536]{2,1,0:T(8,128)(2,1)S(1)}, u32[]{:S(2)}, u32[]{:S(2)}) collective-permute-start(bf16[2,40,1536]{2,1,0:T(8,128)(2,1)S(1)} %reply.6), channel_id=1, source_target_pairs={{0,2},{1,3},{2,0},{3,1},{4,6},{5,7},{6,4},{7,5},{8,10},{9,11},{10,... | collective-permute-start | bytes 737288 | tf_op jit(solution)/shard_map/ppermute | solution.py:27
  142.7 2.0 %collective-permute-done.31.refs_2_ = bf16[2,40,1536]{2,1,0:T(8,128)(2,1)S(1)} collective-permute-done((bf16[2,40,1536]{2,1,0:T(8,128)(2,1)S(1)}, bf16[2,40,1536]{2,1,0:T(8,128)(2,1)S(1)}, u32[]{:S(2)}, u32[]{:S(2)}) %collective-permute-start.31) | collective-permute-done | bytes 245792 | tf_op jit(solution)/shard_map/ppermute | solution.py:27
  144.9 3.1 %collective-permute-done.32.refs_1_ = bf16[2,40,1536]{2,1,0:T(8,128)(2,1)S(1)} collective-permute-done((bf16[2,40,1536]{2,1,0:T(8,128)(2,1)S(1)}, bf16[2,40,1536]{2,1,0:T(8,128)(2,1)S(1)}, u32[]{:S(2)}, u32[]{:S(2)}) %collective-permute-start.32) | collective-permute-done | bytes 245792 | tf_op jit(solution)/shard_map/ppermute | solution.py:27
  148.6 1.7 %collective-permute-done.33 = bf16[256,768]{1,0:T(8,128)(2,1)S(1)} collective-permute-done((bf16[256,768]{1,0:T(8,128)(2,1)S(1)}, bf16[256,768]{1,0:T(8,128)(2,1)S(1)}, u32[]{:S(2)}, u32[]{:S(2)}) %collective-permute-start.33) | collective-permute-done | bytes 393248 | tf_op jit(solution)/shard_map/ppermute | solution.py:27
  (91 shorter events, 11.6 us)
Async XLA Ops:
  3.8 20.6 %collective-permute-start = (bf16[12,128,128]{2,1,0:T(8,128)(2,1)}, bf16[12,128,128]{2,1,0:T(8,128)(2,1)S(1)}, u32[]{:S(2)}, u32[]{:S(2)}) collective-permute-start(bf16[12,128,128]{2,1,0:T(8,128)(2,1)} %get-tuple-element.57), channel_id=1, source_target_pairs={{0,8},{8,0},{16,24},{1,9},{9,1},{17,25},{2,10},{10,2},{18,26},{3,1... | collective-permute-start | bytes 1179656 | tf_op jit(solution)/shard_map/ppermute | solution.py:27
  9.7 14.7 %collective-permute-start.1 = (f32[2,12,1,1]{1,0,3,2:T(2,128)S(1)}, f32[2,12,1,1]{1,0,3,2:T(2,128)S(1)}, u32[]{:S(2)}, u32[]{:S(2)}) collective-permute-start(f32[2,12,1,1]{1,0,3,2:T(2,128)S(1)} %exp.14), channel_id=1, source_target_pairs={{0,8},{8,0},{16,24},{24,16},{1,9},{9,1},{17,25},{25,17},{2,10},{10... | collective-permute-start | bytes 296 | tf_op jit(solution)/shard_map/ppermute | solution.py:27
  9.7 14.7 %collective-permute-start.3 = (f32[2,12,1,1]{1,0,3,2:T(2,128)S(1)}, f32[2,12,1,1]{1,0,3,2:T(2,128)S(1)}, u32[]{:S(2)}, u32[]{:S(2)}) collective-permute-start(f32[2,12,1,1]{1,0,3,2:T(2,128)S(1)} %exp.14), channel_id=1, source_target_pairs={{0,24},{8,16},{16,8},{24,0},{1,25},{9,17},{17,9},{25,1},{2,26},{10... | collective-permute-start | bytes 296 | tf_op jit(solution)/shard_map/ppermute | solution.py:27
  12.7 11.7 %collective-permute-start.4 = (bf16[12,128,128]{2,1,0:T(8,128)(2,1)}, bf16[12,128,128]{2,1,0:T(8,128)(2,1)S(1)}, u32[]{:S(2)}, u32[]{:S(2)}) collective-permute-start(bf16[12,128,128]{2,1,0:T(8,128)(2,1)} %get-tuple-element.58), channel_id=1, source_target_pairs={{0,16},{8,24},{1,17},{9,25},{2,18},{10,26},{3,19},{11,27},{4,20},{... | collective-permute-start | bytes 1179656 | tf_op jit(solution)/shard_map/ppermute | solution.py:27
  15.6 8.8 %copy-start.9 = (bf16[12,128,128]{2,1,0:T(8,128)(2,1)S(1)}, bf16[12,128,128]{2,1,0:T(8,128)(2,1)}, u32[]{:S(2)}) copy-start(bf16[12,128,128]{2,1,0:T(8,128)(2,1)} %get-tuple-element.58) | copy-start | bytes 1179652
  15.6 11.8 %copy-start.8 = (bf16[12,128,128]{2,1,0:T(8,128)(2,1)S(1)}, bf16[12,128,128]{2,1,0:T(8,128)(2,1)}, u32[]{:S(2)}) copy-start(bf16[12,128,128]{2,1,0:T(8,128)(2,1)} %get-tuple-element.57) | copy-start | bytes 1179652
  15.6 15.1 %copy-start.10 = (f32[768]{0:T(1024)S(1)}, f32[768]{0:T(1024)}, u32[]{:S(2)}) copy-start(f32[768]{0:T(1024)} %param.13) | copy-start | bytes 9220
  15.6 15.1 %copy-start.2 = (bf16[4,64,768]{2,1,0:T(8,128)(2,1)S(1)}, bf16[4,64,768]{2,1,0:T(8,128)(2,1)}, u32[]{:S(2)}) copy-start(bf16[4,64,768]{2,1,0:T(8,128)(2,1)} %refs_0_.3) | copy-start | bytes 1179652
  15.6 15.1 %copy-start.3 = (bf16[4,64,768]{2,1,0:T(8,128)(2,1)S(1)}, bf16[4,64,768]{2,1,0:T(8,128)(2,1)}, u32[]{:S(2)}) copy-start(bf16[4,64,768]{2,1,0:T(8,128)(2,1)} %keys.1) | copy-start | bytes 1179652
  15.6 15.1 %copy-start.4 = (bf16[4,64,768]{2,1,0:T(8,128)(2,1)S(1)}, bf16[4,64,768]{2,1,0:T(8,128)(2,1)}, u32[]{:S(2)}) copy-start(bf16[4,64,768]{2,1,0:T(8,128)(2,1)} %values.1) | copy-start | bytes 1179652
  15.6 15.1 %copy-start.5 = (f32[4,64,6]{1,0,2:T(4,128)S(1)}, f32[4,64,6]{1,0,2:T(4,128)}, u32[]{:S(2)}) copy-start(f32[4,64,6]{1,0,2:T(4,128)} %param.12) | copy-start | bytes 18436
  15.7 15.1 %copy-start.7 = (s32[64,4,2]{0,2,1:T(2,128)S(1)}, s32[64,4,2]{0,2,1:T(2,128)}, u32[]{:S(2)}) copy-start(s32[64,4,2]{0,2,1:T(2,128)} %param.17) | copy-start | bytes 6148
  20.0 2.2 %copy-start = (bf16[2,768,1536]{2,1,0:T(8,128)(2,1)}, bf16[2,768,1536]{2,1,0:T(8,128)(2,1)S(1)}, u32[]{:S(2)}) copy-start(bf16[2,768,1536]{2,1,0:T(8,128)(2,1)S(1)} %get-tuple-element.61.refs_4_) | copy-start | bytes 14155780
  25.4 12.9 %collective-permute-start.5 = (bf16[12,128,128]{2,1,0:T(8,128)(2,1)}, bf16[12,128,128]{2,1,0:T(8,128)(2,1)S(1)}, u32[]{:S(2)}, u32[]{:S(2)}) collective-permute-start(bf16[12,128,128]{2,1,0:T(8,128)(2,1)} %fusion.7), channel_id=1, source_target_pairs={{0,8},{16,24},{24,16},{1,9},{17,25},{25,17},{2,10},{18,26},{26,18}... | collective-permute-start | bytes 1179656 | tf_op jit(solution)/shard_map/ppermute | solution.py:27
  27.6 10.9 %collective-permute-start.2 = (bf16[12,128,128]{2,1,0:T(8,128)(2,1)S(1)}, bf16[12,128,128]{2,1,0:T(8,128)(2,1)S(1)}, u32[]{:S(2)}, u32[]{:S(2)}) collective-permute-start(bf16[12,128,128]{2,1,0:T(8,128)(2,1)S(1)} %fusion.3), channel_id=1, source_target_pairs={{0,16},{8,24},{1,17},{9,25},{2,18},{10,26},{3,19},{11,27},{4,20},{... | collective-permute-start | bytes 1179656 | tf_op jit(solution)/shard_map/ppermute | solution.py:27
  38.3 34.2 %slice-start.2 = ((s8[4718592]{0:T(1024)(128)(4,1)}), s8[4194304]{0:T(1024)(128)(4,1)S(1)}, s32[]{:S(2)}) async-start(s8[4718592]{0:T(1024)(128)(4,1)} %bitcast.21), calls=%async_computation.2 | async-start | bytes 8388608
  38.7 33.7 %slice-start.3 = ((s8[4718592]{0:T(1024)(128)(4,1)}), s8[524288]{0:T(1024)(128)(4,1)S(1)}, s32[]{:S(2)}) async-start(s8[4718592]{0:T(1024)(128)(4,1)} %bitcast.21), calls=%async_computation.3 | async-start | bytes 1048576
  43.6 1.8 %collective-permute-start.6 = (bf16[256,768]{1,0:T(8,128)(2,1)S(1)}, bf16[256,768]{1,0:T(8,128)(2,1)S(1)}, u32[]{:S(2)}, u32[]{:S(2)}) collective-permute-start(bf16[256,768]{1,0:T(8,128)(2,1)S(1)} %get-tuple-element.64.refs_0_.normed), channel_id=1, source_target_pairs={{0,1},{1,0},{2,3},{3,2},{4,5},{5,4},{6,7},{7,6},{8,9},{9,8},{10,11... | collective-permute-start | bytes 1179656 | tf_op jit(solution)/shard_map/ppermute | solution.py:27
  45.9 11.4 %collective-permute-start.7 = (bf16[2,40,1536]{2,1,0:T(8,128)(2,1)S(1)}, bf16[2,40,1536]{2,1,0:T(8,128)(2,1)S(1)}, u32[]{:S(2)}, u32[]{:S(2)}) collective-permute-start(bf16[2,40,1536]{2,1,0:T(8,128)(2,1)S(1)} %get-tuple-element.68), channel_id=1, source_target_pairs={{0,2},{1,3},{2,0},{3,1},{4,6},{5,7},{6,4},{7,5},{8,10},{9,11},{10,... | collective-permute-start | bytes 737288 | tf_op jit(solution)/shard_map/ppermute | solution.py:27
  47.7 10.6 %collective-permute-start.14 = (bf16[2,40,1536]{2,1,0:T(8,128)(2,1)S(1)}, bf16[2,40,1536]{2,1,0:T(8,128)(2,1)S(1)}, u32[]{:S(2)}, u32[]{:S(2)}) collective-permute-start(bf16[2,40,1536]{2,1,0:T(8,128)(2,1)S(1)} %get-tuple-element.67.refs_0_), channel_id=1, source_target_pairs={{0,8},{8,0},{16,24},{24,16},{1,9},{9,1},{17,25},{25,17},{2,10},{10... | collective-permute-start | bytes 737288 | tf_op jit(solution)/shard_map/ppermute | solution.py:27
  49.2 12.7 %collective-permute-start.15 = (bf16[2,40,1536]{2,1,0:T(8,128)(2,1)S(1)}, bf16[2,40,1536]{2,1,0:T(8,128)(2,1)S(1)}, u32[]{:S(2)}, u32[]{:S(2)}) collective-permute-start(bf16[2,40,1536]{2,1,0:T(8,128)(2,1)S(1)} %get-tuple-element.67.refs_0_), channel_id=1, source_target_pairs={{0,16},{8,24},{16,0},{24,8},{1,17},{9,25},{17,1},{25,9},{2,18},{10... | collective-permute-start | bytes 737288 | tf_op jit(solution)/shard_map/ppermute | solution.py:27
  50.1 20.3 %collective-permute-start.8 = (bf16[2,40,1536]{2,1,0:T(8,128)(2,1)S(1)}, bf16[2,40,1536]{2,1,0:T(8,128)(2,1)S(1)}, u32[]{:S(2)}, u32[]{:S(2)}) collective-permute-start(bf16[2,40,1536]{2,1,0:T(8,128)(2,1)S(1)} %get-tuple-element.69), channel_id=1, source_target_pairs={{0,4},{1,5},{2,6},{3,7},{4,0},{5,1},{6,2},{7,3},{8,12},{9,13},{10,... | collective-permute-start | bytes 737288 | tf_op jit(solution)/shard_map/ppermute | solution.py:27
  57.2 13.2 %collective-permute-start.19 = (bf16[2,40,1536]{2,1,0:T(8,128)(2,1)S(1)}, bf16[2,40,1536]{2,1,0:T(8,128)(2,1)S(1)}, u32[]{:S(2)}, u32[]{:S(2)}) collective-permute-start(bf16[2,40,1536]{2,1,0:T(8,128)(2,1)S(1)} %collective-permute-done.7.refs_1_.refs_0_), channel_id=1, source_target_pairs={{0,16},{8,24},{16,0},{24,8},{1,17},{9,25},{17,1},{25,9},{2,18},{10... | collective-permute-start | bytes 737288 | tf_op jit(solution)/shard_map/ppermute | solution.py:27
  58.2 14.2 %collective-permute-start.16 = (bf16[2,40,1536]{2,1,0:T(8,128)(2,1)S(1)}, bf16[2,40,1536]{2,1,0:T(8,128)(2,1)S(1)}, u32[]{:S(2)}, u32[]{:S(2)}) collective-permute-start(bf16[2,40,1536]{2,1,0:T(8,128)(2,1)S(1)} %collective-permute-done.14.refs_1_), channel_id=1, source_target_pairs={{0,16},{8,24},{16,0},{24,8},{1,17},{9,25},{17,1},{25,9},{2,18},{10... | collective-permute-start | bytes 737288 | tf_op jit(solution)/shard_map/ppermute | solution.py:27
  59.3 21.9 %slice-start = ((s8[4718592]{0:T(1024)(128)(4,1)}), s8[4194304]{0:T(1024)(128)(4,1)S(1)}, s32[]{:S(2)}) async-start(s8[4718592]{0:T(1024)(128)(4,1)} %bitcast.19), calls=%async_computation | async-start | bytes 8388608
  59.3 21.9 %slice-start.1 = ((s8[4718592]{0:T(1024)(128)(4,1)}), s8[524288]{0:T(1024)(128)(4,1)S(1)}, s32[]{:S(2)}) async-start(s8[4718592]{0:T(1024)(128)(4,1)} %bitcast.19), calls=%async_computation.1 | async-start | bytes 1048576
  59.3 17.9 %collective-permute-start.9 = (bf16[2,40,1536]{2,1,0:T(8,128)(2,1)S(1)}, bf16[2,40,1536]{2,1,0:T(8,128)(2,1)S(1)}, u32[]{:S(2)}, u32[]{:S(2)}) collective-permute-start(bf16[2,40,1536]{2,1,0:T(8,128)(2,1)S(1)} %get-tuple-element.70), channel_id=1, source_target_pairs={{0,6},{1,7},{2,4},{3,5},{4,2},{5,3},{6,0},{7,1},{8,14},{9,15},{10,... | collective-permute-start | bytes 737288 | tf_op jit(solution)/shard_map/ppermute | solution.py:27
  61.9 17.3 %collective-permute-start.18 = (bf16[2,40,1536]{2,1,0:T(8,128)(2,1)S(1)}, bf16[2,40,1536]{2,1,0:T(8,128)(2,1)S(1)}, u32[]{:S(2)}, u32[]{:S(2)}) collective-permute-start(bf16[2,40,1536]{2,1,0:T(8,128)(2,1)S(1)} %collective-permute-done.7.refs_1_.refs_0_), channel_id=1, source_target_pairs={{0,8},{8,0},{16,24},{24,16},{1,9},{9,1},{17,25},{25,17},{2,10},{10... | collective-permute-start | bytes 737288 | tf_op jit(solution)/shard_map/ppermute | solution.py:27
  70.4 8.8 %collective-permute-start.10 = (bf16[2,40,1536]{2,1,0:T(8,128)(2,1)S(1)}, bf16[2,40,1536]{2,1,0:T(8,128)(2,1)S(1)}, u32[]{:S(2)}, u32[]{:S(2)}) collective-permute-start(bf16[2,40,1536]{2,1,0:T(8,128)(2,1)S(1)} %collective-permute-done.8.refs_2_.refs_0_), channel_id=1, source_target_pairs={{0,8},{8,0},{16,24},{24,16},{1,9},{9,1},{17,25},{25,17},{2,10},{10... | collective-permute-start | bytes 737288 | tf_op jit(solution)/shard_map/ppermute | solution.py:27
  70.4 10.7 %collective-permute-start.20 = (bf16[2,40,1536]{2,1,0:T(8,128)(2,1)S(1)}, bf16[2,40,1536]{2,1,0:T(8,128)(2,1)S(1)}, u32[]{:S(2)}, u32[]{:S(2)}) collective-permute-start(bf16[2,40,1536]{2,1,0:T(8,128)(2,1)S(1)} %collective-permute-done.19.refs_2_), channel_id=1, source_target_pairs={{0,8},{8,0},{16,24},{24,16},{1,9},{9,1},{17,25},{25,17},{2,10},{10... | collective-permute-start | bytes 737288 | tf_op jit(solution)/shard_map/ppermute | solution.py:27
  77.1 10.1 %copy-start.6 = (bf16[6144,16]{0,1:T(8,128)(2,1)S(1)}, bf16[6144,16]{0,1:T(8,128)(2,1)}, u32[]{:S(2)}) copy-start(bf16[6144,16]{0,1:T(8,128)(2,1)} %param.14) | copy-start | bytes 589828
  77.1 8.3 %collective-permute-start.17 = (bf16[2,40,1536]{2,1,0:T(8,128)(2,1)S(1)}, bf16[2,40,1536]{2,1,0:T(8,128)(2,1)S(1)}, u32[]{:S(2)}, u32[]{:S(2)}) collective-permute-start(bf16[2,40,1536]{2,1,0:T(8,128)(2,1)S(1)} %collective-permute-done.9.refs_3_.refs_4_), channel_id=1, source_target_pairs={{0,16},{8,24},{16,0},{24,8},{1,17},{9,25},{17,1},{25,9},{2,18},{10... | collective-permute-start | bytes 737288 | tf_op jit(solution)/shard_map/ppermute | solution.py:27
  78.3 10.0 %collective-permute-start.11 = (bf16[2,40,1536]{2,1,0:T(8,128)(2,1)S(1)}, bf16[2,40,1536]{2,1,0:T(8,128)(2,1)S(1)}, u32[]{:S(2)}, u32[]{:S(2)}) collective-permute-start(bf16[2,40,1536]{2,1,0:T(8,128)(2,1)S(1)} %collective-permute-done.8.refs_2_.refs_0_), channel_id=1, source_target_pairs={{0,16},{8,24},{16,0},{24,8},{1,17},{9,25},{17,1},{25,9},{2,18},{10... | collective-permute-start | bytes 737288 | tf_op jit(solution)/shard_map/ppermute | solution.py:27
  79.2 9.1 %collective-permute-start.13 = (bf16[2,40,1536]{2,1,0:T(8,128)(2,1)S(1)}, bf16[2,40,1536]{2,1,0:T(8,128)(2,1)S(1)}, u32[]{:S(2)}, u32[]{:S(2)}) collective-permute-start(bf16[2,40,1536]{2,1,0:T(8,128)(2,1)S(1)} %collective-permute-done.9.refs_3_.refs_4_), channel_id=1, source_target_pairs={{0,8},{8,0},{16,24},{24,16},{1,9},{9,1},{17,25},{25,17},{2,10},{10... | collective-permute-start | bytes 737288 | tf_op jit(solution)/shard_map/ppermute | solution.py:27
  79.2 10.5 %collective-permute-start.12 = (bf16[2,40,1536]{2,1,0:T(8,128)(2,1)S(1)}, bf16[2,40,1536]{2,1,0:T(8,128)(2,1)S(1)}, u32[]{:S(2)}, u32[]{:S(2)}) collective-permute-start(bf16[2,40,1536]{2,1,0:T(8,128)(2,1)S(1)} %collective-permute-done.10.refs_1_), channel_id=1, source_target_pairs={{0,16},{8,24},{16,0},{24,8},{1,17},{9,25},{17,1},{25,9},{2,18},{10... | collective-permute-start | bytes 737288 | tf_op jit(solution)/shard_map/ppermute | solution.py:27
  85.4 6.3 %collective-permute-start.21 = (bf16[2,40,1536]{2,1,0:T(8,128)(2,1)S(1)}, bf16[2,40,1536]{2,1,0:T(8,128)(2,1)S(1)}, u32[]{:S(2)}, u32[]{:S(2)}) collective-permute-start(bf16[2,40,1536]{2,1,0:T(8,128)(2,1)S(1)} %collective-permute-done.17.refs_6_), channel_id=1, source_target_pairs={{0,8},{8,0},{16,24},{24,16},{1,9},{9,1},{17,25},{25,17},{2,10},{10... | collective-permute-start | bytes 737288 | tf_op jit(solution)/shard_map/ppermute | solution.py:27
  100.3 14.6 %collective-permute-start.22 = (bf16[2,2,40,1536]{3,2,1,0:T(8,128)(2,1)S(1)}, bf16[2,2,40,1536]{3,2,1,0:T(8,128)(2,1)S(1)}, u32[]{:S(2)}, u32[]{:S(2)}) collective-permute-start(bf16[2,2,40,1536]{3,2,1,0:T(8,128)(2,1)S(1)} %get-tuple-element.79), channel_id=1, source_target_pairs={{0,16},{8,24},{16,0},{24,8},{1,17},{9,25},{17,1},{25,9},{2,18},{10... | collective-permute-start | bytes 1474568 | tf_op jit(solution)/shard_map/ppermute | solution.py:27
  106.6 15.6 %collective-permute-start.24 = (bf16[2,2,40,1536]{3,2,1,0:T(8,128)(2,1)S(1)}, bf16[2,2,40,1536]{3,2,1,0:T(8,128)(2,1)S(1)}, u32[]{:S(2)}, u32[]{:S(2)}) collective-permute-start(bf16[2,2,40,1536]{3,2,1,0:T(8,128)(2,1)S(1)} %get-tuple-element.81), channel_id=1, source_target_pairs={{0,8},{8,0},{16,24},{24,16},{1,9},{9,1},{17,25},{25,17},{2,10},{10... | collective-permute-start | bytes 1474568 | tf_op jit(solution)/shard_map/ppermute | solution.py:27
  113.6 11.7 %collective-permute-start.26 = (bf16[2,2,40,1536]{3,2,1,0:T(8,128)(2,1)S(1)}, bf16[2,2,40,1536]{3,2,1,0:T(8,128)(2,1)S(1)}, u32[]{:S(2)}, u32[]{:S(2)}) collective-permute-start(bf16[2,2,40,1536]{3,2,1,0:T(8,128)(2,1)S(1)} %get-tuple-element.83), channel_id=1, source_target_pairs={{0,16},{8,24},{16,0},{24,8},{1,17},{9,25},{17,1},{25,9},{2,18},{10... | collective-permute-start | bytes 1474568 | tf_op jit(solution)/shard_map/ppermute | solution.py:27
  115.0 9.2 %collective-permute-start.27 = (bf16[1,2,40,1536]{3,2,1,0:T(8,128)(2,1)S(1)}, bf16[1,2,40,1536]{3,2,1,0:T(8,128)(2,1)S(1)}, u32[]{:S(2)}, u32[]{:S(2)}) collective-permute-start(bf16[1,2,40,1536]{3,2,1,0:T(8,128)(2,1)S(1)} %get-tuple-element.85), channel_id=1, source_target_pairs={{0,8},{8,0},{16,24},{24,16},{1,9},{9,1},{17,25},{25,17},{2,10},{10... | collective-permute-start | bytes 737288 | tf_op jit(solution)/shard_map/ppermute | solution.py:27
  120.2 14.6 %collective-permute-start.23 = (bf16[2,2,40,1536]{3,2,1,0:T(8,128)(2,1)S(1)}, bf16[2,2,40,1536]{3,2,1,0:T(8,128)(2,1)S(1)}, u32[]{:S(2)}, u32[]{:S(2)}) collective-permute-start(bf16[2,2,40,1536]{3,2,1,0:T(8,128)(2,1)S(1)} %get-tuple-element.88), channel_id=1, source_target_pairs={{0,8},{8,0},{16,24},{24,16},{1,9},{9,1},{17,25},{25,17},{2,10},{10... | collective-permute-start | bytes 1474568 | tf_op jit(solution)/shard_map/ppermute | solution.py:27
  122.3 6.3 %collective-permute-start.25 = (bf16[1,2,40,1536]{3,2,1,0:T(8,128)(2,1)S(1)}, bf16[1,2,40,1536]{3,2,1,0:T(8,128)(2,1)S(1)}, u32[]{:S(2)}, u32[]{:S(2)}) collective-permute-start(bf16[1,2,40,1536]{3,2,1,0:T(8,128)(2,1)S(1)} %get-tuple-element.92), channel_id=1, source_target_pairs={{0,16},{8,24},{16,0},{24,8},{1,17},{9,25},{17,1},{25,9},{2,18},{10... | collective-permute-start | bytes 737288 | tf_op jit(solution)/shard_map/ppermute | solution.py:27
  125.4 12.2 %collective-permute-start.29 = (bf16[1,2,40,1536]{3,2,1,0:T(8,128)(2,1)S(1)}, bf16[1,2,40,1536]{3,2,1,0:T(8,128)(2,1)S(1)}, u32[]{:S(2)}, u32[]{:S(2)}) collective-permute-start(bf16[1,2,40,1536]{3,2,1,0:T(8,128)(2,1)S(1)} %get-tuple-element.97), channel_id=1, source_target_pairs={{0,8},{8,0},{16,24},{24,16},{1,9},{9,1},{17,25},{25,17},{2,10},{10... | collective-permute-start | bytes 737288 | tf_op jit(solution)/shard_map/ppermute | solution.py:27
  126.3 11.3 %collective-permute-start.30 = (bf16[2,40,1536]{2,1,0:T(8,128)(2,1)S(1)}, bf16[2,40,1536]{2,1,0:T(8,128)(2,1)S(1)}, u32[]{:S(2)}, u32[]{:S(2)}) collective-permute-start(bf16[2,40,1536]{2,1,0:T(8,128)(2,1)S(1)} %reply.4), channel_id=1, source_target_pairs={{0,6},{1,7},{2,4},{3,5},{4,2},{5,3},{6,0},{7,1},{8,14},{9,15},{10,... | collective-permute-start | bytes 737288 | tf_op jit(solution)/shard_map/ppermute | solution.py:27
  128.7 16.0 %collective-permute-start.31 = (bf16[2,40,1536]{2,1,0:T(8,128)(2,1)S(1)}, bf16[2,40,1536]{2,1,0:T(8,128)(2,1)S(1)}, u32[]{:S(2)}, u32[]{:S(2)}) collective-permute-start(bf16[2,40,1536]{2,1,0:T(8,128)(2,1)S(1)} %reply.5), channel_id=1, source_target_pairs={{0,4},{1,5},{2,6},{3,7},{4,0},{5,1},{6,2},{7,3},{8,12},{9,13},{10,... | collective-permute-start | bytes 737288 | tf_op jit(solution)/shard_map/ppermute | solution.py:27
  134.8 9.9 %collective-permute-start.28 = (bf16[1,2,40,1536]{3,2,1,0:T(8,128)(2,1)S(1)}, bf16[1,2,40,1536]{3,2,1,0:T(8,128)(2,1)S(1)}, u32[]{:S(2)}, u32[]{:S(2)}) collective-permute-start(bf16[1,2,40,1536]{3,2,1,0:T(8,128)(2,1)S(1)} %get-tuple-element.101), channel_id=1, source_target_pairs={{0,16},{8,24},{16,0},{24,8},{1,17},{9,25},{17,1},{25,9},{2,18},{10... | collective-permute-start | bytes 737288 | tf_op jit(solution)/shard_map/ppermute | solution.py:27
  137.7 10.3 %collective-permute-start.32 = (bf16[2,40,1536]{2,1,0:T(8,128)(2,1)S(1)}, bf16[2,40,1536]{2,1,0:T(8,128)(2,1)S(1)}, u32[]{:S(2)}, u32[]{:S(2)}) collective-permute-start(bf16[2,40,1536]{2,1,0:T(8,128)(2,1)S(1)} %reply.6), channel_id=1, source_target_pairs={{0,2},{1,3},{2,0},{3,1},{4,6},{5,7},{6,4},{7,5},{8,10},{9,11},{10,... | collective-permute-start | bytes 737288 | tf_op jit(solution)/shard_map/ppermute | solution.py:27
  148.6 1.8 %collective-permute-start.33 = (bf16[256,768]{1,0:T(8,128)(2,1)S(1)}, bf16[256,768]{1,0:T(8,128)(2,1)S(1)}, u32[]{:S(2)}, u32[]{:S(2)}) collective-permute-start(bf16[256,768]{1,0:T(8,128)(2,1)S(1)} %get-tuple-element.106), channel_id=1, source_target_pairs={{0,1},{1,0},{2,3},{3,2},{4,5},{5,4},{6,7},{7,6},{8,9},{9,8},{10,11... | collective-permute-start | bytes 1179656 | tf_op jit(solution)/shard_map/ppermute | solution.py:27
  (1 other events, 2.2 us)

commit v6 on v5

--- a/solution.py
+++ b/solution.py
@@ -99,7 +99,7 @@
         in_specs=[SMEM, ANY, ANY] + [VMEM] * len(args),
         out_specs=[VMEM] * (len(out_shape) + len(shapes)),
         out_shape=list(out_shape) + shapes,
-        scratch_shapes=[pltpu.SemaphoreType.DMA((len(pieces), 2, 2))],
+        scratch_shapes=[pltpu.SemaphoreType.DMA((max(len(pieces), 1), 2, 2))],
         compiler_params=params(24),
         name=name,
     )(place, up, down, *args)
@@ -460,20 +460,23 @@
     return incoming
 
 
-def prefix_of_four(states, decay, me, token):
+def prefix_of_four(states, decay, me, beside_first, beside_last):
     high, low = (me & 2) != 0, (me & 1) != 0
     near = swap(decay, "ctx", 4, 1)
     far = swap(decay, "ctx", 4, 3)
     one, two = states
-    got_one = after(swap(one, "ctx", 4, 1, lambda i: i != 3), *token).astype(F32)
+    first = beside_first(one)
+    got_one = after(swap(one, "ctx", 4, 1, lambda i: i != 3), *first).astype(F32)
     got_two = swap(two, "ctx", 4, 2, lambda i: i < 2).astype(F32)
     sent_one = jnp.where(low, 1.0, near[0]) * one.astype(F32) + jnp.where(low, decay[0], 1.0) * got_one
     sent_two = (
         jnp.where(high & low, 0.0, 1.0) * two.astype(F32)
         + jnp.where(high, jnp.where(low, 1.0, far[1] * decay[1]), 0.0) * got_two
     )
-    last_one = swap(sent_one.astype(BF16), "ctx", 4, 2, lambda i: i < 2).astype(F32)
-    last_two = swap(sent_two.astype(BF16), "ctx", 4, 1, lambda i: i != 1).astype(F32)
+    sent_one, sent_two = sent_one.astype(BF16), sent_two.astype(BF16)
+    last = beside_last(sent_two)
+    last_one = after(swap(sent_one, "ctx", 4, 2, lambda i: i < 2), *last).astype(F32)
+    last_two = swap(sent_two, "ctx", 4, 1, lambda i: i != 1).astype(F32)
     return [
         (jnp.where(low, 1.0, 0.0) * got_one + jnp.where(low, near[0], 1.0) * last_one).astype(BF16),
         (jnp.where(low, near[1], far[1]) * got_two + last_two).astype(BF16),
@@ -494,9 +497,7 @@
     me = lax.axis_index("ctx")
     place = jnp.stack([me, lax.axis_index("exp")]).astype(jnp.int32)
     struct = jax.ShapeDtypeStruct
-    early_pieces = [("up", k) for k in range(min(2, chunks - 2))]
-    later_pieces = [("up", k) for k in range(max(chunks - 2, 0), chunks)]
-    last_pieces = [("down", chunks - 1)]
+    early_pieces = [("up", k) for k in range(max(chunks - 2, 0), chunks)] + [("down", chunks - 1)]
     decay_rows = jnp.transpose(log_decay, (2, 0, 1)).reshape(heads * requests, length)
 
     states = pl.pallas_call(
@@ -513,33 +514,43 @@
         name="local_state",
     )(keys, values, decay_rows)
     decay = jnp.exp(jnp.sum(after(log_decay, *states), axis=1)).reshape(halves, pairs, 1, 1)
-    _, held = call_with_held(
-        None, early_pieces, chunks, after(place, *states), expert_up, expert_down, [], [], "early_weights"
-    )
+    part = {}
+
+    def beside_first(token):
+        part["inside"], _ = call_with_held(
+            inside_kernel,
+            [],
+            chunks,
+            after(place, token),
+            expert_up,
+            expert_down,
+            [queries, keys, values, decay_rows, jnp.transpose(expert_ids, (1, 2, 0))],
+            [
+                struct((requests, length, features), F32),
+                struct((chunks * own * CAP, tokens), BF16),
+                struct((own * CAP, 128), jnp.int32),
+            ],
+            "inside_and_placement",
+        )
+        return part["inside"][:1]
+
+    def beside_last(token):
+        _, part["held"] = call_with_held(
+            None, early_pieces, chunks, after(place, token), expert_up, expert_down, [], [], "early_weights"
+        )
+        return list(part["held"].values())
+
     if n_ctx == 4 and halves == 2:
-        incoming = prefix_of_four(states, decay, me, list(held.values()))
+        incoming = prefix_of_four(states, decay, me, beside_first, beside_last)
     else:
         incoming = prefix_by_doubling(states, decay, me, n_ctx)
-
-    (inside, placement, other), more = call_with_held(
-        inside_kernel,
-        later_pieces,
-        chunks,
-        place,
-        expert_up,
-        expert_down,
-        [queries, keys, values, decay_rows, jnp.transpose(expert_ids, (1, 2, 0))],
-        [
-            struct((requests, length, features), F32),
-            struct((chunks * own * CAP, tokens), BF16),
-            struct((own * CAP, 128), jnp.int32),
-        ],
-        "inside_and_placement",
-    )
-    held = {**held, **more}
-    (normed,), more = call_with_held(
+        beside_first(states[0])
+        beside_last(states[0])
+    inside, placement, other = part["inside"]
+    held = part["held"]
+    (normed,), _ = call_with_held(
         output_kernel,
-        last_pieces,
+        [],
         chunks,
         place,
         expert_up,
@@ -548,7 +559,6 @@
         [struct((tokens, features), BF16)],
         "normed",
     )
-    held = {**held, **more}
 
     outgoing = pl.pallas_call(
         dispatch_kernel,
@@ -573,30 +583,18 @@
 
     routes = [route_of(order, n_ctx) for order in orders]
     gathered = [None] * chunks
-    total, done = None, 0
-
-    def advance(upto):
-        nonlocal total, done
-        for k in range(done, upto + 1):
-            (total,) = project(
-                place, [k], chunks, gathered, expert_up, expert_down, held, total, None
-            )
-        done = max(done, upto + 1)
-        return total
-
     for k in range(chunks):
         have = {0: arrived[k]}
+        if k == 1:
+            have[0] = after(arrived[k], *[gathered[0][bit] for bit in bits])
         for bit in orders[k]:
-            token = advance(k - 3) if k >= 3 and bit == orders[k][0] else None
-            if k == chunks - 1 and k >= 2 and bit == orders[k][-1] and len(bits) > 1:
-                token = advance(k - 2)
-            found = {}
-            for rel, block in have.items():
-                if token is not None and (rel or bit == orders[k][0]):
-                    block = after(block, token)
-                found[rel | bit] = swap(block, "ctx", n_ctx, bit)
-            have.update(found)
+            have.update({rel | bit: swap(a, "ctx", n_ctx, bit) for rel, a in list(have.items())})
         gathered[k] = [have[rel] for rel in range(n_ctx)]
+    total, done = None, max(chunks - 2, 0)
+    for k in range(done):
+        (total,) = project(
+            after(place, arrived[-1]), [k], chunks, gathered, expert_up, expert_down, held, total, None
+        )
     hidden, *far = project(
         after(place, weight),
         list(range(done, chunks)),

time: 152 us -> 146 us (0.961)
  starting transfers between devices: 54.6 us -> 49.4 us
  Pallas kernels: 56.3 us -> 53.6 us
  waiting for transfers between devices: 31.6 us -> 34.2 us
    ppermute x34, starting transfers between devices: 54.6 us -> 49.4 us  [swap(): return lax.ppermute(x, axis, [(i, i ^ k) for i in range(n) if keep(i)])]
    pallas_call x3, Pallas kernels: 16.8 us -> 12.7 us  [call_with_held(): pl.pallas_call(functools.partial(with_held, kernel, pieces), in_specs=[SM...]
    ppermute x34, waiting for transfers between devices: 31.6 us -> 34.2 us  [swap(): return lax.ppermute(x, axis, [(i, i ^ k) for i in range(n) if keep(i)])]
    unnamed x30 -> x22, local copies, waits for them, and re-layouts: 4.41 us -> 4.41 us
  transfers between devices with their start and end apart: 34 -> 34, of which waited for: 14 -> 13; matrix products, arithmetic and copies ran while one was open for 1% -> 1% of each run, Pallas kernels for 25% -> 26%
where the time goes in v6:
time: 146 us; the launch traced here: 145 us
  Pallas kernels  53.6 us (37%)
  starting transfers between devices  49.4 us (34%)
  waiting for transfers between devices  34.2 us (23%)
  local copies, waits for them, and re-layouts  4.96 us (3%)
  other arithmetic  2.56 us (2%)
    ppermute x34, starting transfers between devices, swap(): return lax.ppermute(x, axis, [(i, i ^ k) for i in range(n) if keep(i)])  49.4 us
    ppermute x34, waiting for transfers between devices, swap(): return lax.ppermute(x, axis, [(i, i ^ k) for i in range(n) if keep(i)])  34.2 us
    pallas_call x3, Pallas kernels, project(): pl.pallas_call(functools.partial(project_kernel, chunks=chunks, parts=par...  18.8 us
    pallas_call x3, Pallas kernels, down_chunk(): pl.pallas_call(functools.partial(down_kernel, chunk=chunk, route=route),...  15.3 us
    pallas_call x3, Pallas kernels, call_with_held(): pl.pallas_call(functools.partial(with_held, kernel, pieces), in_specs=[SM...  12.7 us
    unnamed x22, local copies, waits for them, and re-layouts  4.41 us
    pallas_call x1, Pallas kernels, body(): pl.pallas_call(state_kernel, in_specs=[ANY] * 2 + [VMEM], out_specs=[VMEM...  3.84 us
  transfers between devices with their start and end apart: 34, of which 13 were waited for; matrix products, arithmetic and copies ran while one was open for 1% of the time, Pallas kernels for 26%

profile of v6, /device:TPU:0, one launch (start us, length us, event | category | flops | bytes accessed | tf_op | source)
XLA Modules:
  0.0 145.1 jit_solution(11385639508659104515)
XLA Ops:
  0.0 3.8 %local_state.1 = (bf16[12,128,128]{2,1,0:T(8,128)(2,1)}, bf16[12,128,128]{2,1,0:T(8,128)(2,1)}) custom-call(bf16[4,64,768]{2,1,0:T(8,128)(2,1)} %refs_1_.1, bf16[4,64,768]{2,1,0:T(8,128)(2,1)} %refs_2_.1, f32[24,64]{1,0:T(8,128)} %bitcast.19), custom_call_target="tpu_custom_call" | custom-call | tf_op jit(solution)/shard_map/local_state/pallas_call | solution.py:503
  4.8 2.9 %collective-permute-start.1 = (f32[2,12,1,1]{1,0,3,2:T(2,128)S(1)}, f32[2,12,1,1]{1,0,3,2:T(2,128)S(1)}, u32[]{:S(2)}, u32[]{:S(2)}) collective-permute-start(f32[2,12,1,1]{1,0,3,2:T(2,128)S(1)} %exp.14), channel_id=1, source_target_pairs={{0,8},{8,0},{16,24},{24,16},{1,9},{9,1},{17,25},{25,17},{2,10},{10... | collective-permute-start | bytes 296 | tf_op jit(solution)/shard_map/ppermute | solution.py:27
  7.8 1.5 %collective-permute-start.3 = (f32[2,12,1,1]{1,0,3,2:T(2,128)S(1)}, f32[2,12,1,1]{1,0,3,2:T(2,128)S(1)}, u32[]{:S(2)}, u32[]{:S(2)}) collective-permute-start(f32[2,12,1,1]{1,0,3,2:T(2,128)S(1)} %exp.14), channel_id=1, source_target_pairs={{0,24},{8,16},{16,8},{24,0},{1,25},{9,17},{17,9},{25,1},{2,26},{10... | collective-permute-start | bytes 296 | tf_op jit(solution)/shard_map/ppermute | solution.py:27
  9.3 2.0 %collective-permute-start.4 = (bf16[12,128,128]{2,1,0:T(8,128)(2,1)}, bf16[12,128,128]{2,1,0:T(8,128)(2,1)S(1)}, u32[]{:S(2)}, u32[]{:S(2)}) collective-permute-start(bf16[12,128,128]{2,1,0:T(8,128)(2,1)} %get-tuple-element.59), channel_id=1, source_target_pairs={{0,16},{8,24},{1,17},{9,25},{2,18},{10,26},{3,19},{11,27},{4,20},{... | collective-permute-start | bytes 1179656 | tf_op jit(solution)/shard_map/ppermute | solution.py:27
  11.2 3.9 %collective-permute-start = (bf16[12,128,128]{2,1,0:T(8,128)(2,1)}, bf16[12,128,128]{2,1,0:T(8,128)(2,1)S(1)}, u32[]{:S(2)}, u32[]{:S(2)}) collective-permute-start(bf16[12,128,128]{2,1,0:T(8,128)(2,1)} %get-tuple-element.55), channel_id=1, source_target_pairs={{0,8},{8,0},{16,24},{1,9},{9,1},{17,25},{2,10},{10,2},{18,26},{3,1... | collective-permute-start | bytes 1179656 | tf_op jit(solution)/shard_map/ppermute | solution.py:27
  15.6 1.0 copy-done
  16.6 1.0 copy-done.2
  17.6 1.0 copy-done.3
  20.0 4.3 %inside_and_placement.1 = (f32[4,64,768]{2,1,0:T(8,128)S(1)}, bf16[320,256]{1,0:T(8,128)(2,1)S(1)}, s32[80,128]{1,0:T(8,128)S(1)}) custom-call(s32[2]{0:T(128)S(1)} %pad_add_fusion.place, bf16[2,6144,1536]{2,1,0:T(8,128)(2,1)} %up.11, bf16[2,1536,6144]{2,1,0:T(8,128)(2,1)} %weights.5, bf16[4,64,768]{2,1,0:T(8,128)(2,1)S(1)} %copy-done, ...), custom_call_target="tpu_custom_call" | custom-call | tf_op jit(solution)/shard_map/inside_and_placement/pallas_call | solution.py:97
  24.6 1.3 collective-permute-start.2
  26.2 3.3 %collective-permute-start.5 = (bf16[12,128,128]{2,1,0:T(8,128)(2,1)S(1)}, bf16[12,128,128]{2,1,0:T(8,128)(2,1)S(1)}, u32[]{:S(2)}, u32[]{:S(2)}) collective-permute-start(bf16[12,128,128]{2,1,0:T(8,128)(2,1)S(1)} %fusion.5), channel_id=1, source_target_pairs={{0,8},{16,24},{24,16},{1,9},{17,25},{25,17},{2,10},{18,26},{26,18}... | collective-permute-start | bytes 1179656 | tf_op jit(solution)/shard_map/ppermute | solution.py:27
  29.5 5.8 %early_weights.1 = (bf16[2,768,1536]{2,1,0:T(8,128)(2,1)S(1)}, bf16[2,768,1536]{2,1,0:T(8,128)(2,1)S(1)}, bf16[2,1536,768]{2,1,0:T(8,128)(2,1)S(1)}) custom-call(s32[2]{0:T(128)S(1)} %pad_add_fusion.place, bf16[2,6144,1536]{2,1,0:T(8,128)(2,1)} %up.11, bf16[2,1536,6144]{2,1,0:T(8,128)(2,1)} %weights.5), custom_call_target="tpu_custom_call" | custom-call | tf_op jit(solution)/shard_map/early_weights/pallas_call | solution.py:97
  36.1 2.6 %normed.1.refs_0_ = bf16[256,768]{1,0:T(8,128)(2,1)S(1)} custom-call(s32[2]{0:T(128)S(1)} %pad_add_fusion.place, bf16[2,6144,1536]{2,1,0:T(8,128)(2,1)} %up.11, bf16[2,1536,6144]{2,1,0:T(8,128)(2,1)} %weights.5, bf16[4,64,768]{2,1,0:T(8,128)(2,1)S(1)} %copy-done.1, f32[4,64,768]{2,1,0:T(8,128)S(1)} %get-tuple-element.57.refs_1_, f32[24,64]{1,0:T(8,128)S(1)} %bitcast.21, ...), custom_call_target="tpu_custom_call" | custom-call | tf_op jit(solution)/shard_map/normed/pallas_call | solution.py:97
  38.8 1.7 %collective-permute-done.6.refs_1_ = bf16[256,768]{1,0:T(8,128)(2,1)S(1)} collective-permute-done((bf16[256,768]{1,0:T(8,128)(2,1)S(1)}, bf16[256,768]{1,0:T(8,128)(2,1)S(1)}, u32[]{:S(2)}, u32[]{:S(2)}) %collective-permute-start.6) | collective-permute-done | bytes 393248 | tf_op jit(solution)/shard_map/ppermute | solution.py:27
  41.0 2.5 %collective-permute-start.16 = (bf16[2,40,1536]{2,1,0:T(8,128)(2,1)S(1)}, bf16[2,40,1536]{2,1,0:T(8,128)(2,1)S(1)}, u32[]{:S(2)}, u32[]{:S(2)}) collective-permute-start(bf16[2,40,1536]{2,1,0:T(8,128)(2,1)S(1)} %get-tuple-element.68.refs_0_), channel_id=1, source_target_pairs={{0,8},{8,0},{16,24},{24,16},{1,9},{9,1},{17,25},{25,17},{2,10},{10... | collective-permute-start | bytes 737288 | tf_op jit(solution)/shard_map/ppermute | solution.py:27
  43.5 1.6 %collective-permute-start.7 = (bf16[2,40,1536]{2,1,0:T(8,128)(2,1)S(1)}, bf16[2,40,1536]{2,1,0:T(8,128)(2,1)S(1)}, u32[]{:S(2)}, u32[]{:S(2)}) collective-permute-start(bf16[2,40,1536]{2,1,0:T(8,128)(2,1)S(1)} %get-tuple-element.69), channel_id=1, source_target_pairs={{0,2},{1,3},{2,0},{3,1},{4,6},{5,7},{6,4},{7,5},{8,10},{9,11},{10,... | collective-permute-start | bytes 737288 | tf_op jit(solution)/shard_map/ppermute | solution.py:27
  45.1 2.6 %collective-permute-start.8 = (bf16[2,40,1536]{2,1,0:T(8,128)(2,1)S(1)}, bf16[2,40,1536]{2,1,0:T(8,128)(2,1)S(1)}, u32[]{:S(2)}, u32[]{:S(2)}) collective-permute-start(bf16[2,40,1536]{2,1,0:T(8,128)(2,1)S(1)} %get-tuple-element.70), channel_id=1, source_target_pairs={{0,4},{1,5},{2,6},{3,7},{4,0},{5,1},{6,2},{7,3},{8,12},{9,13},{10,... | collective-permute-start | bytes 737288 | tf_op jit(solution)/shard_map/ppermute | solution.py:27
  47.9 1.9 %collective-permute-done.16.refs_1_ = bf16[2,40,1536]{2,1,0:T(8,128)(2,1)S(1)} collective-permute-done((bf16[2,40,1536]{2,1,0:T(8,128)(2,1)S(1)}, bf16[2,40,1536]{2,1,0:T(8,128)(2,1)S(1)}, u32[]{:S(2)}, u32[]{:S(2)}) %collective-permute-start.16) | collective-permute-done | bytes 245792 | tf_op jit(solution)/shard_map/ppermute | solution.py:27
  49.8 1.5 %collective-permute-done.17.refs_2_ = bf16[2,40,1536]{2,1,0:T(8,128)(2,1)S(1)} collective-permute-done((bf16[2,40,1536]{2,1,0:T(8,128)(2,1)S(1)}, bf16[2,40,1536]{2,1,0:T(8,128)(2,1)S(1)}, u32[]{:S(2)}, u32[]{:S(2)}) %collective-permute-start.17) | collective-permute-done | bytes 245792 | tf_op jit(solution)/shard_map/ppermute | solution.py:27
  51.2 4.5 %collective-permute-done.7.refs_1_.refs_0_ = bf16[2,40,1536]{2,1,0:T(8,128)(2,1)S(1)} collective-permute-done((bf16[2,40,1536]{2,1,0:T(8,128)(2,1)S(1)}, bf16[2,40,1536]{2,1,0:T(8,128)(2,1)S(1)}, u32[]{:S(2)}, u32[]{:S(2)}) %collective-permute-start.7) | collective-permute-done | bytes 245792 | tf_op jit(solution)/shard_map/ppermute | solution.py:27
  55.7 1.6 %collective-permute-start.19 = (bf16[2,40,1536]{2,1,0:T(8,128)(2,1)S(1)}, bf16[2,40,1536]{2,1,0:T(8,128)(2,1)S(1)}, u32[]{:S(2)}, u32[]{:S(2)}) collective-permute-start(bf16[2,40,1536]{2,1,0:T(8,128)(2,1)S(1)} %collective-permute-done.7.refs_1_.refs_0_), channel_id=1, source_target_pairs={{0,16},{8,24},{16,0},{24,8},{1,17},{9,25},{17,1},{25,9},{2,18},{10... | collective-permute-start | bytes 737288 | tf_op jit(solution)/shard_map/ppermute | solution.py:27
  58.4 7.0 %collective-permute-done.8.refs_2_.refs_0_ = bf16[2,40,1536]{2,1,0:T(8,128)(2,1)S(1)} collective-permute-done((bf16[2,40,1536]{2,1,0:T(8,128)(2,1)S(1)}, bf16[2,40,1536]{2,1,0:T(8,128)(2,1)S(1)}, u32[]{:S(2)}, u32[]{:S(2)}) %collective-permute-start.8) | collective-permute-done | bytes 245792 | tf_op jit(solution)/shard_map/ppermute | solution.py:27
  65.4 1.1 collective-permute-start.10
  66.5 1.0 collective-permute-start.14
  67.5 2.0 %collective-permute-start.20 = (bf16[2,40,1536]{2,1,0:T(8,128)(2,1)S(1)}, bf16[2,40,1536]{2,1,0:T(8,128)(2,1)S(1)}, u32[]{:S(2)}, u32[]{:S(2)}) collective-permute-start(bf16[2,40,1536]{2,1,0:T(8,128)(2,1)S(1)} %collective-permute-done.19.refs_2_), channel_id=1, source_target_pairs={{0,8},{8,0},{16,24},{24,16},{1,9},{9,1},{17,25},{25,17},{2,10},{10... | collective-permute-start | bytes 737288 | tf_op jit(solution)/shard_map/ppermute | solution.py:27
  69.5 1.1 gate.1.weight
  70.8 1.2 collective-permute-start.13
  72.0 2.3 %collective-permute-done.10.refs_1_ = bf16[2,40,1536]{2,1,0:T(8,128)(2,1)S(1)} collective-permute-done((bf16[2,40,1536]{2,1,0:T(8,128)(2,1)S(1)}, bf16[2,40,1536]{2,1,0:T(8,128)(2,1)S(1)}, u32[]{:S(2)}, u32[]{:S(2)}) %collective-permute-start.10) | collective-permute-done | bytes 245792 | tf_op jit(solution)/shard_map/ppermute | solution.py:27
  74.3 2.0 %collective-permute-start.12 = (bf16[2,40,1536]{2,1,0:T(8,128)(2,1)S(1)}, bf16[2,40,1536]{2,1,0:T(8,128)(2,1)S(1)}, u32[]{:S(2)}, u32[]{:S(2)}) collective-permute-start(bf16[2,40,1536]{2,1,0:T(8,128)(2,1)S(1)} %collective-permute-done.10.refs_1_), channel_id=1, source_target_pairs={{0,16},{8,24},{16,0},{24,8},{1,17},{9,25},{17,1},{25,9},{2,18},{10... | collective-permute-start | bytes 737288 | tf_op jit(solution)/shard_map/ppermute | solution.py:27
  76.4 5.3 %project_0.1.refs_4_ = f32[2,160,1536]{2,1,0:T(8,128)S(1)} custom-call(s32[2]{0:T(128)S(1)} %pad_add_fusion.place, bf16[2,6144,1536]{2,1,0:T(8,128)(2,1)} %up.11, bf16[2,1536,6144]{2,1,0:T(8,128)(2,1)} %weights.5, bf16[2,40,1536]{2,1,0:T(8,128)(2,1)S(1)} %get-tuple-element.68.refs_0_, bf16[2,40,1536]{2,1,0:T(8,128)(2,1)S(1)} %collective-permute-done.16.refs_1_, ...), custom_call_target="tpu_custom_call" | custom-call | flops 1509949440 | bytes 9437184 | tf_op jit(solution)/shard_map/project_0/pallas_call | solution.py:309
  81.7 4.9 %project_1.1.refs_11_ = f32[2,160,1536]{2,1,0:T(8,128)S(1)} custom-call(s32[2]{0:T(128)S(1)} %pad_add_fusion.place, bf16[2,6144,1536]{2,1,0:T(8,128)(2,1)} %up.11, bf16[2,1536,6144]{2,1,0:T(8,128)(2,1)} %weights.5, bf16[2,40,1536]{2,1,0:T(8,128)(2,1)S(1)} %collective-permute-done.7.refs_1_.refs_0_, bf16[2,40,1536]{2,1,0:T(8,128)(2,1)S(1)} %collective-permute-done.18.refs_1_, ...), custom_call_target="tpu_custom_call" | custom-call | flops 1509949440 | bytes 9437184 | tf_op jit(solution)/shard_map/project_1/pallas_call | solution.py:309
  86.6 8.7 %project_2.1 = (bf16[2,160,1536]{2,1,0:T(8,128)(2,1)S(1)}, bf16[2,2,40,1536]{3,2,1,0:T(8,128)(2,1)S(1)}, bf16[2,2,40,1536]{3,2,1,0:T(8,128)(2,1)S(1)}) custom-call(s32[2]{0:T(128)S(1)} %pad_add_fusion.place, bf16[2,6144,1536]{2,1,0:T(8,128)(2,1)} %up.11, bf16[2,1536,6144]{2,1,0:T(8,128)(2,1)} %weights.5, ...), custom_call_target="tpu_custom_call" | custom-call | flops 4529848320 | bytes 28311552 | tf_op jit(solution)/shard_map/project_2/pallas_call | solution.py:309
  95.3 2.0 %collective-permute-start.22 = (bf16[2,2,40,1536]{3,2,1,0:T(8,128)(2,1)S(1)}, bf16[2,2,40,1536]{3,2,1,0:T(8,128)(2,1)S(1)}, u32[]{:S(2)}, u32[]{:S(2)}) collective-permute-start(bf16[2,2,40,1536]{3,2,1,0:T(8,128)(2,1)S(1)} %get-tuple-element.77), channel_id=1, source_target_pairs={{0,16},{8,24},{16,0},{24,8},{1,17},{9,25},{17,1},{25,9},{2,18},{10... | collective-permute-start | bytes 1474568 | tf_op jit(solution)/shard_map/ppermute | solution.py:27
  97.3 5.2 %down_2.1 = (bf16[2,2,40,1536]{3,2,1,0:T(8,128)(2,1)S(1)}, bf16[2,2,40,1536]{3,2,1,0:T(8,128)(2,1)S(1)}) custom-call(s32[2]{0:T(128)S(1)} %pad_add_fusion.place, bf16[2,1536,6144]{2,1,0:T(8,128)(2,1)} %weights.5, bf16[2,160,1536]{2,1,0:T(8,128)(2,1)S(1)} %get-tuple-element.84.hidden), custom_call_target="tpu_custom_call" | custom-call | flops 1509949440 | bytes 9437184 | tf_op jit(solution)/shard_map/down_2/pallas_call | solution.py:364
  102.7 5.0 %down_1.1 = (bf16[2,2,40,1536]{3,2,1,0:T(8,128)(2,1)S(1)}, bf16[2,2,40,1536]{3,2,1,0:T(8,128)(2,1)S(1)}) custom-call(s32[2]{0:T(128)S(1)} %pad_add_fusion.place, bf16[2,1536,6144]{2,1,0:T(8,128)(2,1)} %weights.5, bf16[2,160,1536]{2,1,0:T(8,128)(2,1)S(1)} %get-tuple-element.84.hidden), custom_call_target="tpu_custom_call" | custom-call | flops 1509949440 | bytes 9437184 | tf_op jit(solution)/shard_map/down_1/pallas_call | solution.py:364
  107.7 2.0 %collective-permute-start.26 = (bf16[2,2,40,1536]{3,2,1,0:T(8,128)(2,1)S(1)}, bf16[2,2,40,1536]{3,2,1,0:T(8,128)(2,1)S(1)}, u32[]{:S(2)}, u32[]{:S(2)}) collective-permute-start(bf16[2,2,40,1536]{3,2,1,0:T(8,128)(2,1)S(1)} %get-tuple-element.81), channel_id=1, source_target_pairs={{0,16},{8,24},{16,0},{24,8},{1,17},{9,25},{17,1},{25,9},{2,18},{10... | collective-permute-start | bytes 1474568 | tf_op jit(solution)/shard_map/ppermute | solution.py:27
  110.0 5.0 %down_0.1 = (bf16[2,2,40,1536]{3,2,1,0:T(8,128)(2,1)S(1)}, bf16[2,2,40,1536]{3,2,1,0:T(8,128)(2,1)S(1)}) custom-call(s32[2]{0:T(128)S(1)} %pad_add_fusion.place, bf16[2,1536,6144]{2,1,0:T(8,128)(2,1)} %weights.5, bf16[2,160,1536]{2,1,0:T(8,128)(2,1)S(1)} %get-tuple-element.84.hidden), custom_call_target="tpu_custom_call" | custom-call | flops 1509949440 | bytes 9437184 | tf_op jit(solution)/shard_map/down_0/pallas_call | solution.py:364
  115.1 2.0 %collective-permute-start.23 = (bf16[2,2,40,1536]{3,2,1,0:T(8,128)(2,1)S(1)}, bf16[2,2,40,1536]{3,2,1,0:T(8,128)(2,1)S(1)}, u32[]{:S(2)}, u32[]{:S(2)}) collective-permute-start(bf16[2,2,40,1536]{3,2,1,0:T(8,128)(2,1)S(1)} %get-tuple-element.86), channel_id=1, source_target_pairs={{0,8},{8,0},{16,24},{24,16},{1,9},{9,1},{17,25},{25,17},{2,10},{10... | collective-permute-start | bytes 1474568 | tf_op jit(solution)/shard_map/ppermute | solution.py:27
  117.3 4.2 %collective-permute-done.27.got = bf16[1,2,40,1536]{3,2,1,0:T(8,128)(2,1)S(1)} collective-permute-done((bf16[1,2,40,1536]{3,2,1,0:T(8,128)(2,1)S(1)}, bf16[1,2,40,1536]{3,2,1,0:T(8,128)(2,1)S(1)}, u32[]{:S(2)}, u32[]{:S(2)}) %collective-permute-start.27) | collective-permute-done | bytes 245792 | tf_op jit(solution)/shard_map/ppermute | solution.py:27
  121.9 2.8 %collective-permute-start.30 = (bf16[2,40,1536]{2,1,0:T(8,128)(2,1)S(1)}, bf16[2,40,1536]{2,1,0:T(8,128)(2,1)S(1)}, u32[]{:S(2)}, u32[]{:S(2)}) collective-permute-start(bf16[2,40,1536]{2,1,0:T(8,128)(2,1)S(1)} %reply.4), channel_id=1, source_target_pairs={{0,6},{1,7},{2,4},{3,5},{4,2},{5,3},{6,0},{7,1},{8,14},{9,15},{10,... | collective-permute-start | bytes 737288 | tf_op jit(solution)/shard_map/ppermute | solution.py:27
  124.8 2.5 %collective-permute-start.31 = (bf16[2,40,1536]{2,1,0:T(8,128)(2,1)S(1)}, bf16[2,40,1536]{2,1,0:T(8,128)(2,1)S(1)}, u32[]{:S(2)}, u32[]{:S(2)}) collective-permute-start(bf16[2,40,1536]{2,1,0:T(8,128)(2,1)S(1)} %reply.5), channel_id=1, source_target_pairs={{0,4},{1,5},{2,6},{3,7},{4,0},{5,1},{6,2},{7,3},{8,12},{9,13},{10,... | collective-permute-start | bytes 737288 | tf_op jit(solution)/shard_map/ppermute | solution.py:27
  127.3 2.4 %collective-permute-done.23.got = bf16[2,2,40,1536]{3,2,1,0:T(8,128)(2,1)S(1)} collective-permute-done((bf16[2,2,40,1536]{3,2,1,0:T(8,128)(2,1)S(1)}, bf16[2,2,40,1536]{3,2,1,0:T(8,128)(2,1)S(1)}, u32[]{:S(2)}, u32[]{:S(2)}) %collective-permute-start.23) | collective-permute-done | bytes 491552 | tf_op jit(solution)/shard_map/ppermute | solution.py:27
  130.1 2.2 %collective-permute-done.29.got = bf16[1,2,40,1536]{3,2,1,0:T(8,128)(2,1)S(1)} collective-permute-done((bf16[1,2,40,1536]{3,2,1,0:T(8,128)(2,1)S(1)}, bf16[1,2,40,1536]{3,2,1,0:T(8,128)(2,1)S(1)}, u32[]{:S(2)}, u32[]{:S(2)}) %collective-permute-start.29) | collective-permute-done | bytes 245792 | tf_op jit(solution)/shard_map/ppermute | solution.py:27
  132.4 5.0 %collective-permute-start.32 = (bf16[2,40,1536]{2,1,0:T(8,128)(2,1)S(1)}, bf16[2,40,1536]{2,1,0:T(8,128)(2,1)S(1)}, u32[]{:S(2)}, u32[]{:S(2)}) collective-permute-start(bf16[2,40,1536]{2,1,0:T(8,128)(2,1)S(1)} %reply.6), channel_id=1, source_target_pairs={{0,2},{1,3},{2,0},{3,1},{4,6},{5,7},{6,4},{7,5},{8,10},{9,11},{10,... | collective-permute-start | bytes 737288 | tf_op jit(solution)/shard_map/ppermute | solution.py:27
  137.4 1.9 %collective-permute-done.31.refs_2_ = bf16[2,40,1536]{2,1,0:T(8,128)(2,1)S(1)} collective-permute-done((bf16[2,40,1536]{2,1,0:T(8,128)(2,1)S(1)}, bf16[2,40,1536]{2,1,0:T(8,128)(2,1)S(1)}, u32[]{:S(2)}, u32[]{:S(2)}) %collective-permute-start.31) | collective-permute-done | bytes 245792 | tf_op jit(solution)/shard_map/ppermute | solution.py:27
  139.5 2.5 %collective-permute-done.32.refs_1_ = bf16[2,40,1536]{2,1,0:T(8,128)(2,1)S(1)} collective-permute-done((bf16[2,40,1536]{2,1,0:T(8,128)(2,1)S(1)}, bf16[2,40,1536]{2,1,0:T(8,128)(2,1)S(1)}, u32[]{:S(2)}, u32[]{:S(2)}) %collective-permute-start.32) | collective-permute-done | bytes 245792 | tf_op jit(solution)/shard_map/ppermute | solution.py:27
  142.6 1.7 %collective-permute-done.33 = bf16[256,768]{1,0:T(8,128)(2,1)S(1)} collective-permute-done((bf16[256,768]{1,0:T(8,128)(2,1)S(1)}, bf16[256,768]{1,0:T(8,128)(2,1)S(1)}, u32[]{:S(2)}, u32[]{:S(2)}) %collective-permute-start.33) | collective-permute-done | bytes 393248 | tf_op jit(solution)/shard_map/ppermute | solution.py:27
  144.3 0.8 add_convert_fusion
  (81 shorter events, 8.5 us)
Async XLA Ops:
  4.8 19.5 %collective-permute-start.1 = (f32[2,12,1,1]{1,0,3,2:T(2,128)S(1)}, f32[2,12,1,1]{1,0,3,2:T(2,128)S(1)}, u32[]{:S(2)}, u32[]{:S(2)}) collective-permute-start(f32[2,12,1,1]{1,0,3,2:T(2,128)S(1)} %exp.14), channel_id=1, source_target_pairs={{0,8},{8,0},{16,24},{24,16},{1,9},{9,1},{17,25},{25,17},{2,10},{10... | collective-permute-start | bytes 296 | tf_op jit(solution)/shard_map/ppermute | solution.py:27
  7.8 18.1 %collective-permute-start.3 = (f32[2,12,1,1]{1,0,3,2:T(2,128)S(1)}, f32[2,12,1,1]{1,0,3,2:T(2,128)S(1)}, u32[]{:S(2)}, u32[]{:S(2)}) collective-permute-start(f32[2,12,1,1]{1,0,3,2:T(2,128)S(1)} %exp.14), channel_id=1, source_target_pairs={{0,24},{8,16},{16,8},{24,0},{1,25},{9,17},{17,9},{25,1},{2,26},{10... | collective-permute-start | bytes 296 | tf_op jit(solution)/shard_map/ppermute | solution.py:27
  9.3 16.7 %collective-permute-start.4 = (bf16[12,128,128]{2,1,0:T(8,128)(2,1)}, bf16[12,128,128]{2,1,0:T(8,128)(2,1)S(1)}, u32[]{:S(2)}, u32[]{:S(2)}) collective-permute-start(bf16[12,128,128]{2,1,0:T(8,128)(2,1)} %get-tuple-element.59), channel_id=1, source_target_pairs={{0,16},{8,24},{1,17},{9,25},{2,18},{10,26},{3,19},{11,27},{4,20},{... | collective-permute-start | bytes 1179656 | tf_op jit(solution)/shard_map/ppermute | solution.py:27
  11.2 13.1 %collective-permute-start = (bf16[12,128,128]{2,1,0:T(8,128)(2,1)}, bf16[12,128,128]{2,1,0:T(8,128)(2,1)S(1)}, u32[]{:S(2)}, u32[]{:S(2)}) collective-permute-start(bf16[12,128,128]{2,1,0:T(8,128)(2,1)} %get-tuple-element.55), channel_id=1, source_target_pairs={{0,8},{8,0},{16,24},{1,9},{9,1},{17,25},{2,10},{10,2},{18,26},{3,1... | collective-permute-start | bytes 1179656 | tf_op jit(solution)/shard_map/ppermute | solution.py:27
  15.6 1.0 copy-start
  16.6 1.0 copy-start.2
  17.6 1.0 copy-start.3
  18.6 0.7 copy-start.4
  19.3 0.7 copy-start.7
  20.0 4.3 %copy-start.9 = (bf16[12,128,128]{2,1,0:T(8,128)(2,1)S(1)}, bf16[12,128,128]{2,1,0:T(8,128)(2,1)}, u32[]{:S(2)}) copy-start(bf16[12,128,128]{2,1,0:T(8,128)(2,1)} %get-tuple-element.55) | copy-start | bytes 1179652
  20.0 5.9 %copy-start.8 = (bf16[12,128,128]{2,1,0:T(8,128)(2,1)S(1)}, bf16[12,128,128]{2,1,0:T(8,128)(2,1)}, u32[]{:S(2)}) copy-start(bf16[12,128,128]{2,1,0:T(8,128)(2,1)} %get-tuple-element.59) | copy-start | bytes 1179652
  20.0 9.5 %copy-start.10 = (f32[768]{0:T(1024)S(1)}, f32[768]{0:T(1024)}, u32[]{:S(2)}) copy-start(f32[768]{0:T(1024)} %param.13) | copy-start | bytes 9220
  24.6 10.8 %collective-permute-start.2 = (bf16[12,128,128]{2,1,0:T(8,128)(2,1)S(1)}, bf16[12,128,128]{2,1,0:T(8,128)(2,1)S(1)}, u32[]{:S(2)}, u32[]{:S(2)}) collective-permute-start(bf16[12,128,128]{2,1,0:T(8,128)(2,1)S(1)} %fusion.3), channel_id=1, source_target_pairs={{0,16},{8,24},{1,17},{9,25},{2,18},{10,26},{3,19},{11,27},{4,20},{... | collective-permute-start | bytes 1179656 | tf_op jit(solution)/shard_map/ppermute | solution.py:27
  26.2 9.7 %collective-permute-start.5 = (bf16[12,128,128]{2,1,0:T(8,128)(2,1)S(1)}, bf16[12,128,128]{2,1,0:T(8,128)(2,1)S(1)}, u32[]{:S(2)}, u32[]{:S(2)}) collective-permute-start(bf16[12,128,128]{2,1,0:T(8,128)(2,1)S(1)} %fusion.5), channel_id=1, source_target_pairs={{0,8},{16,24},{24,16},{1,9},{17,25},{25,17},{2,10},{18,26},{26,18}... | collective-permute-start | bytes 1179656 | tf_op jit(solution)/shard_map/ppermute | solution.py:27
  29.5 6.6 %copy-start.1 = (bf16[4,64,768]{2,1,0:T(8,128)(2,1)S(1)}, bf16[4,64,768]{2,1,0:T(8,128)(2,1)}, u32[]{:S(2)}) copy-start(bf16[4,64,768]{2,1,0:T(8,128)(2,1)} %refs_0_.3) | copy-start | bytes 1179652
  29.5 6.6 %copy-start.5 = (f32[4,64,6]{1,0,2:T(4,128)S(1)}, f32[4,64,6]{1,0,2:T(4,128)}, u32[]{:S(2)}) copy-start(f32[4,64,6]{1,0,2:T(4,128)} %param.12) | copy-start | bytes 18436
  36.1 33.4 %copy-start.6 = (bf16[6144,16]{0,1:T(8,128)(2,1)S(1)}, bf16[6144,16]{0,1:T(8,128)(2,1)}, u32[]{:S(2)}) copy-start(bf16[6144,16]{0,1:T(8,128)(2,1)} %param.14) | copy-start | bytes 589828
  38.7 1.8 %collective-permute-start.6 = (bf16[256,768]{1,0:T(8,128)(2,1)S(1)}, bf16[256,768]{1,0:T(8,128)(2,1)S(1)}, u32[]{:S(2)}, u32[]{:S(2)}) collective-permute-start(bf16[256,768]{1,0:T(8,128)(2,1)S(1)} %normed.1.refs_0_), channel_id=1, source_target_pairs={{0,1},{1,0},{2,3},{3,2},{4,5},{5,4},{6,7},{7,6},{8,9},{9,8},{10,11... | collective-permute-start | bytes 1179656 | tf_op jit(solution)/shard_map/ppermute | solution.py:27
  41.0 8.8 %collective-permute-start.16 = (bf16[2,40,1536]{2,1,0:T(8,128)(2,1)S(1)}, bf16[2,40,1536]{2,1,0:T(8,128)(2,1)S(1)}, u32[]{:S(2)}, u32[]{:S(2)}) collective-permute-start(bf16[2,40,1536]{2,1,0:T(8,128)(2,1)S(1)} %get-tuple-element.68.refs_0_), channel_id=1, source_target_pairs={{0,8},{8,0},{16,24},{24,16},{1,9},{9,1},{17,25},{25,17},{2,10},{10... | collective-permute-start | bytes 737288 | tf_op jit(solution)/shard_map/ppermute | solution.py:27
  43.5 7.7 %collective-permute-start.17 = (bf16[2,40,1536]{2,1,0:T(8,128)(2,1)S(1)}, bf16[2,40,1536]{2,1,0:T(8,128)(2,1)S(1)}, u32[]{:S(2)}, u32[]{:S(2)}) collective-permute-start(bf16[2,40,1536]{2,1,0:T(8,128)(2,1)S(1)} %get-tuple-element.68.refs_0_), channel_id=1, source_target_pairs={{0,16},{8,24},{16,0},{24,8},{1,17},{9,25},{17,1},{25,9},{2,18},{10... | collective-permute-start | bytes 737288 | tf_op jit(solution)/shard_map/ppermute | solution.py:27
  43.5 12.2 %collective-permute-start.7 = (bf16[2,40,1536]{2,1,0:T(8,128)(2,1)S(1)}, bf16[2,40,1536]{2,1,0:T(8,128)(2,1)S(1)}, u32[]{:S(2)}, u32[]{:S(2)}) collective-permute-start(bf16[2,40,1536]{2,1,0:T(8,128)(2,1)S(1)} %get-tuple-element.69), channel_id=1, source_target_pairs={{0,2},{1,3},{2,0},{3,1},{4,6},{5,7},{6,4},{7,5},{8,10},{9,11},{10,... | collective-permute-start | bytes 737288 | tf_op jit(solution)/shard_map/ppermute | solution.py:27
  45.1 20.3 %collective-permute-start.8 = (bf16[2,40,1536]{2,1,0:T(8,128)(2,1)S(1)}, bf16[2,40,1536]{2,1,0:T(8,128)(2,1)S(1)}, u32[]{:S(2)}, u32[]{:S(2)}) collective-permute-start(bf16[2,40,1536]{2,1,0:T(8,128)(2,1)S(1)} %get-tuple-element.70), channel_id=1, source_target_pairs={{0,4},{1,5},{2,6},{3,7},{4,0},{5,1},{6,2},{7,3},{8,12},{9,13},{10,... | collective-permute-start | bytes 737288 | tf_op jit(solution)/shard_map/ppermute | solution.py:27
  47.7 18.8 %collective-permute-start.9 = (bf16[2,40,1536]{2,1,0:T(8,128)(2,1)S(1)}, bf16[2,40,1536]{2,1,0:T(8,128)(2,1)S(1)}, u32[]{:S(2)}, u32[]{:S(2)}) collective-permute-start(bf16[2,40,1536]{2,1,0:T(8,128)(2,1)S(1)} %get-tuple-element.71), channel_id=1, source_target_pairs={{0,6},{1,7},{2,4},{3,5},{4,2},{5,3},{6,0},{7,1},{8,14},{9,15},{10,... | collective-permute-start | bytes 737288 | tf_op jit(solution)/shard_map/ppermute | solution.py:27
  55.7 11.8 %collective-permute-start.19 = (bf16[2,40,1536]{2,1,0:T(8,128)(2,1)S(1)}, bf16[2,40,1536]{2,1,0:T(8,128)(2,1)S(1)}, u32[]{:S(2)}, u32[]{:S(2)}) collective-permute-start(bf16[2,40,1536]{2,1,0:T(8,128)(2,1)S(1)} %collective-permute-done.7.refs_1_.refs_0_), channel_id=1, source_target_pairs={{0,16},{8,24},{16,0},{24,8},{1,17},{9,25},{17,1},{25,9},{2,18},{10... | collective-permute-start | bytes 737288 | tf_op jit(solution)/shard_map/ppermute | solution.py:27
  57.3 13.2 %collective-permute-start.21 = (bf16[2,40,1536]{2,1,0:T(8,128)(2,1)S(1)}, bf16[2,40,1536]{2,1,0:T(8,128)(2,1)S(1)}, u32[]{:S(2)}, u32[]{:S(2)}) collective-permute-start(bf16[2,40,1536]{2,1,0:T(8,128)(2,1)S(1)} %collective-permute-done.16.refs_1_), channel_id=1, source_target_pairs={{0,16},{8,24},{16,0},{24,8},{1,17},{9,25},{17,1},{25,9},{2,18},{10... | collective-permute-start | bytes 737288 | tf_op jit(solution)/shard_map/ppermute | solution.py:27
  57.8 13.1 %collective-permute-start.18 = (bf16[2,40,1536]{2,1,0:T(8,128)(2,1)S(1)}, bf16[2,40,1536]{2,1,0:T(8,128)(2,1)S(1)}, u32[]{:S(2)}, u32[]{:S(2)}) collective-permute-start(bf16[2,40,1536]{2,1,0:T(8,128)(2,1)S(1)} %collective-permute-done.7.refs_1_.refs_0_), channel_id=1, source_target_pairs={{0,8},{8,0},{16,24},{24,16},{1,9},{9,1},{17,25},{25,17},{2,10},{10... | collective-permute-start | bytes 737288 | tf_op jit(solution)/shard_map/ppermute | solution.py:27
  65.4 8.9 %collective-permute-start.10 = (bf16[2,40,1536]{2,1,0:T(8,128)(2,1)S(1)}, bf16[2,40,1536]{2,1,0:T(8,128)(2,1)S(1)}, u32[]{:S(2)}, u32[]{:S(2)}) collective-permute-start(bf16[2,40,1536]{2,1,0:T(8,128)(2,1)S(1)} %collective-permute-done.8.refs_2_.refs_0_), channel_id=1, source_target_pairs={{0,8},{8,0},{16,24},{24,16},{1,9},{9,1},{17,25},{25,17},{2,10},{10... | collective-permute-start | bytes 737288 | tf_op jit(solution)/shard_map/ppermute | solution.py:27
  66.5 9.8 %collective-permute-start.14 = (bf16[2,40,1536]{2,1,0:T(8,128)(2,1)S(1)}, bf16[2,40,1536]{2,1,0:T(8,128)(2,1)S(1)}, u32[]{:S(2)}, u32[]{:S(2)}) collective-permute-start(bf16[2,40,1536]{2,1,0:T(8,128)(2,1)S(1)} %collective-permute-done.9.refs_3_.refs_4_), channel_id=1, source_target_pairs={{0,16},{8,24},{16,0},{24,8},{1,17},{9,25},{17,1},{25,9},{2,18},{10... | collective-permute-start | bytes 737288 | tf_op jit(solution)/shard_map/ppermute | solution.py:27
  67.5 14.2 %collective-permute-start.20 = (bf16[2,40,1536]{2,1,0:T(8,128)(2,1)S(1)}, bf16[2,40,1536]{2,1,0:T(8,128)(2,1)S(1)}, u32[]{:S(2)}, u32[]{:S(2)}) collective-permute-start(bf16[2,40,1536]{2,1,0:T(8,128)(2,1)S(1)} %collective-permute-done.19.refs_2_), channel_id=1, source_target_pairs={{0,8},{8,0},{16,24},{24,16},{1,9},{9,1},{17,25},{25,17},{2,10},{10... | collective-permute-start | bytes 737288 | tf_op jit(solution)/shard_map/ppermute | solution.py:27
  70.6 16.0 %collective-permute-start.11 = (bf16[2,40,1536]{2,1,0:T(8,128)(2,1)S(1)}, bf16[2,40,1536]{2,1,0:T(8,128)(2,1)S(1)}, u32[]{:S(2)}, u32[]{:S(2)}) collective-permute-start(bf16[2,40,1536]{2,1,0:T(8,128)(2,1)S(1)} %collective-permute-done.8.refs_2_.refs_0_), channel_id=1, source_target_pairs={{0,16},{8,24},{16,0},{24,8},{1,17},{9,25},{17,1},{25,9},{2,18},{10... | collective-permute-start | bytes 737288 | tf_op jit(solution)/shard_map/ppermute | solution.py:27
  70.8 15.8 %collective-permute-start.13 = (bf16[2,40,1536]{2,1,0:T(8,128)(2,1)S(1)}, bf16[2,40,1536]{2,1,0:T(8,128)(2,1)S(1)}, u32[]{:S(2)}, u32[]{:S(2)}) collective-permute-start(bf16[2,40,1536]{2,1,0:T(8,128)(2,1)S(1)} %collective-permute-done.9.refs_3_.refs_4_), channel_id=1, source_target_pairs={{0,8},{8,0},{16,24},{24,16},{1,9},{9,1},{17,25},{25,17},{2,10},{10... | collective-permute-start | bytes 737288 | tf_op jit(solution)/shard_map/ppermute | solution.py:27
  74.3 12.3 %collective-permute-start.12 = (bf16[2,40,1536]{2,1,0:T(8,128)(2,1)S(1)}, bf16[2,40,1536]{2,1,0:T(8,128)(2,1)S(1)}, u32[]{:S(2)}, u32[]{:S(2)}) collective-permute-start(bf16[2,40,1536]{2,1,0:T(8,128)(2,1)S(1)} %collective-permute-done.10.refs_1_), channel_id=1, source_target_pairs={{0,16},{8,24},{16,0},{24,8},{1,17},{9,25},{17,1},{25,9},{2,18},{10... | collective-permute-start | bytes 737288 | tf_op jit(solution)/shard_map/ppermute | solution.py:27
  76.3 10.3 %collective-permute-start.15 = (bf16[2,40,1536]{2,1,0:T(8,128)(2,1)S(1)}, bf16[2,40,1536]{2,1,0:T(8,128)(2,1)S(1)}, u32[]{:S(2)}, u32[]{:S(2)}) collective-permute-start(bf16[2,40,1536]{2,1,0:T(8,128)(2,1)S(1)} %collective-permute-done.14.refs_6_), channel_id=1, source_target_pairs={{0,8},{8,0},{16,24},{24,16},{1,9},{9,1},{17,25},{25,17},{2,10},{10... | collective-permute-start | bytes 737288 | tf_op jit(solution)/shard_map/ppermute | solution.py:27
  95.3 14.5 %collective-permute-start.22 = (bf16[2,2,40,1536]{3,2,1,0:T(8,128)(2,1)S(1)}, bf16[2,2,40,1536]{3,2,1,0:T(8,128)(2,1)S(1)}, u32[]{:S(2)}, u32[]{:S(2)}) collective-permute-start(bf16[2,2,40,1536]{3,2,1,0:T(8,128)(2,1)S(1)} %get-tuple-element.77), channel_id=1, source_target_pairs={{0,16},{8,24},{16,0},{24,8},{1,17},{9,25},{17,1},{25,9},{2,18},{10... | collective-permute-start | bytes 1474568 | tf_op jit(solution)/shard_map/ppermute | solution.py:27
  102.5 14.5 %collective-permute-start.24 = (bf16[2,2,40,1536]{3,2,1,0:T(8,128)(2,1)S(1)}, bf16[2,2,40,1536]{3,2,1,0:T(8,128)(2,1)S(1)}, u32[]{:S(2)}, u32[]{:S(2)}) collective-permute-start(bf16[2,2,40,1536]{3,2,1,0:T(8,128)(2,1)S(1)} %get-tuple-element.79), channel_id=1, source_target_pairs={{0,8},{8,0},{16,24},{24,16},{1,9},{9,1},{17,25},{25,17},{2,10},{10... | collective-permute-start | bytes 1474568 | tf_op jit(solution)/shard_map/ppermute | solution.py:27
  107.7 13.9 %collective-permute-start.26 = (bf16[2,2,40,1536]{3,2,1,0:T(8,128)(2,1)S(1)}, bf16[2,2,40,1536]{3,2,1,0:T(8,128)(2,1)S(1)}, u32[]{:S(2)}, u32[]{:S(2)}) collective-permute-start(bf16[2,2,40,1536]{3,2,1,0:T(8,128)(2,1)S(1)} %get-tuple-element.81), channel_id=1, source_target_pairs={{0,16},{8,24},{16,0},{24,8},{1,17},{9,25},{17,1},{25,9},{2,18},{10... | collective-permute-start | bytes 1474568 | tf_op jit(solution)/shard_map/ppermute | solution.py:27
  109.9 11.7 %collective-permute-start.27 = (bf16[1,2,40,1536]{3,2,1,0:T(8,128)(2,1)S(1)}, bf16[1,2,40,1536]{3,2,1,0:T(8,128)(2,1)S(1)}, u32[]{:S(2)}, u32[]{:S(2)}) collective-permute-start(bf16[1,2,40,1536]{3,2,1,0:T(8,128)(2,1)S(1)} %get-tuple-element.83), channel_id=1, source_target_pairs={{0,8},{8,0},{16,24},{24,16},{1,9},{9,1},{17,25},{25,17},{2,10},{10... | collective-permute-start | bytes 737288 | tf_op jit(solution)/shard_map/ppermute | solution.py:27
  115.1 14.6 %collective-permute-start.23 = (bf16[2,2,40,1536]{3,2,1,0:T(8,128)(2,1)S(1)}, bf16[2,2,40,1536]{3,2,1,0:T(8,128)(2,1)S(1)}, u32[]{:S(2)}, u32[]{:S(2)}) collective-permute-start(bf16[2,2,40,1536]{3,2,1,0:T(8,128)(2,1)S(1)} %get-tuple-element.86), channel_id=1, source_target_pairs={{0,8},{8,0},{16,24},{24,16},{1,9},{9,1},{17,25},{25,17},{2,10},{10... | collective-permute-start | bytes 1474568 | tf_op jit(solution)/shard_map/ppermute | solution.py:27
  117.2 7.5 %collective-permute-start.25 = (bf16[1,2,40,1536]{3,2,1,0:T(8,128)(2,1)S(1)}, bf16[1,2,40,1536]{3,2,1,0:T(8,128)(2,1)S(1)}, u32[]{:S(2)}, u32[]{:S(2)}) collective-permute-start(bf16[1,2,40,1536]{3,2,1,0:T(8,128)(2,1)S(1)} %get-tuple-element.90), channel_id=1, source_target_pairs={{0,16},{8,24},{16,0},{24,8},{1,17},{9,25},{17,1},{25,9},{2,18},{10... | collective-permute-start | bytes 737288 | tf_op jit(solution)/shard_map/ppermute | solution.py:27
  121.8 10.5 %collective-permute-start.29 = (bf16[1,2,40,1536]{3,2,1,0:T(8,128)(2,1)S(1)}, bf16[1,2,40,1536]{3,2,1,0:T(8,128)(2,1)S(1)}, u32[]{:S(2)}, u32[]{:S(2)}) collective-permute-start(bf16[1,2,40,1536]{3,2,1,0:T(8,128)(2,1)S(1)} %get-tuple-element.95), channel_id=1, source_target_pairs={{0,8},{8,0},{16,24},{24,16},{1,9},{9,1},{17,25},{25,17},{2,10},{10... | collective-permute-start | bytes 737288 | tf_op jit(solution)/shard_map/ppermute | solution.py:27
  121.9 10.5 %collective-permute-start.30 = (bf16[2,40,1536]{2,1,0:T(8,128)(2,1)S(1)}, bf16[2,40,1536]{2,1,0:T(8,128)(2,1)S(1)}, u32[]{:S(2)}, u32[]{:S(2)}) collective-permute-start(bf16[2,40,1536]{2,1,0:T(8,128)(2,1)S(1)} %reply.4), channel_id=1, source_target_pairs={{0,6},{1,7},{2,4},{3,5},{4,2},{5,3},{6,0},{7,1},{8,14},{9,15},{10,... | collective-permute-start | bytes 737288 | tf_op jit(solution)/shard_map/ppermute | solution.py:27
  124.8 14.6 %collective-permute-start.31 = (bf16[2,40,1536]{2,1,0:T(8,128)(2,1)S(1)}, bf16[2,40,1536]{2,1,0:T(8,128)(2,1)S(1)}, u32[]{:S(2)}, u32[]{:S(2)}) collective-permute-start(bf16[2,40,1536]{2,1,0:T(8,128)(2,1)S(1)} %reply.5), channel_id=1, source_target_pairs={{0,4},{1,5},{2,6},{3,7},{4,0},{5,1},{6,2},{7,3},{8,12},{9,13},{10,... | collective-permute-start | bytes 737288 | tf_op jit(solution)/shard_map/ppermute | solution.py:27
  129.8 9.5 %collective-permute-start.28 = (bf16[1,2,40,1536]{3,2,1,0:T(8,128)(2,1)S(1)}, bf16[1,2,40,1536]{3,2,1,0:T(8,128)(2,1)S(1)}, u32[]{:S(2)}, u32[]{:S(2)}) collective-permute-start(bf16[1,2,40,1536]{3,2,1,0:T(8,128)(2,1)S(1)} %get-tuple-element.99), channel_id=1, source_target_pairs={{0,16},{8,24},{16,0},{24,8},{1,17},{9,25},{17,1},{25,9},{2,18},{10... | collective-permute-start | bytes 737288 | tf_op jit(solution)/shard_map/ppermute | solution.py:27
  132.4 9.5 %collective-permute-start.32 = (bf16[2,40,1536]{2,1,0:T(8,128)(2,1)S(1)}, bf16[2,40,1536]{2,1,0:T(8,128)(2,1)S(1)}, u32[]{:S(2)}, u32[]{:S(2)}) collective-permute-start(bf16[2,40,1536]{2,1,0:T(8,128)(2,1)S(1)} %reply.6), channel_id=1, source_target_pairs={{0,2},{1,3},{2,0},{3,1},{4,6},{5,7},{6,4},{7,5},{8,10},{9,11},{10,... | collective-permute-start | bytes 737288 | tf_op jit(solution)/shard_map/ppermute | solution.py:27
  142.5 1.8 %collective-permute-start.33 = (bf16[256,768]{1,0:T(8,128)(2,1)S(1)}, bf16[256,768]{1,0:T(8,128)(2,1)S(1)}, u32[]{:S(2)}, u32[]{:S(2)}) collective-permute-start(bf16[256,768]{1,0:T(8,128)(2,1)S(1)} %get-tuple-element.104), channel_id=1, source_target_pairs={{0,1},{1,0},{2,3},{3,2},{4,5},{5,4},{6,7},{7,6},{8,9},{9,8},{10,11... | collective-permute-start | bytes 1179656 | tf_op jit(solution)/shard_map/ppermute | solution.py:27

commit v7 on v6

--- a/solution.py
+++ b/solution.py
@@ -135,14 +135,28 @@
             ).astype(BF16)
 
 
-def inside_kernel(place, queries, keys, values, log_decay, ids, inside, placement, other):
+def inside_kernel(place, queries, keys, values, log_decay, ids, inside, placement, other, *scratch):
+    sources, buffers, sems = (queries, keys, values), scratch[:3], scratch[3]
     requests, length, features = keys.shape
     heads = log_decay.shape[0] // requests
     dim = features // heads
+    copies = []
+    for r in range(requests):
+        mine = [
+            pltpu.make_async_copy(source.at[r], buffer.at[r], sems.at[i, r])
+            for i, (source, buffer) in enumerate(zip(sources, buffers))
+        ]
+        for copy in mine:
+            copy.start()
+        copies.append(mine)
+    place_tokens(place, ids, placement, other, requests, length)
+    queries, keys, values = buffers
     causal = iota((length, length), 0) >= iota((length, length), 1)
     cum = running_sum(log_decay[...])
     rows = running_sum_rows(log_decay[...])
     for r in range(requests):
+        for copy in copies[r]:
+            copy.wait()
         for h in range(heads):
             lanes = slice(h * dim, (h + 1) * dim)
             at = h * requests + r
@@ -150,6 +164,9 @@
             mask = jnp.where(causal, jnp.exp(jnp.minimum(spread, 0.0)), 0.0)
             scores = dot(queries[r, :, lanes], keys[r, :, lanes], 1, 1)
             inside[r, :, lanes] = dot((scores * mask).astype(BF16), values[r, :, lanes])
+
+
+def place_tokens(place, ids, placement, other, requests, length):
     slots, tokens = placement.shape
     experts = slots // CAP
     own = other.shape[0] // CAP
@@ -462,8 +479,8 @@
 
 def prefix_of_four(states, decay, me, beside_first, beside_last):
     high, low = (me & 2) != 0, (me & 1) != 0
-    near = swap(decay, "ctx", 4, 1)
-    far = swap(decay, "ctx", 4, 3)
+    near = swap(decay, "ctx", 4, 1, lambda i: i in (1, 2))
+    far = swap(decay, "ctx", 4, 3, lambda i: i == 1)
     one, two = states
     first = beside_first(one)
     got_one = after(swap(one, "ctx", 4, 1, lambda i: i != 3), *first).astype(F32)
@@ -517,20 +534,26 @@
     part = {}
 
     def beside_first(token):
-        part["inside"], _ = call_with_held(
+        part["inside"] = pl.pallas_call(
             inside_kernel,
-            [],
-            chunks,
-            after(place, token),
-            expert_up,
-            expert_down,
-            [queries, keys, values, decay_rows, jnp.transpose(expert_ids, (1, 2, 0))],
-            [
+            in_specs=[SMEM] + [ANY] * 3 + [VMEM] * 2,
+            out_specs=[VMEM] * 3,
+            out_shape=[
                 struct((requests, length, features), F32),
                 struct((chunks * own * CAP, tokens), BF16),
                 struct((own * CAP, 128), jnp.int32),
             ],
-            "inside_and_placement",
+            scratch_shapes=[pltpu.VMEM(keys.shape, BF16)] * 3
+            + [pltpu.SemaphoreType.DMA((3, requests))],
+            compiler_params=params(56),
+            name="inside_and_placement",
+        )(
+            after(place, token),
+            queries,
+            keys,
+            values,
+            decay_rows,
+            jnp.transpose(expert_ids, (1, 2, 0)),
         )
         return part["inside"][:1]
 
@@ -629,7 +652,7 @@
         if i >= 3:
             k = order[i - 3]
             kept, got = open_sums[k]
-            early = [returned[order[i - 5]]] if i >= 5 else []
+            early = [returned[m] for m in order[:-2]] if i == chunks + 2 else []
             token = reply_of(kept, after(got, token, *early), weight)
             returned[k] = swap(token, "exp", n_exp, 2 * k) if k else token
 

time: 146 us -> 151 us (1.034)
  waiting for transfers between devices: 34.2 us -> 38.3 us
  local copies, waits for them, and re-layouts: 4.96 us -> 1.84 us
  other arithmetic: 2.56 us -> 5.03 us
  Pallas kernels: 53.6 us -> 55.6 us
    pallas_call x0 -> x1, Pallas kernels: none -> 6.31 us  [beside_first(): pl.pallas_call(inside_kernel, in_specs=[SMEM] + [ANY] * 3 + [VMEM] * 2, o...]
    pallas_call x3 -> x2, Pallas kernels: 12.7 us -> 8.42 us  [call_with_held(): pl.pallas_call(functools.partial(with_held, kernel, pieces), in_specs=[SM...]
    ppermute x34, waiting for transfers between devices: 34.2 us -> 38.3 us  [swap(): return lax.ppermute(x, axis, [(i, i ^ k) for i in range(n) if keep(i)])]
    unnamed x22 -> x16, local copies, waits for them, and re-layouts: 4.41 us -> 0.6 us
    convert_element_type x2, other arithmetic: 0.41 us -> 2.39 us  [prefix_of_four(): sent_one, sent_two = (sent_one.astype(BF16), sent_two.astype(BF16))]
  transfers between devices with their start and end apart: 34 -> 34, of which waited for: 13 -> 13; matrix products, arithmetic and copies ran while one was open for 1% -> 3% of each run, Pallas kernels for 26% -> 26%
where the time goes in v7:
time: 151 us; the launch traced here: 150 us
  Pallas kernels  55.6 us (37%)
  starting transfers between devices  48.9 us (32%)
  waiting for transfers between devices  38.3 us (25%)
  other arithmetic  5.03 us (3%)
  local copies, waits for them, and re-layouts  1.84 us (1%)
    ppermute x34, starting transfers between devices, swap(): return lax.ppermute(x, axis, [(i, i ^ k) for i in range(n) if keep(i)])  48.9 us
    ppermute x34, waiting for transfers between devices, swap(): return lax.ppermute(x, axis, [(i, i ^ k) for i in range(n) if keep(i)])  38.3 us
    pallas_call x3, Pallas kernels, project(): pl.pallas_call(functools.partial(project_kernel, chunks=chunks, parts=par...  18.8 us
    pallas_call x3, Pallas kernels, down_chunk(): pl.pallas_call(functools.partial(down_kernel, chunk=chunk, route=route),...  15.3 us
    pallas_call x2, Pallas kernels, call_with_held(): pl.pallas_call(functools.partial(with_held, kernel, pieces), in_specs=[SM...  8.42 us
    pallas_call x1, Pallas kernels, beside_first(): pl.pallas_call(inside_kernel, in_specs=[SMEM] + [ANY] * 3 + [VMEM] * 2, o...  6.31 us
    pallas_call x1, Pallas kernels, body(): pl.pallas_call(state_kernel, in_specs=[ANY] * 2 + [VMEM], out_specs=[VMEM...  3.84 us
  transfers between devices with their start and end apart: 34, of which 13 were waited for; matrix products, arithmetic and copies ran while one was open for 3% of the time, Pallas kernels for 26%

profile of v7, /device:TPU:0, one launch (start us, length us, event | category | flops | bytes accessed | tf_op | source)
XLA Modules:
  0.0 150.1 jit_solution(12405303524816882774)
XLA Ops:
  0.0 3.8 %local_state.1 = (bf16[12,128,128]{2,1,0:T(8,128)(2,1)}, bf16[12,128,128]{2,1,0:T(8,128)(2,1)}) custom-call(bf16[4,64,768]{2,1,0:T(8,128)(2,1)} %keys.3, bf16[4,64,768]{2,1,0:T(8,128)(2,1)} %values.3, f32[24,64]{1,0:T(8,128)} %bitcast.19), custom_call_target="tpu_custom_call" | custom-call | tf_op jit(solution)/shard_map/local_state/pallas_call | solution.py:520
  3.8 0.8 reduce_sum.9
  4.8 1.3 collective-permute-start.1
  6.8 7.6 %collective-permute-start.4 = (bf16[12,128,128]{2,1,0:T(8,128)(2,1)}, bf16[12,128,128]{2,1,0:T(8,128)(2,1)S(1)}, u32[]{:S(2)}, u32[]{:S(2)}) collective-permute-start(bf16[12,128,128]{2,1,0:T(8,128)(2,1)} %get-tuple-element.59), channel_id=1, source_target_pairs={{0,16},{8,24},{1,17},{9,25},{2,18},{10,26},{3,19},{11,27},{4,20},{... | collective-permute-start | bytes 1179656 | tf_op jit(solution)/shard_map/ppermute | solution.py:27
  14.4 3.4 %collective-permute-start = (bf16[12,128,128]{2,1,0:T(8,128)(2,1)}, bf16[12,128,128]{2,1,0:T(8,128)(2,1)S(1)}, u32[]{:S(2)}, u32[]{:S(2)}) collective-permute-start(bf16[12,128,128]{2,1,0:T(8,128)(2,1)} %get-tuple-element.55), channel_id=1, source_target_pairs={{0,8},{8,0},{16,24},{1,9},{9,1},{17,25},{2,10},{10,2},{18,26},{3,1... | collective-permute-start | bytes 1179656 | tf_op jit(solution)/shard_map/ppermute | solution.py:27
  18.8 6.3 %inside_and_placement.1 = (f32[4,64,768]{2,1,0:T(8,128)}, bf16[320,256]{1,0:T(8,128)(2,1)}, s32[80,128]{1,0:T(8,128)}) custom-call(s32[2]{0:T(128)} %pad_add_fusion.place, bf16[4,64,768]{2,1,0:T(8,128)(2,1)} %refs_0_.1, bf16[4,64,768]{2,1,0:T(8,128)(2,1)} %keys.3, bf16[4,64,768]{2,1,0:T(8,128)(2,1)} %values.3, f32[24,64]{1,0:T(8,128)} %bitcast.20, ...), custom_call_target="tpu_custom_call" | custom-call | tf_op jit(solution)/shard_map/inside_and_placement/pallas_call | solution.py:537
  25.1 1.7 %collective-permute-done = bf16[12,128,128]{2,1,0:T(8,128)(2,1)S(1)} collective-permute-done((bf16[12,128,128]{2,1,0:T(8,128)(2,1)}, bf16[12,128,128]{2,1,0:T(8,128)(2,1)S(1)}, u32[]{:S(2)}, u32[]{:S(2)}) %collective-permute-start) | collective-permute-done | bytes 393248 | tf_op jit(solution)/shard_map/ppermute | solution.py:27
  26.8 1.2 fusion.3
  28.0 1.3 collective-permute-start.2
  29.4 1.2 fusion.5
  30.6 3.6 %collective-permute-start.5 = (bf16[12,128,128]{2,1,0:T(8,128)(2,1)S(1)}, bf16[12,128,128]{2,1,0:T(8,128)(2,1)S(1)}, u32[]{:S(2)}, u32[]{:S(2)}) collective-permute-start(bf16[12,128,128]{2,1,0:T(8,128)(2,1)S(1)} %fusion.5), channel_id=1, source_target_pairs={{0,8},{16,24},{24,16},{1,9},{17,25},{25,17},{2,10},{18,26},{26,18}... | collective-permute-start | bytes 1179656 | tf_op jit(solution)/shard_map/ppermute | solution.py:27
  34.2 0.7 reshape.84.refs_3_
  35.4 5.8 %early_weights.1 = (bf16[2,768,1536]{2,1,0:T(8,128)(2,1)S(1)}, bf16[2,768,1536]{2,1,0:T(8,128)(2,1)S(1)}, bf16[2,1536,768]{2,1,0:T(8,128)(2,1)S(1)}) custom-call(s32[2]{0:T(128)S(1)} %copy-done.5, bf16[2,6144,1536]{2,1,0:T(8,128)(2,1)} %up.9, bf16[2,1536,6144]{2,1,0:T(8,128)(2,1)} %weights.5), custom_call_target="tpu_custom_call" | custom-call | tf_op jit(solution)/shard_map/early_weights/pallas_call | solution.py:97
  41.8 2.6 %normed.1.refs_0_ = bf16[256,768]{1,0:T(8,128)(2,1)S(1)} custom-call(s32[2]{0:T(128)S(1)} %copy-done.5, bf16[2,6144,1536]{2,1,0:T(8,128)(2,1)} %up.9, bf16[2,1536,6144]{2,1,0:T(8,128)(2,1)} %weights.5, bf16[4,64,768]{2,1,0:T(8,128)(2,1)S(1)} %copy-done, f32[4,64,768]{2,1,0:T(8,128)S(1)} %copy-done.1, f32[24,64]{1,0:T(8,128)S(1)} %bitcast.21, ...), custom_call_target="tpu_custom_call" | custom-call | tf_op jit(solution)/shard_map/normed/pallas_call | solution.py:97
  44.5 1.7 %collective-permute-done.6.refs_1_ = bf16[256,768]{1,0:T(8,128)(2,1)S(1)} collective-permute-done((bf16[256,768]{1,0:T(8,128)(2,1)S(1)}, bf16[256,768]{1,0:T(8,128)(2,1)S(1)}, u32[]{:S(2)}, u32[]{:S(2)}) %collective-permute-start.6) | collective-permute-done | bytes 393248 | tf_op jit(solution)/shard_map/ppermute | solution.py:27
  46.6 1.9 %collective-permute-start.16 = (bf16[2,40,1536]{2,1,0:T(8,128)(2,1)S(1)}, bf16[2,40,1536]{2,1,0:T(8,128)(2,1)S(1)}, u32[]{:S(2)}, u32[]{:S(2)}) collective-permute-start(bf16[2,40,1536]{2,1,0:T(8,128)(2,1)S(1)} %get-tuple-element.68.refs_0_), channel_id=1, source_target_pairs={{0,8},{8,0},{16,24},{24,16},{1,9},{9,1},{17,25},{25,17},{2,10},{10... | collective-permute-start | bytes 737288 | tf_op jit(solution)/shard_map/ppermute | solution.py:27
  48.5 1.6 %collective-permute-start.7 = (bf16[2,40,1536]{2,1,0:T(8,128)(2,1)S(1)}, bf16[2,40,1536]{2,1,0:T(8,128)(2,1)S(1)}, u32[]{:S(2)}, u32[]{:S(2)}) collective-permute-start(bf16[2,40,1536]{2,1,0:T(8,128)(2,1)S(1)} %get-tuple-element.69), channel_id=1, source_target_pairs={{0,2},{1,3},{2,0},{3,1},{4,6},{5,7},{6,4},{7,5},{8,10},{9,11},{10,... | collective-permute-start | bytes 737288 | tf_op jit(solution)/shard_map/ppermute | solution.py:27
  50.1 2.6 %collective-permute-start.8 = (bf16[2,40,1536]{2,1,0:T(8,128)(2,1)S(1)}, bf16[2,40,1536]{2,1,0:T(8,128)(2,1)S(1)}, u32[]{:S(2)}, u32[]{:S(2)}) collective-permute-start(bf16[2,40,1536]{2,1,0:T(8,128)(2,1)S(1)} %get-tuple-element.70), channel_id=1, source_target_pairs={{0,4},{1,5},{2,6},{3,7},{4,0},{5,1},{6,2},{7,3},{8,12},{9,13},{10,... | collective-permute-start | bytes 737288 | tf_op jit(solution)/shard_map/ppermute | solution.py:27
  52.9 1.9 %collective-permute-done.16.refs_1_ = bf16[2,40,1536]{2,1,0:T(8,128)(2,1)S(1)} collective-permute-done((bf16[2,40,1536]{2,1,0:T(8,128)(2,1)S(1)}, bf16[2,40,1536]{2,1,0:T(8,128)(2,1)S(1)}, u32[]{:S(2)}, u32[]{:S(2)}) %collective-permute-start.16) | collective-permute-done | bytes 245792 | tf_op jit(solution)/shard_map/ppermute | solution.py:27
  54.8 1.5 collective-permute-done.17.refs_2_
  56.2 4.5 %collective-permute-done.7.refs_1_.refs_0_ = bf16[2,40,1536]{2,1,0:T(8,128)(2,1)S(1)} collective-permute-done((bf16[2,40,1536]{2,1,0:T(8,128)(2,1)S(1)}, bf16[2,40,1536]{2,1,0:T(8,128)(2,1)S(1)}, u32[]{:S(2)}, u32[]{:S(2)}) %collective-permute-start.7) | collective-permute-done | bytes 245792 | tf_op jit(solution)/shard_map/ppermute | solution.py:27
  60.7 1.6 %collective-permute-start.19 = (bf16[2,40,1536]{2,1,0:T(8,128)(2,1)S(1)}, bf16[2,40,1536]{2,1,0:T(8,128)(2,1)S(1)}, u32[]{:S(2)}, u32[]{:S(2)}) collective-permute-start(bf16[2,40,1536]{2,1,0:T(8,128)(2,1)S(1)} %collective-permute-done.7.refs_1_.refs_0_), channel_id=1, source_target_pairs={{0,16},{8,24},{16,0},{24,8},{1,17},{9,25},{17,1},{25,9},{2,18},{10... | collective-permute-start | bytes 737288 | tf_op jit(solution)/shard_map/ppermute | solution.py:27
  63.3 7.1 %collective-permute-done.8.refs_2_.refs_0_ = bf16[2,40,1536]{2,1,0:T(8,128)(2,1)S(1)} collective-permute-done((bf16[2,40,1536]{2,1,0:T(8,128)(2,1)S(1)}, bf16[2,40,1536]{2,1,0:T(8,128)(2,1)S(1)}, u32[]{:S(2)}, u32[]{:S(2)}) %collective-permute-start.8) | collective-permute-done | bytes 245792 | tf_op jit(solution)/shard_map/ppermute | solution.py:27
  70.6 2.1 %collective-permute-start.14 = (bf16[2,40,1536]{2,1,0:T(8,128)(2,1)S(1)}, bf16[2,40,1536]{2,1,0:T(8,128)(2,1)S(1)}, u32[]{:S(2)}, u32[]{:S(2)}) collective-permute-start(bf16[2,40,1536]{2,1,0:T(8,128)(2,1)S(1)} %collective-permute-done.9.refs_3_.refs_4_), channel_id=1, source_target_pairs={{0,16},{8,24},{16,0},{24,8},{1,17},{9,25},{17,1},{25,9},{2,18},{10... | collective-permute-start | bytes 737288 | tf_op jit(solution)/shard_map/ppermute | solution.py:27
  72.7 1.8 %collective-permute-start.20 = (bf16[2,40,1536]{2,1,0:T(8,128)(2,1)S(1)}, bf16[2,40,1536]{2,1,0:T(8,128)(2,1)S(1)}, u32[]{:S(2)}, u32[]{:S(2)}) collective-permute-start(bf16[2,40,1536]{2,1,0:T(8,128)(2,1)S(1)} %collective-permute-done.19.refs_2_), channel_id=1, source_target_pairs={{0,8},{8,0},{16,24},{24,16},{1,9},{9,1},{17,25},{25,17},{2,10},{10... | collective-permute-start | bytes 737288 | tf_op jit(solution)/shard_map/ppermute | solution.py:27
  74.5 1.1 gate.1.weight
  75.8 1.0 collective-permute-start.13
  76.8 2.5 %collective-permute-done.10.refs_1_ = bf16[2,40,1536]{2,1,0:T(8,128)(2,1)S(1)} collective-permute-done((bf16[2,40,1536]{2,1,0:T(8,128)(2,1)S(1)}, bf16[2,40,1536]{2,1,0:T(8,128)(2,1)S(1)}, u32[]{:S(2)}, u32[]{:S(2)}) %collective-permute-start.10) | collective-permute-done | bytes 245792 | tf_op jit(solution)/shard_map/ppermute | solution.py:27
  79.3 2.0 %collective-permute-start.12 = (bf16[2,40,1536]{2,1,0:T(8,128)(2,1)S(1)}, bf16[2,40,1536]{2,1,0:T(8,128)(2,1)S(1)}, u32[]{:S(2)}, u32[]{:S(2)}) collective-permute-start(bf16[2,40,1536]{2,1,0:T(8,128)(2,1)S(1)} %collective-permute-done.10.refs_1_), channel_id=1, source_target_pairs={{0,16},{8,24},{16,0},{24,8},{1,17},{9,25},{17,1},{25,9},{2,18},{10... | collective-permute-start | bytes 737288 | tf_op jit(solution)/shard_map/ppermute | solution.py:27
  81.4 5.3 %project_0.1.refs_4_ = f32[2,160,1536]{2,1,0:T(8,128)S(1)} custom-call(s32[2]{0:T(128)S(1)} %copy-done.6, bf16[2,6144,1536]{2,1,0:T(8,128)(2,1)} %up.9, bf16[2,1536,6144]{2,1,0:T(8,128)(2,1)} %weights.5, bf16[2,40,1536]{2,1,0:T(8,128)(2,1)S(1)} %get-tuple-element.68.refs_0_, bf16[2,40,1536]{2,1,0:T(8,128)(2,1)S(1)} %collective-permute-done.16.refs_1_, ...), custom_call_target="tpu_custom_call" | custom-call | flops 1509949440 | bytes 9437184 | tf_op jit(solution)/shard_map/project_0/pallas_call | solution.py:326
  86.7 4.9 %project_1.1.refs_11_ = f32[2,160,1536]{2,1,0:T(8,128)S(1)} custom-call(s32[2]{0:T(128)S(1)} %copy-done.6, bf16[2,6144,1536]{2,1,0:T(8,128)(2,1)} %up.9, bf16[2,1536,6144]{2,1,0:T(8,128)(2,1)} %weights.5, bf16[2,40,1536]{2,1,0:T(8,128)(2,1)S(1)} %collective-permute-done.7.refs_1_.refs_0_, bf16[2,40,1536]{2,1,0:T(8,128)(2,1)S(1)} %collective-permute-done.18.refs_1_, ...), custom_call_target="tpu_custom_call" | custom-call | flops 1509949440 | bytes 9437184 | tf_op jit(solution)/shard_map/project_1/pallas_call | solution.py:326
  91.6 8.7 %project_2.1 = (bf16[2,160,1536]{2,1,0:T(8,128)(2,1)S(1)}, bf16[2,2,40,1536]{3,2,1,0:T(8,128)(2,1)S(1)}, bf16[2,2,40,1536]{3,2,1,0:T(8,128)(2,1)S(1)}) custom-call(s32[2]{0:T(128)S(1)} %copy-done.6, bf16[2,6144,1536]{2,1,0:T(8,128)(2,1)} %up.9, bf16[2,1536,6144]{2,1,0:T(8,128)(2,1)} %weights.5, ...), custom_call_target="tpu_custom_call" | custom-call | flops 4529848320 | bytes 28311552 | tf_op jit(solution)/shard_map/project_2/pallas_call | solution.py:326
  100.3 2.1 %collective-permute-start.22 = (bf16[2,2,40,1536]{3,2,1,0:T(8,128)(2,1)S(1)}, bf16[2,2,40,1536]{3,2,1,0:T(8,128)(2,1)S(1)}, u32[]{:S(2)}, u32[]{:S(2)}) collective-permute-start(bf16[2,2,40,1536]{3,2,1,0:T(8,128)(2,1)S(1)} %get-tuple-element.77), channel_id=1, source_target_pairs={{0,16},{8,24},{16,0},{24,8},{1,17},{9,25},{17,1},{25,9},{2,18},{10... | collective-permute-start | bytes 1474568 | tf_op jit(solution)/shard_map/ppermute | solution.py:27
  102.3 5.2 %down_2.1 = (bf16[2,2,40,1536]{3,2,1,0:T(8,128)(2,1)S(1)}, bf16[2,2,40,1536]{3,2,1,0:T(8,128)(2,1)S(1)}) custom-call(s32[2]{0:T(128)S(1)} %copy-done.6, bf16[2,1536,6144]{2,1,0:T(8,128)(2,1)} %weights.5, bf16[2,160,1536]{2,1,0:T(8,128)(2,1)S(1)} %get-tuple-element.84.hidden), custom_call_target="tpu_custom_call" | custom-call | flops 1509949440 | bytes 9437184 | tf_op jit(solution)/shard_map/down_2/pallas_call | solution.py:381
  107.9 5.0 %down_1.1 = (bf16[2,2,40,1536]{3,2,1,0:T(8,128)(2,1)S(1)}, bf16[2,2,40,1536]{3,2,1,0:T(8,128)(2,1)S(1)}) custom-call(s32[2]{0:T(128)S(1)} %copy-done.6, bf16[2,1536,6144]{2,1,0:T(8,128)(2,1)} %weights.5, bf16[2,160,1536]{2,1,0:T(8,128)(2,1)S(1)} %get-tuple-element.84.hidden), custom_call_target="tpu_custom_call" | custom-call | flops 1509949440 | bytes 9437184 | tf_op jit(solution)/shard_map/down_1/pallas_call | solution.py:381
  112.9 1.9 %collective-permute-start.26 = (bf16[2,2,40,1536]{3,2,1,0:T(8,128)(2,1)S(1)}, bf16[2,2,40,1536]{3,2,1,0:T(8,128)(2,1)S(1)}, u32[]{:S(2)}, u32[]{:S(2)}) collective-permute-start(bf16[2,2,40,1536]{3,2,1,0:T(8,128)(2,1)S(1)} %get-tuple-element.81), channel_id=1, source_target_pairs={{0,16},{8,24},{16,0},{24,8},{1,17},{9,25},{17,1},{25,9},{2,18},{10... | collective-permute-start | bytes 1474568 | tf_op jit(solution)/shard_map/ppermute | solution.py:27
  115.0 5.0 %down_0.1 = (bf16[2,2,40,1536]{3,2,1,0:T(8,128)(2,1)S(1)}, bf16[2,2,40,1536]{3,2,1,0:T(8,128)(2,1)S(1)}) custom-call(s32[2]{0:T(128)S(1)} %copy-done.6, bf16[2,1536,6144]{2,1,0:T(8,128)(2,1)} %weights.5, bf16[2,160,1536]{2,1,0:T(8,128)(2,1)S(1)} %get-tuple-element.84.hidden), custom_call_target="tpu_custom_call" | custom-call | flops 1509949440 | bytes 9437184 | tf_op jit(solution)/shard_map/down_0/pallas_call | solution.py:381
  120.0 2.1 %collective-permute-start.23 = (bf16[2,2,40,1536]{3,2,1,0:T(8,128)(2,1)S(1)}, bf16[2,2,40,1536]{3,2,1,0:T(8,128)(2,1)S(1)}, u32[]{:S(2)}, u32[]{:S(2)}) collective-permute-start(bf16[2,2,40,1536]{3,2,1,0:T(8,128)(2,1)S(1)} %get-tuple-element.86), channel_id=1, source_target_pairs={{0,8},{8,0},{16,24},{24,16},{1,9},{9,1},{17,25},{25,17},{2,10},{10... | collective-permute-start | bytes 1474568 | tf_op jit(solution)/shard_map/ppermute | solution.py:27
  122.5 4.2 %collective-permute-done.27.got = bf16[1,2,40,1536]{3,2,1,0:T(8,128)(2,1)S(1)} collective-permute-done((bf16[1,2,40,1536]{3,2,1,0:T(8,128)(2,1)S(1)}, bf16[1,2,40,1536]{3,2,1,0:T(8,128)(2,1)S(1)}, u32[]{:S(2)}, u32[]{:S(2)}) %collective-permute-start.27) | collective-permute-done | bytes 245792 | tf_op jit(solution)/shard_map/ppermute | solution.py:27
  127.0 2.3 %collective-permute-start.30 = (bf16[2,40,1536]{2,1,0:T(8,128)(2,1)S(1)}, bf16[2,40,1536]{2,1,0:T(8,128)(2,1)S(1)}, u32[]{:S(2)}, u32[]{:S(2)}) collective-permute-start(bf16[2,40,1536]{2,1,0:T(8,128)(2,1)S(1)} %reply.4), channel_id=1, source_target_pairs={{0,6},{1,7},{2,4},{3,5},{4,2},{5,3},{6,0},{7,1},{8,14},{9,15},{10,... | collective-permute-start | bytes 737288 | tf_op jit(solution)/shard_map/ppermute | solution.py:27
  129.4 3.0 %collective-permute-start.31 = (bf16[2,40,1536]{2,1,0:T(8,128)(2,1)S(1)}, bf16[2,40,1536]{2,1,0:T(8,128)(2,1)S(1)}, u32[]{:S(2)}, u32[]{:S(2)}) collective-permute-start(bf16[2,40,1536]{2,1,0:T(8,128)(2,1)S(1)} %reply.5), channel_id=1, source_target_pairs={{0,4},{1,5},{2,6},{3,7},{4,0},{5,1},{6,2},{7,3},{8,12},{9,13},{10,... | collective-permute-start | bytes 737288 | tf_op jit(solution)/shard_map/ppermute | solution.py:27
  132.4 2.5 %collective-permute-done.23.got = bf16[2,2,40,1536]{3,2,1,0:T(8,128)(2,1)S(1)} collective-permute-done((bf16[2,2,40,1536]{3,2,1,0:T(8,128)(2,1)S(1)}, bf16[2,2,40,1536]{3,2,1,0:T(8,128)(2,1)S(1)}, u32[]{:S(2)}, u32[]{:S(2)}) %collective-permute-start.23) | collective-permute-done | bytes 491552 | tf_op jit(solution)/shard_map/ppermute | solution.py:27
  135.1 2.4 %collective-permute-done.29.got = bf16[1,2,40,1536]{3,2,1,0:T(8,128)(2,1)S(1)} collective-permute-done((bf16[1,2,40,1536]{3,2,1,0:T(8,128)(2,1)S(1)}, bf16[1,2,40,1536]{3,2,1,0:T(8,128)(2,1)S(1)}, u32[]{:S(2)}, u32[]{:S(2)}) %collective-permute-start.29) | collective-permute-done | bytes 245792 | tf_op jit(solution)/shard_map/ppermute | solution.py:27
  137.6 2.5 %collective-permute-start.32 = (bf16[2,40,1536]{2,1,0:T(8,128)(2,1)S(1)}, bf16[2,40,1536]{2,1,0:T(8,128)(2,1)S(1)}, u32[]{:S(2)}, u32[]{:S(2)}) collective-permute-start(bf16[2,40,1536]{2,1,0:T(8,128)(2,1)S(1)} %reply.6), channel_id=1, source_target_pairs={{0,2},{1,3},{2,0},{3,1},{4,6},{5,7},{6,4},{7,5},{8,10},{9,11},{10,... | collective-permute-start | bytes 737288 | tf_op jit(solution)/shard_map/ppermute | solution.py:27
  140.2 4.2 %collective-permute-done.31.refs_2_ = bf16[2,40,1536]{2,1,0:T(8,128)(2,1)S(1)} collective-permute-done((bf16[2,40,1536]{2,1,0:T(8,128)(2,1)S(1)}, bf16[2,40,1536]{2,1,0:T(8,128)(2,1)S(1)}, u32[]{:S(2)}, u32[]{:S(2)}) %collective-permute-start.31) | collective-permute-done | bytes 245792 | tf_op jit(solution)/shard_map/ppermute | solution.py:27
  144.5 2.4 %collective-permute-done.32.refs_1_ = bf16[2,40,1536]{2,1,0:T(8,128)(2,1)S(1)} collective-permute-done((bf16[2,40,1536]{2,1,0:T(8,128)(2,1)S(1)}, bf16[2,40,1536]{2,1,0:T(8,128)(2,1)S(1)}, u32[]{:S(2)}, u32[]{:S(2)}) %collective-permute-start.32) | collective-permute-done | bytes 245792 | tf_op jit(solution)/shard_map/ppermute | solution.py:27
  147.6 1.7 %collective-permute-done.33 = bf16[256,768]{1,0:T(8,128)(2,1)S(1)} collective-permute-done((bf16[256,768]{1,0:T(8,128)(2,1)S(1)}, bf16[256,768]{1,0:T(8,128)(2,1)S(1)}, u32[]{:S(2)}, u32[]{:S(2)}) %collective-permute-start.33) | collective-permute-done | bytes 393248 | tf_op jit(solution)/shard_map/ppermute | solution.py:27
  149.3 0.8 add_convert_fusion
  (75 shorter events, 7.4 us)
Async XLA Ops:
  4.8 20.3 %collective-permute-start.1 = (f32[2,12,1,1]{1,0,3,2:T(2,128)S(1)}, f32[2,12,1,1]{1,0,3,2:T(2,128)S(1)}, u32[]{:S(2)}, u32[]{:S(2)}) collective-permute-start(f32[2,12,1,1]{1,0,3,2:T(2,128)S(1)} %exp.14), channel_id=1, source_target_pairs={{8,0},{16,24},{9,1},{17,25},{10,2},{18,26},{11,3},{19,27},{12,4},{... | collective-permute-start | bytes 296 | tf_op jit(solution)/shard_map/ppermute | solution.py:27
  6.1 23.2 %collective-permute-start.3 = (f32[2,12,1,1]{1,0,3,2:T(2,128)S(1)}, f32[2,12,1,1]{1,0,3,2:T(2,128)S(1)}, u32[]{:S(2)}, u32[]{:S(2)}) collective-permute-start(f32[2,12,1,1]{1,0,3,2:T(2,128)S(1)} %exp.14), channel_id=1, source_target_pairs={{8,16},{9,17},{10,18},{11,19},{12,20},{13,21},{14,22},{15,23}} | collective-permute-start | bytes 296 | tf_op jit(solution)/shard_map/ppermute | solution.py:27
  6.8 22.6 %collective-permute-start.4 = (bf16[12,128,128]{2,1,0:T(8,128)(2,1)}, bf16[12,128,128]{2,1,0:T(8,128)(2,1)S(1)}, u32[]{:S(2)}, u32[]{:S(2)}) collective-permute-start(bf16[12,128,128]{2,1,0:T(8,128)(2,1)} %get-tuple-element.59), channel_id=1, source_target_pairs={{0,16},{8,24},{1,17},{9,25},{2,18},{10,26},{3,19},{11,27},{4,20},{... | collective-permute-start | bytes 1179656 | tf_op jit(solution)/shard_map/ppermute | solution.py:27
  14.4 12.4 %collective-permute-start = (bf16[12,128,128]{2,1,0:T(8,128)(2,1)}, bf16[12,128,128]{2,1,0:T(8,128)(2,1)S(1)}, u32[]{:S(2)}, u32[]{:S(2)}) collective-permute-start(bf16[12,128,128]{2,1,0:T(8,128)(2,1)} %get-tuple-element.55), channel_id=1, source_target_pairs={{0,8},{8,0},{16,24},{1,9},{9,1},{17,25},{2,10},{10,2},{18,26},{3,1... | collective-permute-start | bytes 1179656 | tf_op jit(solution)/shard_map/ppermute | solution.py:27
  28.0 13.2 %collective-permute-start.2 = (bf16[12,128,128]{2,1,0:T(8,128)(2,1)S(1)}, bf16[12,128,128]{2,1,0:T(8,128)(2,1)S(1)}, u32[]{:S(2)}, u32[]{:S(2)}) collective-permute-start(bf16[12,128,128]{2,1,0:T(8,128)(2,1)S(1)} %fusion.3), channel_id=1, source_target_pairs={{0,16},{8,24},{1,17},{9,25},{2,18},{10,26},{3,19},{11,27},{4,20},{... | collective-permute-start | bytes 1179656 | tf_op jit(solution)/shard_map/ppermute | solution.py:27
  30.6 10.9 %collective-permute-start.5 = (bf16[12,128,128]{2,1,0:T(8,128)(2,1)S(1)}, bf16[12,128,128]{2,1,0:T(8,128)(2,1)S(1)}, u32[]{:S(2)}, u32[]{:S(2)}) collective-permute-start(bf16[12,128,128]{2,1,0:T(8,128)(2,1)S(1)} %fusion.5), channel_id=1, source_target_pairs={{0,8},{16,24},{24,16},{1,9},{17,25},{25,17},{2,10},{18,26},{26,18}... | collective-permute-start | bytes 1179656 | tf_op jit(solution)/shard_map/ppermute | solution.py:27
  34.9 0.6 copy-start.5
  35.4 6.2 %copy-start = (bf16[4,64,768]{2,1,0:T(8,128)(2,1)S(1)}, bf16[4,64,768]{2,1,0:T(8,128)(2,1)}, u32[]{:S(2)}) copy-start(bf16[4,64,768]{2,1,0:T(8,128)(2,1)} %refs_0_.1) | copy-start | bytes 1179652
  35.4 6.3 %copy-start.1 = (f32[4,64,768]{2,1,0:T(8,128)S(1)}, f32[4,64,768]{2,1,0:T(8,128)}, u32[]{:S(2)}) copy-start(f32[4,64,768]{2,1,0:T(8,128)} %get-tuple-element.57.refs_1_) | copy-start | bytes 2359300
  35.4 6.3 %copy-start.3 = (f32[4,64,6]{1,0,2:T(4,128)S(1)}, f32[4,64,6]{1,0,2:T(4,128)}, u32[]{:S(2)}) copy-start(f32[4,64,6]{1,0,2:T(4,128)} %param.12) | copy-start | bytes 18436
  41.7 4.5 %copy-start.2 = (bf16[320,256]{1,0:T(8,128)(2,1)S(1)}, bf16[320,256]{1,0:T(8,128)(2,1)}, u32[]{:S(2)}) copy-start(bf16[320,256]{1,0:T(8,128)(2,1)} %get-tuple-element.66.placement) | copy-start | bytes 491524
  41.7 32.8 %copy-start.4 = (bf16[6144,16]{0,1:T(8,128)(2,1)S(1)}, bf16[6144,16]{0,1:T(8,128)(2,1)}, u32[]{:S(2)}) copy-start(bf16[6144,16]{0,1:T(8,128)(2,1)} %param.14) | copy-start | bytes 589828
  41.7 32.8 %copy-start.6 = (s32[2]{0:T(128)S(1)}, s32[2]{0:T(128)}, u32[]{:S(2)}) copy-start(s32[2]{0:T(128)} %pad_add_fusion.place) | copy-start | bytes 28
  41.7 32.8 %copy-start.7 = (s32[80,128]{1,0:T(8,128)S(1)}, s32[80,128]{1,0:T(8,128)}, u32[]{:S(2)}) copy-start(s32[80,128]{1,0:T(8,128)} %get-tuple-element.67.other) | copy-start | bytes 122884
  44.4 1.8 %collective-permute-start.6 = (bf16[256,768]{1,0:T(8,128)(2,1)S(1)}, bf16[256,768]{1,0:T(8,128)(2,1)S(1)}, u32[]{:S(2)}, u32[]{:S(2)}) collective-permute-start(bf16[256,768]{1,0:T(8,128)(2,1)S(1)} %normed.1.refs_0_), channel_id=1, source_target_pairs={{0,1},{1,0},{2,3},{3,2},{4,5},{5,4},{6,7},{7,6},{8,9},{9,8},{10,11... | collective-permute-start | bytes 1179656 | tf_op jit(solution)/shard_map/ppermute | solution.py:27
  46.6 8.2 %collective-permute-start.16 = (bf16[2,40,1536]{2,1,0:T(8,128)(2,1)S(1)}, bf16[2,40,1536]{2,1,0:T(8,128)(2,1)S(1)}, u32[]{:S(2)}, u32[]{:S(2)}) collective-permute-start(bf16[2,40,1536]{2,1,0:T(8,128)(2,1)S(1)} %get-tuple-element.68.refs_0_), channel_id=1, source_target_pairs={{0,8},{8,0},{16,24},{24,16},{1,9},{9,1},{17,25},{25,17},{2,10},{10... | collective-permute-start | bytes 737288 | tf_op jit(solution)/shard_map/ppermute | solution.py:27
  48.5 7.7 %collective-permute-start.17 = (bf16[2,40,1536]{2,1,0:T(8,128)(2,1)S(1)}, bf16[2,40,1536]{2,1,0:T(8,128)(2,1)S(1)}, u32[]{:S(2)}, u32[]{:S(2)}) collective-permute-start(bf16[2,40,1536]{2,1,0:T(8,128)(2,1)S(1)} %get-tuple-element.68.refs_0_), channel_id=1, source_target_pairs={{0,16},{8,24},{16,0},{24,8},{1,17},{9,25},{17,1},{25,9},{2,18},{10... | collective-permute-start | bytes 737288 | tf_op jit(solution)/shard_map/ppermute | solution.py:27
  48.5 12.2 %collective-permute-start.7 = (bf16[2,40,1536]{2,1,0:T(8,128)(2,1)S(1)}, bf16[2,40,1536]{2,1,0:T(8,128)(2,1)S(1)}, u32[]{:S(2)}, u32[]{:S(2)}) collective-permute-start(bf16[2,40,1536]{2,1,0:T(8,128)(2,1)S(1)} %get-tuple-element.69), channel_id=1, source_target_pairs={{0,2},{1,3},{2,0},{3,1},{4,6},{5,7},{6,4},{7,5},{8,10},{9,11},{10,... | collective-permute-start | bytes 737288 | tf_op jit(solution)/shard_map/ppermute | solution.py:27
  50.1 20.3 %collective-permute-start.8 = (bf16[2,40,1536]{2,1,0:T(8,128)(2,1)S(1)}, bf16[2,40,1536]{2,1,0:T(8,128)(2,1)S(1)}, u32[]{:S(2)}, u32[]{:S(2)}) collective-permute-start(bf16[2,40,1536]{2,1,0:T(8,128)(2,1)S(1)} %get-tuple-element.70), channel_id=1, source_target_pairs={{0,4},{1,5},{2,6},{3,7},{4,0},{5,1},{6,2},{7,3},{8,12},{9,13},{10,... | collective-permute-start | bytes 737288 | tf_op jit(solution)/shard_map/ppermute | solution.py:27
  52.7 17.9 %collective-permute-start.9 = (bf16[2,40,1536]{2,1,0:T(8,128)(2,1)S(1)}, bf16[2,40,1536]{2,1,0:T(8,128)(2,1)S(1)}, u32[]{:S(2)}, u32[]{:S(2)}) collective-permute-start(bf16[2,40,1536]{2,1,0:T(8,128)(2,1)S(1)} %get-tuple-element.71), channel_id=1, source_target_pairs={{0,6},{1,7},{2,4},{3,5},{4,2},{5,3},{6,0},{7,1},{8,14},{9,15},{10,... | collective-permute-start | bytes 737288 | tf_op jit(solution)/shard_map/ppermute | solution.py:27
  60.7 11.9 %collective-permute-start.19 = (bf16[2,40,1536]{2,1,0:T(8,128)(2,1)S(1)}, bf16[2,40,1536]{2,1,0:T(8,128)(2,1)S(1)}, u32[]{:S(2)}, u32[]{:S(2)}) collective-permute-start(bf16[2,40,1536]{2,1,0:T(8,128)(2,1)S(1)} %collective-permute-done.7.refs_1_.refs_0_), channel_id=1, source_target_pairs={{0,16},{8,24},{16,0},{24,8},{1,17},{9,25},{17,1},{25,9},{2,18},{10... | collective-permute-start | bytes 737288 | tf_op jit(solution)/shard_map/ppermute | solution.py:27
  62.3 13.2 %collective-permute-start.21 = (bf16[2,40,1536]{2,1,0:T(8,128)(2,1)S(1)}, bf16[2,40,1536]{2,1,0:T(8,128)(2,1)S(1)}, u32[]{:S(2)}, u32[]{:S(2)}) collective-permute-start(bf16[2,40,1536]{2,1,0:T(8,128)(2,1)S(1)} %collective-permute-done.16.refs_1_), channel_id=1, source_target_pairs={{0,16},{8,24},{16,0},{24,8},{1,17},{9,25},{17,1},{25,9},{2,18},{10... | collective-permute-start | bytes 737288 | tf_op jit(solution)/shard_map/ppermute | solution.py:27
  62.8 13.1 %collective-permute-start.18 = (bf16[2,40,1536]{2,1,0:T(8,128)(2,1)S(1)}, bf16[2,40,1536]{2,1,0:T(8,128)(2,1)S(1)}, u32[]{:S(2)}, u32[]{:S(2)}) collective-permute-start(bf16[2,40,1536]{2,1,0:T(8,128)(2,1)S(1)} %collective-permute-done.7.refs_1_.refs_0_), channel_id=1, source_target_pairs={{0,8},{8,0},{16,24},{24,16},{1,9},{9,1},{17,25},{25,17},{2,10},{10... | collective-permute-start | bytes 737288 | tf_op jit(solution)/shard_map/ppermute | solution.py:27
  70.4 8.9 %collective-permute-start.10 = (bf16[2,40,1536]{2,1,0:T(8,128)(2,1)S(1)}, bf16[2,40,1536]{2,1,0:T(8,128)(2,1)S(1)}, u32[]{:S(2)}, u32[]{:S(2)}) collective-permute-start(bf16[2,40,1536]{2,1,0:T(8,128)(2,1)S(1)} %collective-permute-done.8.refs_2_.refs_0_), channel_id=1, source_target_pairs={{0,8},{8,0},{16,24},{24,16},{1,9},{9,1},{17,25},{25,17},{2,10},{10... | collective-permute-start | bytes 737288 | tf_op jit(solution)/shard_map/ppermute | solution.py:27
  70.6 10.7 %collective-permute-start.14 = (bf16[2,40,1536]{2,1,0:T(8,128)(2,1)S(1)}, bf16[2,40,1536]{2,1,0:T(8,128)(2,1)S(1)}, u32[]{:S(2)}, u32[]{:S(2)}) collective-permute-start(bf16[2,40,1536]{2,1,0:T(8,128)(2,1)S(1)} %collective-permute-done.9.refs_3_.refs_4_), channel_id=1, source_target_pairs={{0,16},{8,24},{16,0},{24,8},{1,17},{9,25},{17,1},{25,9},{2,18},{10... | collective-permute-start | bytes 737288 | tf_op jit(solution)/shard_map/ppermute | solution.py:27
  72.7 14.0 %collective-permute-start.20 = (bf16[2,40,1536]{2,1,0:T(8,128)(2,1)S(1)}, bf16[2,40,1536]{2,1,0:T(8,128)(2,1)S(1)}, u32[]{:S(2)}, u32[]{:S(2)}) collective-permute-start(bf16[2,40,1536]{2,1,0:T(8,128)(2,1)S(1)} %collective-permute-done.19.refs_2_), channel_id=1, source_target_pairs={{0,8},{8,0},{16,24},{24,16},{1,9},{9,1},{17,25},{25,17},{2,10},{10... | collective-permute-start | bytes 737288 | tf_op jit(solution)/shard_map/ppermute | solution.py:27
  75.6 16.0 %collective-permute-start.11 = (bf16[2,40,1536]{2,1,0:T(8,128)(2,1)S(1)}, bf16[2,40,1536]{2,1,0:T(8,128)(2,1)S(1)}, u32[]{:S(2)}, u32[]{:S(2)}) collective-permute-start(bf16[2,40,1536]{2,1,0:T(8,128)(2,1)S(1)} %collective-permute-done.8.refs_2_.refs_0_), channel_id=1, source_target_pairs={{0,16},{8,24},{16,0},{24,8},{1,17},{9,25},{17,1},{25,9},{2,18},{10... | collective-permute-start | bytes 737288 | tf_op jit(solution)/shard_map/ppermute | solution.py:27
  75.8 15.7 %collective-permute-start.13 = (bf16[2,40,1536]{2,1,0:T(8,128)(2,1)S(1)}, bf16[2,40,1536]{2,1,0:T(8,128)(2,1)S(1)}, u32[]{:S(2)}, u32[]{:S(2)}) collective-permute-start(bf16[2,40,1536]{2,1,0:T(8,128)(2,1)S(1)} %collective-permute-done.9.refs_3_.refs_4_), channel_id=1, source_target_pairs={{0,8},{8,0},{16,24},{24,16},{1,9},{9,1},{17,25},{25,17},{2,10},{10... | collective-permute-start | bytes 737288 | tf_op jit(solution)/shard_map/ppermute | solution.py:27
  79.3 12.3 %collective-permute-start.12 = (bf16[2,40,1536]{2,1,0:T(8,128)(2,1)S(1)}, bf16[2,40,1536]{2,1,0:T(8,128)(2,1)S(1)}, u32[]{:S(2)}, u32[]{:S(2)}) collective-permute-start(bf16[2,40,1536]{2,1,0:T(8,128)(2,1)S(1)} %collective-permute-done.10.refs_1_), channel_id=1, source_target_pairs={{0,16},{8,24},{16,0},{24,8},{1,17},{9,25},{17,1},{25,9},{2,18},{10... | collective-permute-start | bytes 737288 | tf_op jit(solution)/shard_map/ppermute | solution.py:27
  81.3 10.2 %collective-permute-start.15 = (bf16[2,40,1536]{2,1,0:T(8,128)(2,1)S(1)}, bf16[2,40,1536]{2,1,0:T(8,128)(2,1)S(1)}, u32[]{:S(2)}, u32[]{:S(2)}) collective-permute-start(bf16[2,40,1536]{2,1,0:T(8,128)(2,1)S(1)} %collective-permute-done.14.refs_6_), channel_id=1, source_target_pairs={{0,8},{8,0},{16,24},{24,16},{1,9},{9,1},{17,25},{25,17},{2,10},{10... | collective-permute-start | bytes 737288 | tf_op jit(solution)/shard_map/ppermute | solution.py:27
  100.3 14.5 %collective-permute-start.22 = (bf16[2,2,40,1536]{3,2,1,0:T(8,128)(2,1)S(1)}, bf16[2,2,40,1536]{3,2,1,0:T(8,128)(2,1)S(1)}, u32[]{:S(2)}, u32[]{:S(2)}) collective-permute-start(bf16[2,2,40,1536]{3,2,1,0:T(8,128)(2,1)S(1)} %get-tuple-element.77), channel_id=1, source_target_pairs={{0,16},{8,24},{16,0},{24,8},{1,17},{9,25},{17,1},{25,9},{2,18},{10... | collective-permute-start | bytes 1474568 | tf_op jit(solution)/shard_map/ppermute | solution.py:27
  107.6 14.5 %collective-permute-start.24 = (bf16[2,2,40,1536]{3,2,1,0:T(8,128)(2,1)S(1)}, bf16[2,2,40,1536]{3,2,1,0:T(8,128)(2,1)S(1)}, u32[]{:S(2)}, u32[]{:S(2)}) collective-permute-start(bf16[2,2,40,1536]{3,2,1,0:T(8,128)(2,1)S(1)} %get-tuple-element.79), channel_id=1, source_target_pairs={{0,8},{8,0},{16,24},{24,16},{1,9},{9,1},{17,25},{25,17},{2,10},{10... | collective-permute-start | bytes 1474568 | tf_op jit(solution)/shard_map/ppermute | solution.py:27
  112.9 13.9 %collective-permute-start.26 = (bf16[2,2,40,1536]{3,2,1,0:T(8,128)(2,1)S(1)}, bf16[2,2,40,1536]{3,2,1,0:T(8,128)(2,1)S(1)}, u32[]{:S(2)}, u32[]{:S(2)}) collective-permute-start(bf16[2,2,40,1536]{3,2,1,0:T(8,128)(2,1)S(1)} %get-tuple-element.81), channel_id=1, source_target_pairs={{0,16},{8,24},{16,0},{24,8},{1,17},{9,25},{17,1},{25,9},{2,18},{10... | collective-permute-start | bytes 1474568 | tf_op jit(solution)/shard_map/ppermute | solution.py:27
  114.9 11.8 %collective-permute-start.27 = (bf16[1,2,40,1536]{3,2,1,0:T(8,128)(2,1)S(1)}, bf16[1,2,40,1536]{3,2,1,0:T(8,128)(2,1)S(1)}, u32[]{:S(2)}, u32[]{:S(2)}) collective-permute-start(bf16[1,2,40,1536]{3,2,1,0:T(8,128)(2,1)S(1)} %get-tuple-element.83), channel_id=1, source_target_pairs={{0,8},{8,0},{16,24},{24,16},{1,9},{9,1},{17,25},{25,17},{2,10},{10... | collective-permute-start | bytes 737288 | tf_op jit(solution)/shard_map/ppermute | solution.py:27
  120.0 14.9 %collective-permute-start.23 = (bf16[2,2,40,1536]{3,2,1,0:T(8,128)(2,1)S(1)}, bf16[2,2,40,1536]{3,2,1,0:T(8,128)(2,1)S(1)}, u32[]{:S(2)}, u32[]{:S(2)}) collective-permute-start(bf16[2,2,40,1536]{3,2,1,0:T(8,128)(2,1)S(1)} %get-tuple-element.86), channel_id=1, source_target_pairs={{0,8},{8,0},{16,24},{24,16},{1,9},{9,1},{17,25},{25,17},{2,10},{10... | collective-permute-start | bytes 1474568 | tf_op jit(solution)/shard_map/ppermute | solution.py:27
  122.2 7.1 %collective-permute-start.25 = (bf16[1,2,40,1536]{3,2,1,0:T(8,128)(2,1)S(1)}, bf16[1,2,40,1536]{3,2,1,0:T(8,128)(2,1)S(1)}, u32[]{:S(2)}, u32[]{:S(2)}) collective-permute-start(bf16[1,2,40,1536]{3,2,1,0:T(8,128)(2,1)S(1)} %get-tuple-element.90), channel_id=1, source_target_pairs={{0,16},{8,24},{16,0},{24,8},{1,17},{9,25},{17,1},{25,9},{2,18},{10... | collective-permute-start | bytes 737288 | tf_op jit(solution)/shard_map/ppermute | solution.py:27
  126.9 10.6 %collective-permute-start.29 = (bf16[1,2,40,1536]{3,2,1,0:T(8,128)(2,1)S(1)}, bf16[1,2,40,1536]{3,2,1,0:T(8,128)(2,1)S(1)}, u32[]{:S(2)}, u32[]{:S(2)}) collective-permute-start(bf16[1,2,40,1536]{3,2,1,0:T(8,128)(2,1)S(1)} %get-tuple-element.95), channel_id=1, source_target_pairs={{0,8},{8,0},{16,24},{24,16},{1,9},{9,1},{17,25},{25,17},{2,10},{10... | collective-permute-start | bytes 737288 | tf_op jit(solution)/shard_map/ppermute | solution.py:27
  127.0 17.4 %collective-permute-start.30 = (bf16[2,40,1536]{2,1,0:T(8,128)(2,1)S(1)}, bf16[2,40,1536]{2,1,0:T(8,128)(2,1)S(1)}, u32[]{:S(2)}, u32[]{:S(2)}) collective-permute-start(bf16[2,40,1536]{2,1,0:T(8,128)(2,1)S(1)} %reply.4), channel_id=1, source_target_pairs={{0,6},{1,7},{2,4},{3,5},{4,2},{5,3},{6,0},{7,1},{8,14},{9,15},{10,... | collective-permute-start | bytes 737288 | tf_op jit(solution)/shard_map/ppermute | solution.py:27
  129.4 14.9 %collective-permute-start.31 = (bf16[2,40,1536]{2,1,0:T(8,128)(2,1)S(1)}, bf16[2,40,1536]{2,1,0:T(8,128)(2,1)S(1)}, u32[]{:S(2)}, u32[]{:S(2)}) collective-permute-start(bf16[2,40,1536]{2,1,0:T(8,128)(2,1)S(1)} %reply.5), channel_id=1, source_target_pairs={{0,4},{1,5},{2,6},{3,7},{4,0},{5,1},{6,2},{7,3},{8,12},{9,13},{10,... | collective-permute-start | bytes 737288 | tf_op jit(solution)/shard_map/ppermute | solution.py:27
  135.0 9.4 %collective-permute-start.28 = (bf16[1,2,40,1536]{3,2,1,0:T(8,128)(2,1)S(1)}, bf16[1,2,40,1536]{3,2,1,0:T(8,128)(2,1)S(1)}, u32[]{:S(2)}, u32[]{:S(2)}) collective-permute-start(bf16[1,2,40,1536]{3,2,1,0:T(8,128)(2,1)S(1)} %get-tuple-element.99), channel_id=1, source_target_pairs={{0,16},{8,24},{16,0},{24,8},{1,17},{9,25},{17,1},{25,9},{2,18},{10... | collective-permute-start | bytes 737288 | tf_op jit(solution)/shard_map/ppermute | solution.py:27
  137.6 9.3 %collective-permute-start.32 = (bf16[2,40,1536]{2,1,0:T(8,128)(2,1)S(1)}, bf16[2,40,1536]{2,1,0:T(8,128)(2,1)S(1)}, u32[]{:S(2)}, u32[]{:S(2)}) collective-permute-start(bf16[2,40,1536]{2,1,0:T(8,128)(2,1)S(1)} %reply.6), channel_id=1, source_target_pairs={{0,2},{1,3},{2,0},{3,1},{4,6},{5,7},{6,4},{7,5},{8,10},{9,11},{10,... | collective-permute-start | bytes 737288 | tf_op jit(solution)/shard_map/ppermute | solution.py:27
  147.5 1.8 %collective-permute-start.33 = (bf16[256,768]{1,0:T(8,128)(2,1)S(1)}, bf16[256,768]{1,0:T(8,128)(2,1)S(1)}, u32[]{:S(2)}, u32[]{:S(2)}) collective-permute-start(bf16[256,768]{1,0:T(8,128)(2,1)S(1)} %get-tuple-element.104), channel_id=1, source_target_pairs={{0,1},{1,0},{2,3},{3,2},{4,5},{5,4},{6,7},{7,6},{8,9},{9,8},{10,11... | collective-permute-start | bytes 1179656 | tf_op jit(solution)/shard_map/ppermute | solution.py:27

commit v8 on v7

--- a/solution.py
+++ b/solution.py
@@ -479,8 +479,8 @@
 
 def prefix_of_four(states, decay, me, beside_first, beside_last):
     high, low = (me & 2) != 0, (me & 1) != 0
-    near = swap(decay, "ctx", 4, 1, lambda i: i in (1, 2))
-    far = swap(decay, "ctx", 4, 3, lambda i: i == 1)
+    near = swap(decay, "ctx", 4, 1)
+    far = swap(decay, "ctx", 4, 3)
     one, two = states
     first = beside_first(one)
     got_one = after(swap(one, "ctx", 4, 1, lambda i: i != 3), *first).astype(F32)
@@ -514,7 +514,7 @@
     me = lax.axis_index("ctx")
     place = jnp.stack([me, lax.axis_index("exp")]).astype(jnp.int32)
     struct = jax.ShapeDtypeStruct
-    early_pieces = [("up", k) for k in range(max(chunks - 2, 0), chunks)] + [("down", chunks - 1)]
+    early_pieces = [("up", k) for k in ([1, 3] if chunks == 4 else range(max(chunks - 2, 0), chunks))] + [("down", chunks - 1)]
     decay_rows = jnp.transpose(log_decay, (2, 0, 1)).reshape(heads * requests, length)
 
     states = pl.pallas_call(
@@ -602,25 +602,34 @@
     )(place, other, router.T, *arrived)
 
     bits = bits_of(n_ctx)
+    zs = [0, 2, 1] + list(range(3, chunks)) if chunks > 3 else list(range(chunks))
     orders = [bits if k % 2 == 0 else bits[::-1] for k in range(chunks)]
 
     routes = [route_of(order, n_ctx) for order in orders]
-    gathered = [None] * chunks
-    for k in range(chunks):
+    gathered = {}
+    total, done = None, max(chunks - 2, 0)
+
+    def advance(i, *others):
+        return project(
+            after(place, *others), [zs[i]], chunks, gathered, expert_up, expert_down, held, total, None
+        )[0]
+
+    for i, k in enumerate(zs):
         have = {0: arrived[k]}
-        if k == 1:
-            have[0] = after(arrived[k], *[gathered[0][bit] for bit in bits])
-        for bit in orders[k]:
+        if i == 1:
+            have[0] = after(arrived[k], *[gathered[zs[0]][bit] for bit in bits])
+        if i == 2:
+            total = advance(0)
+        if i >= 2 and i < 9:
+            have[0] = after(arrived[k], total)
+        for bit in orders[i]:
             have.update({rel | bit: swap(a, "ctx", n_ctx, bit) for rel, a in list(have.items())})
         gathered[k] = [have[rel] for rel in range(n_ctx)]
-    total, done = None, max(chunks - 2, 0)
-    for k in range(done):
-        (total,) = project(
-            after(place, arrived[-1]), [k], chunks, gathered, expert_up, expert_down, held, total, None
-        )
+    for i in range(1 if chunks > 2 else 0, done):
+        total = advance(i)
     hidden, *far = project(
         after(place, weight),
-        list(range(done, chunks)),
+        zs[done:],
         chunks,
         gathered,
         expert_up,

time: 151 us -> 155 us (1.026)
  starting transfers between devices: 48.9 us -> 54.3 us
    ppermute x34, starting transfers between devices: 48.9 us -> 54.3 us  [swap(): return lax.ppermute(x, axis, [(i, i ^ k) for i in range(n) if keep(i)])]
  transfers between devices with their start and end apart: 34 -> 34, of which waited for: 13 -> 14; matrix products, arithmetic and copies ran while one was open for 3% -> 3% of each run, Pallas kernels for 26% -> 26%
where the time goes in v8:
time: 155 us; the launch traced here: 154 us
  Pallas kernels  55.6 us (36%)
  starting transfers between devices  54.3 us (35%)
  waiting for transfers between devices  37.1 us (24%)
  other arithmetic  5.03 us (3%)
  local copies, waits for them, and re-layouts  1.83 us (1%)
    ppermute x34, starting transfers between devices, swap(): return lax.ppermute(x, axis, [(i, i ^ k) for i in range(n) if keep(i)])  54.3 us
    ppermute x34, waiting for transfers between devices, swap(): return lax.ppermute(x, axis, [(i, i ^ k) for i in range(n) if keep(i)])  37.1 us
    pallas_call x3, Pallas kernels, project(): pl.pallas_call(functools.partial(project_kernel, chunks=chunks, parts=par...  18.9 us
    pallas_call x3, Pallas kernels, down_chunk(): pl.pallas_call(functools.partial(down_kernel, chunk=chunk, route=route),...  15.3 us
    pallas_call x2, Pallas kernels, call_with_held(): pl.pallas_call(functools.partial(with_held, kernel, pieces), in_specs=[SM...  8.35 us
    pallas_call x1, Pallas kernels, beside_first(): pl.pallas_call(inside_kernel, in_specs=[SMEM] + [ANY] * 3 + [VMEM] * 2, o...  6.31 us
    pallas_call x1, Pallas kernels, body(): pl.pallas_call(state_kernel, in_specs=[ANY] * 2 + [VMEM], out_specs=[VMEM...  3.84 us
  transfers between devices with their start and end apart: 34, of which 14 were waited for; matrix products, arithmetic and copies ran while one was open for 3% of the time, Pallas kernels for 26%

profile of v8, /device:TPU:0, one launch (start us, length us, event | category | flops | bytes accessed | tf_op | source)
XLA Modules:
  0.0 154.2 jit_solution(4683057845557711757)
XLA Ops:
  0.0 3.8 %local_state.1 = (bf16[12,128,128]{2,1,0:T(8,128)(2,1)}, bf16[12,128,128]{2,1,0:T(8,128)(2,1)}) custom-call(bf16[4,64,768]{2,1,0:T(8,128)(2,1)} %keys.3, bf16[4,64,768]{2,1,0:T(8,128)(2,1)} %values.3, f32[24,64]{1,0:T(8,128)} %bitcast.19), custom_call_target="tpu_custom_call" | custom-call | tf_op jit(solution)/shard_map/local_state/pallas_call | solution.py:520
  4.8 2.9 %collective-permute-start.1 = (f32[2,12,1,1]{1,0,3,2:T(2,128)S(1)}, f32[2,12,1,1]{1,0,3,2:T(2,128)S(1)}, u32[]{:S(2)}, u32[]{:S(2)}) collective-permute-start(f32[2,12,1,1]{1,0,3,2:T(2,128)S(1)} %exp.14), channel_id=1, source_target_pairs={{0,8},{8,0},{16,24},{24,16},{1,9},{9,1},{17,25},{25,17},{2,10},{10... | collective-permute-start | bytes 296 | tf_op jit(solution)/shard_map/ppermute | solution.py:27
  7.8 1.5 collective-permute-start.3
  9.3 2.0 %collective-permute-start.4 = (bf16[12,128,128]{2,1,0:T(8,128)(2,1)}, bf16[12,128,128]{2,1,0:T(8,128)(2,1)S(1)}, u32[]{:S(2)}, u32[]{:S(2)}) collective-permute-start(bf16[12,128,128]{2,1,0:T(8,128)(2,1)} %get-tuple-element.60), channel_id=1, source_target_pairs={{0,16},{8,24},{1,17},{9,25},{2,18},{10,26},{3,19},{11,27},{4,20},{... | collective-permute-start | bytes 1179656 | tf_op jit(solution)/shard_map/ppermute | solution.py:27
  11.2 3.9 %collective-permute-start = (bf16[12,128,128]{2,1,0:T(8,128)(2,1)}, bf16[12,128,128]{2,1,0:T(8,128)(2,1)S(1)}, u32[]{:S(2)}, u32[]{:S(2)}) collective-permute-start(bf16[12,128,128]{2,1,0:T(8,128)(2,1)} %get-tuple-element.56), channel_id=1, source_target_pairs={{0,8},{8,0},{16,24},{1,9},{9,1},{17,25},{2,10},{10,2},{18,26},{3,1... | collective-permute-start | bytes 1179656 | tf_op jit(solution)/shard_map/ppermute | solution.py:27
  16.1 6.3 %inside_and_placement.1 = (f32[4,64,768]{2,1,0:T(8,128)}, bf16[320,256]{1,0:T(8,128)(2,1)}, s32[80,128]{1,0:T(8,128)}) custom-call(s32[2]{0:T(128)} %pad_add_fusion.place, bf16[4,64,768]{2,1,0:T(8,128)(2,1)} %refs_0_.1, bf16[4,64,768]{2,1,0:T(8,128)(2,1)} %keys.3, bf16[4,64,768]{2,1,0:T(8,128)(2,1)} %values.3, f32[24,64]{1,0:T(8,128)} %bitcast.20, ...), custom_call_target="tpu_custom_call" | custom-call | tf_op jit(solution)/shard_map/inside_and_placement/pallas_call | solution.py:537
  22.4 1.2 collective-permute-done
  23.6 1.2 fusion.3
  24.8 1.3 collective-permute-start.2
  26.2 1.2 fusion.5
  27.4 4.1 %collective-permute-start.5 = (bf16[12,128,128]{2,1,0:T(8,128)(2,1)S(1)}, bf16[12,128,128]{2,1,0:T(8,128)(2,1)S(1)}, u32[]{:S(2)}, u32[]{:S(2)}) collective-permute-start(bf16[12,128,128]{2,1,0:T(8,128)(2,1)S(1)} %fusion.5), channel_id=1, source_target_pairs={{0,8},{16,24},{24,16},{1,9},{17,25},{25,17},{2,10},{18,26},{26,18}... | collective-permute-start | bytes 1179656 | tf_op jit(solution)/shard_map/ppermute | solution.py:27
  32.7 5.7 %early_weights.1 = (bf16[2,768,1536]{2,1,0:T(8,128)(2,1)S(1)}, bf16[2,768,1536]{2,1,0:T(8,128)(2,1)S(1)}, bf16[2,1536,768]{2,1,0:T(8,128)(2,1)S(1)}) custom-call(s32[2]{0:T(128)S(1)} %copy-done.5, bf16[2,6144,1536]{2,1,0:T(8,128)(2,1)} %up.9, bf16[2,1536,6144]{2,1,0:T(8,128)(2,1)} %weights.5), custom_call_target="tpu_custom_call" | custom-call | tf_op jit(solution)/shard_map/early_weights/pallas_call | solution.py:97
  38.9 2.6 %normed.1.refs_0_ = bf16[256,768]{1,0:T(8,128)(2,1)S(1)} custom-call(s32[2]{0:T(128)S(1)} %copy-done.5, bf16[2,6144,1536]{2,1,0:T(8,128)(2,1)} %up.9, bf16[2,1536,6144]{2,1,0:T(8,128)(2,1)} %weights.5, bf16[4,64,768]{2,1,0:T(8,128)(2,1)S(1)} %copy-done, f32[4,64,768]{2,1,0:T(8,128)S(1)} %copy-done.1, f32[24,64]{1,0:T(8,128)S(1)} %bitcast.21, ...), custom_call_target="tpu_custom_call" | custom-call | tf_op jit(solution)/shard_map/normed/pallas_call | solution.py:97
  41.6 1.7 %collective-permute-done.6.refs_1_ = bf16[256,768]{1,0:T(8,128)(2,1)S(1)} collective-permute-done((bf16[256,768]{1,0:T(8,128)(2,1)S(1)}, bf16[256,768]{1,0:T(8,128)(2,1)S(1)}, u32[]{:S(2)}, u32[]{:S(2)}) %collective-permute-start.6) | collective-permute-done | bytes 393248 | tf_op jit(solution)/shard_map/ppermute | solution.py:27
  43.8 1.7 %collective-permute-start.10 = (bf16[2,40,1536]{2,1,0:T(8,128)(2,1)S(1)}, bf16[2,40,1536]{2,1,0:T(8,128)(2,1)S(1)}, u32[]{:S(2)}, u32[]{:S(2)}) collective-permute-start(bf16[2,40,1536]{2,1,0:T(8,128)(2,1)S(1)} %get-tuple-element.69.refs_0_), channel_id=1, source_target_pairs={{0,8},{8,0},{16,24},{24,16},{1,9},{9,1},{17,25},{25,17},{2,10},{10... | collective-permute-start | bytes 737288 | tf_op jit(solution)/shard_map/ppermute | solution.py:27
  45.5 2.6 %collective-permute-start.8 = (bf16[2,40,1536]{2,1,0:T(8,128)(2,1)S(1)}, bf16[2,40,1536]{2,1,0:T(8,128)(2,1)S(1)}, u32[]{:S(2)}, u32[]{:S(2)}) collective-permute-start(bf16[2,40,1536]{2,1,0:T(8,128)(2,1)S(1)} %get-tuple-element.71), channel_id=1, source_target_pairs={{0,4},{1,5},{2,6},{3,7},{4,0},{5,1},{6,2},{7,3},{8,12},{9,13},{10,... | collective-permute-start | bytes 737288 | tf_op jit(solution)/shard_map/ppermute | solution.py:27
  48.1 3.8 %collective-permute-done.10.refs_1_ = bf16[2,40,1536]{2,1,0:T(8,128)(2,1)S(1)} collective-permute-done((bf16[2,40,1536]{2,1,0:T(8,128)(2,1)S(1)}, bf16[2,40,1536]{2,1,0:T(8,128)(2,1)S(1)}, u32[]{:S(2)}, u32[]{:S(2)}) %collective-permute-start.10) | collective-permute-done | bytes 245792 | tf_op jit(solution)/shard_map/ppermute | solution.py:27
  51.9 3.6 %collective-permute-start.9 = (bf16[2,40,1536]{2,1,0:T(8,128)(2,1)S(1)}, bf16[2,40,1536]{2,1,0:T(8,128)(2,1)S(1)}, u32[]{:S(2)}, u32[]{:S(2)}) collective-permute-start(bf16[2,40,1536]{2,1,0:T(8,128)(2,1)S(1)} %get-tuple-element.72), channel_id=1, source_target_pairs={{0,6},{1,7},{2,4},{3,5},{4,2},{5,3},{6,0},{7,1},{8,14},{9,15},{10,... | collective-permute-start | bytes 737288 | tf_op jit(solution)/shard_map/ppermute | solution.py:27
  55.5 10.3 %collective-permute-done.8.refs_2_.refs_0_ = bf16[2,40,1536]{2,1,0:T(8,128)(2,1)S(1)} collective-permute-done((bf16[2,40,1536]{2,1,0:T(8,128)(2,1)S(1)}, bf16[2,40,1536]{2,1,0:T(8,128)(2,1)S(1)}, u32[]{:S(2)}, u32[]{:S(2)}) %collective-permute-start.8) | collective-permute-done | bytes 245792 | tf_op jit(solution)/shard_map/ppermute | solution.py:27
  65.8 1.8 %collective-permute-start.20 = (bf16[2,40,1536]{2,1,0:T(8,128)(2,1)S(1)}, bf16[2,40,1536]{2,1,0:T(8,128)(2,1)S(1)}, u32[]{:S(2)}, u32[]{:S(2)}) collective-permute-start(bf16[2,40,1536]{2,1,0:T(8,128)(2,1)S(1)} %collective-permute-done.8.refs_2_.refs_0_), channel_id=1, source_target_pairs={{0,16},{8,24},{16,0},{24,8},{1,17},{9,25},{17,1},{25,9},{2,18},{10... | collective-permute-start | bytes 737288 | tf_op jit(solution)/shard_map/ppermute | solution.py:27
  68.0 5.3 %project_0.1.refs_4_ = f32[2,160,1536]{2,1,0:T(8,128)S(1)} custom-call(s32[2]{0:T(128)S(1)} %copy-done.6, bf16[2,6144,1536]{2,1,0:T(8,128)(2,1)} %up.9, bf16[2,1536,6144]{2,1,0:T(8,128)(2,1)} %weights.5, bf16[2,40,1536]{2,1,0:T(8,128)(2,1)S(1)} %get-tuple-element.69.refs_0_, bf16[2,40,1536]{2,1,0:T(8,128)(2,1)S(1)} %collective-permute-done.10.refs_1_, ...), custom_call_target="tpu_custom_call" | custom-call | flops 1509949440 | bytes 9437184 | tf_op jit(solution)/shard_map/project_0/pallas_call | solution.py:326
  73.6 1.6 %collective-permute-start.13 = (bf16[2,40,1536]{2,1,0:T(8,128)(2,1)S(1)}, bf16[2,40,1536]{2,1,0:T(8,128)(2,1)S(1)}, u32[]{:S(2)}, u32[]{:S(2)}) collective-permute-start(bf16[2,40,1536]{2,1,0:T(8,128)(2,1)S(1)} %collective-permute-done.7.refs_1_.refs_0_), channel_id=1, source_target_pairs={{0,8},{8,0},{16,24},{24,16},{1,9},{9,1},{17,25},{25,17},{2,10},{10... | collective-permute-start | bytes 737288 | tf_op jit(solution)/shard_map/ppermute | solution.py:27
  75.6 1.6 %collective-permute-start.16 = (bf16[2,40,1536]{2,1,0:T(8,128)(2,1)S(1)}, bf16[2,40,1536]{2,1,0:T(8,128)(2,1)S(1)}, u32[]{:S(2)}, u32[]{:S(2)}) collective-permute-start(bf16[2,40,1536]{2,1,0:T(8,128)(2,1)S(1)} %collective-permute-done.9.refs_3_.refs_4_), channel_id=1, source_target_pairs={{0,8},{8,0},{16,24},{24,16},{1,9},{9,1},{17,25},{25,17},{2,10},{10... | collective-permute-start | bytes 737288 | tf_op jit(solution)/shard_map/ppermute | solution.py:27
  77.2 1.8 %collective-permute-start.14 = (bf16[2,40,1536]{2,1,0:T(8,128)(2,1)S(1)}, bf16[2,40,1536]{2,1,0:T(8,128)(2,1)S(1)}, u32[]{:S(2)}, u32[]{:S(2)}) collective-permute-start(bf16[2,40,1536]{2,1,0:T(8,128)(2,1)S(1)} %collective-permute-done.7.refs_1_.refs_0_), channel_id=1, source_target_pairs={{0,16},{8,24},{16,0},{24,8},{1,17},{9,25},{17,1},{25,9},{2,18},{10... | collective-permute-start | bytes 737288 | tf_op jit(solution)/shard_map/ppermute | solution.py:27
  79.0 3.1 %collective-permute-done.17.refs_6_ = bf16[2,40,1536]{2,1,0:T(8,128)(2,1)S(1)} collective-permute-done((bf16[2,40,1536]{2,1,0:T(8,128)(2,1)S(1)}, bf16[2,40,1536]{2,1,0:T(8,128)(2,1)S(1)}, u32[]{:S(2)}, u32[]{:S(2)}) %collective-permute-start.17) | collective-permute-done | bytes 245792 | tf_op jit(solution)/shard_map/ppermute | solution.py:27
  82.2 1.7 %collective-permute-start.18 = (bf16[2,40,1536]{2,1,0:T(8,128)(2,1)S(1)}, bf16[2,40,1536]{2,1,0:T(8,128)(2,1)S(1)}, u32[]{:S(2)}, u32[]{:S(2)}) collective-permute-start(bf16[2,40,1536]{2,1,0:T(8,128)(2,1)S(1)} %collective-permute-done.17.refs_6_), channel_id=1, source_target_pairs={{0,8},{8,0},{16,24},{24,16},{1,9},{9,1},{17,25},{25,17},{2,10},{10... | collective-permute-start | bytes 737288 | tf_op jit(solution)/shard_map/ppermute | solution.py:27
  84.3 1.1 gate.1.weight
  85.4 2.3 %collective-permute-done.21.refs_3_ = bf16[2,40,1536]{2,1,0:T(8,128)(2,1)S(1)} collective-permute-done((bf16[2,40,1536]{2,1,0:T(8,128)(2,1)S(1)}, bf16[2,40,1536]{2,1,0:T(8,128)(2,1)S(1)}, u32[]{:S(2)}, u32[]{:S(2)}) %collective-permute-start.21) | collective-permute-done | bytes 245792 | tf_op jit(solution)/shard_map/ppermute | solution.py:27
  87.7 4.9 %project_2.1.refs_11_ = f32[2,160,1536]{2,1,0:T(8,128)S(1)} custom-call(s32[2]{0:T(128)S(1)} %copy-done.6, bf16[2,6144,1536]{2,1,0:T(8,128)(2,1)} %up.9, bf16[2,1536,6144]{2,1,0:T(8,128)(2,1)} %weights.5, bf16[2,40,1536]{2,1,0:T(8,128)(2,1)S(1)} %collective-permute-done.8.refs_2_.refs_0_, bf16[2,40,1536]{2,1,0:T(8,128)(2,1)S(1)} %collective-permute-done.19.refs_1_, ...), custom_call_target="tpu_custom_call" | custom-call | flops 1509949440 | bytes 9437184 | tf_op jit(solution)/shard_map/project_2/pallas_call | solution.py:326
  92.7 2.2 %collective-permute-done.18.refs_7_ = bf16[2,40,1536]{2,1,0:T(8,128)(2,1)S(1)} collective-permute-done((bf16[2,40,1536]{2,1,0:T(8,128)(2,1)S(1)}, bf16[2,40,1536]{2,1,0:T(8,128)(2,1)S(1)}, u32[]{:S(2)}, u32[]{:S(2)}) %collective-permute-start.18) | collective-permute-done | bytes 245792 | tf_op jit(solution)/shard_map/ppermute | solution.py:27
  94.9 8.7 %project_1.1 = (bf16[2,160,1536]{2,1,0:T(8,128)(2,1)S(1)}, bf16[2,2,40,1536]{3,2,1,0:T(8,128)(2,1)S(1)}, bf16[2,2,40,1536]{3,2,1,0:T(8,128)(2,1)S(1)}) custom-call(s32[2]{0:T(128)S(1)} %copy-done.6, bf16[2,6144,1536]{2,1,0:T(8,128)(2,1)} %up.9, bf16[2,1536,6144]{2,1,0:T(8,128)(2,1)} %weights.5, ...), custom_call_target="tpu_custom_call" | custom-call | flops 4529848320 | bytes 28311552 | tf_op jit(solution)/shard_map/project_1/pallas_call | solution.py:326
  103.5 1.1 collective-permute-start.22
  104.6 5.2 %down_2.1 = (bf16[2,2,40,1536]{3,2,1,0:T(8,128)(2,1)S(1)}, bf16[2,2,40,1536]{3,2,1,0:T(8,128)(2,1)S(1)}) custom-call(s32[2]{0:T(128)S(1)} %copy-done.6, bf16[2,1536,6144]{2,1,0:T(8,128)(2,1)} %weights.5, bf16[2,160,1536]{2,1,0:T(8,128)(2,1)S(1)} %get-tuple-element.86.hidden), custom_call_target="tpu_custom_call" | custom-call | flops 1509949440 | bytes 9437184 | tf_op jit(solution)/shard_map/down_2/pallas_call | solution.py:381
  109.8 1.8 %collective-permute-start.24 = (bf16[2,2,40,1536]{3,2,1,0:T(8,128)(2,1)S(1)}, bf16[2,2,40,1536]{3,2,1,0:T(8,128)(2,1)S(1)}, u32[]{:S(2)}, u32[]{:S(2)}) collective-permute-start(bf16[2,2,40,1536]{3,2,1,0:T(8,128)(2,1)S(1)} %get-tuple-element.81), channel_id=1, source_target_pairs={{0,8},{8,0},{16,24},{24,16},{1,9},{9,1},{17,25},{25,17},{2,10},{10... | collective-permute-start | bytes 1474568 | tf_op jit(solution)/shard_map/ppermute | solution.py:27
  111.6 5.0 %down_1.1 = (bf16[2,2,40,1536]{3,2,1,0:T(8,128)(2,1)S(1)}, bf16[2,2,40,1536]{3,2,1,0:T(8,128)(2,1)S(1)}) custom-call(s32[2]{0:T(128)S(1)} %copy-done.6, bf16[2,1536,6144]{2,1,0:T(8,128)(2,1)} %weights.5, bf16[2,160,1536]{2,1,0:T(8,128)(2,1)S(1)} %get-tuple-element.86.hidden), custom_call_target="tpu_custom_call" | custom-call | flops 1509949440 | bytes 9437184 | tf_op jit(solution)/shard_map/down_1/pallas_call | solution.py:381
  117.2 1.0 collective-permute-start.27
  118.2 5.0 %down_0.1 = (bf16[2,2,40,1536]{3,2,1,0:T(8,128)(2,1)S(1)}, bf16[2,2,40,1536]{3,2,1,0:T(8,128)(2,1)S(1)}) custom-call(s32[2]{0:T(128)S(1)} %copy-done.6, bf16[2,1536,6144]{2,1,0:T(8,128)(2,1)} %weights.5, bf16[2,160,1536]{2,1,0:T(8,128)(2,1)S(1)} %get-tuple-element.86.hidden), custom_call_target="tpu_custom_call" | custom-call | flops 1509949440 | bytes 9437184 | tf_op jit(solution)/shard_map/down_0/pallas_call | solution.py:381
  123.3 1.1 collective-permute-start.23
  124.6 1.7 %collective-permute-start.25 = (bf16[1,2,40,1536]{3,2,1,0:T(8,128)(2,1)S(1)}, bf16[1,2,40,1536]{3,2,1,0:T(8,128)(2,1)S(1)}, u32[]{:S(2)}, u32[]{:S(2)}) collective-permute-start(bf16[1,2,40,1536]{3,2,1,0:T(8,128)(2,1)S(1)} %get-tuple-element.92), channel_id=1, source_target_pairs={{0,16},{8,24},{16,0},{24,8},{1,17},{9,25},{17,1},{25,9},{2,18},{10... | collective-permute-start | bytes 737288 | tf_op jit(solution)/shard_map/ppermute | solution.py:27
  127.0 1.2 collective-permute-done.26.got
  128.3 1.4 collective-permute-start.29
  129.7 6.2 %collective-permute-start.30 = (bf16[2,40,1536]{2,1,0:T(8,128)(2,1)S(1)}, bf16[2,40,1536]{2,1,0:T(8,128)(2,1)S(1)}, u32[]{:S(2)}, u32[]{:S(2)}) collective-permute-start(bf16[2,40,1536]{2,1,0:T(8,128)(2,1)S(1)} %reply.4), channel_id=1, source_target_pairs={{0,6},{1,7},{2,4},{3,5},{4,2},{5,3},{6,0},{7,1},{8,14},{9,15},{10,... | collective-permute-start | bytes 737288 | tf_op jit(solution)/shard_map/ppermute | solution.py:27
  136.1 1.1 collective-permute-done.23.got
  137.3 1.8 %collective-permute-start.28 = (bf16[1,2,40,1536]{3,2,1,0:T(8,128)(2,1)S(1)}, bf16[1,2,40,1536]{3,2,1,0:T(8,128)(2,1)S(1)}, u32[]{:S(2)}, u32[]{:S(2)}) collective-permute-start(bf16[1,2,40,1536]{3,2,1,0:T(8,128)(2,1)S(1)} %get-tuple-element.101), channel_id=1, source_target_pairs={{0,16},{8,24},{16,0},{24,8},{1,17},{9,25},{17,1},{25,9},{2,18},{10... | collective-permute-start | bytes 737288 | tf_op jit(solution)/shard_map/ppermute | solution.py:27
  139.9 4.0 %collective-permute-start.32 = (bf16[2,40,1536]{2,1,0:T(8,128)(2,1)S(1)}, bf16[2,40,1536]{2,1,0:T(8,128)(2,1)S(1)}, u32[]{:S(2)}, u32[]{:S(2)}) collective-permute-start(bf16[2,40,1536]{2,1,0:T(8,128)(2,1)S(1)} %reply.6), channel_id=1, source_target_pairs={{0,2},{1,3},{2,0},{3,1},{4,6},{5,7},{6,4},{7,5},{8,10},{9,11},{10,... | collective-permute-start | bytes 737288 | tf_op jit(solution)/shard_map/ppermute | solution.py:27
  143.9 6.0 %collective-permute-done.31.refs_2_ = bf16[2,40,1536]{2,1,0:T(8,128)(2,1)S(1)} collective-permute-done((bf16[2,40,1536]{2,1,0:T(8,128)(2,1)S(1)}, bf16[2,40,1536]{2,1,0:T(8,128)(2,1)S(1)}, u32[]{:S(2)}, u32[]{:S(2)}) %collective-permute-start.31) | collective-permute-done | bytes 245792 | tf_op jit(solution)/shard_map/ppermute | solution.py:27
  150.0 1.0 collective-permute-done.32.refs_1_
  151.7 1.7 %collective-permute-done.33 = bf16[256,768]{1,0:T(8,128)(2,1)S(1)} collective-permute-done((bf16[256,768]{1,0:T(8,128)(2,1)S(1)}, bf16[256,768]{1,0:T(8,128)(2,1)S(1)}, u32[]{:S(2)}, u32[]{:S(2)}) %collective-permute-start.33) | collective-permute-done | bytes 393248 | tf_op jit(solution)/shard_map/ppermute | solution.py:27
  (75 shorter events, 9.9 us)
Async XLA Ops:
  4.8 17.6 %collective-permute-start.1 = (f32[2,12,1,1]{1,0,3,2:T(2,128)S(1)}, f32[2,12,1,1]{1,0,3,2:T(2,128)S(1)}, u32[]{:S(2)}, u32[]{:S(2)}) collective-permute-start(f32[2,12,1,1]{1,0,3,2:T(2,128)S(1)} %exp.14), channel_id=1, source_target_pairs={{0,8},{8,0},{16,24},{24,16},{1,9},{9,1},{17,25},{25,17},{2,10},{10... | collective-permute-start | bytes 296 | tf_op jit(solution)/shard_map/ppermute | solution.py:27
  7.8 18.4 %collective-permute-start.3 = (f32[2,12,1,1]{1,0,3,2:T(2,128)S(1)}, f32[2,12,1,1]{1,0,3,2:T(2,128)S(1)}, u32[]{:S(2)}, u32[]{:S(2)}) collective-permute-start(f32[2,12,1,1]{1,0,3,2:T(2,128)S(1)} %exp.14), channel_id=1, source_target_pairs={{0,24},{8,16},{16,8},{24,0},{1,25},{9,17},{17,9},{25,1},{2,26},{10... | collective-permute-start | bytes 296 | tf_op jit(solution)/shard_map/ppermute | solution.py:27
  9.3 16.9 %collective-permute-start.4 = (bf16[12,128,128]{2,1,0:T(8,128)(2,1)}, bf16[12,128,128]{2,1,0:T(8,128)(2,1)S(1)}, u32[]{:S(2)}, u32[]{:S(2)}) collective-permute-start(bf16[12,128,128]{2,1,0:T(8,128)(2,1)} %get-tuple-element.60), channel_id=1, source_target_pairs={{0,16},{8,24},{1,17},{9,25},{2,18},{10,26},{3,19},{11,27},{4,20},{... | collective-permute-start | bytes 1179656 | tf_op jit(solution)/shard_map/ppermute | solution.py:27
  11.2 12.4 %collective-permute-start = (bf16[12,128,128]{2,1,0:T(8,128)(2,1)}, bf16[12,128,128]{2,1,0:T(8,128)(2,1)S(1)}, u32[]{:S(2)}, u32[]{:S(2)}) collective-permute-start(bf16[12,128,128]{2,1,0:T(8,128)(2,1)} %get-tuple-element.56), channel_id=1, source_target_pairs={{0,8},{8,0},{16,24},{1,9},{9,1},{17,25},{2,10},{10,2},{18,26},{3,1... | collective-permute-start | bytes 1179656 | tf_op jit(solution)/shard_map/ppermute | solution.py:27
  24.8 13.6 %collective-permute-start.2 = (bf16[12,128,128]{2,1,0:T(8,128)(2,1)S(1)}, bf16[12,128,128]{2,1,0:T(8,128)(2,1)S(1)}, u32[]{:S(2)}, u32[]{:S(2)}) collective-permute-start(bf16[12,128,128]{2,1,0:T(8,128)(2,1)S(1)} %fusion.3), channel_id=1, source_target_pairs={{0,16},{8,24},{1,17},{9,25},{2,18},{10,26},{3,19},{11,27},{4,20},{... | collective-permute-start | bytes 1179656 | tf_op jit(solution)/shard_map/ppermute | solution.py:27
  27.4 11.3 %collective-permute-start.5 = (bf16[12,128,128]{2,1,0:T(8,128)(2,1)S(1)}, bf16[12,128,128]{2,1,0:T(8,128)(2,1)S(1)}, u32[]{:S(2)}, u32[]{:S(2)}) collective-permute-start(bf16[12,128,128]{2,1,0:T(8,128)(2,1)S(1)} %fusion.5), channel_id=1, source_target_pairs={{0,8},{16,24},{24,16},{1,9},{17,25},{25,17},{2,10},{18,26},{26,18}... | collective-permute-start | bytes 1179656 | tf_op jit(solution)/shard_map/ppermute | solution.py:27
  32.1 0.6 copy-start.5
  32.7 6.2 %copy-start = (bf16[4,64,768]{2,1,0:T(8,128)(2,1)S(1)}, bf16[4,64,768]{2,1,0:T(8,128)(2,1)}, u32[]{:S(2)}) copy-start(bf16[4,64,768]{2,1,0:T(8,128)(2,1)} %refs_0_.1) | copy-start | bytes 1179652
  32.7 6.2 %copy-start.1 = (f32[4,64,768]{2,1,0:T(8,128)S(1)}, f32[4,64,768]{2,1,0:T(8,128)}, u32[]{:S(2)}) copy-start(f32[4,64,768]{2,1,0:T(8,128)} %get-tuple-element.58.refs_1_) | copy-start | bytes 2359300
  32.7 6.2 %copy-start.3 = (f32[4,64,6]{1,0,2:T(4,128)S(1)}, f32[4,64,6]{1,0,2:T(4,128)}, u32[]{:S(2)}) copy-start(f32[4,64,6]{1,0,2:T(4,128)} %param.12) | copy-start | bytes 18436
  38.9 4.4 %copy-start.2 = (bf16[320,256]{1,0:T(8,128)(2,1)S(1)}, bf16[320,256]{1,0:T(8,128)(2,1)}, u32[]{:S(2)}) copy-start(bf16[320,256]{1,0:T(8,128)(2,1)} %get-tuple-element.67.placement) | copy-start | bytes 491524
  38.9 29.1 %copy-start.6 = (s32[2]{0:T(128)S(1)}, s32[2]{0:T(128)}, u32[]{:S(2)}) copy-start(s32[2]{0:T(128)} %pad_add_fusion.place) | copy-start | bytes 28
  41.6 1.8 %collective-permute-start.6 = (bf16[256,768]{1,0:T(8,128)(2,1)S(1)}, bf16[256,768]{1,0:T(8,128)(2,1)S(1)}, u32[]{:S(2)}, u32[]{:S(2)}) collective-permute-start(bf16[256,768]{1,0:T(8,128)(2,1)S(1)} %normed.1.refs_0_), channel_id=1, source_target_pairs={{0,1},{1,0},{2,3},{3,2},{4,5},{5,4},{6,7},{7,6},{8,9},{9,8},{10,11... | collective-permute-start | bytes 1179656 | tf_op jit(solution)/shard_map/ppermute | solution.py:27
  43.8 8.1 %collective-permute-start.10 = (bf16[2,40,1536]{2,1,0:T(8,128)(2,1)S(1)}, bf16[2,40,1536]{2,1,0:T(8,128)(2,1)S(1)}, u32[]{:S(2)}, u32[]{:S(2)}) collective-permute-start(bf16[2,40,1536]{2,1,0:T(8,128)(2,1)S(1)} %get-tuple-element.69.refs_0_), channel_id=1, source_target_pairs={{0,8},{8,0},{16,24},{24,16},{1,9},{9,1},{17,25},{25,17},{2,10},{10... | collective-permute-start | bytes 737288 | tf_op jit(solution)/shard_map/ppermute | solution.py:27
  45.5 10.0 %collective-permute-start.11 = (bf16[2,40,1536]{2,1,0:T(8,128)(2,1)S(1)}, bf16[2,40,1536]{2,1,0:T(8,128)(2,1)S(1)}, u32[]{:S(2)}, u32[]{:S(2)}) collective-permute-start(bf16[2,40,1536]{2,1,0:T(8,128)(2,1)S(1)} %get-tuple-element.69.refs_0_), channel_id=1, source_target_pairs={{0,16},{8,24},{16,0},{24,8},{1,17},{9,25},{17,1},{25,9},{2,18},{10... | collective-permute-start | bytes 737288 | tf_op jit(solution)/shard_map/ppermute | solution.py:27
  45.5 20.3 %collective-permute-start.8 = (bf16[2,40,1536]{2,1,0:T(8,128)(2,1)S(1)}, bf16[2,40,1536]{2,1,0:T(8,128)(2,1)S(1)}, u32[]{:S(2)}, u32[]{:S(2)}) collective-permute-start(bf16[2,40,1536]{2,1,0:T(8,128)(2,1)S(1)} %get-tuple-element.71), channel_id=1, source_target_pairs={{0,4},{1,5},{2,6},{3,7},{4,0},{5,1},{6,2},{7,3},{8,12},{9,13},{10,... | collective-permute-start | bytes 737288 | tf_op jit(solution)/shard_map/ppermute | solution.py:27
  51.8 16.2 %collective-permute-start.12 = (bf16[2,40,1536]{2,1,0:T(8,128)(2,1)S(1)}, bf16[2,40,1536]{2,1,0:T(8,128)(2,1)S(1)}, u32[]{:S(2)}, u32[]{:S(2)}) collective-permute-start(bf16[2,40,1536]{2,1,0:T(8,128)(2,1)S(1)} %collective-permute-done.10.refs_1_), channel_id=1, source_target_pairs={{0,16},{8,24},{16,0},{24,8},{1,17},{9,25},{17,1},{25,9},{2,18},{10... | collective-permute-start | bytes 737288 | tf_op jit(solution)/shard_map/ppermute | solution.py:27
  51.9 21.4 %collective-permute-start.9 = (bf16[2,40,1536]{2,1,0:T(8,128)(2,1)S(1)}, bf16[2,40,1536]{2,1,0:T(8,128)(2,1)S(1)}, u32[]{:S(2)}, u32[]{:S(2)}) collective-permute-start(bf16[2,40,1536]{2,1,0:T(8,128)(2,1)S(1)} %get-tuple-element.72), channel_id=1, source_target_pairs={{0,6},{1,7},{2,4},{3,5},{4,2},{5,3},{6,0},{7,1},{8,14},{9,15},{10,... | collective-permute-start | bytes 737288 | tf_op jit(solution)/shard_map/ppermute | solution.py:27
  55.5 28.8 %copy-start.4 = (bf16[6144,16]{0,1:T(8,128)(2,1)S(1)}, bf16[6144,16]{0,1:T(8,128)(2,1)}, u32[]{:S(2)}) copy-start(bf16[6144,16]{0,1:T(8,128)(2,1)} %param.14) | copy-start | bytes 589828
  55.5 28.8 %copy-start.7 = (s32[80,128]{1,0:T(8,128)S(1)}, s32[80,128]{1,0:T(8,128)}, u32[]{:S(2)}) copy-start(s32[80,128]{1,0:T(8,128)} %get-tuple-element.68.other) | copy-start | bytes 122884
  55.5 18.1 %collective-permute-start.7 = (bf16[2,40,1536]{2,1,0:T(8,128)(2,1)S(1)}, bf16[2,40,1536]{2,1,0:T(8,128)(2,1)S(1)}, u32[]{:S(2)}, u32[]{:S(2)}) collective-permute-start(bf16[2,40,1536]{2,1,0:T(8,128)(2,1)S(1)} %get-tuple-element.70), channel_id=1, source_target_pairs={{0,2},{1,3},{2,0},{3,1},{4,6},{5,7},{6,4},{7,5},{8,10},{9,11},{10,... | collective-permute-start | bytes 737288 | tf_op jit(solution)/shard_map/ppermute | solution.py:27
  65.8 9.4 %collective-permute-start.20 = (bf16[2,40,1536]{2,1,0:T(8,128)(2,1)S(1)}, bf16[2,40,1536]{2,1,0:T(8,128)(2,1)S(1)}, u32[]{:S(2)}, u32[]{:S(2)}) collective-permute-start(bf16[2,40,1536]{2,1,0:T(8,128)(2,1)S(1)} %collective-permute-done.8.refs_2_.refs_0_), channel_id=1, source_target_pairs={{0,16},{8,24},{16,0},{24,8},{1,17},{9,25},{17,1},{25,9},{2,18},{10... | collective-permute-start | bytes 737288 | tf_op jit(solution)/shard_map/ppermute | solution.py:27
  67.6 9.6 %collective-permute-start.19 = (bf16[2,40,1536]{2,1,0:T(8,128)(2,1)S(1)}, bf16[2,40,1536]{2,1,0:T(8,128)(2,1)S(1)}, u32[]{:S(2)}, u32[]{:S(2)}) collective-permute-start(bf16[2,40,1536]{2,1,0:T(8,128)(2,1)S(1)} %collective-permute-done.8.refs_2_.refs_0_), channel_id=1, source_target_pairs={{0,8},{8,0},{16,24},{24,16},{1,9},{9,1},{17,25},{25,17},{2,10},{10... | collective-permute-start | bytes 737288 | tf_op jit(solution)/shard_map/ppermute | solution.py:27
  73.3 8.9 %collective-permute-start.17 = (bf16[2,40,1536]{2,1,0:T(8,128)(2,1)S(1)}, bf16[2,40,1536]{2,1,0:T(8,128)(2,1)S(1)}, u32[]{:S(2)}, u32[]{:S(2)}) collective-permute-start(bf16[2,40,1536]{2,1,0:T(8,128)(2,1)S(1)} %collective-permute-done.9.refs_3_.refs_4_), channel_id=1, source_target_pairs={{0,16},{8,24},{16,0},{24,8},{1,17},{9,25},{17,1},{25,9},{2,18},{10... | collective-permute-start | bytes 737288 | tf_op jit(solution)/shard_map/ppermute | solution.py:27
  73.6 10.3 %collective-permute-start.13 = (bf16[2,40,1536]{2,1,0:T(8,128)(2,1)S(1)}, bf16[2,40,1536]{2,1,0:T(8,128)(2,1)S(1)}, u32[]{:S(2)}, u32[]{:S(2)}) collective-permute-start(bf16[2,40,1536]{2,1,0:T(8,128)(2,1)S(1)} %collective-permute-done.7.refs_1_.refs_0_), channel_id=1, source_target_pairs={{0,8},{8,0},{16,24},{24,16},{1,9},{9,1},{17,25},{25,17},{2,10},{10... | collective-permute-start | bytes 737288 | tf_op jit(solution)/shard_map/ppermute | solution.py:27
  75.2 12.5 %collective-permute-start.21 = (bf16[2,40,1536]{2,1,0:T(8,128)(2,1)S(1)}, bf16[2,40,1536]{2,1,0:T(8,128)(2,1)S(1)}, u32[]{:S(2)}, u32[]{:S(2)}) collective-permute-start(bf16[2,40,1536]{2,1,0:T(8,128)(2,1)S(1)} %collective-permute-done.20.refs_2_), channel_id=1, source_target_pairs={{0,8},{8,0},{16,24},{24,16},{1,9},{9,1},{17,25},{25,17},{2,10},{10... | collective-permute-start | bytes 737288 | tf_op jit(solution)/shard_map/ppermute | solution.py:27
  75.6 17.1 %collective-permute-start.16 = (bf16[2,40,1536]{2,1,0:T(8,128)(2,1)S(1)}, bf16[2,40,1536]{2,1,0:T(8,128)(2,1)S(1)}, u32[]{:S(2)}, u32[]{:S(2)}) collective-permute-start(bf16[2,40,1536]{2,1,0:T(8,128)(2,1)S(1)} %collective-permute-done.9.refs_3_.refs_4_), channel_id=1, source_target_pairs={{0,8},{8,0},{16,24},{24,16},{1,9},{9,1},{17,25},{25,17},{2,10},{10... | collective-permute-start | bytes 737288 | tf_op jit(solution)/shard_map/ppermute | solution.py:27
  77.2 15.4 %collective-permute-start.14 = (bf16[2,40,1536]{2,1,0:T(8,128)(2,1)S(1)}, bf16[2,40,1536]{2,1,0:T(8,128)(2,1)S(1)}, u32[]{:S(2)}, u32[]{:S(2)}) collective-permute-start(bf16[2,40,1536]{2,1,0:T(8,128)(2,1)S(1)} %collective-permute-done.7.refs_1_.refs_0_), channel_id=1, source_target_pairs={{0,16},{8,24},{16,0},{24,8},{1,17},{9,25},{17,1},{25,9},{2,18},{10... | collective-permute-start | bytes 737288 | tf_op jit(solution)/shard_map/ppermute | solution.py:27
  82.2 12.7 %collective-permute-start.18 = (bf16[2,40,1536]{2,1,0:T(8,128)(2,1)S(1)}, bf16[2,40,1536]{2,1,0:T(8,128)(2,1)S(1)}, u32[]{:S(2)}, u32[]{:S(2)}) collective-permute-start(bf16[2,40,1536]{2,1,0:T(8,128)(2,1)S(1)} %collective-permute-done.17.refs_6_), channel_id=1, source_target_pairs={{0,8},{8,0},{16,24},{24,16},{1,9},{9,1},{17,25},{25,17},{2,10},{10... | collective-permute-start | bytes 737288 | tf_op jit(solution)/shard_map/ppermute | solution.py:27
  83.9 11.0 %collective-permute-start.15 = (bf16[2,40,1536]{2,1,0:T(8,128)(2,1)S(1)}, bf16[2,40,1536]{2,1,0:T(8,128)(2,1)S(1)}, u32[]{:S(2)}, u32[]{:S(2)}) collective-permute-start(bf16[2,40,1536]{2,1,0:T(8,128)(2,1)S(1)} %collective-permute-done.13.refs_1_), channel_id=1, source_target_pairs={{0,16},{8,24},{16,0},{24,8},{1,17},{9,25},{17,1},{25,9},{2,18},{10... | collective-permute-start | bytes 737288 | tf_op jit(solution)/shard_map/ppermute | solution.py:27
  103.5 13.6 %collective-permute-start.22 = (bf16[2,2,40,1536]{3,2,1,0:T(8,128)(2,1)S(1)}, bf16[2,2,40,1536]{3,2,1,0:T(8,128)(2,1)S(1)}, u32[]{:S(2)}, u32[]{:S(2)}) collective-permute-start(bf16[2,2,40,1536]{3,2,1,0:T(8,128)(2,1)S(1)} %get-tuple-element.79), channel_id=1, source_target_pairs={{0,16},{8,24},{16,0},{24,8},{1,17},{9,25},{17,1},{25,9},{2,18},{10... | collective-permute-start | bytes 1474568 | tf_op jit(solution)/shard_map/ppermute | solution.py:27
  109.8 14.6 %collective-permute-start.24 = (bf16[2,2,40,1536]{3,2,1,0:T(8,128)(2,1)S(1)}, bf16[2,2,40,1536]{3,2,1,0:T(8,128)(2,1)S(1)}, u32[]{:S(2)}, u32[]{:S(2)}) collective-permute-start(bf16[2,2,40,1536]{3,2,1,0:T(8,128)(2,1)S(1)} %get-tuple-element.81), channel_id=1, source_target_pairs={{0,8},{8,0},{16,24},{24,16},{1,9},{9,1},{17,25},{25,17},{2,10},{10... | collective-permute-start | bytes 1474568 | tf_op jit(solution)/shard_map/ppermute | solution.py:27
  116.7 11.5 %collective-permute-start.26 = (bf16[2,2,40,1536]{3,2,1,0:T(8,128)(2,1)S(1)}, bf16[2,2,40,1536]{3,2,1,0:T(8,128)(2,1)S(1)}, u32[]{:S(2)}, u32[]{:S(2)}) collective-permute-start(bf16[2,2,40,1536]{3,2,1,0:T(8,128)(2,1)S(1)} %get-tuple-element.83), channel_id=1, source_target_pairs={{0,16},{8,24},{16,0},{24,8},{1,17},{9,25},{17,1},{25,9},{2,18},{10... | collective-permute-start | bytes 1474568 | tf_op jit(solution)/shard_map/ppermute | solution.py:27
  117.2 9.7 %collective-permute-start.27 = (bf16[1,2,40,1536]{3,2,1,0:T(8,128)(2,1)S(1)}, bf16[1,2,40,1536]{3,2,1,0:T(8,128)(2,1)S(1)}, u32[]{:S(2)}, u32[]{:S(2)}) collective-permute-start(bf16[1,2,40,1536]{3,2,1,0:T(8,128)(2,1)S(1)} %get-tuple-element.85), channel_id=1, source_target_pairs={{0,8},{8,0},{16,24},{24,16},{1,9},{9,1},{17,25},{25,17},{2,10},{10... | collective-permute-start | bytes 737288 | tf_op jit(solution)/shard_map/ppermute | solution.py:27
  123.3 13.9 %collective-permute-start.23 = (bf16[2,2,40,1536]{3,2,1,0:T(8,128)(2,1)S(1)}, bf16[2,2,40,1536]{3,2,1,0:T(8,128)(2,1)S(1)}, u32[]{:S(2)}, u32[]{:S(2)}) collective-permute-start(bf16[2,2,40,1536]{3,2,1,0:T(8,128)(2,1)S(1)} %get-tuple-element.88), channel_id=1, source_target_pairs={{0,8},{8,0},{16,24},{24,16},{1,9},{9,1},{17,25},{25,17},{2,10},{10... | collective-permute-start | bytes 1474568 | tf_op jit(solution)/shard_map/ppermute | solution.py:27
  124.6 11.4 %collective-permute-start.25 = (bf16[1,2,40,1536]{3,2,1,0:T(8,128)(2,1)S(1)}, bf16[1,2,40,1536]{3,2,1,0:T(8,128)(2,1)S(1)}, u32[]{:S(2)}, u32[]{:S(2)}) collective-permute-start(bf16[1,2,40,1536]{3,2,1,0:T(8,128)(2,1)S(1)} %get-tuple-element.92), channel_id=1, source_target_pairs={{0,16},{8,24},{16,0},{24,8},{1,17},{9,25},{17,1},{25,9},{2,18},{10... | collective-permute-start | bytes 737288 | tf_op jit(solution)/shard_map/ppermute | solution.py:27
  128.3 11.5 %collective-permute-start.29 = (bf16[1,2,40,1536]{3,2,1,0:T(8,128)(2,1)S(1)}, bf16[1,2,40,1536]{3,2,1,0:T(8,128)(2,1)S(1)}, u32[]{:S(2)}, u32[]{:S(2)}) collective-permute-start(bf16[1,2,40,1536]{3,2,1,0:T(8,128)(2,1)S(1)} %get-tuple-element.97), channel_id=1, source_target_pairs={{0,8},{8,0},{16,24},{24,16},{1,9},{9,1},{17,25},{25,17},{2,10},{10... | collective-permute-start | bytes 737288 | tf_op jit(solution)/shard_map/ppermute | solution.py:27
  129.7 20.2 %collective-permute-start.30 = (bf16[2,40,1536]{2,1,0:T(8,128)(2,1)S(1)}, bf16[2,40,1536]{2,1,0:T(8,128)(2,1)S(1)}, u32[]{:S(2)}, u32[]{:S(2)}) collective-permute-start(bf16[2,40,1536]{2,1,0:T(8,128)(2,1)S(1)} %reply.4), channel_id=1, source_target_pairs={{0,6},{1,7},{2,4},{3,5},{4,2},{5,3},{6,0},{7,1},{8,14},{9,15},{10,... | collective-permute-start | bytes 737288 | tf_op jit(solution)/shard_map/ppermute | solution.py:27
  136.0 13.8 %collective-permute-start.31 = (bf16[2,40,1536]{2,1,0:T(8,128)(2,1)S(1)}, bf16[2,40,1536]{2,1,0:T(8,128)(2,1)S(1)}, u32[]{:S(2)}, u32[]{:S(2)}) collective-permute-start(bf16[2,40,1536]{2,1,0:T(8,128)(2,1)S(1)} %reply.5), channel_id=1, source_target_pairs={{0,4},{1,5},{2,6},{3,7},{4,0},{5,1},{6,2},{7,3},{8,12},{9,13},{10,... | collective-permute-start | bytes 737288 | tf_op jit(solution)/shard_map/ppermute | solution.py:27
  137.3 12.6 %collective-permute-start.28 = (bf16[1,2,40,1536]{3,2,1,0:T(8,128)(2,1)S(1)}, bf16[1,2,40,1536]{3,2,1,0:T(8,128)(2,1)S(1)}, u32[]{:S(2)}, u32[]{:S(2)}) collective-permute-start(bf16[1,2,40,1536]{3,2,1,0:T(8,128)(2,1)S(1)} %get-tuple-element.101), channel_id=1, source_target_pairs={{0,16},{8,24},{16,0},{24,8},{1,17},{9,25},{17,1},{25,9},{2,18},{10... | collective-permute-start | bytes 737288 | tf_op jit(solution)/shard_map/ppermute | solution.py:27
  139.9 11.1 %collective-permute-start.32 = (bf16[2,40,1536]{2,1,0:T(8,128)(2,1)S(1)}, bf16[2,40,1536]{2,1,0:T(8,128)(2,1)S(1)}, u32[]{:S(2)}, u32[]{:S(2)}) collective-permute-start(bf16[2,40,1536]{2,1,0:T(8,128)(2,1)S(1)} %reply.6), channel_id=1, source_target_pairs={{0,2},{1,3},{2,0},{3,1},{4,6},{5,7},{6,4},{7,5},{8,10},{9,11},{10,... | collective-permute-start | bytes 737288 | tf_op jit(solution)/shard_map/ppermute | solution.py:27
  151.6 1.8 %collective-permute-start.33 = (bf16[256,768]{1,0:T(8,128)(2,1)S(1)}, bf16[256,768]{1,0:T(8,128)(2,1)S(1)}, u32[]{:S(2)}, u32[]{:S(2)}) collective-permute-start(bf16[256,768]{1,0:T(8,128)(2,1)S(1)} %get-tuple-element.106), channel_id=1, source_target_pairs={{0,1},{1,0},{2,3},{3,2},{4,5},{5,4},{6,7},{7,6},{8,9},{9,8},{10,11... | collective-permute-start | bytes 1179656 | tf_op jit(solution)/shard_map/ppermute | solution.py:27

commit v9 on v6

--- a/solution.py
+++ b/solution.py
@@ -335,7 +335,7 @@
     )
 
 
-def down_kernel(place, weights, hidden, *refs, chunk, route):
+def down_kernel(place, weights, hidden, *refs, chunk, shares):
     outs, (buffer, sems) = refs[:-2], refs[-2:]
     own = hidden.shape[0]
     half = buffer.shape[3]
@@ -346,26 +346,32 @@
             copy.start()
         copies.append(mine)
     for j in range(own):
+        (share,) = [i for i, (first, last, _) in enumerate(shares) if first <= j < last]
+        first, _, route = shares[share]
         for side in range(2):
             for copy in copies[j][2 * side : 2 * side + 2]:
                 copy.wait()
             result = dot(hidden[j], buffer[j, side])
             lanes = slice(side * half, (side + 1) * half)
-            for out, members in zip(outs, route):
+            for out, members in zip(outs[2 * share : 2 * share + 2], route):
                 for i, member in enumerate(members):
-                    out[i, j, :, lanes] = result[member * CAP : (member + 1) * CAP].astype(BF16)
-
-
-def down_chunk(place, chunk, count, hidden, weights, route):
+                    out[i, j - first, :, lanes] = result[member * CAP : (member + 1) * CAP].astype(BF16)
+
+
+def down_chunk(place, chunk, count, hidden, weights, shares):
     own, rows, depth = hidden.shape
     parts = rows // CAP
     shape = piece_shape("down", weights, count)
     width = 2 * shape[2]
-    return pl.pallas_call(
-        functools.partial(down_kernel, chunk=chunk, route=route),
+    outs = pl.pallas_call(
+        functools.partial(down_kernel, chunk=chunk, shares=shares),
         in_specs=[SMEM, ANY, VMEM],
-        out_specs=[VMEM] * 2,
-        out_shape=[jax.ShapeDtypeStruct((parts // 2, own, CAP, width), BF16)] * 2,
+        out_specs=[VMEM] * (2 * len(shares)),
+        out_shape=[
+            jax.ShapeDtypeStruct((parts // 2, last - first, CAP, width), BF16)
+            for first, last, _ in shares
+            for _ in range(2)
+        ],
         scratch_shapes=[pltpu.VMEM((own, *shape), BF16), pltpu.SemaphoreType.DMA((own, 2, 2))],
         compiler_params=params(24),
         cost_estimate=pl.CostEstimate(
@@ -375,14 +381,14 @@
         ),
         name=f"down_{chunk}",
     )(place, weights, hidden)
+    return [tuple(outs[2 * i : 2 * i + 2]) for i in range(len(shares))]
 
 
 def combine_kernel(normed, placement, *refs):
     blocks, (mine, theirs) = refs[:-2], refs[-2:]
-    own = blocks[0].shape[0]
     features = normed.shape[1]
     replies = jnp.concatenate(
-        [block[j].astype(F32) for block in blocks for j in range(own)], axis=0
+        [block[j].astype(F32) for block in blocks for j in range(block.shape[0])], axis=0
     ).astype(BF16)
     combined = dot(placement[...], replies, 0, 0)
     mine[...] = normed[...].astype(F32) + combined[:, :features]
@@ -419,14 +425,14 @@
     )(kept, got)
 
 
-def reply_kernel(kept, got, weight, out):
+def reply_kernel(kept, got, weight, out, *, first):
     total = kept[0].astype(F32) + got[0].astype(F32)
-    out[...] = (total * weight[:, :, :1]).astype(BF16)
-
-
-def reply_of(kept, got, weight):
+    out[...] = (total * weight[first : first + out.shape[0], :, :1]).astype(BF16)
+
+
+def reply_of(kept, got, weight, first):
     return pl.pallas_call(
-        reply_kernel,
+        functools.partial(reply_kernel, first=first),
         in_specs=[VMEM] * 3,
         out_specs=VMEM,
         out_shape=jax.ShapeDtypeStruct(kept.shape[1:], BF16),
@@ -593,7 +599,15 @@
     total, done = None, max(chunks - 2, 0)
     for k in range(done):
         (total,) = project(
-            after(place, arrived[-1]), [k], chunks, gathered, expert_up, expert_down, held, total, None
+            after(place, arrived[-1]),
+            [k],
+            chunks,
+            gathered,
+            expert_up,
+            expert_down,
+            held,
+            total,
+            None,
         )
     hidden, *far = project(
         after(place, weight),
@@ -612,30 +626,46 @@
     for i in range(chunks + 3):
         if i < chunks:
             k = order[i]
-            sent, kept = far
+            if i == chunks - 1 and i and own % 2 == 0:
+                paths = [(0, own // 2, bits), (own // 2, own, bits[::-1])]
+            else:
+                paths = [(0, own, orders[k])]
+            results = [far]
             if i:
-                sent, kept = down_chunk(
-                    place, k, chunks, after(hidden, token), expert_down, routes[k]
+                results = down_chunk(
+                    place,
+                    k,
+                    chunks,
+                    after(hidden, token),
+                    expert_down,
+                    [(first, last, route_of(path, n_ctx)) for first, last, path in paths],
                 )
-            open_sums[k] = kept, swap(sent, "ctx", n_ctx, orders[k][0])
-            token = sent
+            open_sums[k] = [
+                (first, path, kept, swap(sent, "ctx", n_ctx, path[0]))
+                for (first, _, path), (sent, kept) in zip(paths, results)
+            ]
+            token = results[0][0]
         if 2 <= i < chunks + 2:
             k = order[i - 2]
-            for bit in orders[k][1:]:
-                kept, got = open_sums[k]
-                kept, sent = halve(kept, after(got, token))
-                open_sums[k] = kept, swap(sent, "ctx", n_ctx, bit)
-                token = sent
+            sums = []
+            for first, path, kept, got in open_sums[k]:
+                for bit in path[1:]:
+                    kept, sent = halve(kept, after(got, token))
+                    got, token = swap(sent, "ctx", n_ctx, bit), sent
+                sums.append((first, path, kept, got))
+            open_sums[k] = sums
         if i >= 3:
             k = order[i - 3]
-            kept, got = open_sums[k]
-            early = [returned[order[i - 5]]] if i >= 5 else []
-            token = reply_of(kept, after(got, token, *early), weight)
-            returned[k] = swap(token, "exp", n_exp, 2 * k) if k else token
+            early = [block for m in order[:-2] for block in returned[m]] if i == chunks + 2 else []
+            returned[k] = []
+            for first, path, kept, got in open_sums[k]:
+                token = reply_of(kept, after(got, token, *early), weight, first)
+                returned[k].append(swap(token, "exp", n_exp, 2 * k) if k else token)
+    returned = [block for blocks in returned for block in blocks]
 
     mine, theirs = pl.pallas_call(
         combine_kernel,
-        in_specs=[VMEM] * (2 + chunks),
+        in_specs=[VMEM] * (2 + len(returned)),
         out_specs=[VMEM] * 2,
         out_shape=[struct((tokens, features), F32), struct((tokens, features), BF16)],
         compiler_params=params(24),

time: 146 us -> 144 us (0.986)
  waiting for transfers between devices: 34.2 us -> 30 us
  starting transfers between devices: 49.4 us -> 52.1 us
    ppermute x34 -> x36, waiting for transfers between devices: 34.2 us -> 30 us  [swap(): return lax.ppermute(x, axis, [(i, i ^ k) for i in range(n) if keep(i)])]
    ppermute x34 -> x36, starting transfers between devices: 49.4 us -> 52.1 us  [swap(): return lax.ppermute(x, axis, [(i, i ^ k) for i in range(n) if keep(i)])]
    pallas_call x8 -> x9, Pallas kernels: 16.3 us -> 16.4 us  [the longest x3 15.3 us: down_chunk(): pl.pallas_call(functools.partial(down_kernel, chunk=chunk, shares=shares)...]
  transfers between devices with their start and end apart: 34 -> 36, of which waited for: 13 -> 14; matrix products, arithmetic and copies ran while one was open for 1% -> 1% of each run, Pallas kernels for 26% -> 26%
where the time goes in v9:
time: 144 us
  Pallas kernels  53.7 us (37%)
  starting transfers between devices  52.1 us (36%)
  waiting for transfers between devices  30 us (21%)
  local copies, waits for them, and re-layouts  4.96 us (3%)
  other arithmetic  2.56 us (2%)
    ppermute x36, starting transfers between devices, swap(): return lax.ppermute(x, axis, [(i, i ^ k) for i in range(n) if keep(i)])  52.1 us
    ppermute x36, waiting for transfers between devices, swap(): return lax.ppermute(x, axis, [(i, i ^ k) for i in range(n) if keep(i)])  30 us
    pallas_call x3, Pallas kernels, project(): pl.pallas_call(functools.partial(project_kernel, chunks=chunks, parts=par...  18.8 us
    pallas_call x3, Pallas kernels, down_chunk(): pl.pallas_call(functools.partial(down_kernel, chunk=chunk, shares=shares)...  15.3 us
    pallas_call x3, Pallas kernels, call_with_held(): pl.pallas_call(functools.partial(with_held, kernel, pieces), in_specs=[SM...  12.7 us
    unnamed x22, local copies, waits for them, and re-layouts  4.41 us
    pallas_call x1, Pallas kernels, body(): pl.pallas_call(state_kernel, in_specs=[ANY] * 2 + [VMEM], out_specs=[VMEM...  3.83 us
  transfers between devices with their start and end apart: 36, of which 14 were waited for; matrix products, arithmetic and copies ran while one was open for 1% of the time, Pallas kernels for 26%

profile of v9, /device:TPU:0, one launch (start us, length us, event | category | flops | bytes accessed | tf_op | source)
XLA Modules:
  0.0 143.8 jit_solution(6670689892771459184)
XLA Ops:
  0.0 3.8 %local_state.1 = (bf16[12,128,128]{2,1,0:T(8,128)(2,1)}, bf16[12,128,128]{2,1,0:T(8,128)(2,1)}) custom-call(bf16[4,64,768]{2,1,0:T(8,128)(2,1)} %refs_1_.1, bf16[4,64,768]{2,1,0:T(8,128)(2,1)} %refs_2_.1, f32[24,64]{1,0:T(8,128)} %bitcast.19), custom_call_target="tpu_custom_call" | custom-call | tf_op jit(solution)/shard_map/local_state/pallas_call | solution.py:509
  4.8 2.9 %collective-permute-start.1 = (f32[2,12,1,1]{1,0,3,2:T(2,128)S(1)}, f32[2,12,1,1]{1,0,3,2:T(2,128)S(1)}, u32[]{:S(2)}, u32[]{:S(2)}) collective-permute-start(f32[2,12,1,1]{1,0,3,2:T(2,128)S(1)} %exp.14), channel_id=1, source_target_pairs={{0,8},{8,0},{16,24},{24,16},{1,9},{9,1},{17,25},{25,17},{2,10},{10... | collective-permute-start | bytes 296 | tf_op jit(solution)/shard_map/ppermute | solution.py:27
  7.8 1.5 %collective-permute-start.3 = (f32[2,12,1,1]{1,0,3,2:T(2,128)S(1)}, f32[2,12,1,1]{1,0,3,2:T(2,128)S(1)}, u32[]{:S(2)}, u32[]{:S(2)}) collective-permute-start(f32[2,12,1,1]{1,0,3,2:T(2,128)S(1)} %exp.14), channel_id=1, source_target_pairs={{0,24},{8,16},{16,8},{24,0},{1,25},{9,17},{17,9},{25,1},{2,26},{10... | collective-permute-start | bytes 296 | tf_op jit(solution)/shard_map/ppermute | solution.py:27
  9.3 2.0 %collective-permute-start.4 = (bf16[12,128,128]{2,1,0:T(8,128)(2,1)}, bf16[12,128,128]{2,1,0:T(8,128)(2,1)S(1)}, u32[]{:S(2)}, u32[]{:S(2)}) collective-permute-start(bf16[12,128,128]{2,1,0:T(8,128)(2,1)} %get-tuple-element.65), channel_id=1, source_target_pairs={{0,16},{8,24},{1,17},{9,25},{2,18},{10,26},{3,19},{11,27},{4,20},{... | collective-permute-start | bytes 1179656 | tf_op jit(solution)/shard_map/ppermute | solution.py:27
  11.2 3.9 %collective-permute-start = (bf16[12,128,128]{2,1,0:T(8,128)(2,1)}, bf16[12,128,128]{2,1,0:T(8,128)(2,1)S(1)}, u32[]{:S(2)}, u32[]{:S(2)}) collective-permute-start(bf16[12,128,128]{2,1,0:T(8,128)(2,1)} %get-tuple-element.61), channel_id=1, source_target_pairs={{0,8},{8,0},{16,24},{1,9},{9,1},{17,25},{2,10},{10,2},{18,26},{3,1... | collective-permute-start | bytes 1179656 | tf_op jit(solution)/shard_map/ppermute | solution.py:27
  15.6 1.0 copy-done
  16.6 1.0 copy-done.2
  17.6 1.0 copy-done.3
  20.0 4.3 %inside_and_placement.1 = (f32[4,64,768]{2,1,0:T(8,128)S(1)}, bf16[320,256]{1,0:T(8,128)(2,1)S(1)}, s32[80,128]{1,0:T(8,128)S(1)}) custom-call(s32[2]{0:T(128)S(1)} %pad_add_fusion.place, bf16[2,6144,1536]{2,1,0:T(8,128)(2,1)} %up.11, bf16[2,1536,6144]{2,1,0:T(8,128)(2,1)} %weights.5, bf16[4,64,768]{2,1,0:T(8,128)(2,1)S(1)} %copy-done, ...), custom_call_target="tpu_custom_call" | custom-call | tf_op jit(solution)/shard_map/inside_and_placement/pallas_call | solution.py:97
  24.6 1.3 collective-permute-start.2
  26.1 3.3 %collective-permute-start.5 = (bf16[12,128,128]{2,1,0:T(8,128)(2,1)S(1)}, bf16[12,128,128]{2,1,0:T(8,128)(2,1)S(1)}, u32[]{:S(2)}, u32[]{:S(2)}) collective-permute-start(bf16[12,128,128]{2,1,0:T(8,128)(2,1)S(1)} %fusion.5), channel_id=1, source_target_pairs={{0,8},{16,24},{24,16},{1,9},{17,25},{25,17},{2,10},{18,26},{26,18}... | collective-permute-start | bytes 1179656 | tf_op jit(solution)/shard_map/ppermute | solution.py:27
  29.5 5.8 %early_weights.1 = (bf16[2,768,1536]{2,1,0:T(8,128)(2,1)S(1)}, bf16[2,768,1536]{2,1,0:T(8,128)(2,1)S(1)}, bf16[2,1536,768]{2,1,0:T(8,128)(2,1)S(1)}) custom-call(s32[2]{0:T(128)S(1)} %pad_add_fusion.place, bf16[2,6144,1536]{2,1,0:T(8,128)(2,1)} %up.11, bf16[2,1536,6144]{2,1,0:T(8,128)(2,1)} %weights.5), custom_call_target="tpu_custom_call" | custom-call | tf_op jit(solution)/shard_map/early_weights/pallas_call | solution.py:97
  36.1 2.6 %normed.1.refs_0_ = bf16[256,768]{1,0:T(8,128)(2,1)S(1)} custom-call(s32[2]{0:T(128)S(1)} %pad_add_fusion.place, bf16[2,6144,1536]{2,1,0:T(8,128)(2,1)} %up.11, bf16[2,1536,6144]{2,1,0:T(8,128)(2,1)} %weights.5, bf16[4,64,768]{2,1,0:T(8,128)(2,1)S(1)} %copy-done.1, f32[4,64,768]{2,1,0:T(8,128)S(1)} %get-tuple-element.63.refs_1_, f32[24,64]{1,0:T(8,128)S(1)} %bitcast.21, ...), custom_call_target="tpu_custom_call" | custom-call | tf_op jit(solution)/shard_map/normed/pallas_call | solution.py:97
  38.8 1.7 %collective-permute-done.6.refs_1_ = bf16[256,768]{1,0:T(8,128)(2,1)S(1)} collective-permute-done((bf16[256,768]{1,0:T(8,128)(2,1)S(1)}, bf16[256,768]{1,0:T(8,128)(2,1)S(1)}, u32[]{:S(2)}, u32[]{:S(2)}) %collective-permute-start.6) | collective-permute-done | bytes 393248 | tf_op jit(solution)/shard_map/ppermute | solution.py:27
  40.9 2.5 %collective-permute-start.16 = (bf16[2,40,1536]{2,1,0:T(8,128)(2,1)S(1)}, bf16[2,40,1536]{2,1,0:T(8,128)(2,1)S(1)}, u32[]{:S(2)}, u32[]{:S(2)}) collective-permute-start(bf16[2,40,1536]{2,1,0:T(8,128)(2,1)S(1)} %get-tuple-element.74.refs_0_), channel_id=1, source_target_pairs={{0,8},{8,0},{16,24},{24,16},{1,9},{9,1},{17,25},{25,17},{2,10},{10... | collective-permute-start | bytes 737288 | tf_op jit(solution)/shard_map/ppermute | solution.py:27
  43.5 1.6 %collective-permute-start.7 = (bf16[2,40,1536]{2,1,0:T(8,128)(2,1)S(1)}, bf16[2,40,1536]{2,1,0:T(8,128)(2,1)S(1)}, u32[]{:S(2)}, u32[]{:S(2)}) collective-permute-start(bf16[2,40,1536]{2,1,0:T(8,128)(2,1)S(1)} %get-tuple-element.75), channel_id=1, source_target_pairs={{0,2},{1,3},{2,0},{3,1},{4,6},{5,7},{6,4},{7,5},{8,10},{9,11},{10,... | collective-permute-start | bytes 737288 | tf_op jit(solution)/shard_map/ppermute | solution.py:27
  45.1 2.6 %collective-permute-start.8 = (bf16[2,40,1536]{2,1,0:T(8,128)(2,1)S(1)}, bf16[2,40,1536]{2,1,0:T(8,128)(2,1)S(1)}, u32[]{:S(2)}, u32[]{:S(2)}) collective-permute-start(bf16[2,40,1536]{2,1,0:T(8,128)(2,1)S(1)} %get-tuple-element.76), channel_id=1, source_target_pairs={{0,4},{1,5},{2,6},{3,7},{4,0},{5,1},{6,2},{7,3},{8,12},{9,13},{10,... | collective-permute-start | bytes 737288 | tf_op jit(solution)/shard_map/ppermute | solution.py:27
  47.9 1.9 %collective-permute-done.16.refs_1_ = bf16[2,40,1536]{2,1,0:T(8,128)(2,1)S(1)} collective-permute-done((bf16[2,40,1536]{2,1,0:T(8,128)(2,1)S(1)}, bf16[2,40,1536]{2,1,0:T(8,128)(2,1)S(1)}, u32[]{:S(2)}, u32[]{:S(2)}) %collective-permute-start.16) | collective-permute-done | bytes 245792 | tf_op jit(solution)/shard_map/ppermute | solution.py:27
  49.7 1.5 %collective-permute-done.17.refs_2_ = bf16[2,40,1536]{2,1,0:T(8,128)(2,1)S(1)} collective-permute-done((bf16[2,40,1536]{2,1,0:T(8,128)(2,1)S(1)}, bf16[2,40,1536]{2,1,0:T(8,128)(2,1)S(1)}, u32[]{:S(2)}, u32[]{:S(2)}) %collective-permute-start.17) | collective-permute-done | bytes 245792 | tf_op jit(solution)/shard_map/ppermute | solution.py:27
  51.2 4.5 %collective-permute-done.7.refs_1_.refs_0_ = bf16[2,40,1536]{2,1,0:T(8,128)(2,1)S(1)} collective-permute-done((bf16[2,40,1536]{2,1,0:T(8,128)(2,1)S(1)}, bf16[2,40,1536]{2,1,0:T(8,128)(2,1)S(1)}, u32[]{:S(2)}, u32[]{:S(2)}) %collective-permute-start.7) | collective-permute-done | bytes 245792 | tf_op jit(solution)/shard_map/ppermute | solution.py:27
  55.7 1.6 %collective-permute-start.19 = (bf16[2,40,1536]{2,1,0:T(8,128)(2,1)S(1)}, bf16[2,40,1536]{2,1,0:T(8,128)(2,1)S(1)}, u32[]{:S(2)}, u32[]{:S(2)}) collective-permute-start(bf16[2,40,1536]{2,1,0:T(8,128)(2,1)S(1)} %collective-permute-done.7.refs_1_.refs_0_), channel_id=1, source_target_pairs={{0,16},{8,24},{16,0},{24,8},{1,17},{9,25},{17,1},{25,9},{2,18},{10... | collective-permute-start | bytes 737288 | tf_op jit(solution)/shard_map/ppermute | solution.py:27
  58.4 7.0 %collective-permute-done.8.refs_2_.refs_0_ = bf16[2,40,1536]{2,1,0:T(8,128)(2,1)S(1)} collective-permute-done((bf16[2,40,1536]{2,1,0:T(8,128)(2,1)S(1)}, bf16[2,40,1536]{2,1,0:T(8,128)(2,1)S(1)}, u32[]{:S(2)}, u32[]{:S(2)}) %collective-permute-start.8) | collective-permute-done | bytes 245792 | tf_op jit(solution)/shard_map/ppermute | solution.py:27
  65.4 1.1 collective-permute-start.10
  66.5 1.0 collective-permute-start.14
  67.5 2.0 %collective-permute-start.20 = (bf16[2,40,1536]{2,1,0:T(8,128)(2,1)S(1)}, bf16[2,40,1536]{2,1,0:T(8,128)(2,1)S(1)}, u32[]{:S(2)}, u32[]{:S(2)}) collective-permute-start(bf16[2,40,1536]{2,1,0:T(8,128)(2,1)S(1)} %collective-permute-done.19.refs_2_), channel_id=1, source_target_pairs={{0,8},{8,0},{16,24},{24,16},{1,9},{9,1},{17,25},{25,17},{2,10},{10... | collective-permute-start | bytes 737288 | tf_op jit(solution)/shard_map/ppermute | solution.py:27
  69.5 1.1 gate.1.weight
  70.8 1.2 collective-permute-start.13
  72.0 2.3 %collective-permute-done.10.refs_1_ = bf16[2,40,1536]{2,1,0:T(8,128)(2,1)S(1)} collective-permute-done((bf16[2,40,1536]{2,1,0:T(8,128)(2,1)S(1)}, bf16[2,40,1536]{2,1,0:T(8,128)(2,1)S(1)}, u32[]{:S(2)}, u32[]{:S(2)}) %collective-permute-start.10) | collective-permute-done | bytes 245792 | tf_op jit(solution)/shard_map/ppermute | solution.py:27
  74.3 2.0 %collective-permute-start.12 = (bf16[2,40,1536]{2,1,0:T(8,128)(2,1)S(1)}, bf16[2,40,1536]{2,1,0:T(8,128)(2,1)S(1)}, u32[]{:S(2)}, u32[]{:S(2)}) collective-permute-start(bf16[2,40,1536]{2,1,0:T(8,128)(2,1)S(1)} %collective-permute-done.10.refs_1_), channel_id=1, source_target_pairs={{0,16},{8,24},{16,0},{24,8},{1,17},{9,25},{17,1},{25,9},{2,18},{10... | collective-permute-start | bytes 737288 | tf_op jit(solution)/shard_map/ppermute | solution.py:27
  76.4 5.3 %project_0.1.refs_4_ = f32[2,160,1536]{2,1,0:T(8,128)S(1)} custom-call(s32[2]{0:T(128)S(1)} %pad_add_fusion.place, bf16[2,6144,1536]{2,1,0:T(8,128)(2,1)} %up.11, bf16[2,1536,6144]{2,1,0:T(8,128)(2,1)} %weights.5, bf16[2,40,1536]{2,1,0:T(8,128)(2,1)S(1)} %get-tuple-element.74.refs_0_, bf16[2,40,1536]{2,1,0:T(8,128)(2,1)S(1)} %collective-permute-done.16.refs_1_, ...), custom_call_target="tpu_custom_call" | custom-call | flops 1509949440 | bytes 9437184 | tf_op jit(solution)/shard_map/project_0/pallas_call | solution.py:309
  81.7 4.9 %project_1.1.refs_11_ = f32[2,160,1536]{2,1,0:T(8,128)S(1)} custom-call(s32[2]{0:T(128)S(1)} %pad_add_fusion.place, bf16[2,6144,1536]{2,1,0:T(8,128)(2,1)} %up.11, bf16[2,1536,6144]{2,1,0:T(8,128)(2,1)} %weights.5, bf16[2,40,1536]{2,1,0:T(8,128)(2,1)S(1)} %collective-permute-done.7.refs_1_.refs_0_, bf16[2,40,1536]{2,1,0:T(8,128)(2,1)S(1)} %collective-permute-done.18.refs_1_, ...), custom_call_target="tpu_custom_call" | custom-call | flops 1509949440 | bytes 9437184 | tf_op jit(solution)/shard_map/project_1/pallas_call | solution.py:309
  86.6 8.7 %project_2.1 = (bf16[2,160,1536]{2,1,0:T(8,128)(2,1)S(1)}, bf16[2,2,40,1536]{3,2,1,0:T(8,128)(2,1)S(1)}, bf16[2,2,40,1536]{3,2,1,0:T(8,128)(2,1)S(1)}) custom-call(s32[2]{0:T(128)S(1)} %pad_add_fusion.place, bf16[2,6144,1536]{2,1,0:T(8,128)(2,1)} %up.11, bf16[2,1536,6144]{2,1,0:T(8,128)(2,1)} %weights.5, ...), custom_call_target="tpu_custom_call" | custom-call | flops 4529848320 | bytes 28311552 | tf_op jit(solution)/shard_map/project_2/pallas_call | solution.py:309
  95.3 2.0 %collective-permute-start.22 = (bf16[2,2,40,1536]{3,2,1,0:T(8,128)(2,1)S(1)}, bf16[2,2,40,1536]{3,2,1,0:T(8,128)(2,1)S(1)}, u32[]{:S(2)}, u32[]{:S(2)}) collective-permute-start(bf16[2,2,40,1536]{3,2,1,0:T(8,128)(2,1)S(1)} %get-tuple-element.83), channel_id=1, source_target_pairs={{0,16},{8,24},{16,0},{24,8},{1,17},{9,25},{17,1},{25,9},{2,18},{10... | collective-permute-start | bytes 1474568 | tf_op jit(solution)/shard_map/ppermute | solution.py:27
  97.3 5.2 %down_2.1 = (bf16[2,2,40,1536]{3,2,1,0:T(8,128)(2,1)S(1)}, bf16[2,2,40,1536]{3,2,1,0:T(8,128)(2,1)S(1)}) custom-call(s32[2]{0:T(128)S(1)} %pad_add_fusion.place, bf16[2,1536,6144]{2,1,0:T(8,128)(2,1)} %weights.5, bf16[2,160,1536]{2,1,0:T(8,128)(2,1)S(1)} %get-tuple-element.90.hidden), custom_call_target="tpu_custom_call" | custom-call | flops 1509949440 | bytes 9437184 | tf_op jit(solution)/shard_map/down_2/pallas_call | solution.py:366
  102.7 5.0 %down_1.1 = (bf16[2,2,40,1536]{3,2,1,0:T(8,128)(2,1)S(1)}, bf16[2,2,40,1536]{3,2,1,0:T(8,128)(2,1)S(1)}) custom-call(s32[2]{0:T(128)S(1)} %pad_add_fusion.place, bf16[2,1536,6144]{2,1,0:T(8,128)(2,1)} %weights.5, bf16[2,160,1536]{2,1,0:T(8,128)(2,1)S(1)} %get-tuple-element.90.hidden), custom_call_target="tpu_custom_call" | custom-call | flops 1509949440 | bytes 9437184 | tf_op jit(solution)/shard_map/down_1/pallas_call | solution.py:366
  107.7 2.0 %collective-permute-start.26 = (bf16[2,2,40,1536]{3,2,1,0:T(8,128)(2,1)S(1)}, bf16[2,2,40,1536]{3,2,1,0:T(8,128)(2,1)S(1)}, u32[]{:S(2)}, u32[]{:S(2)}) collective-permute-start(bf16[2,2,40,1536]{3,2,1,0:T(8,128)(2,1)S(1)} %get-tuple-element.87), channel_id=1, source_target_pairs={{0,16},{8,24},{16,0},{24,8},{1,17},{9,25},{17,1},{25,9},{2,18},{10... | collective-permute-start | bytes 1474568 | tf_op jit(solution)/shard_map/ppermute | solution.py:27
  110.0 5.0 %down_0.1 = (bf16[2,1,40,1536]{3,2,1,0:T(8,128)(2,1)S(1)}, bf16[2,1,40,1536]{3,2,1,0:T(8,128)(2,1)S(1)}, bf16[2,1,40,1536]{3,2,1,0:T(8,128)(2,1)S(1)}, bf16[2,1,40,1536]{3,2,1,0:T(8,128)(2,1)S(1)}) custom-call(s32[2]{0:T(128)S(1)} %pad_add_fusion.place, bf16[2,1536,6144]{2,1,0:T(8,128)(2,1)} %weights.5, bf16[2,160,1536]{2,1,0:T(8,128)(2,1)S(1)} %get-tuple-element.90.hidden), custom_call_target="tpu_custom_call" | custom-call | flops 1509949440 | bytes 9437184 | tf_op jit(solution)/shard_map/down_0/pallas_call | solution.py:366
  115.3 1.9 %collective-permute-start.25 = (bf16[1,2,40,1536]{3,2,1,0:T(8,128)(2,1)S(1)}, bf16[1,2,40,1536]{3,2,1,0:T(8,128)(2,1)S(1)}, u32[]{:S(2)}, u32[]{:S(2)}) collective-permute-start(bf16[1,2,40,1536]{3,2,1,0:T(8,128)(2,1)S(1)} %get-tuple-element.96), channel_id=1, source_target_pairs={{0,16},{8,24},{16,0},{24,8},{1,17},{9,25},{17,1},{25,9},{2,18},{10... | collective-permute-start | bytes 737288 | tf_op jit(solution)/shard_map/ppermute | solution.py:27
  117.3 1.9 %collective-permute-start.30 = (bf16[2,1,40,1536]{3,2,1,0:T(8,128)(2,1)S(1)}, bf16[2,1,40,1536]{3,2,1,0:T(8,128)(2,1)S(1)}, u32[]{:S(2)}, u32[]{:S(2)}) collective-permute-start(bf16[2,1,40,1536]{3,2,1,0:T(8,128)(2,1)S(1)} %get-tuple-element.108), channel_id=1, source_target_pairs={{0,16},{8,24},{16,0},{24,8},{1,17},{9,25},{17,1},{25,9},{2,18},{10... | collective-permute-start | bytes 737288 | tf_op jit(solution)/shard_map/ppermute | solution.py:27
  119.2 1.3 collective-permute-done.27.got
  120.6 1.1 collective-permute-done.26.got
  121.8 1.9 %collective-permute-start.29 = (bf16[1,2,40,1536]{3,2,1,0:T(8,128)(2,1)S(1)}, bf16[1,2,40,1536]{3,2,1,0:T(8,128)(2,1)S(1)}, u32[]{:S(2)}, u32[]{:S(2)}) collective-permute-start(bf16[1,2,40,1536]{3,2,1,0:T(8,128)(2,1)S(1)} %get-tuple-element.101), channel_id=1, source_target_pairs={{0,8},{8,0},{16,24},{24,16},{1,9},{9,1},{17,25},{25,17},{2,10},{10... | collective-permute-start | bytes 737288 | tf_op jit(solution)/shard_map/ppermute | solution.py:27
  123.7 2.4 %collective-permute-start.31 = (bf16[2,40,1536]{2,1,0:T(8,128)(2,1)S(1)}, bf16[2,40,1536]{2,1,0:T(8,128)(2,1)S(1)}, u32[]{:S(2)}, u32[]{:S(2)}) collective-permute-start(bf16[2,40,1536]{2,1,0:T(8,128)(2,1)S(1)} %reply.5), channel_id=1, source_target_pairs={{0,6},{1,7},{2,4},{3,5},{4,2},{5,3},{6,0},{7,1},{8,14},{9,15},{10,... | collective-permute-start | bytes 737288 | tf_op jit(solution)/shard_map/ppermute | solution.py:27
  126.2 3.5 %collective-permute-start.32 = (bf16[2,40,1536]{2,1,0:T(8,128)(2,1)S(1)}, bf16[2,40,1536]{2,1,0:T(8,128)(2,1)S(1)}, u32[]{:S(2)}, u32[]{:S(2)}) collective-permute-start(bf16[2,40,1536]{2,1,0:T(8,128)(2,1)S(1)} %reply.6), channel_id=1, source_target_pairs={{0,4},{1,5},{2,6},{3,7},{4,0},{5,1},{6,2},{7,3},{8,12},{9,13},{10,... | collective-permute-start | bytes 737288 | tf_op jit(solution)/shard_map/ppermute | solution.py:27
  130.0 3.8 %collective-permute-start.34 = (bf16[2,40,1536]{2,1,0:T(8,128)(2,1)S(1)}, bf16[2,40,1536]{2,1,0:T(8,128)(2,1)S(1)}, u32[]{:S(2)}, u32[]{:S(2)}) collective-permute-start(bf16[2,40,1536]{2,1,0:T(8,128)(2,1)S(1)} %reply.7), channel_id=1, source_target_pairs={{0,2},{1,3},{2,0},{3,1},{4,6},{5,7},{6,4},{7,5},{8,10},{9,11},{10,... | collective-permute-start | bytes 737288 | tf_op jit(solution)/shard_map/ppermute | solution.py:27
  133.8 4.9 %collective-permute-done.28.got = bf16[1,1,40,1536]{3,2,1,0:T(8,128)(2,1)S(1)} collective-permute-done((bf16[1,1,40,1536]{3,2,1,0:T(8,128)(2,1)S(1)}, bf16[1,1,40,1536]{3,2,1,0:T(8,128)(2,1)S(1)}, u32[]{:S(2)}, u32[]{:S(2)}) %collective-permute-start.28) | collective-permute-done | bytes 122912 | tf_op jit(solution)/shard_map/ppermute | solution.py:27
  138.7 1.0 collective-permute-done.32.refs_3_
  141.3 1.7 %collective-permute-done.35 = bf16[256,768]{1,0:T(8,128)(2,1)S(1)} collective-permute-done((bf16[256,768]{1,0:T(8,128)(2,1)S(1)}, bf16[256,768]{1,0:T(8,128)(2,1)S(1)}, u32[]{:S(2)}, u32[]{:S(2)}) %collective-permute-start.35) | collective-permute-done | bytes 393248 | tf_op jit(solution)/shard_map/ppermute | solution.py:27
  (87 shorter events, 9.9 us)
Async XLA Ops:
  4.8 19.5 %collective-permute-start.1 = (f32[2,12,1,1]{1,0,3,2:T(2,128)S(1)}, f32[2,12,1,1]{1,0,3,2:T(2,128)S(1)}, u32[]{:S(2)}, u32[]{:S(2)}) collective-permute-start(f32[2,12,1,1]{1,0,3,2:T(2,128)S(1)} %exp.14), channel_id=1, source_target_pairs={{0,8},{8,0},{16,24},{24,16},{1,9},{9,1},{17,25},{25,17},{2,10},{10... | collective-permute-start | bytes 296 | tf_op jit(solution)/shard_map/ppermute | solution.py:27
  7.8 18.1 %collective-permute-start.3 = (f32[2,12,1,1]{1,0,3,2:T(2,128)S(1)}, f32[2,12,1,1]{1,0,3,2:T(2,128)S(1)}, u32[]{:S(2)}, u32[]{:S(2)}) collective-permute-start(f32[2,12,1,1]{1,0,3,2:T(2,128)S(1)} %exp.14), channel_id=1, source_target_pairs={{0,24},{8,16},{16,8},{24,0},{1,25},{9,17},{17,9},{25,1},{2,26},{10... | collective-permute-start | bytes 296 | tf_op jit(solution)/shard_map/ppermute | solution.py:27
  9.3 16.7 %collective-permute-start.4 = (bf16[12,128,128]{2,1,0:T(8,128)(2,1)}, bf16[12,128,128]{2,1,0:T(8,128)(2,1)S(1)}, u32[]{:S(2)}, u32[]{:S(2)}) collective-permute-start(bf16[12,128,128]{2,1,0:T(8,128)(2,1)} %get-tuple-element.65), channel_id=1, source_target_pairs={{0,16},{8,24},{1,17},{9,25},{2,18},{10,26},{3,19},{11,27},{4,20},{... | collective-permute-start | bytes 1179656 | tf_op jit(solution)/shard_map/ppermute | solution.py:27
  11.2 13.1 %collective-permute-start = (bf16[12,128,128]{2,1,0:T(8,128)(2,1)}, bf16[12,128,128]{2,1,0:T(8,128)(2,1)S(1)}, u32[]{:S(2)}, u32[]{:S(2)}) collective-permute-start(bf16[12,128,128]{2,1,0:T(8,128)(2,1)} %get-tuple-element.61), channel_id=1, source_target_pairs={{0,8},{8,0},{16,24},{1,9},{9,1},{17,25},{2,10},{10,2},{18,26},{3,1... | collective-permute-start | bytes 1179656 | tf_op jit(solution)/shard_map/ppermute | solution.py:27
  15.6 1.0 copy-start
  16.6 1.0 copy-start.2
  17.6 1.0 copy-start.3
  18.6 0.7 copy-start.4
  19.3 0.7 copy-start.7
  20.0 4.4 %copy-start.9 = (bf16[12,128,128]{2,1,0:T(8,128)(2,1)S(1)}, bf16[12,128,128]{2,1,0:T(8,128)(2,1)}, u32[]{:S(2)}) copy-start(bf16[12,128,128]{2,1,0:T(8,128)(2,1)} %get-tuple-element.61) | copy-start | bytes 1179652
  20.0 5.9 %copy-start.8 = (bf16[12,128,128]{2,1,0:T(8,128)(2,1)S(1)}, bf16[12,128,128]{2,1,0:T(8,128)(2,1)}, u32[]{:S(2)}) copy-start(bf16[12,128,128]{2,1,0:T(8,128)(2,1)} %get-tuple-element.65) | copy-start | bytes 1179652
  20.0 9.5 %copy-start.10 = (f32[768]{0:T(1024)S(1)}, f32[768]{0:T(1024)}, u32[]{:S(2)}) copy-start(f32[768]{0:T(1024)} %param.13) | copy-start | bytes 9220
  24.6 10.7 %collective-permute-start.2 = (bf16[12,128,128]{2,1,0:T(8,128)(2,1)S(1)}, bf16[12,128,128]{2,1,0:T(8,128)(2,1)S(1)}, u32[]{:S(2)}, u32[]{:S(2)}) collective-permute-start(bf16[12,128,128]{2,1,0:T(8,128)(2,1)S(1)} %fusion.3), channel_id=1, source_target_pairs={{0,16},{8,24},{1,17},{9,25},{2,18},{10,26},{3,19},{11,27},{4,20},{... | collective-permute-start | bytes 1179656 | tf_op jit(solution)/shard_map/ppermute | solution.py:27
  26.1 9.7 %collective-permute-start.5 = (bf16[12,128,128]{2,1,0:T(8,128)(2,1)S(1)}, bf16[12,128,128]{2,1,0:T(8,128)(2,1)S(1)}, u32[]{:S(2)}, u32[]{:S(2)}) collective-permute-start(bf16[12,128,128]{2,1,0:T(8,128)(2,1)S(1)} %fusion.5), channel_id=1, source_target_pairs={{0,8},{16,24},{24,16},{1,9},{17,25},{25,17},{2,10},{18,26},{26,18}... | collective-permute-start | bytes 1179656 | tf_op jit(solution)/shard_map/ppermute | solution.py:27
  29.5 6.6 %copy-start.1 = (bf16[4,64,768]{2,1,0:T(8,128)(2,1)S(1)}, bf16[4,64,768]{2,1,0:T(8,128)(2,1)}, u32[]{:S(2)}) copy-start(bf16[4,64,768]{2,1,0:T(8,128)(2,1)} %refs_0_.3) | copy-start | bytes 1179652
  29.5 6.6 %copy-start.5 = (f32[4,64,6]{1,0,2:T(4,128)S(1)}, f32[4,64,6]{1,0,2:T(4,128)}, u32[]{:S(2)}) copy-start(f32[4,64,6]{1,0,2:T(4,128)} %param.12) | copy-start | bytes 18436
  36.1 33.4 %copy-start.6 = (bf16[6144,16]{0,1:T(8,128)(2,1)S(1)}, bf16[6144,16]{0,1:T(8,128)(2,1)}, u32[]{:S(2)}) copy-start(bf16[6144,16]{0,1:T(8,128)(2,1)} %param.14) | copy-start | bytes 589828
  38.7 1.8 %collective-permute-start.6 = (bf16[256,768]{1,0:T(8,128)(2,1)S(1)}, bf16[256,768]{1,0:T(8,128)(2,1)S(1)}, u32[]{:S(2)}, u32[]{:S(2)}) collective-permute-start(bf16[256,768]{1,0:T(8,128)(2,1)S(1)} %normed.1.refs_0_), channel_id=1, source_target_pairs={{0,1},{1,0},{2,3},{3,2},{4,5},{5,4},{6,7},{7,6},{8,9},{9,8},{10,11... | collective-permute-start | bytes 1179656 | tf_op jit(solution)/shard_map/ppermute | solution.py:27
  40.9 8.8 %collective-permute-start.16 = (bf16[2,40,1536]{2,1,0:T(8,128)(2,1)S(1)}, bf16[2,40,1536]{2,1,0:T(8,128)(2,1)S(1)}, u32[]{:S(2)}, u32[]{:S(2)}) collective-permute-start(bf16[2,40,1536]{2,1,0:T(8,128)(2,1)S(1)} %get-tuple-element.74.refs_0_), channel_id=1, source_target_pairs={{0,8},{8,0},{16,24},{24,16},{1,9},{9,1},{17,25},{25,17},{2,10},{10... | collective-permute-start | bytes 737288 | tf_op jit(solution)/shard_map/ppermute | solution.py:27
  43.5 7.7 %collective-permute-start.17 = (bf16[2,40,1536]{2,1,0:T(8,128)(2,1)S(1)}, bf16[2,40,1536]{2,1,0:T(8,128)(2,1)S(1)}, u32[]{:S(2)}, u32[]{:S(2)}) collective-permute-start(bf16[2,40,1536]{2,1,0:T(8,128)(2,1)S(1)} %get-tuple-element.74.refs_0_), channel_id=1, source_target_pairs={{0,16},{8,24},{16,0},{24,8},{1,17},{9,25},{17,1},{25,9},{2,18},{10... | collective-permute-start | bytes 737288 | tf_op jit(solution)/shard_map/ppermute | solution.py:27
  43.5 12.2 %collective-permute-start.7 = (bf16[2,40,1536]{2,1,0:T(8,128)(2,1)S(1)}, bf16[2,40,1536]{2,1,0:T(8,128)(2,1)S(1)}, u32[]{:S(2)}, u32[]{:S(2)}) collective-permute-start(bf16[2,40,1536]{2,1,0:T(8,128)(2,1)S(1)} %get-tuple-element.75), channel_id=1, source_target_pairs={{0,2},{1,3},{2,0},{3,1},{4,6},{5,7},{6,4},{7,5},{8,10},{9,11},{10,... | collective-permute-start | bytes 737288 | tf_op jit(solution)/shard_map/ppermute | solution.py:27
  45.1 20.3 %collective-permute-start.8 = (bf16[2,40,1536]{2,1,0:T(8,128)(2,1)S(1)}, bf16[2,40,1536]{2,1,0:T(8,128)(2,1)S(1)}, u32[]{:S(2)}, u32[]{:S(2)}) collective-permute-start(bf16[2,40,1536]{2,1,0:T(8,128)(2,1)S(1)} %get-tuple-element.76), channel_id=1, source_target_pairs={{0,4},{1,5},{2,6},{3,7},{4,0},{5,1},{6,2},{7,3},{8,12},{9,13},{10,... | collective-permute-start | bytes 737288 | tf_op jit(solution)/shard_map/ppermute | solution.py:27
  47.7 18.8 %collective-permute-start.9 = (bf16[2,40,1536]{2,1,0:T(8,128)(2,1)S(1)}, bf16[2,40,1536]{2,1,0:T(8,128)(2,1)S(1)}, u32[]{:S(2)}, u32[]{:S(2)}) collective-permute-start(bf16[2,40,1536]{2,1,0:T(8,128)(2,1)S(1)} %get-tuple-element.77), channel_id=1, source_target_pairs={{0,6},{1,7},{2,4},{3,5},{4,2},{5,3},{6,0},{7,1},{8,14},{9,15},{10,... | collective-permute-start | bytes 737288 | tf_op jit(solution)/shard_map/ppermute | solution.py:27
  55.7 11.8 %collective-permute-start.19 = (bf16[2,40,1536]{2,1,0:T(8,128)(2,1)S(1)}, bf16[2,40,1536]{2,1,0:T(8,128)(2,1)S(1)}, u32[]{:S(2)}, u32[]{:S(2)}) collective-permute-start(bf16[2,40,1536]{2,1,0:T(8,128)(2,1)S(1)} %collective-permute-done.7.refs_1_.refs_0_), channel_id=1, source_target_pairs={{0,16},{8,24},{16,0},{24,8},{1,17},{9,25},{17,1},{25,9},{2,18},{10... | collective-permute-start | bytes 737288 | tf_op jit(solution)/shard_map/ppermute | solution.py:27
  57.3 13.2 %collective-permute-start.21 = (bf16[2,40,1536]{2,1,0:T(8,128)(2,1)S(1)}, bf16[2,40,1536]{2,1,0:T(8,128)(2,1)S(1)}, u32[]{:S(2)}, u32[]{:S(2)}) collective-permute-start(bf16[2,40,1536]{2,1,0:T(8,128)(2,1)S(1)} %collective-permute-done.16.refs_1_), channel_id=1, source_target_pairs={{0,16},{8,24},{16,0},{24,8},{1,17},{9,25},{17,1},{25,9},{2,18},{10... | collective-permute-start | bytes 737288 | tf_op jit(solution)/shard_map/ppermute | solution.py:27
  57.7 13.1 %collective-permute-start.18 = (bf16[2,40,1536]{2,1,0:T(8,128)(2,1)S(1)}, bf16[2,40,1536]{2,1,0:T(8,128)(2,1)S(1)}, u32[]{:S(2)}, u32[]{:S(2)}) collective-permute-start(bf16[2,40,1536]{2,1,0:T(8,128)(2,1)S(1)} %collective-permute-done.7.refs_1_.refs_0_), channel_id=1, source_target_pairs={{0,8},{8,0},{16,24},{24,16},{1,9},{9,1},{17,25},{25,17},{2,10},{10... | collective-permute-start | bytes 737288 | tf_op jit(solution)/shard_map/ppermute | solution.py:27
  65.4 8.9 %collective-permute-start.10 = (bf16[2,40,1536]{2,1,0:T(8,128)(2,1)S(1)}, bf16[2,40,1536]{2,1,0:T(8,128)(2,1)S(1)}, u32[]{:S(2)}, u32[]{:S(2)}) collective-permute-start(bf16[2,40,1536]{2,1,0:T(8,128)(2,1)S(1)} %collective-permute-done.8.refs_2_.refs_0_), channel_id=1, source_target_pairs={{0,8},{8,0},{16,24},{24,16},{1,9},{9,1},{17,25},{25,17},{2,10},{10... | collective-permute-start | bytes 737288 | tf_op jit(solution)/shard_map/ppermute | solution.py:27
  66.5 9.8 %collective-permute-start.14 = (bf16[2,40,1536]{2,1,0:T(8,128)(2,1)S(1)}, bf16[2,40,1536]{2,1,0:T(8,128)(2,1)S(1)}, u32[]{:S(2)}, u32[]{:S(2)}) collective-permute-start(bf16[2,40,1536]{2,1,0:T(8,128)(2,1)S(1)} %collective-permute-done.9.refs_3_.refs_4_), channel_id=1, source_target_pairs={{0,16},{8,24},{16,0},{24,8},{1,17},{9,25},{17,1},{25,9},{2,18},{10... | collective-permute-start | bytes 737288 | tf_op jit(solution)/shard_map/ppermute | solution.py:27
  67.5 14.2 %collective-permute-start.20 = (bf16[2,40,1536]{2,1,0:T(8,128)(2,1)S(1)}, bf16[2,40,1536]{2,1,0:T(8,128)(2,1)S(1)}, u32[]{:S(2)}, u32[]{:S(2)}) collective-permute-start(bf16[2,40,1536]{2,1,0:T(8,128)(2,1)S(1)} %collective-permute-done.19.refs_2_), channel_id=1, source_target_pairs={{0,8},{8,0},{16,24},{24,16},{1,9},{9,1},{17,25},{25,17},{2,10},{10... | collective-permute-start | bytes 737288 | tf_op jit(solution)/shard_map/ppermute | solution.py:27
  70.6 16.0 %collective-permute-start.11 = (bf16[2,40,1536]{2,1,0:T(8,128)(2,1)S(1)}, bf16[2,40,1536]{2,1,0:T(8,128)(2,1)S(1)}, u32[]{:S(2)}, u32[]{:S(2)}) collective-permute-start(bf16[2,40,1536]{2,1,0:T(8,128)(2,1)S(1)} %collective-permute-done.8.refs_2_.refs_0_), channel_id=1, source_target_pairs={{0,16},{8,24},{16,0},{24,8},{1,17},{9,25},{17,1},{25,9},{2,18},{10... | collective-permute-start | bytes 737288 | tf_op jit(solution)/shard_map/ppermute | solution.py:27
  70.8 15.8 %collective-permute-start.13 = (bf16[2,40,1536]{2,1,0:T(8,128)(2,1)S(1)}, bf16[2,40,1536]{2,1,0:T(8,128)(2,1)S(1)}, u32[]{:S(2)}, u32[]{:S(2)}) collective-permute-start(bf16[2,40,1536]{2,1,0:T(8,128)(2,1)S(1)} %collective-permute-done.9.refs_3_.refs_4_), channel_id=1, source_target_pairs={{0,8},{8,0},{16,24},{24,16},{1,9},{9,1},{17,25},{25,17},{2,10},{10... | collective-permute-start | bytes 737288 | tf_op jit(solution)/shard_map/ppermute | solution.py:27
  74.3 12.3 %collective-permute-start.12 = (bf16[2,40,1536]{2,1,0:T(8,128)(2,1)S(1)}, bf16[2,40,1536]{2,1,0:T(8,128)(2,1)S(1)}, u32[]{:S(2)}, u32[]{:S(2)}) collective-permute-start(bf16[2,40,1536]{2,1,0:T(8,128)(2,1)S(1)} %collective-permute-done.10.refs_1_), channel_id=1, source_target_pairs={{0,16},{8,24},{16,0},{24,8},{1,17},{9,25},{17,1},{25,9},{2,18},{10... | collective-permute-start | bytes 737288 | tf_op jit(solution)/shard_map/ppermute | solution.py:27
  76.3 10.3 %collective-permute-start.15 = (bf16[2,40,1536]{2,1,0:T(8,128)(2,1)S(1)}, bf16[2,40,1536]{2,1,0:T(8,128)(2,1)S(1)}, u32[]{:S(2)}, u32[]{:S(2)}) collective-permute-start(bf16[2,40,1536]{2,1,0:T(8,128)(2,1)S(1)} %collective-permute-done.14.refs_6_), channel_id=1, source_target_pairs={{0,8},{8,0},{16,24},{24,16},{1,9},{9,1},{17,25},{25,17},{2,10},{10... | collective-permute-start | bytes 737288 | tf_op jit(solution)/shard_map/ppermute | solution.py:27
  95.3 14.5 %collective-permute-start.22 = (bf16[2,2,40,1536]{3,2,1,0:T(8,128)(2,1)S(1)}, bf16[2,2,40,1536]{3,2,1,0:T(8,128)(2,1)S(1)}, u32[]{:S(2)}, u32[]{:S(2)}) collective-permute-start(bf16[2,2,40,1536]{3,2,1,0:T(8,128)(2,1)S(1)} %get-tuple-element.83), channel_id=1, source_target_pairs={{0,16},{8,24},{16,0},{24,8},{1,17},{9,25},{17,1},{25,9},{2,18},{10... | collective-permute-start | bytes 1474568 | tf_op jit(solution)/shard_map/ppermute | solution.py:27
  102.5 12.7 %collective-permute-start.24 = (bf16[2,2,40,1536]{3,2,1,0:T(8,128)(2,1)S(1)}, bf16[2,2,40,1536]{3,2,1,0:T(8,128)(2,1)S(1)}, u32[]{:S(2)}, u32[]{:S(2)}) collective-permute-start(bf16[2,2,40,1536]{3,2,1,0:T(8,128)(2,1)S(1)} %get-tuple-element.85), channel_id=1, source_target_pairs={{0,8},{8,0},{16,24},{24,16},{1,9},{9,1},{17,25},{25,17},{2,10},{10... | collective-permute-start | bytes 1474568 | tf_op jit(solution)/shard_map/ppermute | solution.py:27
  107.7 14.0 %collective-permute-start.26 = (bf16[2,2,40,1536]{3,2,1,0:T(8,128)(2,1)S(1)}, bf16[2,2,40,1536]{3,2,1,0:T(8,128)(2,1)S(1)}, u32[]{:S(2)}, u32[]{:S(2)}) collective-permute-start(bf16[2,2,40,1536]{3,2,1,0:T(8,128)(2,1)S(1)} %get-tuple-element.87), channel_id=1, source_target_pairs={{0,16},{8,24},{16,0},{24,8},{1,17},{9,25},{17,1},{25,9},{2,18},{10... | collective-permute-start | bytes 1474568 | tf_op jit(solution)/shard_map/ppermute | solution.py:27
  109.9 10.6 %collective-permute-start.27 = (bf16[1,2,40,1536]{3,2,1,0:T(8,128)(2,1)S(1)}, bf16[1,2,40,1536]{3,2,1,0:T(8,128)(2,1)S(1)}, u32[]{:S(2)}, u32[]{:S(2)}) collective-permute-start(bf16[1,2,40,1536]{3,2,1,0:T(8,128)(2,1)S(1)} %get-tuple-element.89), channel_id=1, source_target_pairs={{0,8},{8,0},{16,24},{24,16},{1,9},{9,1},{17,25},{25,17},{2,10},{10... | collective-permute-start | bytes 737288 | tf_op jit(solution)/shard_map/ppermute | solution.py:27
  115.3 10.8 %collective-permute-start.25 = (bf16[1,2,40,1536]{3,2,1,0:T(8,128)(2,1)S(1)}, bf16[1,2,40,1536]{3,2,1,0:T(8,128)(2,1)S(1)}, u32[]{:S(2)}, u32[]{:S(2)}) collective-permute-start(bf16[1,2,40,1536]{3,2,1,0:T(8,128)(2,1)S(1)} %get-tuple-element.96), channel_id=1, source_target_pairs={{0,16},{8,24},{16,0},{24,8},{1,17},{9,25},{17,1},{25,9},{2,18},{10... | collective-permute-start | bytes 737288 | tf_op jit(solution)/shard_map/ppermute | solution.py:27
  117.2 12.6 %collective-permute-start.23 = (bf16[2,1,40,1536]{3,2,1,0:T(8,128)(2,1)S(1)}, bf16[2,1,40,1536]{3,2,1,0:T(8,128)(2,1)S(1)}, u32[]{:S(2)}, u32[]{:S(2)}) collective-permute-start(bf16[2,1,40,1536]{3,2,1,0:T(8,128)(2,1)S(1)} %get-tuple-element.92), channel_id=1, source_target_pairs={{0,8},{8,0},{16,24},{24,16},{1,9},{9,1},{17,25},{25,17},{2,10},{10... | collective-permute-start | bytes 737288 | tf_op jit(solution)/shard_map/ppermute | solution.py:27
  117.3 12.6 %collective-permute-start.30 = (bf16[2,1,40,1536]{3,2,1,0:T(8,128)(2,1)S(1)}, bf16[2,1,40,1536]{3,2,1,0:T(8,128)(2,1)S(1)}, u32[]{:S(2)}, u32[]{:S(2)}) collective-permute-start(bf16[2,1,40,1536]{3,2,1,0:T(8,128)(2,1)S(1)} %get-tuple-element.108), channel_id=1, source_target_pairs={{0,16},{8,24},{16,0},{24,8},{1,17},{9,25},{17,1},{25,9},{2,18},{10... | collective-permute-start | bytes 737288 | tf_op jit(solution)/shard_map/ppermute | solution.py:27
  121.8 8.1 %collective-permute-start.29 = (bf16[1,2,40,1536]{3,2,1,0:T(8,128)(2,1)S(1)}, bf16[1,2,40,1536]{3,2,1,0:T(8,128)(2,1)S(1)}, u32[]{:S(2)}, u32[]{:S(2)}) collective-permute-start(bf16[1,2,40,1536]{3,2,1,0:T(8,128)(2,1)S(1)} %get-tuple-element.101), channel_id=1, source_target_pairs={{0,8},{8,0},{16,24},{24,16},{1,9},{9,1},{17,25},{25,17},{2,10},{10... | collective-permute-start | bytes 737288 | tf_op jit(solution)/shard_map/ppermute | solution.py:27
  123.7 16.0 %collective-permute-start.31 = (bf16[2,40,1536]{2,1,0:T(8,128)(2,1)S(1)}, bf16[2,40,1536]{2,1,0:T(8,128)(2,1)S(1)}, u32[]{:S(2)}, u32[]{:S(2)}) collective-permute-start(bf16[2,40,1536]{2,1,0:T(8,128)(2,1)S(1)} %reply.5), channel_id=1, source_target_pairs={{0,6},{1,7},{2,4},{3,5},{4,2},{5,3},{6,0},{7,1},{8,14},{9,15},{10,... | collective-permute-start | bytes 737288 | tf_op jit(solution)/shard_map/ppermute | solution.py:27
  126.2 13.5 %collective-permute-start.32 = (bf16[2,40,1536]{2,1,0:T(8,128)(2,1)S(1)}, bf16[2,40,1536]{2,1,0:T(8,128)(2,1)S(1)}, u32[]{:S(2)}, u32[]{:S(2)}) collective-permute-start(bf16[2,40,1536]{2,1,0:T(8,128)(2,1)S(1)} %reply.6), channel_id=1, source_target_pairs={{0,4},{1,5},{2,6},{3,7},{4,0},{5,1},{6,2},{7,3},{8,12},{9,13},{10,... | collective-permute-start | bytes 737288 | tf_op jit(solution)/shard_map/ppermute | solution.py:27
  130.0 10.6 %collective-permute-start.34 = (bf16[2,40,1536]{2,1,0:T(8,128)(2,1)S(1)}, bf16[2,40,1536]{2,1,0:T(8,128)(2,1)S(1)}, u32[]{:S(2)}, u32[]{:S(2)}) collective-permute-start(bf16[2,40,1536]{2,1,0:T(8,128)(2,1)S(1)} %reply.7), channel_id=1, source_target_pairs={{0,2},{1,3},{2,0},{3,1},{4,6},{5,7},{6,4},{7,5},{8,10},{9,11},{10,... | collective-permute-start | bytes 737288 | tf_op jit(solution)/shard_map/ppermute | solution.py:27
  133.8 4.9 %collective-permute-start.28 = (bf16[1,1,40,1536]{3,2,1,0:T(8,128)(2,1)S(1)}, bf16[1,1,40,1536]{3,2,1,0:T(8,128)(2,1)S(1)}, u32[]{:S(2)}, u32[]{:S(2)}) collective-permute-start(bf16[1,1,40,1536]{3,2,1,0:T(8,128)(2,1)S(1)} %get-tuple-element.105), channel_id=1, source_target_pairs={{0,16},{8,24},{16,0},{24,8},{1,17},{9,25},{17,1},{25,9},{2,18},{10... | collective-permute-start | bytes 368648 | tf_op jit(solution)/shard_map/ppermute | solution.py:27
  133.8 6.0 %collective-permute-start.33 = (bf16[1,1,40,1536]{3,2,1,0:T(8,128)(2,1)S(1)}, bf16[1,1,40,1536]{3,2,1,0:T(8,128)(2,1)S(1)}, u32[]{:S(2)}, u32[]{:S(2)}) collective-permute-start(bf16[1,1,40,1536]{3,2,1,0:T(8,128)(2,1)S(1)} %get-tuple-element.110), channel_id=1, source_target_pairs={{0,8},{8,0},{16,24},{24,16},{1,9},{9,1},{17,25},{25,17},{2,10},{10... | collective-permute-start | bytes 368648 | tf_op jit(solution)/shard_map/ppermute | solution.py:27
  141.2 1.8 %collective-permute-start.35 = (bf16[256,768]{1,0:T(8,128)(2,1)S(1)}, bf16[256,768]{1,0:T(8,128)(2,1)S(1)}, u32[]{:S(2)}, u32[]{:S(2)}) collective-permute-start(bf16[256,768]{1,0:T(8,128)(2,1)S(1)} %get-tuple-element.116), channel_id=1, source_target_pairs={{0,1},{1,0},{2,3},{3,2},{4,5},{5,4},{6,7},{7,6},{8,9},{9,8},{10,11... | collective-permute-start | bytes 1179656 | tf_op jit(solution)/shard_map/ppermute | solution.py:27

commit v10 on v9

--- a/solution.py
+++ b/solution.py
@@ -575,14 +575,16 @@
         name="dispatch",
     )(placement, normed, swap(normed, "exp", n_exp, 1))
     arrived = [outgoing[0]] + [swap(outgoing[k], "exp", n_exp, 2 * k) for k in range(1, chunks)]
-    weight = pl.pallas_call(
-        gate_kernel,
-        in_specs=[SMEM] + [VMEM] * (2 + chunks),
-        out_specs=VMEM,
-        out_shape=struct((own, CAP, 128), F32),
-        compiler_params=params(24),
-        name="gate",
-    )(place, other, router.T, *arrived)
+
+    def gate(token):
+        return pl.pallas_call(
+            gate_kernel,
+            in_specs=[SMEM] + [VMEM] * (2 + chunks),
+            out_specs=VMEM,
+            out_shape=struct((own, CAP, 128), F32),
+            compiler_params=params(24),
+            name="gate",
+        )(after(place, token), other, router.T, *arrived)
 
     bits = bits_of(n_ctx)
     orders = [bits if k % 2 == 0 else bits[::-1] for k in range(chunks)]
@@ -610,7 +612,7 @@
             None,
         )
     hidden, *far = project(
-        after(place, weight),
+        place,
         list(range(done, chunks)),
         chunks,
         gathered,
@@ -645,6 +647,8 @@
                 for (first, _, path), (sent, kept) in zip(paths, results)
             ]
             token = results[0][0]
+            if i == min(3, chunks - 1):
+                weight = gate(token)
         if 2 <= i < chunks + 2:
             k = order[i - 2]
             sums = []

time: 144 us -> 143 us (level)
  transfers between devices with their start and end apart: 36 -> 36, of which waited for: 14 -> 13; matrix products, arithmetic and copies ran while one was open for 1% -> 1% of each run, Pallas kernels for 26% -> 26%
where the time goes in v10:
time: 143 us
  Pallas kernels  53.7 us (38%)
  starting transfers between devices  52.4 us (37%)
  waiting for transfers between devices  28.8 us (20%)
  local copies, waits for them, and re-layouts  4.96 us (3%)
  other arithmetic  2.56 us (2%)
    ppermute x36, starting transfers between devices, swap(): return lax.ppermute(x, axis, [(i, i ^ k) for i in range(n) if keep(i)])  52.4 us
    ppermute x36, waiting for transfers between devices, swap(): return lax.ppermute(x, axis, [(i, i ^ k) for i in range(n) if keep(i)])  28.8 us
    pallas_call x3, Pallas kernels, project(): pl.pallas_call(functools.partial(project_kernel, chunks=chunks, parts=par...  18.8 us
    pallas_call x3, Pallas kernels, down_chunk(): pl.pallas_call(functools.partial(down_kernel, chunk=chunk, shares=shares)...  15.4 us
    pallas_call x3, Pallas kernels, call_with_held(): pl.pallas_call(functools.partial(with_held, kernel, pieces), in_specs=[SM...  12.7 us
    unnamed x22, local copies, waits for them, and re-layouts  4.41 us
    pallas_call x1, Pallas kernels, body(): pl.pallas_call(state_kernel, in_specs=[ANY] * 2 + [VMEM], out_specs=[VMEM...  3.83 us
  transfers between devices with their start and end apart: 36, of which 13 were waited for; matrix products, arithmetic and copies ran while one was open for 1% of the time, Pallas kernels for 26%

profile of v10, /device:TPU:0, one launch (start us, length us, event | category | flops | bytes accessed | tf_op | source)
XLA Modules:
  0.0 142.9 jit_solution(10788160555403265434)
XLA Ops:
  0.0 3.8 %local_state.1 = (bf16[12,128,128]{2,1,0:T(8,128)(2,1)}, bf16[12,128,128]{2,1,0:T(8,128)(2,1)}) custom-call(bf16[4,64,768]{2,1,0:T(8,128)(2,1)} %refs_1_.1, bf16[4,64,768]{2,1,0:T(8,128)(2,1)} %refs_2_.1, f32[24,64]{1,0:T(8,128)} %bitcast.19), custom_call_target="tpu_custom_call" | custom-call | tf_op jit(solution)/shard_map/local_state/pallas_call | solution.py:509
  4.8 2.9 %collective-permute-start.1 = (f32[2,12,1,1]{1,0,3,2:T(2,128)S(1)}, f32[2,12,1,1]{1,0,3,2:T(2,128)S(1)}, u32[]{:S(2)}, u32[]{:S(2)}) collective-permute-start(f32[2,12,1,1]{1,0,3,2:T(2,128)S(1)} %exp.14), channel_id=1, source_target_pairs={{0,8},{8,0},{16,24},{24,16},{1,9},{9,1},{17,25},{25,17},{2,10},{10... | collective-permute-start | bytes 296 | tf_op jit(solution)/shard_map/ppermute | solution.py:27
  7.8 1.5 %collective-permute-start.3 = (f32[2,12,1,1]{1,0,3,2:T(2,128)S(1)}, f32[2,12,1,1]{1,0,3,2:T(2,128)S(1)}, u32[]{:S(2)}, u32[]{:S(2)}) collective-permute-start(f32[2,12,1,1]{1,0,3,2:T(2,128)S(1)} %exp.14), channel_id=1, source_target_pairs={{0,24},{8,16},{16,8},{24,0},{1,25},{9,17},{17,9},{25,1},{2,26},{10... | collective-permute-start | bytes 296 | tf_op jit(solution)/shard_map/ppermute | solution.py:27
  9.3 2.0 %collective-permute-start.4 = (bf16[12,128,128]{2,1,0:T(8,128)(2,1)}, bf16[12,128,128]{2,1,0:T(8,128)(2,1)S(1)}, u32[]{:S(2)}, u32[]{:S(2)}) collective-permute-start(bf16[12,128,128]{2,1,0:T(8,128)(2,1)} %get-tuple-element.65), channel_id=1, source_target_pairs={{0,16},{8,24},{1,17},{9,25},{2,18},{10,26},{3,19},{11,27},{4,20},{... | collective-permute-start | bytes 1179656 | tf_op jit(solution)/shard_map/ppermute | solution.py:27
  11.2 3.9 %collective-permute-start = (bf16[12,128,128]{2,1,0:T(8,128)(2,1)}, bf16[12,128,128]{2,1,0:T(8,128)(2,1)S(1)}, u32[]{:S(2)}, u32[]{:S(2)}) collective-permute-start(bf16[12,128,128]{2,1,0:T(8,128)(2,1)} %get-tuple-element.61), channel_id=1, source_target_pairs={{0,8},{8,0},{16,24},{1,9},{9,1},{17,25},{2,10},{10,2},{18,26},{3,1... | collective-permute-start | bytes 1179656 | tf_op jit(solution)/shard_map/ppermute | solution.py:27
  15.6 1.0 copy-done
  16.6 1.0 copy-done.2
  17.6 1.0 copy-done.3
  20.0 4.3 %inside_and_placement.1 = (f32[4,64,768]{2,1,0:T(8,128)S(1)}, bf16[320,256]{1,0:T(8,128)(2,1)S(1)}, s32[80,128]{1,0:T(8,128)S(1)}) custom-call(s32[2]{0:T(128)S(1)} %pad_add_fusion.place, bf16[2,6144,1536]{2,1,0:T(8,128)(2,1)} %up.11, bf16[2,1536,6144]{2,1,0:T(8,128)(2,1)} %weights.5, bf16[4,64,768]{2,1,0:T(8,128)(2,1)S(1)} %copy-done, ...), custom_call_target="tpu_custom_call" | custom-call | tf_op jit(solution)/shard_map/inside_and_placement/pallas_call | solution.py:97
  24.6 1.3 collective-permute-start.2
  26.1 3.3 %collective-permute-start.5 = (bf16[12,128,128]{2,1,0:T(8,128)(2,1)S(1)}, bf16[12,128,128]{2,1,0:T(8,128)(2,1)S(1)}, u32[]{:S(2)}, u32[]{:S(2)}) collective-permute-start(bf16[12,128,128]{2,1,0:T(8,128)(2,1)S(1)} %fusion.5), channel_id=1, source_target_pairs={{0,8},{16,24},{24,16},{1,9},{17,25},{25,17},{2,10},{18,26},{26,18}... | collective-permute-start | bytes 1179656 | tf_op jit(solution)/shard_map/ppermute | solution.py:27
  29.5 5.8 %early_weights.1 = (bf16[2,768,1536]{2,1,0:T(8,128)(2,1)S(1)}, bf16[2,768,1536]{2,1,0:T(8,128)(2,1)S(1)}, bf16[2,1536,768]{2,1,0:T(8,128)(2,1)S(1)}) custom-call(s32[2]{0:T(128)S(1)} %pad_add_fusion.place, bf16[2,6144,1536]{2,1,0:T(8,128)(2,1)} %up.11, bf16[2,1536,6144]{2,1,0:T(8,128)(2,1)} %weights.5), custom_call_target="tpu_custom_call" | custom-call | tf_op jit(solution)/shard_map/early_weights/pallas_call | solution.py:97
  36.1 2.6 %normed.1.refs_0_ = bf16[256,768]{1,0:T(8,128)(2,1)S(1)} custom-call(s32[2]{0:T(128)S(1)} %pad_add_fusion.place, bf16[2,6144,1536]{2,1,0:T(8,128)(2,1)} %up.11, bf16[2,1536,6144]{2,1,0:T(8,128)(2,1)} %weights.5, bf16[4,64,768]{2,1,0:T(8,128)(2,1)S(1)} %copy-done.1, f32[4,64,768]{2,1,0:T(8,128)S(1)} %get-tuple-element.63.refs_1_, f32[24,64]{1,0:T(8,128)S(1)} %bitcast.21, ...), custom_call_target="tpu_custom_call" | custom-call | tf_op jit(solution)/shard_map/normed/pallas_call | solution.py:97
  38.8 1.7 %collective-permute-done.6.refs_1_ = bf16[256,768]{1,0:T(8,128)(2,1)S(1)} collective-permute-done((bf16[256,768]{1,0:T(8,128)(2,1)S(1)}, bf16[256,768]{1,0:T(8,128)(2,1)S(1)}, u32[]{:S(2)}, u32[]{:S(2)}) %collective-permute-start.6) | collective-permute-done | bytes 393248 | tf_op jit(solution)/shard_map/ppermute | solution.py:27
  40.9 2.5 %collective-permute-start.16 = (bf16[2,40,1536]{2,1,0:T(8,128)(2,1)S(1)}, bf16[2,40,1536]{2,1,0:T(8,128)(2,1)S(1)}, u32[]{:S(2)}, u32[]{:S(2)}) collective-permute-start(bf16[2,40,1536]{2,1,0:T(8,128)(2,1)S(1)} %get-tuple-element.77.refs_0_), channel_id=1, source_target_pairs={{0,8},{8,0},{16,24},{24,16},{1,9},{9,1},{17,25},{25,17},{2,10},{10... | collective-permute-start | bytes 737288 | tf_op jit(solution)/shard_map/ppermute | solution.py:27
  43.5 1.6 %collective-permute-start.15 = (bf16[2,40,1536]{2,1,0:T(8,128)(2,1)S(1)}, bf16[2,40,1536]{2,1,0:T(8,128)(2,1)S(1)}, u32[]{:S(2)}, u32[]{:S(2)}) collective-permute-start(bf16[2,40,1536]{2,1,0:T(8,128)(2,1)S(1)} %get-tuple-element.76), channel_id=1, source_target_pairs={{0,2},{1,3},{2,0},{3,1},{4,6},{5,7},{6,4},{7,5},{8,10},{9,11},{10,... | collective-permute-start | bytes 737288 | tf_op jit(solution)/shard_map/ppermute | solution.py:27
  45.1 2.6 %collective-permute-start.7 = (bf16[2,40,1536]{2,1,0:T(8,128)(2,1)S(1)}, bf16[2,40,1536]{2,1,0:T(8,128)(2,1)S(1)}, u32[]{:S(2)}, u32[]{:S(2)}) collective-permute-start(bf16[2,40,1536]{2,1,0:T(8,128)(2,1)S(1)} %get-tuple-element.73), channel_id=1, source_target_pairs={{0,4},{1,5},{2,6},{3,7},{4,0},{5,1},{6,2},{7,3},{8,12},{9,13},{10,... | collective-permute-start | bytes 737288 | tf_op jit(solution)/shard_map/ppermute | solution.py:27
  47.9 1.9 %collective-permute-done.16.refs_1_ = bf16[2,40,1536]{2,1,0:T(8,128)(2,1)S(1)} collective-permute-done((bf16[2,40,1536]{2,1,0:T(8,128)(2,1)S(1)}, bf16[2,40,1536]{2,1,0:T(8,128)(2,1)S(1)}, u32[]{:S(2)}, u32[]{:S(2)}) %collective-permute-start.16) | collective-permute-done | bytes 245792 | tf_op jit(solution)/shard_map/ppermute | solution.py:27
  49.7 1.5 %collective-permute-done.17.refs_2_ = bf16[2,40,1536]{2,1,0:T(8,128)(2,1)S(1)} collective-permute-done((bf16[2,40,1536]{2,1,0:T(8,128)(2,1)S(1)}, bf16[2,40,1536]{2,1,0:T(8,128)(2,1)S(1)}, u32[]{:S(2)}, u32[]{:S(2)}) %collective-permute-start.17) | collective-permute-done | bytes 245792 | tf_op jit(solution)/shard_map/ppermute | solution.py:27
  51.2 4.5 %collective-permute-done.15.refs_0_.refs_1_ = bf16[2,40,1536]{2,1,0:T(8,128)(2,1)S(1)} collective-permute-done((bf16[2,40,1536]{2,1,0:T(8,128)(2,1)S(1)}, bf16[2,40,1536]{2,1,0:T(8,128)(2,1)S(1)}, u32[]{:S(2)}, u32[]{:S(2)}) %collective-permute-start.15) | collective-permute-done | bytes 245792 | tf_op jit(solution)/shard_map/ppermute | solution.py:27
  55.7 1.6 %collective-permute-start.19 = (bf16[2,40,1536]{2,1,0:T(8,128)(2,1)S(1)}, bf16[2,40,1536]{2,1,0:T(8,128)(2,1)S(1)}, u32[]{:S(2)}, u32[]{:S(2)}) collective-permute-start(bf16[2,40,1536]{2,1,0:T(8,128)(2,1)S(1)} %collective-permute-done.15.refs_0_.refs_1_), channel_id=1, source_target_pairs={{0,16},{8,24},{16,0},{24,8},{1,17},{9,25},{17,1},{25,9},{2,18},{10... | collective-permute-start | bytes 737288 | tf_op jit(solution)/shard_map/ppermute | solution.py:27
  58.4 7.0 %collective-permute-done.7.refs_0_.refs_2_ = bf16[2,40,1536]{2,1,0:T(8,128)(2,1)S(1)} collective-permute-done((bf16[2,40,1536]{2,1,0:T(8,128)(2,1)S(1)}, bf16[2,40,1536]{2,1,0:T(8,128)(2,1)S(1)}, u32[]{:S(2)}, u32[]{:S(2)}) %collective-permute-start.7) | collective-permute-done | bytes 245792 | tf_op jit(solution)/shard_map/ppermute | solution.py:27
  65.4 1.1 collective-permute-start.8
  66.5 1.0 collective-permute-start.13
  67.5 2.0 %collective-permute-start.20 = (bf16[2,40,1536]{2,1,0:T(8,128)(2,1)S(1)}, bf16[2,40,1536]{2,1,0:T(8,128)(2,1)S(1)}, u32[]{:S(2)}, u32[]{:S(2)}) collective-permute-start(bf16[2,40,1536]{2,1,0:T(8,128)(2,1)S(1)} %collective-permute-done.19.refs_2_), channel_id=1, source_target_pairs={{0,8},{8,0},{16,24},{24,16},{1,9},{9,1},{17,25},{25,17},{2,10},{10... | collective-permute-start | bytes 737288 | tf_op jit(solution)/shard_map/ppermute | solution.py:27
  70.4 1.6 %collective-permute-start.9 = (bf16[2,40,1536]{2,1,0:T(8,128)(2,1)S(1)}, bf16[2,40,1536]{2,1,0:T(8,128)(2,1)S(1)}, u32[]{:S(2)}, u32[]{:S(2)}) collective-permute-start(bf16[2,40,1536]{2,1,0:T(8,128)(2,1)S(1)} %collective-permute-done.7.refs_0_.refs_2_), channel_id=1, source_target_pairs={{0,16},{8,24},{16,0},{24,8},{1,17},{9,25},{17,1},{25,9},{2,18},{10... | collective-permute-start | bytes 737288 | tf_op jit(solution)/shard_map/ppermute | solution.py:27
  72.0 2.3 %collective-permute-done.8.refs_1_ = bf16[2,40,1536]{2,1,0:T(8,128)(2,1)S(1)} collective-permute-done((bf16[2,40,1536]{2,1,0:T(8,128)(2,1)S(1)}, bf16[2,40,1536]{2,1,0:T(8,128)(2,1)S(1)}, u32[]{:S(2)}, u32[]{:S(2)}) %collective-permute-start.8) | collective-permute-done | bytes 245792 | tf_op jit(solution)/shard_map/ppermute | solution.py:27
  74.3 2.0 %collective-permute-start.10 = (bf16[2,40,1536]{2,1,0:T(8,128)(2,1)S(1)}, bf16[2,40,1536]{2,1,0:T(8,128)(2,1)S(1)}, u32[]{:S(2)}, u32[]{:S(2)}) collective-permute-start(bf16[2,40,1536]{2,1,0:T(8,128)(2,1)S(1)} %collective-permute-done.8.refs_1_), channel_id=1, source_target_pairs={{0,16},{8,24},{16,0},{24,8},{1,17},{9,25},{17,1},{25,9},{2,18},{10... | collective-permute-start | bytes 737288 | tf_op jit(solution)/shard_map/ppermute | solution.py:27
  76.4 5.3 %project_0.1.refs_4_ = f32[2,160,1536]{2,1,0:T(8,128)S(1)} custom-call(s32[2]{0:T(128)S(1)} %pad_add_fusion.place, bf16[2,6144,1536]{2,1,0:T(8,128)(2,1)} %up.11, bf16[2,1536,6144]{2,1,0:T(8,128)(2,1)} %weights.5, bf16[2,40,1536]{2,1,0:T(8,128)(2,1)S(1)} %get-tuple-element.77.refs_0_, bf16[2,40,1536]{2,1,0:T(8,128)(2,1)S(1)} %collective-permute-done.16.refs_1_, ...), custom_call_target="tpu_custom_call" | custom-call | flops 1509949440 | bytes 9437184 | tf_op jit(solution)/shard_map/project_0/pallas_call | solution.py:309
  81.7 4.9 %project_1.1.refs_11_ = f32[2,160,1536]{2,1,0:T(8,128)S(1)} custom-call(s32[2]{0:T(128)S(1)} %pad_add_fusion.place, bf16[2,6144,1536]{2,1,0:T(8,128)(2,1)} %up.11, bf16[2,1536,6144]{2,1,0:T(8,128)(2,1)} %weights.5, bf16[2,40,1536]{2,1,0:T(8,128)(2,1)S(1)} %collective-permute-done.15.refs_0_.refs_1_, ...), custom_call_target="tpu_custom_call" | custom-call | flops 1509949440 | bytes 9437184 | tf_op jit(solution)/shard_map/project_1/pallas_call | solution.py:309
  86.6 8.7 %project_2.1 = (bf16[2,160,1536]{2,1,0:T(8,128)(2,1)S(1)}, bf16[2,2,40,1536]{3,2,1,0:T(8,128)(2,1)S(1)}, bf16[2,2,40,1536]{3,2,1,0:T(8,128)(2,1)S(1)}) custom-call(s32[2]{0:T(128)S(1)} %pad_add_fusion.place, bf16[2,6144,1536]{2,1,0:T(8,128)(2,1)} %up.11, bf16[2,1536,6144]{2,1,0:T(8,128)(2,1)} %weights.5, ...), custom_call_target="tpu_custom_call" | custom-call | flops 4529848320 | bytes 28311552 | tf_op jit(solution)/shard_map/project_2/pallas_call | solution.py:309
  95.3 2.0 %collective-permute-start.22 = (bf16[2,2,40,1536]{3,2,1,0:T(8,128)(2,1)S(1)}, bf16[2,2,40,1536]{3,2,1,0:T(8,128)(2,1)S(1)}, u32[]{:S(2)}, u32[]{:S(2)}) collective-permute-start(bf16[2,2,40,1536]{3,2,1,0:T(8,128)(2,1)S(1)} %get-tuple-element.81), channel_id=1, source_target_pairs={{0,16},{8,24},{16,0},{24,8},{1,17},{9,25},{17,1},{25,9},{2,18},{10... | collective-permute-start | bytes 1474568 | tf_op jit(solution)/shard_map/ppermute | solution.py:27
  97.3 5.3 %down_2.1 = (bf16[2,2,40,1536]{3,2,1,0:T(8,128)(2,1)S(1)}, bf16[2,2,40,1536]{3,2,1,0:T(8,128)(2,1)S(1)}) custom-call(s32[2]{0:T(128)S(1)} %pad_add_fusion.place, bf16[2,1536,6144]{2,1,0:T(8,128)(2,1)} %weights.5, bf16[2,160,1536]{2,1,0:T(8,128)(2,1)S(1)} %get-tuple-element.88.hidden), custom_call_target="tpu_custom_call" | custom-call | flops 1509949440 | bytes 9437184 | tf_op jit(solution)/shard_map/down_2/pallas_call | solution.py:366
  102.7 5.0 %down_1.1 = (bf16[2,2,40,1536]{3,2,1,0:T(8,128)(2,1)S(1)}, bf16[2,2,40,1536]{3,2,1,0:T(8,128)(2,1)S(1)}) custom-call(s32[2]{0:T(128)S(1)} %pad_add_fusion.place, bf16[2,1536,6144]{2,1,0:T(8,128)(2,1)} %weights.5, bf16[2,160,1536]{2,1,0:T(8,128)(2,1)S(1)} %get-tuple-element.88.hidden), custom_call_target="tpu_custom_call" | custom-call | flops 1509949440 | bytes 9437184 | tf_op jit(solution)/shard_map/down_1/pallas_call | solution.py:366
  107.7 2.0 %collective-permute-start.26 = (bf16[2,2,40,1536]{3,2,1,0:T(8,128)(2,1)S(1)}, bf16[2,2,40,1536]{3,2,1,0:T(8,128)(2,1)S(1)}, u32[]{:S(2)}, u32[]{:S(2)}) collective-permute-start(bf16[2,2,40,1536]{3,2,1,0:T(8,128)(2,1)S(1)} %get-tuple-element.85), channel_id=1, source_target_pairs={{0,16},{8,24},{16,0},{24,8},{1,17},{9,25},{17,1},{25,9},{2,18},{10... | collective-permute-start | bytes 1474568 | tf_op jit(solution)/shard_map/ppermute | solution.py:27
  110.0 5.0 %down_0.1 = (bf16[2,1,40,1536]{3,2,1,0:T(8,128)(2,1)S(1)}, bf16[2,1,40,1536]{3,2,1,0:T(8,128)(2,1)S(1)}, bf16[2,1,40,1536]{3,2,1,0:T(8,128)(2,1)S(1)}, bf16[2,1,40,1536]{3,2,1,0:T(8,128)(2,1)S(1)}) custom-call(s32[2]{0:T(128)S(1)} %pad_add_fusion.place, bf16[2,1536,6144]{2,1,0:T(8,128)(2,1)} %weights.5, bf16[2,160,1536]{2,1,0:T(8,128)(2,1)S(1)} %get-tuple-element.88.hidden), custom_call_target="tpu_custom_call" | custom-call | flops 1509949440 | bytes 9437184 | tf_op jit(solution)/shard_map/down_0/pallas_call | solution.py:366
  115.1 2.0 %collective-permute-start.23 = (bf16[2,1,40,1536]{3,2,1,0:T(8,128)(2,1)S(1)}, bf16[2,1,40,1536]{3,2,1,0:T(8,128)(2,1)S(1)}, u32[]{:S(2)}, u32[]{:S(2)}) collective-permute-start(bf16[2,1,40,1536]{3,2,1,0:T(8,128)(2,1)S(1)} %get-tuple-element.90), channel_id=1, source_target_pairs={{0,8},{8,0},{16,24},{24,16},{1,9},{9,1},{17,25},{25,17},{2,10},{10... | collective-permute-start | bytes 737288 | tf_op jit(solution)/shard_map/ppermute | solution.py:27
  117.4 2.0 %collective-permute-start.30 = (bf16[2,1,40,1536]{3,2,1,0:T(8,128)(2,1)S(1)}, bf16[2,1,40,1536]{3,2,1,0:T(8,128)(2,1)S(1)}, u32[]{:S(2)}, u32[]{:S(2)}) collective-permute-start(bf16[2,1,40,1536]{3,2,1,0:T(8,128)(2,1)S(1)} %get-tuple-element.108), channel_id=1, source_target_pairs={{0,16},{8,24},{16,0},{24,8},{1,17},{9,25},{17,1},{25,9},{2,18},{10... | collective-permute-start | bytes 737288 | tf_op jit(solution)/shard_map/ppermute | solution.py:27
  119.3 1.1 gate.1.weight
  120.4 1.2 collective-permute-done.27.got
  121.8 2.2 %collective-permute-start.29 = (bf16[1,2,40,1536]{3,2,1,0:T(8,128)(2,1)S(1)}, bf16[1,2,40,1536]{3,2,1,0:T(8,128)(2,1)S(1)}, u32[]{:S(2)}, u32[]{:S(2)}) collective-permute-start(bf16[1,2,40,1536]{3,2,1,0:T(8,128)(2,1)S(1)} %get-tuple-element.101), channel_id=1, source_target_pairs={{0,8},{8,0},{16,24},{24,16},{1,9},{9,1},{17,25},{25,17},{2,10},{10... | collective-permute-start | bytes 737288 | tf_op jit(solution)/shard_map/ppermute | solution.py:27
  124.0 1.8 %collective-permute-start.31 = (bf16[2,40,1536]{2,1,0:T(8,128)(2,1)S(1)}, bf16[2,40,1536]{2,1,0:T(8,128)(2,1)S(1)}, u32[]{:S(2)}, u32[]{:S(2)}) collective-permute-start(bf16[2,40,1536]{2,1,0:T(8,128)(2,1)S(1)} %reply.5), channel_id=1, source_target_pairs={{0,6},{1,7},{2,4},{3,5},{4,2},{5,3},{6,0},{7,1},{8,14},{9,15},{10,... | collective-permute-start | bytes 737288 | tf_op jit(solution)/shard_map/ppermute | solution.py:27
  125.9 4.0 %collective-permute-start.32 = (bf16[2,40,1536]{2,1,0:T(8,128)(2,1)S(1)}, bf16[2,40,1536]{2,1,0:T(8,128)(2,1)S(1)}, u32[]{:S(2)}, u32[]{:S(2)}) collective-permute-start(bf16[2,40,1536]{2,1,0:T(8,128)(2,1)S(1)} %reply.6), channel_id=1, source_target_pairs={{0,4},{1,5},{2,6},{3,7},{4,0},{5,1},{6,2},{7,3},{8,12},{9,13},{10,... | collective-permute-start | bytes 737288 | tf_op jit(solution)/shard_map/ppermute | solution.py:27
  130.1 3.1 %collective-permute-start.34 = (bf16[2,40,1536]{2,1,0:T(8,128)(2,1)S(1)}, bf16[2,40,1536]{2,1,0:T(8,128)(2,1)S(1)}, u32[]{:S(2)}, u32[]{:S(2)}) collective-permute-start(bf16[2,40,1536]{2,1,0:T(8,128)(2,1)S(1)} %reply.7), channel_id=1, source_target_pairs={{0,2},{1,3},{2,0},{3,1},{4,6},{5,7},{6,4},{7,5},{8,10},{9,11},{10,... | collective-permute-start | bytes 737288 | tf_op jit(solution)/shard_map/ppermute | solution.py:27
  133.2 4.9 %collective-permute-done.28.got = bf16[1,1,40,1536]{3,2,1,0:T(8,128)(2,1)S(1)} collective-permute-done((bf16[1,1,40,1536]{3,2,1,0:T(8,128)(2,1)S(1)}, bf16[1,1,40,1536]{3,2,1,0:T(8,128)(2,1)S(1)}, u32[]{:S(2)}, u32[]{:S(2)}) %collective-permute-start.28) | collective-permute-done | bytes 122912 | tf_op jit(solution)/shard_map/ppermute | solution.py:27
  138.1 1.4 collective-permute-done.32.refs_3_
  140.4 1.7 %collective-permute-done.35 = bf16[256,768]{1,0:T(8,128)(2,1)S(1)} collective-permute-done((bf16[256,768]{1,0:T(8,128)(2,1)S(1)}, bf16[256,768]{1,0:T(8,128)(2,1)S(1)}, u32[]{:S(2)}, u32[]{:S(2)}) %collective-permute-start.35) | collective-permute-done | bytes 393248 | tf_op jit(solution)/shard_map/ppermute | solution.py:27
  142.1 0.8 add_convert_fusion
  (87 shorter events, 9.0 us)
Async XLA Ops:
  4.8 19.5 %collective-permute-start.1 = (f32[2,12,1,1]{1,0,3,2:T(2,128)S(1)}, f32[2,12,1,1]{1,0,3,2:T(2,128)S(1)}, u32[]{:S(2)}, u32[]{:S(2)}) collective-permute-start(f32[2,12,1,1]{1,0,3,2:T(2,128)S(1)} %exp.14), channel_id=1, source_target_pairs={{0,8},{8,0},{16,24},{24,16},{1,9},{9,1},{17,25},{25,17},{2,10},{10... | collective-permute-start | bytes 296 | tf_op jit(solution)/shard_map/ppermute | solution.py:27
  7.8 18.1 %collective-permute-start.3 = (f32[2,12,1,1]{1,0,3,2:T(2,128)S(1)}, f32[2,12,1,1]{1,0,3,2:T(2,128)S(1)}, u32[]{:S(2)}, u32[]{:S(2)}) collective-permute-start(f32[2,12,1,1]{1,0,3,2:T(2,128)S(1)} %exp.14), channel_id=1, source_target_pairs={{0,24},{8,16},{16,8},{24,0},{1,25},{9,17},{17,9},{25,1},{2,26},{10... | collective-permute-start | bytes 296 | tf_op jit(solution)/shard_map/ppermute | solution.py:27
  9.3 16.7 %collective-permute-start.4 = (bf16[12,128,128]{2,1,0:T(8,128)(2,1)}, bf16[12,128,128]{2,1,0:T(8,128)(2,1)S(1)}, u32[]{:S(2)}, u32[]{:S(2)}) collective-permute-start(bf16[12,128,128]{2,1,0:T(8,128)(2,1)} %get-tuple-element.65), channel_id=1, source_target_pairs={{0,16},{8,24},{1,17},{9,25},{2,18},{10,26},{3,19},{11,27},{4,20},{... | collective-permute-start | bytes 1179656 | tf_op jit(solution)/shard_map/ppermute | solution.py:27
  11.2 13.1 %collective-permute-start = (bf16[12,128,128]{2,1,0:T(8,128)(2,1)}, bf16[12,128,128]{2,1,0:T(8,128)(2,1)S(1)}, u32[]{:S(2)}, u32[]{:S(2)}) collective-permute-start(bf16[12,128,128]{2,1,0:T(8,128)(2,1)} %get-tuple-element.61), channel_id=1, source_target_pairs={{0,8},{8,0},{16,24},{1,9},{9,1},{17,25},{2,10},{10,2},{18,26},{3,1... | collective-permute-start | bytes 1179656 | tf_op jit(solution)/shard_map/ppermute | solution.py:27
  15.6 1.0 copy-start
  16.6 1.0 copy-start.2
  17.6 1.0 copy-start.3
  18.6 0.7 copy-start.4
  19.3 0.7 copy-start.7
  20.0 4.4 %copy-start.9 = (bf16[12,128,128]{2,1,0:T(8,128)(2,1)S(1)}, bf16[12,128,128]{2,1,0:T(8,128)(2,1)}, u32[]{:S(2)}) copy-start(bf16[12,128,128]{2,1,0:T(8,128)(2,1)} %get-tuple-element.61) | copy-start | bytes 1179652
  20.0 5.9 %copy-start.8 = (bf16[12,128,128]{2,1,0:T(8,128)(2,1)S(1)}, bf16[12,128,128]{2,1,0:T(8,128)(2,1)}, u32[]{:S(2)}) copy-start(bf16[12,128,128]{2,1,0:T(8,128)(2,1)} %get-tuple-element.65) | copy-start | bytes 1179652
  20.0 9.5 %copy-start.10 = (f32[768]{0:T(1024)S(1)}, f32[768]{0:T(1024)}, u32[]{:S(2)}) copy-start(f32[768]{0:T(1024)} %param.13) | copy-start | bytes 9220
  24.6 10.7 %collective-permute-start.2 = (bf16[12,128,128]{2,1,0:T(8,128)(2,1)S(1)}, bf16[12,128,128]{2,1,0:T(8,128)(2,1)S(1)}, u32[]{:S(2)}, u32[]{:S(2)}) collective-permute-start(bf16[12,128,128]{2,1,0:T(8,128)(2,1)S(1)} %fusion.3), channel_id=1, source_target_pairs={{0,16},{8,24},{1,17},{9,25},{2,18},{10,26},{3,19},{11,27},{4,20},{... | collective-permute-start | bytes 1179656 | tf_op jit(solution)/shard_map/ppermute | solution.py:27
  26.1 9.7 %collective-permute-start.5 = (bf16[12,128,128]{2,1,0:T(8,128)(2,1)S(1)}, bf16[12,128,128]{2,1,0:T(8,128)(2,1)S(1)}, u32[]{:S(2)}, u32[]{:S(2)}) collective-permute-start(bf16[12,128,128]{2,1,0:T(8,128)(2,1)S(1)} %fusion.5), channel_id=1, source_target_pairs={{0,8},{16,24},{24,16},{1,9},{17,25},{25,17},{2,10},{18,26},{26,18}... | collective-permute-start | bytes 1179656 | tf_op jit(solution)/shard_map/ppermute | solution.py:27
  29.5 6.6 %copy-start.1 = (bf16[4,64,768]{2,1,0:T(8,128)(2,1)S(1)}, bf16[4,64,768]{2,1,0:T(8,128)(2,1)}, u32[]{:S(2)}) copy-start(bf16[4,64,768]{2,1,0:T(8,128)(2,1)} %refs_0_.3) | copy-start | bytes 1179652
  29.5 6.6 %copy-start.5 = (f32[4,64,6]{1,0,2:T(4,128)S(1)}, f32[4,64,6]{1,0,2:T(4,128)}, u32[]{:S(2)}) copy-start(f32[4,64,6]{1,0,2:T(4,128)} %param.12) | copy-start | bytes 18436
  38.7 1.8 %collective-permute-start.6 = (bf16[256,768]{1,0:T(8,128)(2,1)S(1)}, bf16[256,768]{1,0:T(8,128)(2,1)S(1)}, u32[]{:S(2)}, u32[]{:S(2)}) collective-permute-start(bf16[256,768]{1,0:T(8,128)(2,1)S(1)} %normed.1.refs_0_), channel_id=1, source_target_pairs={{0,1},{1,0},{2,3},{3,2},{4,5},{5,4},{6,7},{7,6},{8,9},{9,8},{10,11... | collective-permute-start | bytes 1179656 | tf_op jit(solution)/shard_map/ppermute | solution.py:27
  40.9 8.8 %collective-permute-start.16 = (bf16[2,40,1536]{2,1,0:T(8,128)(2,1)S(1)}, bf16[2,40,1536]{2,1,0:T(8,128)(2,1)S(1)}, u32[]{:S(2)}, u32[]{:S(2)}) collective-permute-start(bf16[2,40,1536]{2,1,0:T(8,128)(2,1)S(1)} %get-tuple-element.77.refs_0_), channel_id=1, source_target_pairs={{0,8},{8,0},{16,24},{24,16},{1,9},{9,1},{17,25},{25,17},{2,10},{10... | collective-permute-start | bytes 737288 | tf_op jit(solution)/shard_map/ppermute | solution.py:27
  43.5 7.7 %collective-permute-start.17 = (bf16[2,40,1536]{2,1,0:T(8,128)(2,1)S(1)}, bf16[2,40,1536]{2,1,0:T(8,128)(2,1)S(1)}, u32[]{:S(2)}, u32[]{:S(2)}) collective-permute-start(bf16[2,40,1536]{2,1,0:T(8,128)(2,1)S(1)} %get-tuple-element.77.refs_0_), channel_id=1, source_target_pairs={{0,16},{8,24},{16,0},{24,8},{1,17},{9,25},{17,1},{25,9},{2,18},{10... | collective-permute-start | bytes 737288 | tf_op jit(solution)/shard_map/ppermute | solution.py:27
  43.5 12.2 %collective-permute-start.15 = (bf16[2,40,1536]{2,1,0:T(8,128)(2,1)S(1)}, bf16[2,40,1536]{2,1,0:T(8,128)(2,1)S(1)}, u32[]{:S(2)}, u32[]{:S(2)}) collective-permute-start(bf16[2,40,1536]{2,1,0:T(8,128)(2,1)S(1)} %get-tuple-element.76), channel_id=1, source_target_pairs={{0,2},{1,3},{2,0},{3,1},{4,6},{5,7},{6,4},{7,5},{8,10},{9,11},{10,... | collective-permute-start | bytes 737288 | tf_op jit(solution)/shard_map/ppermute | solution.py:27
  45.1 20.3 %collective-permute-start.7 = (bf16[2,40,1536]{2,1,0:T(8,128)(2,1)S(1)}, bf16[2,40,1536]{2,1,0:T(8,128)(2,1)S(1)}, u32[]{:S(2)}, u32[]{:S(2)}) collective-permute-start(bf16[2,40,1536]{2,1,0:T(8,128)(2,1)S(1)} %get-tuple-element.73), channel_id=1, source_target_pairs={{0,4},{1,5},{2,6},{3,7},{4,0},{5,1},{6,2},{7,3},{8,12},{9,13},{10,... | collective-permute-start | bytes 737288 | tf_op jit(solution)/shard_map/ppermute | solution.py:27
  47.6 18.8 %collective-permute-start.11 = (bf16[2,40,1536]{2,1,0:T(8,128)(2,1)S(1)}, bf16[2,40,1536]{2,1,0:T(8,128)(2,1)S(1)}, u32[]{:S(2)}, u32[]{:S(2)}) collective-permute-start(bf16[2,40,1536]{2,1,0:T(8,128)(2,1)S(1)} %get-tuple-element.74), channel_id=1, source_target_pairs={{0,6},{1,7},{2,4},{3,5},{4,2},{5,3},{6,0},{7,1},{8,14},{9,15},{10,... | collective-permute-start | bytes 737288 | tf_op jit(solution)/shard_map/ppermute | solution.py:27
  55.7 11.8 %collective-permute-start.19 = (bf16[2,40,1536]{2,1,0:T(8,128)(2,1)S(1)}, bf16[2,40,1536]{2,1,0:T(8,128)(2,1)S(1)}, u32[]{:S(2)}, u32[]{:S(2)}) collective-permute-start(bf16[2,40,1536]{2,1,0:T(8,128)(2,1)S(1)} %collective-permute-done.15.refs_0_.refs_1_), channel_id=1, source_target_pairs={{0,16},{8,24},{16,0},{24,8},{1,17},{9,25},{17,1},{25,9},{2,18},{10... | collective-permute-start | bytes 737288 | tf_op jit(solution)/shard_map/ppermute | solution.py:27
  57.3 12.6 %collective-permute-start.21 = (bf16[2,40,1536]{2,1,0:T(8,128)(2,1)S(1)}, bf16[2,40,1536]{2,1,0:T(8,128)(2,1)S(1)}, u32[]{:S(2)}, u32[]{:S(2)}) collective-permute-start(bf16[2,40,1536]{2,1,0:T(8,128)(2,1)S(1)} %collective-permute-done.16.refs_1_), channel_id=1, source_target_pairs={{0,16},{8,24},{16,0},{24,8},{1,17},{9,25},{17,1},{25,9},{2,18},{10... | collective-permute-start | bytes 737288 | tf_op jit(solution)/shard_map/ppermute | solution.py:27
  57.7 12.7 %collective-permute-start.18 = (bf16[2,40,1536]{2,1,0:T(8,128)(2,1)S(1)}, bf16[2,40,1536]{2,1,0:T(8,128)(2,1)S(1)}, u32[]{:S(2)}, u32[]{:S(2)}) collective-permute-start(bf16[2,40,1536]{2,1,0:T(8,128)(2,1)S(1)} %collective-permute-done.15.refs_0_.refs_1_), channel_id=1, source_target_pairs={{0,8},{8,0},{16,24},{24,16},{1,9},{9,1},{17,25},{25,17},{2,10},{10... | collective-permute-start | bytes 737288 | tf_op jit(solution)/shard_map/ppermute | solution.py:27
  65.4 8.9 %collective-permute-start.8 = (bf16[2,40,1536]{2,1,0:T(8,128)(2,1)S(1)}, bf16[2,40,1536]{2,1,0:T(8,128)(2,1)S(1)}, u32[]{:S(2)}, u32[]{:S(2)}) collective-permute-start(bf16[2,40,1536]{2,1,0:T(8,128)(2,1)S(1)} %collective-permute-done.7.refs_0_.refs_2_), channel_id=1, source_target_pairs={{0,8},{8,0},{16,24},{24,16},{1,9},{9,1},{17,25},{25,17},{2,10},{10... | collective-permute-start | bytes 737288 | tf_op jit(solution)/shard_map/ppermute | solution.py:27
  66.5 9.8 %collective-permute-start.13 = (bf16[2,40,1536]{2,1,0:T(8,128)(2,1)S(1)}, bf16[2,40,1536]{2,1,0:T(8,128)(2,1)S(1)}, u32[]{:S(2)}, u32[]{:S(2)}) collective-permute-start(bf16[2,40,1536]{2,1,0:T(8,128)(2,1)S(1)} %collective-permute-done.11.refs_4_.refs_3_), channel_id=1, source_target_pairs={{0,16},{8,24},{16,0},{24,8},{1,17},{9,25},{17,1},{25,9},{2,18},{10... | collective-permute-start | bytes 737288 | tf_op jit(solution)/shard_map/ppermute | solution.py:27
  67.5 14.2 %collective-permute-start.20 = (bf16[2,40,1536]{2,1,0:T(8,128)(2,1)S(1)}, bf16[2,40,1536]{2,1,0:T(8,128)(2,1)S(1)}, u32[]{:S(2)}, u32[]{:S(2)}) collective-permute-start(bf16[2,40,1536]{2,1,0:T(8,128)(2,1)S(1)} %collective-permute-done.19.refs_2_), channel_id=1, source_target_pairs={{0,8},{8,0},{16,24},{24,16},{1,9},{9,1},{17,25},{25,17},{2,10},{10... | collective-permute-start | bytes 737288 | tf_op jit(solution)/shard_map/ppermute | solution.py:27
  69.9 16.7 %collective-permute-start.12 = (bf16[2,40,1536]{2,1,0:T(8,128)(2,1)S(1)}, bf16[2,40,1536]{2,1,0:T(8,128)(2,1)S(1)}, u32[]{:S(2)}, u32[]{:S(2)}) collective-permute-start(bf16[2,40,1536]{2,1,0:T(8,128)(2,1)S(1)} %collective-permute-done.11.refs_4_.refs_3_), channel_id=1, source_target_pairs={{0,8},{8,0},{16,24},{24,16},{1,9},{9,1},{17,25},{25,17},{2,10},{10... | collective-permute-start | bytes 737288 | tf_op jit(solution)/shard_map/ppermute | solution.py:27
  70.4 16.2 %collective-permute-start.9 = (bf16[2,40,1536]{2,1,0:T(8,128)(2,1)S(1)}, bf16[2,40,1536]{2,1,0:T(8,128)(2,1)S(1)}, u32[]{:S(2)}, u32[]{:S(2)}) collective-permute-start(bf16[2,40,1536]{2,1,0:T(8,128)(2,1)S(1)} %collective-permute-done.7.refs_0_.refs_2_), channel_id=1, source_target_pairs={{0,16},{8,24},{16,0},{24,8},{1,17},{9,25},{17,1},{25,9},{2,18},{10... | collective-permute-start | bytes 737288 | tf_op jit(solution)/shard_map/ppermute | solution.py:27
  74.3 12.3 %collective-permute-start.10 = (bf16[2,40,1536]{2,1,0:T(8,128)(2,1)S(1)}, bf16[2,40,1536]{2,1,0:T(8,128)(2,1)S(1)}, u32[]{:S(2)}, u32[]{:S(2)}) collective-permute-start(bf16[2,40,1536]{2,1,0:T(8,128)(2,1)S(1)} %collective-permute-done.8.refs_1_), channel_id=1, source_target_pairs={{0,16},{8,24},{16,0},{24,8},{1,17},{9,25},{17,1},{25,9},{2,18},{10... | collective-permute-start | bytes 737288 | tf_op jit(solution)/shard_map/ppermute | solution.py:27
  76.3 10.3 %collective-permute-start.14 = (bf16[2,40,1536]{2,1,0:T(8,128)(2,1)S(1)}, bf16[2,40,1536]{2,1,0:T(8,128)(2,1)S(1)}, u32[]{:S(2)}, u32[]{:S(2)}) collective-permute-start(bf16[2,40,1536]{2,1,0:T(8,128)(2,1)S(1)} %collective-permute-done.13.refs_6_), channel_id=1, source_target_pairs={{0,8},{8,0},{16,24},{24,16},{1,9},{9,1},{17,25},{25,17},{2,10},{10... | collective-permute-start | bytes 737288 | tf_op jit(solution)/shard_map/ppermute | solution.py:27
  95.3 14.5 %collective-permute-start.22 = (bf16[2,2,40,1536]{3,2,1,0:T(8,128)(2,1)S(1)}, bf16[2,2,40,1536]{3,2,1,0:T(8,128)(2,1)S(1)}, u32[]{:S(2)}, u32[]{:S(2)}) collective-permute-start(bf16[2,2,40,1536]{3,2,1,0:T(8,128)(2,1)S(1)} %get-tuple-element.81), channel_id=1, source_target_pairs={{0,16},{8,24},{16,0},{24,8},{1,17},{9,25},{17,1},{25,9},{2,18},{10... | collective-permute-start | bytes 1474568 | tf_op jit(solution)/shard_map/ppermute | solution.py:27
  102.6 14.6 %collective-permute-start.24 = (bf16[2,2,40,1536]{3,2,1,0:T(8,128)(2,1)S(1)}, bf16[2,2,40,1536]{3,2,1,0:T(8,128)(2,1)S(1)}, u32[]{:S(2)}, u32[]{:S(2)}) collective-permute-start(bf16[2,2,40,1536]{3,2,1,0:T(8,128)(2,1)S(1)} %get-tuple-element.83), channel_id=1, source_target_pairs={{0,8},{8,0},{16,24},{24,16},{1,9},{9,1},{17,25},{25,17},{2,10},{10... | collective-permute-start | bytes 1474568 | tf_op jit(solution)/shard_map/ppermute | solution.py:27
  107.7 14.0 %collective-permute-start.26 = (bf16[2,2,40,1536]{3,2,1,0:T(8,128)(2,1)S(1)}, bf16[2,2,40,1536]{3,2,1,0:T(8,128)(2,1)S(1)}, u32[]{:S(2)}, u32[]{:S(2)}) collective-permute-start(bf16[2,2,40,1536]{3,2,1,0:T(8,128)(2,1)S(1)} %get-tuple-element.85), channel_id=1, source_target_pairs={{0,16},{8,24},{16,0},{24,8},{1,17},{9,25},{17,1},{25,9},{2,18},{10... | collective-permute-start | bytes 1474568 | tf_op jit(solution)/shard_map/ppermute | solution.py:27
  109.9 9.4 %copy-start.6 = (bf16[6144,16]{0,1:T(8,128)(2,1)S(1)}, bf16[6144,16]{0,1:T(8,128)(2,1)}, u32[]{:S(2)}) copy-start(bf16[6144,16]{0,1:T(8,128)(2,1)} %param.14) | copy-start | bytes 589828
  109.9 11.7 %collective-permute-start.27 = (bf16[1,2,40,1536]{3,2,1,0:T(8,128)(2,1)S(1)}, bf16[1,2,40,1536]{3,2,1,0:T(8,128)(2,1)S(1)}, u32[]{:S(2)}, u32[]{:S(2)}) collective-permute-start(bf16[1,2,40,1536]{3,2,1,0:T(8,128)(2,1)S(1)} %get-tuple-element.87), channel_id=1, source_target_pairs={{0,8},{8,0},{16,24},{24,16},{1,9},{9,1},{17,25},{25,17},{2,10},{10... | collective-permute-start | bytes 737288 | tf_op jit(solution)/shard_map/ppermute | solution.py:27
  115.1 14.8 %collective-permute-start.23 = (bf16[2,1,40,1536]{3,2,1,0:T(8,128)(2,1)S(1)}, bf16[2,1,40,1536]{3,2,1,0:T(8,128)(2,1)S(1)}, u32[]{:S(2)}, u32[]{:S(2)}) collective-permute-start(bf16[2,1,40,1536]{3,2,1,0:T(8,128)(2,1)S(1)} %get-tuple-element.90), channel_id=1, source_target_pairs={{0,8},{8,0},{16,24},{24,16},{1,9},{9,1},{17,25},{25,17},{2,10},{10... | collective-permute-start | bytes 737288 | tf_op jit(solution)/shard_map/ppermute | solution.py:27
  117.2 8.6 %collective-permute-start.25 = (bf16[1,2,40,1536]{3,2,1,0:T(8,128)(2,1)S(1)}, bf16[1,2,40,1536]{3,2,1,0:T(8,128)(2,1)S(1)}, u32[]{:S(2)}, u32[]{:S(2)}) collective-permute-start(bf16[1,2,40,1536]{3,2,1,0:T(8,128)(2,1)S(1)} %get-tuple-element.94), channel_id=1, source_target_pairs={{0,16},{8,24},{16,0},{24,8},{1,17},{9,25},{17,1},{25,9},{2,18},{10... | collective-permute-start | bytes 737288 | tf_op jit(solution)/shard_map/ppermute | solution.py:27
  117.4 12.6 %collective-permute-start.30 = (bf16[2,1,40,1536]{3,2,1,0:T(8,128)(2,1)S(1)}, bf16[2,1,40,1536]{3,2,1,0:T(8,128)(2,1)S(1)}, u32[]{:S(2)}, u32[]{:S(2)}) collective-permute-start(bf16[2,1,40,1536]{3,2,1,0:T(8,128)(2,1)S(1)} %get-tuple-element.108), channel_id=1, source_target_pairs={{0,16},{8,24},{16,0},{24,8},{1,17},{9,25},{17,1},{25,9},{2,18},{10... | collective-permute-start | bytes 737288 | tf_op jit(solution)/shard_map/ppermute | solution.py:27
  121.8 8.2 %collective-permute-start.29 = (bf16[1,2,40,1536]{3,2,1,0:T(8,128)(2,1)S(1)}, bf16[1,2,40,1536]{3,2,1,0:T(8,128)(2,1)S(1)}, u32[]{:S(2)}, u32[]{:S(2)}) collective-permute-start(bf16[1,2,40,1536]{3,2,1,0:T(8,128)(2,1)S(1)} %get-tuple-element.101), channel_id=1, source_target_pairs={{0,8},{8,0},{16,24},{24,16},{1,9},{9,1},{17,25},{25,17},{2,10},{10... | collective-permute-start | bytes 737288 | tf_op jit(solution)/shard_map/ppermute | solution.py:27
  124.0 15.4 %collective-permute-start.31 = (bf16[2,40,1536]{2,1,0:T(8,128)(2,1)S(1)}, bf16[2,40,1536]{2,1,0:T(8,128)(2,1)S(1)}, u32[]{:S(2)}, u32[]{:S(2)}) collective-permute-start(bf16[2,40,1536]{2,1,0:T(8,128)(2,1)S(1)} %reply.5), channel_id=1, source_target_pairs={{0,6},{1,7},{2,4},{3,5},{4,2},{5,3},{6,0},{7,1},{8,14},{9,15},{10,... | collective-permute-start | bytes 737288 | tf_op jit(solution)/shard_map/ppermute | solution.py:27
  125.9 13.5 %collective-permute-start.32 = (bf16[2,40,1536]{2,1,0:T(8,128)(2,1)S(1)}, bf16[2,40,1536]{2,1,0:T(8,128)(2,1)S(1)}, u32[]{:S(2)}, u32[]{:S(2)}) collective-permute-start(bf16[2,40,1536]{2,1,0:T(8,128)(2,1)S(1)} %reply.6), channel_id=1, source_target_pairs={{0,4},{1,5},{2,6},{3,7},{4,0},{5,1},{6,2},{7,3},{8,12},{9,13},{10,... | collective-permute-start | bytes 737288 | tf_op jit(solution)/shard_map/ppermute | solution.py:27
  130.1 9.6 %collective-permute-start.34 = (bf16[2,40,1536]{2,1,0:T(8,128)(2,1)S(1)}, bf16[2,40,1536]{2,1,0:T(8,128)(2,1)S(1)}, u32[]{:S(2)}, u32[]{:S(2)}) collective-permute-start(bf16[2,40,1536]{2,1,0:T(8,128)(2,1)S(1)} %reply.7), channel_id=1, source_target_pairs={{0,2},{1,3},{2,0},{3,1},{4,6},{5,7},{6,4},{7,5},{8,10},{9,11},{10,... | collective-permute-start | bytes 737288 | tf_op jit(solution)/shard_map/ppermute | solution.py:27
  133.2 4.9 %collective-permute-start.28 = (bf16[1,1,40,1536]{3,2,1,0:T(8,128)(2,1)S(1)}, bf16[1,1,40,1536]{3,2,1,0:T(8,128)(2,1)S(1)}, u32[]{:S(2)}, u32[]{:S(2)}) collective-permute-start(bf16[1,1,40,1536]{3,2,1,0:T(8,128)(2,1)S(1)} %get-tuple-element.105), channel_id=1, source_target_pairs={{0,16},{8,24},{16,0},{24,8},{1,17},{9,25},{17,1},{25,9},{2,18},{10... | collective-permute-start | bytes 368648 | tf_op jit(solution)/shard_map/ppermute | solution.py:27
  133.2 6.3 %collective-permute-start.33 = (bf16[1,1,40,1536]{3,2,1,0:T(8,128)(2,1)S(1)}, bf16[1,1,40,1536]{3,2,1,0:T(8,128)(2,1)S(1)}, u32[]{:S(2)}, u32[]{:S(2)}) collective-permute-start(bf16[1,1,40,1536]{3,2,1,0:T(8,128)(2,1)S(1)} %get-tuple-element.110), channel_id=1, source_target_pairs={{0,8},{8,0},{16,24},{24,16},{1,9},{9,1},{17,25},{25,17},{2,10},{10... | collective-permute-start | bytes 368648 | tf_op jit(solution)/shard_map/ppermute | solution.py:27
  140.3 1.8 %collective-permute-start.35 = (bf16[256,768]{1,0:T(8,128)(2,1)S(1)}, bf16[256,768]{1,0:T(8,128)(2,1)S(1)}, u32[]{:S(2)}, u32[]{:S(2)}) collective-permute-start(bf16[256,768]{1,0:T(8,128)(2,1)S(1)} %get-tuple-element.116), channel_id=1, source_target_pairs={{0,1},{1,0},{2,3},{3,2},{4,5},{5,4},{6,7},{7,6},{8,9},{9,8},{10,11... | collective-permute-start | bytes 1179656 | tf_op jit(solution)/shard_map/ppermute | solution.py:27
